TPU v7x, 128 devices: a whole 4x4x4 slice. The times are simulated.
128 devices in a mesh: dp: 16 (over z_lo, x, core), seq: 8 (over y, z_hi).
Axes of the slice: x: 4, y: 4, z: 4 (z_hi: 2, z_lo: 2; z = z_hi * 2 + z_lo), core: 2. Of those that a mesh axis runs over, the one named last changes fastest.
Arguments:
- enc_states: bfloat16 [16, 256, 4096], P('dp'), may hold values from -6 to 6
- lengths: int32 [16], replicated, may hold values from 1 to 128, as said below
- prompt_owner_sample: int32 [16], replicated, may hold values from 0 to 15, each once
- t5_gain: float32 [4096], replicated, may hold values from 0.5 to 1.5
- t5_in_weight: bfloat16 [2, 4096, 5120], P(None, None, 'seq'), may hold values from -0.09375 to 0.09375
- t5_out_weight: bfloat16 [5120, 4096], P('seq'), may hold values from -0.078125 to 0.078125
- t5_final_gain: float32 [4096], replicated, may hold values from 0.5 to 1.5
- context_weight: bfloat16 [4096, 3072], P('seq', 'dp'), may hold values from -0.09375 to 0.09375
- text_shift: float32 [16, 3072], P('dp'), may hold values from -3 to 3
- text_scale: float32 [16, 3072], P('dp'), may hold values from -0.5 to 0.5
- kv_weight: bfloat16 [3072, 2, 3072], P('dp', None, 'seq'), may hold values from -0.109375 to 0.109375
- text_key_gain: float32 [128], replicated, may hold values from 0.25 to 1.75
- image_query_key_value: bfloat16 [16, 1024, 3, 3072], P('dp', 'seq'), may hold values from -6 to 6
- image_qk_gain: float32 [2, 128], replicated, may hold values from 0.25 to 1.75
- proj_weight: bfloat16 [3072, 3072], P('seq', 'dp'), may hold values from -0.109375 to 0.109375
- dora_a: float32 [3072, 64], P('seq'), may hold values from -0.109375 to 0.109375
- dora_b: float32 [64, 3072], P(None, 'dp'), may hold values from -0.375 to 0.375
- magnitude: float32 [3072], P('dp'), may hold values from 0.5 to 2
- grad_out: bfloat16 [16, 1024, 3072], P('dp', 'seq'), may hold values from -6 to 6
Outputs:
- image_out: bfloat16 [16, 1024, 3072], P('dp', 'seq')
- grad_a: float32 [3072, 64], P('seq')
- grad_b: float32 [64, 3072], P(None, 'dp')
- grad_magnitude: float32 [3072], P('dp')
Inputs may be any that keep to these rules, and one draw needn't show every extreme that they name: `lengths`: prompt token counts; in every draw one prompt has exactly 128 tokens. `prompt_owner_sample`: each DiT sample index appears exactly once.
All inputs are finite; a program needn't handle non-finite values.
Results may differ from a plain program's by a relative error of at most 0.024.
Values may be sent and summed in bfloat16 or wider, within the bound.
No kernel may reach another device: no remote copies, remote signals or barrier semaphores. Data moves between devices by JAX's collectives and lax.ppermute only.
A program may use at most 128 MiB of HBM per device.

v0:
```python
import math

import jax
import jax.numpy as jnp
from jax import lax
from jax.sharding import PartitionSpec as P

HD = 128


EPSILON = 1e-06


def rms_scale(values, gain):
    return values * lax.rsqrt(jnp.mean(values * values, -1, keepdims=True) + EPSILON) * gain


def on_device(
    enc_states,
    lengths,
    prompt_owner_sample,
    t5_gain,
    t5_in_weight,
    t5_out_weight,
    t5_final_gain,
    context_weight,
    text_shift,
    text_scale,
    kv_weight,
    text_key_gain,
    image_query_key_value,
    image_qk_gain,
    proj_weight,
    dora_a,
    dora_b,
    magnitude,
    grad_out,
):
    seq_rank = lax.axis_index("seq")
    data_rank = lax.axis_index("dp")
    seq_devices = lax.axis_size("seq")
    tokens = enc_states[0]
    text_length, width_enc = tokens.shape
    feat_width = width_enc // seq_devices
    own_tokens = lax.dynamic_slice_in_dim(tokens, seq_rank * feat_width, feat_width, 1).astype(
        jnp.float32
    )
    own_final = lax.dynamic_slice_in_dim(t5_final_gain, seq_rank * feat_width, feat_width, 0)
    prompt_indices = jnp.arange(prompt_owner_sample.shape[0], dtype=jnp.int32)
    normed = rms_scale(tokens.astype(jnp.float32), t5_gain).astype(jnp.bfloat16)
    gate_proj = jnp.dot(normed, t5_in_weight[0], preferred_element_type=jnp.float32)
    upward = jnp.dot(normed, t5_in_weight[1], preferred_element_type=jnp.float32)
    hidden = (jax.nn.gelu(gate_proj, approximate=True) * upward).astype(jnp.bfloat16)
    ffn_part = lax.psum_scatter(
        jnp.dot(hidden, t5_out_weight, preferred_element_type=jnp.float32).astype(jnp.bfloat16),
        "seq",
        scatter_dimension=1,
        tiled=True,
    ).astype(jnp.float32)
    encoded = ((own_tokens + ffn_part) * own_final).astype(jnp.bfloat16)
    context_part = jnp.dot(
        encoded,
        lax.all_gather(context_weight, "dp", axis=1, tiled=True),
        preferred_element_type=jnp.float32,
    )
    text_tokens = lax.psum_scatter(
        context_part.astype(jnp.bfloat16), "seq", scatter_dimension=0, tiled=True
    )
    source_sample = jnp.sum(jnp.where(prompt_owner_sample == data_rank, prompt_indices, 0))
    diffusion_length = jnp.sum(jnp.where(prompt_indices == source_sample, lengths, 0))
    shard_piece = lax.all_gather(text_tokens[None], "dp", axis=0, tiled=True)
    chosen = jnp.arange(shard_piece.shape[0], dtype=jnp.int32) == source_sample
    picked = jnp.sum(
        jnp.where(chosen[:, None, None], shard_piece, jnp.zeros_like(shard_piece)), 0, keepdims=True
    )
    routed = picked[0]
    routed_values = routed.astype(jnp.float32)
    centre = jnp.mean(routed_values, -1, keepdims=True)
    spread = jnp.mean((routed_values - centre) * (routed_values - centre), -1, keepdims=True)
    layer_normed = (routed_values - centre) * lax.rsqrt(spread + EPSILON)
    modulated = ((1.0 + text_scale) * layer_normed + text_shift).astype(jnp.bfloat16)
    text_all = lax.all_gather(modulated, "seq", axis=0, tiled=True)
    head_width = kv_weight.shape[2]
    local_heads = head_width // HD
    shard_piece = lax.all_gather(kv_weight, "dp", axis=0, tiled=True)
    key_value = jnp.dot(
        text_all,
        shard_piece.reshape(shard_piece.shape[0], 2 * head_width),
        preferred_element_type=jnp.float32,
    )
    key_value = key_value.reshape(text_length, 2, local_heads, HD)
    prompt_key_rows = rms_scale(key_value[:, 0], text_key_gain).astype(jnp.bfloat16)
    prompt_value_rows = key_value[:, 1].astype(jnp.bfloat16)
    exchanged = lax.all_to_all(
        image_query_key_value[0], "seq", split_axis=2, concat_axis=0, tiled=True
    )
    image_len = exchanged.shape[0]
    split_heads = exchanged.reshape(image_len, 3, local_heads, HD)
    queries = rms_scale(split_heads[:, 0].astype(jnp.float32), image_qk_gain[0]).astype(
        jnp.bfloat16
    )
    key_image = rms_scale(split_heads[:, 1].astype(jnp.float32), image_qk_gain[1]).astype(
        jnp.bfloat16
    )
    value_image = split_heads[:, 2]
    key_valid_mask = jnp.arange(text_length, dtype=jnp.int32) < diffusion_length
    score_scale = 1.0 / math.sqrt(HD)
    query_rows = min(512, image_len)
    block_count = image_len // query_rows

    def attend_block(query_block):
        text_scores = (
            jnp.einsum(
                "qhd,khd->hqk", query_block, prompt_key_rows, preferred_element_type=jnp.float32
            )
            * score_scale
        )
        text_weight = jnp.where(key_valid_mask[None, None, :], jnp.exp(text_scores), 0.0)
        image_scores = (
            jnp.einsum("qhd,khd->hqk", query_block, key_image, preferred_element_type=jnp.float32)
            * score_scale
        )
        image_weight = jnp.exp(image_scores)
        denominator = jnp.sum(text_weight, -1) + jnp.sum(image_weight, -1)
        text_probs = (text_weight / denominator[..., None]).astype(jnp.bfloat16)
        image_probs = (image_weight / denominator[..., None]).astype(jnp.bfloat16)
        mixture = jnp.einsum(
            "hqk,khd->qhd", text_probs, prompt_value_rows, preferred_element_type=jnp.float32
        )
        mixture = mixture + jnp.einsum(
            "hqk,khd->qhd", image_probs, value_image, preferred_element_type=jnp.float32
        )
        return mixture.astype(jnp.bfloat16)

    attended_rows = lax.map(
        attend_block, queries.reshape(block_count, query_rows, local_heads, HD)
    ).reshape(image_len, head_width)
    base_rows = lax.all_gather(proj_weight, "dp", axis=1, tiled=True)
    adapter_up, magnitudes = (
        lax.all_gather(dora_b.astype(jnp.bfloat16), "dp", axis=1, tiled=True).astype(dora_b.dtype),
        lax.all_gather(magnitude.astype(jnp.bfloat16), "dp", axis=0, tiled=True).astype(
            magnitude.dtype
        ),
    )
    direction = base_rows.astype(jnp.float32) + jnp.dot(
        dora_a, adapter_up, precision=lax.Precision.HIGHEST
    )
    column_sq = lax.psum(jnp.sum(direction * direction, 0), "seq")
    column_norm = jnp.sqrt(column_sq + EPSILON)
    column_ratio = magnitudes / column_norm
    scaled = (direction * column_ratio).astype(jnp.bfloat16)
    row_block = attended_rows
    image_out = lax.psum_scatter(
        jnp.dot(row_block, scaled, preferred_element_type=jnp.float32).astype(jnp.bfloat16),
        "seq",
        scatter_dimension=0,
        tiled=True,
    )[None]
    row_block = attended_rows
    weight_grad = jnp.einsum(
        "th,td->hd",
        row_block,
        lax.all_gather(grad_out[0], "seq", axis=0, tiled=True),
        preferred_element_type=jnp.float32,
    )
    own_cols = magnitude.shape[0]
    first_col = data_rank * own_cols
    grad_own = lax.psum_scatter(
        weight_grad.astype(jnp.bfloat16), "dp", scatter_dimension=1, tiled=True
    ).astype(jnp.float32)
    direction_own = lax.dynamic_slice_in_dim(direction, first_col, own_cols, 1)
    norm_own = lax.dynamic_slice_in_dim(column_norm, first_col, own_cols, 0)
    scaled_grad = grad_own * (magnitude / norm_own)
    magnitude_part = jnp.sum(grad_own * direction_own, 0) / norm_own
    up_part = jnp.dot(dora_a.T, scaled_grad, precision=lax.Precision.HIGHEST)
    grad_magnitude, grad_b = (
        lax.psum(magnitude_part.astype(jnp.bfloat16), "seq").astype(jnp.float32),
        lax.psum(up_part.astype(jnp.bfloat16), "seq").astype(jnp.float32),
    )
    down_part = jnp.dot(scaled_grad, dora_b.T, precision=lax.Precision.HIGHEST)
    grad_a = lax.psum(down_part.astype(jnp.bfloat16), "dp").astype(jnp.float32)
    return (image_out, grad_a, grad_b, grad_magnitude)


def solution(mesh):
    return jax.shard_map(
        on_device,
        mesh=mesh,
        in_specs=(
            P("dp", None, None),
            P(),
            P(),
            P(),
            P(None, None, "seq"),
            P("seq", None),
            P(),
            P("seq", "dp"),
            P("dp", None),
            P("dp", None),
            P("dp", None, "seq"),
            P(),
            P("dp", "seq", None, None),
            P(),
            P("seq", "dp"),
            P("seq", None),
            P(None, "dp"),
            P("dp"),
            P("dp", "seq", None),
        ),
        out_specs=(P("dp", "seq", None), P("seq", None), P(None, "dp"), P("dp")),
        check_vma=False,
    )
```

profile of v0, /device:TPU:1, one launch (start us, length us, event | category | flops | bytes accessed | tf_op | source)
XLA Modules:
  0.0 706.1 jit_solution(17486732101180593249)
XLA Ops:
  8.1 2.1 fusion.26
  10.2 5.2 fusion.52
  15.4 8.9 %convolution_convert_fusion.1 = bf16[256,4096]{1,0:T(8,128)(2,1)} fusion(bf16[640,4096]{1,0:T(8,128)(2,1)} %param.26, f32[256,640]{1,0:T(8,128)S(1)} %fusion.52, bf16[2,4096,640]{2,1,0:T(8,128)(2,1)} %param.25, bf16[1,256,4096]{2,1,0:T(8,128)(2,1)S(1)} %copy-done.2, f32[4096]{0:T(1024)S(1)} %copy-done.14, f32[256]{0:T(256)S(1)} %add_rsqrt_fusion.3), kind=kOutput, calls=%fused_computation.31 | convolution fusion | flops 2689925120 | bytes 15352832 | tf_op jit(solution)/shard_map/dot_general | solution.py:55
  25.0 0.8 dynamic_slice.17
  25.7 77.4 %reduce-scatter.7.cloned.1.call-done = bf16[256,512]{1,0:T(8,128)(2,1)} async-done(((bf16[256,4096]{1,0:T(8,128)(2,1)}), bf16[256,512]{1,0:T(8,128)(2,1)}) %reduce-scatter.7.cloned.1.call-update) | async-done | bytes 262160 | tf_op jit(solution)/shard_map/reduce_scatter | solution.py:54
  103.2 4.2 convolution_convert_fusion.2
  107.4 73.2 %reduce-scatter.9.cloned.1.call-done = bf16[32,3072]{1,0:T(8,128)(2,1)} async-done(((bf16[256,3072]{1,0:T(8,128)(2,1)}), bf16[32,3072]{1,0:T(8,128)(2,1)}) %reduce-scatter.9.cloned.1.call-update) | async-done | bytes 196624 | tf_op jit(solution)/shard_map/reduce_scatter | solution.py:66
  181.3 0.6 fusion.76
  181.9 0.6 iota_compare_fusion.1
  182.6 34.2 %all-gather.18.cloned.1.call-done = bf16[512,3072]{1,0:T(8,128)(2,1)} async-done(((bf16[32,3072]{1,0:T(8,128)(2,1)}), bf16[512,3072]{1,0:T(8,128)(2,1)}) %all-gather.18.cloned.1.call-update) | async-done | bytes 3145744 | tf_op jit(solution)/shard_map/all_gather | solution.py:71
  216.8 2.4 select_reduce_fusion
  219.6 0.8 fusion.67
  220.5 0.7 all-gather.20.cloned.1.call-update
  221.2 3.6 copy.45
  224.9 6.3 all-to-all-start
  231.2 0.7 all-gather.16.cloned.1.call-update
  232.2 1.3 select_reduce_fusion.1
  233.4 44.0 %all-to-all-done = bf16[128,3,3072]{0,1,2:T(4,128)(2,1)S(1)} async-done(((bf16[128,3,3072]{0,1,2:T(4,128)(2,1)}), bf16[128,3,3072]{0,1,2:T(4,128)(2,1)S(1)}, u32[]{:S(2)}, u32[]{:S(2)}) %all-to-all-start) | async-done | bytes 2359328 | tf_op jit(solution)/shard_map/all_to_all | solution.py:94
  277.4 3.4 copy.65
  280.8 3.7 reshape.132
  284.5 1.6 slice_bitcast_fusion
  286.5 3.4 reshape.135
  289.9 3.6 copy.48
  293.6 1.1 fusion.36
  294.7 1.6 copy.51
  296.4 2.3 copy.53
  299.2 12.5 %copy.60 = bf16[3072,2,384]{0,2,1:T(8,128)(2,1)} copy(bf16[3072,2,384]{2,1,0:T(2,128)(2,1)} %all-gather.14.cloned.1.call-done) | data formatting | bytes 9437184 | tf_op jit(solution)/shard_map/reshape | solution.py:88
  311.6 29.4 %all-gather.12.cloned.1.call-done = bf16[256,3072]{1,0:T(8,128)(2,1)} async-done(((bf16[32,3072]{1,0:T(8,128)(2,1)}), bf16[256,3072]{1,0:T(8,128)(2,1)}) %all-gather.12.cloned.1.call-update) | async-done | bytes 1572880 | tf_op jit(solution)/shard_map/all_gather | solution.py:82
  341.0 4.3 fusion.37
  345.4 0.8 multiply_convert_fusion.3
  346.2 1.7 copy.50
  347.9 0.8 copy.52
  348.8 10.7 %while.11 = (s32[]{:T(128)}, bf16[2,512,3,128]{3,1,2,0:T(8,128)(2,1)S(1)}, bf16[2,512,3,128]{3,1,2,0:T(8,128)(2,1)S(1)}, bf16[256,3,128]{2,0,1:T(8,128)(2,1)}, b...) while((s32[]{:T(128)}, ...), condition=%wide.region_14.15_spmd.clone, body=%wide.region_11.14_spmd.clone.sunk | while | flops 1016855296 | bytes 21279624 | solution.py:135
  348.8 0.7 iota_compare_fusion.3
  349.4 1.4 fusion.105
  350.8 1.2 fusion.104
  352.0 1.5 fusion.106
  353.6 0.5 fusion.107
  354.1 0.7 iota_compare_fusion.3
  354.8 1.4 fusion.105
  356.2 1.2 fusion.104
  357.4 1.5 fusion.106
  358.9 0.5 fusion.107
  359.5 0.9 copy.54
  360.5 72.1 %all-gather.20.cloned.1.call-done = bf16[1,1024,3072]{2,1,0:T(8,128)(2,1)} async-done(((bf16[1,128,3072]{2,1,0:T(8,128)(2,1)}), bf16[1,1024,3072]{2,1,0:T(8,128)(2,1)}) %all-gather.20.cloned.1.call-update) | async-done | bytes 6291472 | tf_op jit(solution)/shard_map/all_gather | solution.py:163
  432.6 7.8 %fusion.29 = bf16[3072,384]{1,0:T(8,128)(2,1)} fusion(bf16[1024,384]{0,1:T(8,128)(2,1)S(1)} %bitcast.146, bf16[1,1024,3072]{2,1,0:T(8,128)(2,1)} %all-gather.20.cloned.1.call-done), kind=kOutput, calls=%fused_computation.39 | convolution fusion | flops 2417098752 | bytes 9437184 | tf_op jit(solution)/shard_map/th,td->hd/dot_general | solution.py:160
  440.5 21.6 %all-gather.2 = bf16[16,192,64]{1,2,0:T(8,128)(2,1)S(1)} all-gather(bf16[1,192,64]{1,2,0:T(8,128)(2,1)S(1)} %convert_bitcast_fusion), channel_id=1, replica_groups=mesh['dp'=16,'seq'=8] {'dp'}, dimensions={0}, use_global_device_ids=true | all-gather | bytes 417792 | tf_op jit(solution)/shard_map/all_gather | solution.py:140
  462.4 0.5 reshape.144
  462.9 0.6 dynamic-slice.1
  464.2 4.6 all-gather.16.cloned.1.call-done
  468.7 2.8 copy.55
  471.6 4.7 multiply_reduce_fusion
  476.3 34.3 %psum.28 = f32[3072]{0:T(1024)S(1)} all-reduce(f32[3072]{0:T(1024)S(1)} %get-tuple-element.121), channel_id=1, replica_groups=mesh['dp'=16,'seq'=8] {'seq'}, use_global_device_ids=true, to_apply=%region_16.17 | all-reduce | flops 3072 | bytes 24576 | tf_op jit(solution)/shard_map/psum | solution.py:148
  510.6 20.4 %reduce-scatter.13.cloned.1.call-done = bf16[192,384]{1,0:T(8,128)(2,1)} async-done(((bf16[3072,384]{1,0:T(8,128)(2,1)}), bf16[192,384]{1,0:T(8,128)(2,1)}) %reduce-scatter.13.cloned.1.call-update) | async-done | bytes 147472
  531.0 1.0 copy.62
  532.0 1.3 fusion.68
  533.4 0.6 convolution_convert_fusion.3
  534.2 53.4 %all-reduce.1 = (bf16[3072]{0:T(1024)(128)(2,1)S(1)}, bf16[384,64]{0,1:T(8,128)(2,1)S(1)}) all-reduce(bf16[3072]{0:T(1024)(128)(2,1)S(1)} %dynamic-update-slice, bf16[384,64]{0,1:T(8,128)(2,1)S(1)} %convolution_convert_fusion.3), channel_id=1, replica_groups=mesh['dp'=16,'seq'=8] {'dp'}, use_global_device_ids=true, to_apply=%add | all-reduce | flops 27648 | bytes 110592
  587.6 8.7 %convolution_convert_fusion = bf16[1024,3072]{1,0:T(8,128)(2,1)} fusion(bf16[1024,384]{0,1:T(8,128)(2,1)} %bitcast.147, f32[384,3072]{1,0:T(8,128)} %get-tuple-element.122, f32[3072]{0:T(1024)S(1)} %convert_divide_fusion), kind=kOutput, calls=%fused_computation.22 | convolution fusion | flops 2421424128 | bytes 11808768 | tf_op jit(solution)/shard_map/dot_general | solution.py:154
  596.7 35.7 %all-reduce.2 = (bf16[64,192]{1,0:T(8,128)(2,1)S(1)}, bf16[192]{0:T(256)(128)(2,1)S(1)}) all-reduce(bf16[64,192]{1,0:T(8,128)(2,1)S(1)} %fusion.45, bf16[192]{0:T(256)(128)(2,1)S(1)} %get-tuple-element.116), channel_id=1, replica_groups=mesh['dp'=16,'seq'=8] {'seq'}, use_global_device_ids=true, to_apply=%region_20.21 | all-reduce | flops 12480 | bytes 49920 | tf_op jit(solution)/shard_map/psum | solution.py:178
  632.4 0.6 convert_element_type.166
  633.1 0.6 convert_element_type.168
  633.6 0.6 convert_element_type.163
  634.3 64.7 %reduce-scatter.11.cloned.1.call-done = bf16[128,3072]{1,0:T(8,128)(2,1)} async-done(((bf16[1024,3072]{1,0:T(8,128)(2,1)}), bf16[128,3072]{1,0:T(8,128)(2,1)}) %reduce-scatter.11.cloned.1.call-update) | async-done | bytes 786448 | tf_op jit(solution)/shard_map/reduce_scatter | solution.py:153
  (85 shorter events, 4.4 us)
Async XLA Ops:
  8.0 463.6 %copy-start = (f32[384,64]{0,1:T(8,128)S(1)}, f32[384,64]{0,1:T(8,128)}, u32[]{:S(2)}) copy-start(f32[384,64]{0,1:T(8,128)} %param.36) | copy-start | bytes 294916
  8.0 95.2 %reduce-scatter.7.cloned.1.call-start = ((), (), s32[]{:S(2)}) async-start(), calls=%async_computation.5 | async-start | bytes 2359296 | tf_op jit(solution)/shard_map/reduce_scatter | solution.py:54
  10.2 5.2 copy-start.2
  10.2 5.2 copy-start.14
  24.3 78.9 %all-gather.10.cloned.1.call-start = ((), (), s32[]{:S(2)}) async-start(), calls=%async_computation.6 | async-start | bytes 3342336 | tf_op jit(solution)/shard_map/all_gather | solution.py:63
  24.9 155.7 %reduce-scatter.9.cloned.1.call-start = ((), (), s32[]{:S(2)}) async-start(), calls=%async_computation.7 | async-start | bytes 1769472 | tf_op jit(solution)/shard_map/reduce_scatter | solution.py:66
  25.7 155.5 %copy-start.15 = (s32[16]{0:T(128)S(1)}, s32[16]{0:T(128)}, u32[]{:S(2)}) copy-start(s32[16]{0:T(128)} %param.23) | copy-start | bytes 196
  25.7 156.8 %copy-start.10 = (f32[1,3072]{1,0:T(1,128)S(1)}, f32[1,3072]{1,0:T(1,128)}, u32[]{:S(2)}) copy-start(f32[1,3072]{1,0:T(1,128)} %param.30) | copy-start | bytes 36868
  107.3 112.3 %copy-start.9 = (f32[1,3072]{1,0:T(1,128)S(1)}, f32[1,3072]{1,0:T(1,128)}, u32[]{:S(2)}) copy-start(f32[1,3072]{1,0:T(1,128)} %param.29) | copy-start | bytes 36868
  107.4 113.9 %copy-start.3 = (bf16[1,128,3,3072]{3,1,2,0:T(8,128)(2,1)S(1)}, bf16[1,128,3,3072]{3,1,2,0:T(8,128)(2,1)}, u32[]{:S(2)}) copy-start(bf16[1,128,3,3072]{3,1,2,0:T(8,128)(2,1)} %param.33) | copy-start | bytes 7077892
  107.4 109.4 %all-gather.18.cloned.1.call-start = ((), (), s32[]{:S(2)}) async-start(), calls=%async_computation.12 | async-start | bytes 3342336 | tf_op jit(solution)/shard_map/all_gather | solution.py:71
  180.6 118.5 %all-gather.14.cloned.1.call-start = ((), (), s32[]{:S(2)}) async-start(), calls=%async_computation.9 | async-start | bytes 5013504 | tf_op jit(solution)/shard_map/all_gather | solution.py:85
  181.2 159.8 %all-gather.12.cloned.1.call-start = ((), (), s32[]{:S(2)}) async-start(), calls=%async_computation.8 | async-start | bytes 1769472 | tf_op jit(solution)/shard_map/all_gather | solution.py:82
  220.5 212.2 %all-gather.20.cloned.1.call-start = ((), (), s32[]{:S(2)}) async-start(), calls=%async_computation.13 | async-start | bytes 7077888 | tf_op jit(solution)/shard_map/all_gather | solution.py:163
  224.9 7.3 %copy-start.16 = (s32[16]{0:T(128)S(1)}, s32[16]{0:T(128)}, u32[]{:S(2)}) copy-start(s32[16]{0:T(128)} %param.22) | copy-start | bytes 196
  224.9 8.6 %copy-start.11 = (f32[2,128]{1,0:T(2,128)S(1)}, f32[2,128]{1,0:T(2,128)}, u32[]{:S(2)}) copy-start(f32[2,128]{1,0:T(2,128)} %param.34) | copy-start | bytes 3076
  224.9 52.5 %all-to-all-start = ((bf16[128,3,3072]{0,1,2:T(4,128)(2,1)}), bf16[128,3,3072]{0,1,2:T(4,128)(2,1)S(1)}, u32[]{:S(2)}, u32[]{:S(2)}) async-start(bf16[128,3,3072]{0,1,2:T(4,128)(2,1)} %bitcast.141), calls=%async_computation | async-start | bytes 6291456 | tf_op jit(solution)/shard_map/all_to_all | solution.py:94
  231.2 237.6 %all-gather.16.cloned.1.call-start = ((), (), s32[]{:S(2)}) async-start(), calls=%async_computation.10 | async-start | bytes 2506752 | tf_op jit(solution)/shard_map/all_gather | solution.py:138
  231.9 299.1 %reduce-scatter.13.cloned.1.call-start = ((), (), s32[]{:S(2)}) async-start(), calls=%async_computation.14 | async-start | bytes 2506752
  294.7 3.9 copy-start.1
  341.0 4.5 copy-start.13
  341.0 7.8 %copy-start.5 = (bf16[1024,3,128]{2,0,1:T(8,128)(2,1)S(1)}, bf16[1024,3,128]{2,0,1:T(8,128)(2,1)}, u32[]{:S(2)}) copy-start(bf16[1024,3,128]{2,0,1:T(8,128)(2,1)} %copy.53) | copy-start | bytes 2359300
  341.0 7.8 %copy-start.6 = (bf16[2,512,3,128]{3,1,2,0:T(8,128)(2,1)S(1)}, bf16[2,512,3,128]{3,1,2,0:T(8,128)(2,1)}, u32[]{:S(2)}) copy-start(bf16[2,512,3,128]{3,1,2,0:T(8,128)(2,1)} %custom-call) | copy-start | bytes 2359300
  352.0 1.6 copy-start.8
  357.4 1.6 copy-start.8
  360.5 79.9 %copy-start.4 = (bf16[48,8,2,512]{3,1,2,0:T(8,128)(2,1)}, bf16[48,8,2,512]{3,1,2,0:T(8,128)(2,1)S(1)}, u32[]{:S(2)}) copy-start(bf16[48,8,2,512]{3,1,2,0:T(8,128)(2,1)S(1)} %copy.63) | copy-start | bytes 2359300
  432.6 7.8 %copy-start.7 = (f32[64,192]{1,0:T(8,128)S(1)}, f32[64,192]{1,0:T(8,128)}, u32[]{:S(2)}) copy-start(f32[64,192]{1,0:T(8,128)} %param.37) | copy-start | bytes 147460
  440.4 22.5 %copy-start.17 = (u32[128]{0:T(128)S(1)}, u32[128]{0:T(128)}, u32[]{:S(2)}) copy-start(u32[128]{0:T(128)} %constant.75) | copy-start | bytes 1540
  440.4 258.6 %reduce-scatter.11.cloned.1.call-start = ((), (), s32[]{:S(2)}) async-start(), calls=%async_computation.11 | async-start | bytes 7077888 | tf_op jit(solution)/shard_map/reduce_scatter | solution.py:153
  471.6 61.7 %copy-start.12 = (f32[192]{0:T(256)S(1)}, f32[192]{0:T(256)}, u32[]{:S(2)}) copy-start(f32[192]{0:T(256)} %param.38) | copy-start | bytes 2308
Sparse Core Ops, SparseCore 0:
  24.5 78.6 reduce-scatter.6
  107.5 73.0 reduce-scatter.8
  596.5 102.4 reduce-scatter.10
Sparse Core Ops, SparseCore 1:
  26.6 41.1 all-gather.9
  180.7 36.0 all-gather.17
  218.5 70.7 all-gather.13
  291.8 49.1 all-gather.11
  343.6 89.0 all-gather.19
  434.5 34.2 all-gather.15
  471.1 59.8 reduce-scatter.12
where the time goes:
time: 707 us; the launch traced here: 706 us
  waiting for transfers between devices  422 us (60%)
  blocking collectives  145 us (21%)
  matrix products  54 us (8%)
  local copies, waits for them, and re-layouts  44.1 us (6%)
  other arithmetic  17.3 us (2%)
  between operations  16.3 us (2%)
    reduce_scatter x1, waiting for transfers between devices, on_device(): lax.psum_scatter(jnp.dot(hidden, t5_out_weight, preferred_element_type=jn...  77.4 us
    reduce_scatter x1, waiting for transfers between devices, on_device(): lax.psum_scatter(context_part.astype(jnp.bfloat16), 'seq', scatter_dimens...  73.2 us
    all_gather x1, waiting for transfers between devices, on_device(): lax.all_gather(grad_out[0], 'seq', axis=0, tiled=True)  72.1 us
    reduce_scatter x1, waiting for transfers between devices, on_device(): lax.psum_scatter(jnp.dot(row_block, scaled, preferred_element_type=jnp.fl...  64.7 us
    unnamed x1, blocking collectives  53.4 us
    all_to_all x1, waiting for transfers between devices, on_device(): lax.all_to_all(image_query_key_value[0], 'seq', split_axis=2, concat_axis...  44 us
    psum x1, blocking collectives, on_device(): lax.psum(up_part.astype(jnp.bfloat16), 'seq').astype(jnp.float32)  35.7 us
    psum x1, blocking collectives, on_device(): column_sq = lax.psum(jnp.sum(direction * direction, 0), 'seq')  34.3 us
  transfers between devices with their start and end apart: 11, of which 9 were waited for; matrix products, arithmetic and copies ran while one was open for 12% of the time, Pallas kernels for 0%

commit v1 on v0

v1 whole, which is shorter than its diff:
```python
import math

import jax
import jax.numpy as jnp
from jax import lax
from jax.experimental import pallas as pl
from jax.experimental.pallas import tpu as pltpu
from jax.sharding import PartitionSpec as P

HD = 128
BLK = 128
EPSILON = 1e-06
F32 = jnp.float32
BF16 = jnp.bfloat16
Y_GROUPS = [[0, 2, 4, 6], [1, 3, 5, 7]]
Z_GROUPS = [[0, 1], [2, 3], [4, 5], [6, 7]]


def rms_scale(values, gain):
    return values * lax.rsqrt(jnp.mean(values * values, -1, keepdims=True) + EPSILON) * gain


def swap(values, axes, groups=None):
    return lax.all_to_all(values, axes, 0, 0, tiled=True, axis_index_groups=groups)


def dot_t(left, right):
    return lax.dot_general(left, right, (((1,), (1,)), ((), ())), preferred_element_type=F32)


def image_kernel(q_ref, k_ref, v_ref, gain_ref, num_ref, den_ref, keys, values):
    @pl.when(pl.program_id(1) == 0)
    def _():
        k = k_ref[...].reshape(-1, HD).astype(F32)
        keys[...] = rms_scale(k, gain_ref[1:2, :]).astype(BF16)
        values[:, :HD] = v_ref[...].reshape(-1, HD)
        values[:, HD:] = jnp.ones((values.shape[0], HD), BF16)

    q = q_ref[...].reshape(-1, HD).astype(F32)
    q = rms_scale(q, gain_ref[0:1, :] * (math.log2(math.e) / math.sqrt(HD))).astype(BF16)
    weight = jnp.exp2(dot_t(q, keys[...])).astype(BF16)
    both = jnp.dot(weight, values[...], preferred_element_type=F32)
    num_ref[...] = both[:, :HD]
    den_ref[...] = both[:, HD:]


def image_attention(received, gains):
    sources, _, width = received.shape
    heads = width // HD
    image_len = sources * BLK
    step = 2
    rows = step * BLK
    return pl.pallas_call(
        image_kernel,
        grid=(heads, sources // step),
        in_specs=[
            pl.BlockSpec((step, BLK, HD), lambda h, b: (b, 0, h)),
            pl.BlockSpec((sources, BLK, HD), lambda h, b: (0, 1, h)),
            pl.BlockSpec((sources, BLK, HD), lambda h, b: (0, 2, h)),
            pl.BlockSpec((2, HD), lambda h, b: (0, 0)),
        ],
        out_specs=[
            pl.BlockSpec((rows, HD), lambda h, b: (b, h)),
            pl.BlockSpec((rows, HD), lambda h, b: (b, h)),
        ],
        out_shape=[jax.ShapeDtypeStruct((image_len, width), F32)] * 2,
        scratch_shapes=[pltpu.VMEM((image_len, HD), BF16), pltpu.VMEM((image_len, 2 * HD), BF16)],
        compiler_params=pltpu.CompilerParams(vmem_limit_bytes=24 * 1024 * 1024),
        cost_estimate=pl.CostEstimate(
            flops=6 * image_len * image_len * width,
            bytes_accessed=14 * image_len * width,
            transcendentals=heads * image_len * image_len,
        ),
    )(received, received, received, gains)


def text_kernel(length_ref, q_ref, k_ref, v_ref, gain_ref, text_gain_ref, num_ref, den_ref, out_ref):
    k = rms_scale(k_ref[...], text_gain_ref[...]).astype(BF16)
    v = v_ref[...].astype(BF16)
    q = q_ref[...].reshape(-1, HD).astype(F32)
    q = rms_scale(q, gain_ref[0:1, :] * (math.log2(math.e) / math.sqrt(HD))).astype(BF16)
    weight = jnp.exp2(dot_t(q, k))
    valid = lax.broadcasted_iota(jnp.int32, weight.shape, 1) < length_ref[0]
    weight = jnp.where(valid, weight, 0.0).astype(BF16)
    stacked = jnp.concatenate([v, jnp.ones_like(v)], axis=1)
    both = jnp.dot(weight, stacked, preferred_element_type=F32)
    total = num_ref[...] + both[:, :HD]
    out_ref[...] = (total / (den_ref[...] + both[:, HD:])).astype(BF16)


def text_attention(length, received, key_value, gains, text_gain, num, den):
    sources, _, width = received.shape
    heads = width // HD
    image_len = sources * BLK
    step = sources // 2
    rows = step * BLK
    return pl.pallas_call(
        text_kernel,
        grid=(heads, sources // step),
        in_specs=[
            pl.BlockSpec(memory_space=pltpu.SMEM),
            pl.BlockSpec((step, BLK, HD), lambda h, b: (b, 0, h)),
            pl.BlockSpec((BLK, HD), lambda h, b: (0, h)),
            pl.BlockSpec((BLK, HD), lambda h, b: (0, heads + h)),
            pl.BlockSpec((2, HD), lambda h, b: (0, 0)),
            pl.BlockSpec((1, HD), lambda h, b: (0, 0)),
            pl.BlockSpec((rows, HD), lambda h, b: (b, h)),
            pl.BlockSpec((rows, HD), lambda h, b: (b, h)),
        ],
        out_specs=pl.BlockSpec((rows, HD), lambda h, b: (b, h)),
        out_shape=jax.ShapeDtypeStruct((image_len, width), BF16),
        compiler_params=pltpu.CompilerParams(vmem_limit_bytes=24 * 1024 * 1024),
        cost_estimate=pl.CostEstimate(
            flops=6 * image_len * BLK * width,
            bytes_accessed=12 * image_len * width,
            transcendentals=heads * image_len * BLK,
        ),
    )(length, received, key_value, key_value, gains, text_gain, num, den)


def on_device(
    enc_states,
    lengths,
    prompt_owner_sample,
    t5_gain,
    t5_in_weight,
    t5_out_weight,
    t5_final_gain,
    context_weight,
    text_shift,
    text_scale,
    kv_weight,
    text_key_gain,
    image_query_key_value,
    image_qk_gain,
    proj_weight,
    dora_a,
    dora_b,
    magnitude,
    grad_out,
):
    seq_rank = lax.axis_index("seq")
    data_rank = lax.axis_index("dp")
    n_seq = lax.axis_size("seq")
    n_dp = lax.axis_size("dp")
    n_all = n_seq * n_dp
    both = ("dp", "seq")
    rank, own_cols = dora_b.shape
    own_rows = dora_a.shape[0]
    model = own_cols * n_dp
    lanes = 128
    rows_of = model // lanes
    cotangent = grad_out[0]

    context_all = lax.all_gather(context_weight.T, "dp", axis=0, tiled=True)
    kv_all = lax.all_gather(
        kv_weight.reshape(kv_weight.shape[0], -1), "dp", axis=0, tiled=True
    )

    direction_t = proj_weight.T.astype(F32) + lax.dot_general(
        dora_b, dora_a, (((0,), (1,)), ((), ())), precision=lax.Precision.HIGHEST
    )
    image = image_query_key_value[0].reshape(BLK, 3, n_seq, own_rows)
    image = image.transpose(2, 1, 0, 3).reshape(n_seq, 3 * BLK, own_rows)
    packed = jnp.concatenate(
        [image, jnp.broadcast_to(direction_t.astype(BF16)[None], (n_seq, own_cols, own_rows))], 1
    )
    received = swap(packed, "seq")

    tokens = enc_states[0, :BLK]
    feat = tokens.shape[1] // n_seq
    normed = rms_scale(tokens.astype(F32), t5_gain).astype(BF16)
    gate_proj = jnp.dot(normed, t5_in_weight[0], preferred_element_type=F32)
    upward = jnp.dot(normed, t5_in_weight[1], preferred_element_type=F32)
    hidden = (jax.nn.gelu(gate_proj, approximate=True) * upward).astype(BF16)
    ffn = jnp.dot(hidden, t5_out_weight, preferred_element_type=F32).astype(BF16)
    ffn = ffn.reshape(BLK, n_seq, feat).transpose(1, 0, 2)
    ffn_sum = jnp.sum(swap(ffn, "seq").astype(F32), 0)
    own_tokens = lax.dynamic_slice_in_dim(tokens, seq_rank * feat, feat, 1).astype(F32)
    own_final = lax.dynamic_slice_in_dim(t5_final_gain, seq_rank * feat, feat, 0)
    encoded = ((own_tokens + ffn_sum) * own_final).astype(BF16)
    context = dot_t(encoded, context_all).astype(BF16)

    rows_t = received[:, 3 * BLK :, :]
    rows_f = rows_t.astype(F32)
    column_norm = jnp.sqrt(jnp.sum(rows_f * rows_f, (0, 2)) + EPSILON)
    ratio = magnitude / column_norm
    pair = seq_rank % 2
    rows_z = rows_f.reshape(n_seq // 2, 2, own_cols, own_rows)
    rows_z = jnp.where(pair == 0, rows_z[:, 0], rows_z[:, 1])
    scaled_t = (rows_z * ratio[None, :, None]).astype(BF16)
    scaled_t = scaled_t.transpose(1, 0, 2).reshape(own_cols, -1)
    scaled_all = lax.all_gather(scaled_t, "dp", axis=0, tiled=True)

    share = rank // n_seq
    up_rows = share * own_cols // lanes
    up = lax.dynamic_slice_in_dim(dora_b * ratio, seq_rank * share, share, 0).astype(BF16)
    up = jnp.broadcast_to(up.reshape(1, up_rows, lanes), (BLK, up_rows, lanes))
    pad_rows = (-(rows_of + up_rows)) % 8
    message = jnp.concatenate(
        [context.reshape(BLK, rows_of, lanes), up, jnp.zeros((BLK, pad_rows, lanes), BF16)], 1
    )
    arrived = swap(message, both)
    token_of = jnp.sum(
        arrived[:, :rows_of].reshape(n_dp, n_seq, rows_of, lanes).astype(F32), 1
    ).astype(BF16)
    up_all = arrived[:, rows_of : rows_of + up_rows].reshape(n_dp, rank, own_cols)
    up_all = up_all.transpose(1, 0, 2).reshape(rank, model)
    values = token_of.astype(F32)
    centre = jnp.mean(values, (1, 2), keepdims=True)
    spread = jnp.mean((values - centre) * (values - centre), (1, 2), keepdims=True)
    layer_normed = ((values - centre) * lax.rsqrt(spread + EPSILON)).astype(BF16)
    target = jnp.arange(n_all, dtype=jnp.int32) // n_seq
    one_hot = (target[:, None] == prompt_owner_sample[None, :]).astype(BF16)
    outgoing = jnp.einsum("sp,pab->sab", one_hot, layer_normed, preferred_element_type=F32)
    text = swap(outgoing.astype(BF16), both).reshape(BLK, model)
    modulated = ((1.0 + text_scale) * text.astype(F32) + text_shift).astype(BF16)
    length = jnp.sum(jnp.where(prompt_owner_sample == data_rank, lengths, 0))
    key_value = jnp.dot(modulated, kv_all, preferred_element_type=F32)

    num, den = image_attention(received, image_qk_gain)
    attended = text_attention(
        length.reshape(1), received, key_value, image_qk_gain, text_key_gain.reshape(1, HD), num, den
    )

    tokens_y = 2 * BLK
    gathered = swap(attended.reshape(n_seq // 2, tokens_y, own_rows), "seq", Y_GROUPS)
    gathered = gathered.transpose(1, 0, 2).reshape(tokens_y, -1)
    out_part = dot_t(gathered, scaled_all).astype(BF16).reshape(2, BLK, model)
    out = jnp.sum(swap(out_part, "seq", Z_GROUPS).astype(F32), 0)
    image_out = out.astype(BF16)[None]

    down = dot_t(cotangent, up_all).astype(BF16)
    down_all = swap(jnp.broadcast_to(down[None], (n_seq, BLK, rank)), "seq").reshape(-1, rank)
    grad_a_t = lax.dot_general(
        down_all, attended, (((0,), (0,)), ((), ())), preferred_element_type=F32
    ).astype(BF16)
    lowered = jnp.dot(attended, dora_a.astype(BF16), preferred_element_type=F32).astype(BF16)
    lowered = jnp.sum(swap(lowered.reshape(n_seq, BLK, rank), "seq").astype(F32), 0).astype(BF16)
    up_part = lax.dot_general(
        lowered, cotangent, (((0,), (0,)), ((), ())), preferred_element_type=F32
    ).astype(BF16)
    parts = jnp.concatenate(
        [
            jnp.broadcast_to(grad_a_t[None], (n_dp, rank, own_rows)),
            up_part.reshape(rank, n_dp, own_cols).transpose(1, 0, 2),
        ],
        2,
    )
    parts = jnp.sum(swap(parts, "dp").astype(F32), 0)
    grad_a = parts[:, :own_rows].T
    grad_b = parts[:, own_rows:].astype(BF16)
    grad_b = swap(jnp.broadcast_to(grad_b[None], (n_seq, rank, own_cols)), "seq")
    grad_b = jnp.sum(grad_b.astype(F32), 0) * ratio
    magnitude_part = jnp.sum(out * cotangent.astype(F32), 0).astype(BF16)
    magnitude_part = jnp.broadcast_to(
        magnitude_part.reshape(n_dp, 1, own_cols), (n_dp, n_seq, own_cols)
    )
    magnitude_part = swap(magnitude_part.reshape(n_all, own_cols), both)
    grad_magnitude = jnp.sum(magnitude_part.astype(F32), 0) / magnitude
    return (image_out, grad_a, grad_b, grad_magnitude)


def solution(mesh):
    return jax.shard_map(
        on_device,
        mesh=mesh,
        in_specs=(
            P("dp", None, None),
            P(),
            P(),
            P(),
            P(None, None, "seq"),
            P("seq", None),
            P(),
            P("seq", "dp"),
            P("dp", None),
            P("dp", None),
            P("dp", None, "seq"),
            P(),
            P("dp", "seq", None, None),
            P(),
            P("seq", "dp"),
            P("seq", None),
            P(None, "dp"),
            P("dp"),
            P("dp", "seq", None),
        ),
        out_specs=(P("dp", "seq", None), P("seq", None), P(None, "dp"), P("dp")),
        check_vma=False,
    )
```

time: 707 us -> 338 us (0.48)
  waiting for transfers between devices: 422 us -> 149 us
  blocking collectives: 145 us -> 0 us
  starting transfers between devices: 6.91 us -> 70.9 us
  matrix products: 54 us -> 36.5 us
  Pallas kernels: 0 us -> 13.6 us
  local copies, waits for them, and re-layouts: 44.1 us -> 33.8 us
    reduce_scatter x3 -> x0, waiting for transfers between devices: 215 us -> none  [the longest x1 77.4 us: on_device(): lax.psum_scatter(jnp.dot(hidden, t5_out_weight, preferred_element_type=jn...]
    all_gather x6 -> x3, waiting for transfers between devices: 140 us -> 0.02 us  [the longest x1 0.02 us: on_device(): scaled_all = lax.all_gather(scaled_t, 'dp', axis=0, tiled=True)]
    all_to_all x1 -> x11, waiting for transfers between devices: 44 us -> 148 us  [swap(): lax.all_to_all(values, axes, 0, 0, tiled=True, axis_index_groups=groups)]
    psum x2 -> x0, blocking collectives: 70 us -> none  [the longest x1 35.7 us: on_device(): lax.psum(up_part.astype(jnp.bfloat16), 'seq').astype(jnp.float32)]
    all_to_all x1 -> x11, starting transfers between devices: 6.32 us -> 70.8 us  [swap(): lax.all_to_all(values, axes, 0, 0, tiled=True, axis_index_groups=groups)]
    unnamed x1 -> x0, blocking collectives: 53.4 us -> none
    unnamed x11 -> x3, waiting for transfers between devices: 22.9 us -> 0.71 us
    all_gather x1 -> x0, blocking collectives: 21.6 us -> none  [on_device(): lax.all_gather(dora_b.astype(jnp.bfloat16), 'dp', axis=1, tiled=True)]
  transfers between devices with their start and end apart: 11 -> 14, of which waited for: 9 -> 8; matrix products, arithmetic and copies ran while one was open for 12% -> 24% of each run, Pallas kernels for 0% -> 4%
where the time goes in v1:
time: 338 us; the launch traced here: 336 us
  waiting for transfers between devices  149 us (44%)
  starting transfers between devices  70.9 us (21%)
  matrix products  36.5 us (11%)
  local copies, waits for them, and re-layouts  33.8 us (10%)
  other arithmetic  18 us (5%)
  between operations  14.2 us (4%)
  Pallas kernels  13.6 us (4%)
    all_to_all x11, waiting for transfers between devices, swap(): lax.all_to_all(values, axes, 0, 0, tiled=True, axis_index_groups=groups)  148 us
    all_to_all x11, starting transfers between devices, swap(): lax.all_to_all(values, axes, 0, 0, tiled=True, axis_index_groups=groups)  70.8 us
    dot_general x3, matrix products, dot_t(): lax.dot_general(left, right, (((1,), (1,)), ((), ())), preferred_element_...  16.7 us
    pallas_call x1, Pallas kernels, image_attention(): pl.pallas_call(image_kernel, grid=(heads, sources // step), in_specs=[pl....  9.27 us
    unnamed x44, local copies, waits for them, and re-layouts  8.67 us
    dot_general x1, matrix products, on_device(): jnp.dot(hidden, t5_out_weight, preferred_element_type=F32).astype(BF16)  7.32 us
  transfers between devices with their start and end apart: 14, of which 8 were waited for; matrix products, arithmetic and copies ran while one was open for 24% of the time, Pallas kernels for 4%

profile of v1, /device:TPU:1, one launch (start us, length us, event | category | flops | bytes accessed | tf_op | source)
XLA Modules:
  0.0 335.9 jit_solution(4091227710399149993)
XLA Ops:
  7.2 0.7 all-gather.4.cloned.1.call-update
  7.9 1.7 copy.82
  9.7 2.2 copy.80
  13.4 2.1 pad_maximum_fusion
  15.5 8.5 %all-to-all-start = ((bf16[8,576,384]{2,1,0:T(8,128)(2,1)}), bf16[8,576,384]{2,1,0:T(8,128)(2,1)S(1)}, u32[]{:S(2)}, u32[]{:S(2)}) async-start(bf16[8,576,384]{2,1,0:T(8,128)(2,1)} %pad_maximum_fusion), calls=%async_computation | async-start | bytes 7077888 | tf_op jit(solution)/shard_map/all_to_all | solution.py:24
  24.1 50.0 %all-to-all-done.q_ref.k_ref.v_ref = bf16[8,576,384]{2,1,0:T(8,128)(2,1)S(1)} async-done(((bf16[8,576,384]{2,1,0:T(8,128)(2,1)}), bf16[8,576,384]{2,1,0:T(8,128)(2,1)S(1)}, u32[]{:S(2)}, u32[]{:S(2)}) %all-to-all-start) | async-done | bytes 3538976 | tf_op jit(solution)/shard_map/all_to_all | solution.py:24
  74.7 1.4 fusion.14
  76.1 0.9 copy.83
  77.0 1.5 fusion.6
  78.6 4.7 %fusion.39 = f32[128,640]{1,0:T(8,128)} fusion(bf16[2,4096,640]{2,1,0:T(8,128)(2,1)} %param.23, f32[4096]{0:T(1024)} %param.22, f32[128]{0:T(128)S(1)} %add_rsqrt_fusion.1, bf16[1,256,4096]{2,1,0:T(8,128)(2,1)} %param.19), kind=kOutput, calls=%fused_computation.60 | convolution fusion | flops 673841152 | bytes 6636032 | tf_op jit(solution)/shard_map/dot_general | solution.py:173
  83.2 7.3 %convolution_convert_fusion = bf16[128,4096]{1,0:T(8,128)(2,1)} fusion(bf16[640,4096]{1,0:T(8,128)(2,1)} %param.24, f32[128,640]{1,0:T(8,128)} %fusion.39, bf16[2,4096,640]{2,1,0:T(8,128)(2,1)} %param.23, f32[4096]{0:T(1024)} %param.22, f32[128]{0:T(128)S(1)} %add_rsqrt_fusion.1, bf16[1,256,4096]{2,1,0:T(8,128)(2,1)} %param.19), kind=kOutput, calls=%fused_computation.6 | convolution fusion | flops 1344962560 | bytes 12927488 | tf_op jit(solution)/shard_map/dot_general | solution.py:176
  90.5 2.3 copy.101
  92.9 5.7 %all-to-all-start.1 = ((bf16[8,128,512]{2,1,0:T(8,128)(2,1)}), bf16[8,128,512]{2,1,0:T(8,128)(2,1)}, u32[]{:S(2)}, u32[]{:S(2)}) async-start(bf16[8,128,512]{2,1,0:T(8,128)(2,1)} %bitcast.122), calls=%async_computation.1 | async-start | bytes 2097152 | tf_op jit(solution)/shard_map/all_to_all | solution.py:24
  98.5 2.3 slice.31
  100.8 0.8 dynamic_slice.10
  101.7 14.5 %all-to-all-done.1 = bf16[8,128,512]{2,1,0:T(8,128)(2,1)} async-done(((bf16[8,128,512]{2,1,0:T(8,128)(2,1)}), bf16[8,128,512]{2,1,0:T(8,128)(2,1)}, u32[]{:S(2)}, u32[]{:S(2)}) %all-to-all-start.1) | async-done | bytes 1048608 | tf_op jit(solution)/shard_map/all_to_all | solution.py:24
  116.2 2.1 convert_reduce_fusion.2
  118.2 0.7 fusion.59
  119.0 3.3 fusion.11
  122.5 1.4 maximum_maximum_fusion
  123.9 8.6 %all-to-all-start.2 = ((bf16[128,40,128]{2,1,0:T(8,128)(2,1)}), bf16[128,40,128]{2,1,0:T(8,128)(2,1)}, u32[]{:S(2)}, u32[]{:S(2)}) async-start(bf16[128,40,128]{2,1,0:T(8,128)(2,1)} %maximum_maximum_fusion), calls=%async_computation.2 | async-start | bytes 2621440 | tf_op jit(solution)/shard_map/all_to_all | solution.py:24
  132.6 22.7 %all-to-all-done.2 = bf16[128,40,128]{2,1,0:T(8,128)(2,1)} async-done(((bf16[128,40,128]{2,1,0:T(8,128)(2,1)}), bf16[128,40,128]{2,1,0:T(8,128)(2,1)}, u32[]{:S(2)}, u32[]{:S(2)}) %all-to-all-start.2) | async-done | bytes 1310752 | tf_op jit(solution)/shard_map/all_to_all | solution.py:24
  155.2 1.3 bitcast_reduce_fusion
  157.6 1.4 copy.63
  159.0 7.4 %all-to-all-start.3 = ((bf16[128,24,128]{2,1,0:T(8,128)(2,1)}), bf16[128,24,128]{2,1,0:T(8,128)(2,1)}, u32[]{:S(2)}, u32[]{:S(2)}) async-start(bf16[128,24,128]{2,1,0:T(8,128)(2,1)} %copy.63), calls=%async_computation.3 | async-start | bytes 1572864 | tf_op jit(solution)/shard_map/all_to_all | solution.py:24
  166.4 0.7 broadcast_add_fusion
  167.1 1.3 fusion.64
  168.4 9.3 %shard_map.210 = (f32[1024,384]{1,0:T(8,128)S(1)}, f32[1024,384]{1,0:T(8,128)S(1)}) custom-call(bf16[8,576,384]{2,1,0:T(8,128)(2,1)S(1)} %all-to-all-done.q_ref.k_ref.v_ref, bf16[8,576,384]{2,1,0:T(8,128)(2,1)S(1)} %all-to-all-done.q_ref.k_ref.v_ref, bf16[8,576,384]{2,1,0:T(8,128)(2,1)S(1)} %all-to-all-done.q_ref.k_ref.v_ref, f32[2,128]{1,0:T(2,128)S(1)} %copy-done.6), custom_call_target="tpu_custom_call" | custom-call | flops 2415919104 | bytes 5505024 | tf_op jit(solution)/shard_map/pallas_call | solution.py:53
  177.7 1.1 copy-done.2
  178.8 1.1 copy-done.4
  180.0 1.9 slice.45
  181.9 2.2 reshape.172
  184.1 2.1 copy.68
  186.3 2.4 reshape.173
  188.7 2.3 fusion.23
  191.0 1.4 broadcast_in_dim.25
  192.4 7.1 %all-to-all-start.6 = ((bf16[8,128,64]{1,2,0:T(8,128)(2,1)}), bf16[8,128,64]{1,2,0:T(8,128)(2,1)}, u32[]{:S(2)}, u32[]{:S(2)}) async-start(bf16[8,128,64]{1,2,0:T(8,128)(2,1)} %broadcast_in_dim.25), calls=%async_computation.6 | async-start | bytes 262144 | tf_op jit(solution)/shard_map/all_to_all | solution.py:24
  199.5 2.4 copy.64
  201.9 4.8 %fusion.27.k_ref.v_ref = f32[128,768]{1,0:T(8,128)S(1)} fusion(bf16[3072,768]{1,0:T(8,128)(2,1)} %all-gather.6.cloned.1.call-done, bf16[128,3072]{0,1:T(8,128)(2,1)} %bitcast.124, f32[3072]{0:T(1024)} %bitcast.137, f32[3072]{0:T(1024)S(1)} %bitcast.136), kind=kOutput, calls=%fused_computation.44 | convolution fusion | flops 605552640 | bytes 5922816 | tf_op jit(solution)/shard_map/dot_general | solution.py:219
  206.8 4.3 %shard_map.211 = bf16[1024,384]{1,0:T(8,128)(2,1)S(1)} custom-call(s32[1]{0:T(128)} %bitcast.length_ref, bf16[8,576,384]{2,1,0:T(8,128)(2,1)S(1)} %all-to-all-done.q_ref.k_ref.v_ref, f32[128,768]{1,0:T(8,128)S(1)} %fusion.27.k_ref.v_ref, f32[128,768]{1,0:T(8,128)S(1)} %fusion.27.k_ref.v_ref, f32[2,128]{1,0:T(2,128)S(1)} %copy-done.6, ...), custom_call_target="tpu_custom_call" | custom-call | flops 301989888 | bytes 4718592 | tf_op jit(solution)/shard_map/pallas_call | solution.py:97
  211.1 0.9 copy-done
  212.4 0.7 copy.103
  213.0 6.6 %all-to-all-start.7 = ((bf16[8,128,64]{1,2,0:T(8,128)(2,1)}), bf16[8,128,64]{1,2,0:T(8,128)(2,1)S(1)}, u32[]{:S(2)}, u32[]{:S(2)}) async-start(bf16[8,128,64]{1,2,0:T(8,128)(2,1)} %bitcast.116), calls=%async_computation.7 | async-start | bytes 262144 | tf_op jit(solution)/shard_map/all_to_all | solution.py:24
  219.7 1.4 convolution_convert_fusion.6
  221.1 5.3 %all-to-all-done.7 = bf16[8,128,64]{1,2,0:T(8,128)(2,1)S(1)} async-done(((bf16[8,128,64]{1,2,0:T(8,128)(2,1)}), bf16[8,128,64]{1,2,0:T(8,128)(2,1)S(1)}, u32[]{:S(2)}, u32[]{:S(2)}) %all-to-all-start.7) | async-done | bytes 131104 | tf_op jit(solution)/shard_map/all_to_all | solution.py:24
  226.7 0.6 reshape.176
  227.6 1.3 pad_maximum_fusion.1
  228.9 6.9 %all-to-all-start.8 = ((bf16[16,64,576]{2,1,0:T(8,128)(2,1)}), bf16[16,64,576]{2,1,0:T(8,128)(2,1)S(1)}, u32[]{:S(2)}, u32[]{:S(2)}) async-start(bf16[16,64,576]{2,1,0:T(8,128)(2,1)} %pad_maximum_fusion.1), calls=%async_computation.8 | async-start | bytes 2621440 | tf_op jit(solution)/shard_map/all_to_all | solution.py:24
  235.8 1.2 copy.65
  236.9 17.5 %all-to-all-done.8 = bf16[16,64,576]{2,1,0:T(8,128)(2,1)S(1)} async-done(((bf16[16,64,576]{2,1,0:T(8,128)(2,1)}), bf16[16,64,576]{2,1,0:T(8,128)(2,1)S(1)}, u32[]{:S(2)}, u32[]{:S(2)}) %all-to-all-start.8) | async-done | bytes 1179680 | tf_op jit(solution)/shard_map/all_to_all | solution.py:24
  254.4 3.5 %all-to-all-start.4 = ((bf16[4,256,384]{1,2,0:T(8,128)(2,1)}), bf16[4,256,384]{1,2,0:T(8,128)(2,1)S(1)}, u32[]{:S(2)}, u32[]{:S(2)}) async-start(bf16[4,256,384]{1,2,0:T(8,128)(2,1)} %copy.65), calls=%async_computation.4 | async-start | bytes 1572864 | tf_op jit(solution)/shard_map/all_to_all | solution.py:24
  258.1 11.4 %all-to-all-done.4 = bf16[4,256,384]{1,2,0:T(8,128)(2,1)S(1)} async-done(((bf16[4,256,384]{1,2,0:T(8,128)(2,1)}), bf16[4,256,384]{1,2,0:T(8,128)(2,1)S(1)}, u32[]{:S(2)}, u32[]{:S(2)}) %all-to-all-start.4) | async-done | bytes 786464 | tf_op jit(solution)/shard_map/all_to_all | solution.py:24
  269.5 0.7 broadcast_in_dim.27
  270.3 3.4 %all-to-all-start.9 = ((bf16[8,64,192]{2,1,0:T(8,128)(2,1)}), bf16[8,64,192]{2,1,0:T(8,128)(2,1)S(1)}, u32[]{:S(2)}, u32[]{:S(2)}) async-start(bf16[8,64,192]{2,1,0:T(8,128)(2,1)} %broadcast_in_dim.27), calls=%async_computation.9 | async-start | bytes 524288 | tf_op jit(solution)/shard_map/all_to_all | solution.py:24
  273.7 11.1 %convolution_convert_fusion.1 = bf16[256,3072]{1,0:T(8,128)(2,1)} fusion(bf16[256,1536]{0,1:T(8,128)(2,1)S(1)} %bitcast.133, bf16[3072,1536]{1,0:T(8,128)(2,1)} %all-gather.8.cloned.1.call-done), kind=kOutput, calls=%fused_computation.7 | convolution fusion | flops 2416705536 | bytes 11796480 | tf_op jit(solution)/shard_map/dot_general | solution.py:28
  284.8 4.2 %all-to-all-start.5 = ((bf16[2,128,3072]{2,1,0:T(8,128)(2,1)}), bf16[2,128,3072]{2,1,0:T(8,128)(2,1)S(1)}, u32[]{:S(2)}, u32[]{:S(2)}) async-start(bf16[2,128,3072]{2,1,0:T(8,128)(2,1)} %bitcast.130), calls=%async_computation.5 | async-start | bytes 3145728 | tf_op jit(solution)/shard_map/all_to_all | solution.py:24
  289.0 0.6 slice_bitcast_fusion
  289.7 17.7 %all-to-all-done.5 = bf16[2,128,3072]{2,1,0:T(8,128)(2,1)S(1)} async-done(((bf16[2,128,3072]{2,1,0:T(8,128)(2,1)}), bf16[2,128,3072]{2,1,0:T(8,128)(2,1)S(1)}, u32[]{:S(2)}, u32[]{:S(2)}) %all-to-all-start.5) | async-done | bytes 1572896 | tf_op jit(solution)/shard_map/all_to_all | solution.py:24
  307.7 1.1 multiply_reduce_fusion.1
  309.0 0.8 copy.73
  309.7 9.0 %all-to-all-start.10 = ((bf16[128,1,192]{2,1,0:T(2,128)(2,1)}), bf16[128,1,192]{2,1,0:T(2,128)(2,1)S(1)}, u32[]{:S(2)}, u32[]{:S(2)}) async-start(bf16[128,1,192]{2,1,0:T(2,128)(2,1)} %copy.73), calls=%async_computation.10 | async-start | bytes 262144 | tf_op jit(solution)/shard_map/all_to_all | solution.py:24
  318.8 0.6 broadcast_multiply_fusion
  319.4 9.2 %all-to-all-done.10 = bf16[128,1,192]{2,1,0:T(2,128)(2,1)S(1)} async-done(((bf16[128,1,192]{2,1,0:T(2,128)(2,1)}), bf16[128,1,192]{2,1,0:T(2,128)(2,1)S(1)}, u32[]{:S(2)}, u32[]{:S(2)}) %all-to-all-start.10) | async-done | bytes 49184 | tf_op jit(solution)/shard_map/all_to_all | solution.py:24
  328.8 0.6 div.33
  (80 shorter events, 5.6 us)
Async XLA Ops:
  7.2 111.9 %all-gather.4.cloned.1.call-start = ((), (), s32[]{:S(2)}) async-start(), calls=%async_computation.11 | async-start | bytes 3342336 | tf_op jit(solution)/shard_map/all_gather | solution.py:155
  7.9 194.0 %all-gather.6.cloned.1.call-start = ((), (), s32[]{:S(2)}) async-start(), calls=%async_computation.12 | async-start | bytes 5013504 | tf_op jit(solution)/shard_map/all_gather | solution.py:156
  11.9 0.9 copy-start.11
  11.9 1.0 copy-start.13
  11.9 0.9 copy-start.14
  15.5 58.8 %copy-start.17 = (f32[192]{0:T(256)S(1)}, f32[192]{0:T(256)}, u32[]{:S(2)}) copy-start(f32[192]{0:T(256)} %param.36) | copy-start | bytes 2308
  15.5 58.5 %all-to-all-start = ((bf16[8,576,384]{2,1,0:T(8,128)(2,1)}), bf16[8,576,384]{2,1,0:T(8,128)(2,1)S(1)}, u32[]{:S(2)}, u32[]{:S(2)}) async-start(bf16[8,576,384]{2,1,0:T(8,128)(2,1)} %pad_maximum_fusion), calls=%async_computation | async-start | bytes 7077888 | tf_op jit(solution)/shard_map/all_to_all | solution.py:24
  24.0 249.7 %all-gather.8.cloned.1.call-start = ((), (), s32[]{:S(2)}) async-start(), calls=%async_computation.13 | async-start | bytes 10027008 | tf_op jit(solution)/shard_map/all_gather | solution.py:193
  74.4 43.9 %copy-start.15 = (f32[192]{0:T(256)}, f32[192]{0:T(256)S(1)}, u32[]{:S(2)}) copy-start(f32[192]{0:T(256)S(1)} %rsqrt_multiply_fusion) | copy-start | bytes 2308
  92.9 23.3 %all-to-all-start.1 = ((bf16[8,128,512]{2,1,0:T(8,128)(2,1)}), bf16[8,128,512]{2,1,0:T(8,128)(2,1)}, u32[]{:S(2)}, u32[]{:S(2)}) async-start(bf16[8,128,512]{2,1,0:T(8,128)(2,1)} %bitcast.122), calls=%async_computation.1 | async-start | bytes 2097152 | tf_op jit(solution)/shard_map/all_to_all | solution.py:24
  123.9 33.2 %copy-start.19 = (s32[16]{0:T(128)S(1)}, s32[16]{0:T(128)}, u32[]{:S(2)}) copy-start(s32[16]{0:T(128)} %param.21) | copy-start | bytes 196
  123.9 31.3 %all-to-all-start.2 = ((bf16[128,40,128]{2,1,0:T(8,128)(2,1)}), bf16[128,40,128]{2,1,0:T(8,128)(2,1)}, u32[]{:S(2)}, u32[]{:S(2)}) async-start(bf16[128,40,128]{2,1,0:T(8,128)(2,1)} %maximum_maximum_fusion), calls=%async_computation.2 | async-start | bytes 2621440 | tf_op jit(solution)/shard_map/all_to_all | solution.py:24
  157.0 11.4 %copy-start.6 = (f32[2,128]{1,0:T(2,128)S(1)}, f32[2,128]{1,0:T(2,128)}, u32[]{:S(2)}) copy-start(f32[2,128]{1,0:T(2,128)} %gain_ref.3) | copy-start | bytes 3076
  159.0 32.0 %all-to-all-start.3 = ((bf16[128,24,128]{2,1,0:T(8,128)(2,1)}), bf16[128,24,128]{2,1,0:T(8,128)(2,1)}, u32[]{:S(2)}, u32[]{:S(2)}) async-start(bf16[128,24,128]{2,1,0:T(8,128)(2,1)} %copy.63), calls=%async_computation.3 | async-start | bytes 1572864 | tf_op jit(solution)/shard_map/all_to_all | solution.py:24
  177.7 1.1 copy-start.2
  178.8 1.1 copy-start.4
  192.4 20.6 %all-to-all-start.6 = ((bf16[8,128,64]{1,2,0:T(8,128)(2,1)}), bf16[8,128,64]{1,2,0:T(8,128)(2,1)}, u32[]{:S(2)}, u32[]{:S(2)}) async-start(bf16[8,128,64]{1,2,0:T(8,128)(2,1)} %broadcast_in_dim.25), calls=%async_computation.6 | async-start | bytes 262144 | tf_op jit(solution)/shard_map/all_to_all | solution.py:24
  201.9 4.9 %copy-start.3 = (f32[1024,384]{1,0:T(8,128)S(1)}, f32[1024,384]{1,0:T(8,128)}, u32[]{:S(2)}) copy-start(f32[1024,384]{1,0:T(8,128)} %copy-done.2) | copy-start | bytes 4718596
  201.9 4.9 %copy-start.5 = (f32[1024,384]{1,0:T(8,128)S(1)}, f32[1024,384]{1,0:T(8,128)}, u32[]{:S(2)}) copy-start(f32[1024,384]{1,0:T(8,128)} %copy-done.4) | copy-start | bytes 4718596
  201.9 4.9 %copy-start.7 = (f32[128]{0:T(128)S(1)}, f32[128]{0:T(128)}, u32[]{:S(2)}) copy-start(f32[128]{0:T(128)} %param.30) | copy-start | bytes 1540
  206.8 5.2 %copy-start.12 = (f32[384,64]{0,1:T(8,128)S(1)}, f32[384,64]{0,1:T(8,128)}, u32[]{:S(2)}) copy-start(f32[384,64]{0,1:T(8,128)} %param.34) | copy-start | bytes 294916
  211.1 0.9 copy-start
  212.0 14.5 %copy-start.8 = (bf16[1,128,3072]{2,1,0:T(8,128)(2,1)S(1)}, bf16[1,128,3072]{2,1,0:T(8,128)(2,1)}, u32[]{:S(2)}) copy-start(bf16[1,128,3072]{2,1,0:T(8,128)(2,1)} %param.37) | copy-start | bytes 2359300
  213.0 13.4 %all-to-all-start.7 = ((bf16[8,128,64]{1,2,0:T(8,128)(2,1)}), bf16[8,128,64]{1,2,0:T(8,128)(2,1)S(1)}, u32[]{:S(2)}, u32[]{:S(2)}) async-start(bf16[8,128,64]{1,2,0:T(8,128)(2,1)} %bitcast.116), calls=%async_computation.7 | async-start | bytes 262144 | tf_op jit(solution)/shard_map/all_to_all | solution.py:24
  227.6 8.1 %copy-start.1 = (bf16[1024,384]{1,0:T(8,128)(2,1)S(1)}, bf16[1024,384]{1,0:T(8,128)(2,1)}, u32[]{:S(2)}) copy-start(bf16[1024,384]{1,0:T(8,128)(2,1)} %copy-done) | copy-start | bytes 2359300
  228.9 25.5 %all-to-all-start.8 = ((bf16[16,64,576]{2,1,0:T(8,128)(2,1)}), bf16[16,64,576]{2,1,0:T(8,128)(2,1)S(1)}, u32[]{:S(2)}, u32[]{:S(2)}) async-start(bf16[16,64,576]{2,1,0:T(8,128)(2,1)} %pad_maximum_fusion.1), calls=%async_computation.8 | async-start | bytes 2621440 | tf_op jit(solution)/shard_map/all_to_all | solution.py:24
  254.4 15.1 %all-to-all-start.4 = ((bf16[4,256,384]{1,2,0:T(8,128)(2,1)}), bf16[4,256,384]{1,2,0:T(8,128)(2,1)S(1)}, u32[]{:S(2)}, u32[]{:S(2)}) async-start(bf16[4,256,384]{1,2,0:T(8,128)(2,1)} %copy.65), calls=%async_computation.4 | async-start | bytes 1572864 | tf_op jit(solution)/shard_map/all_to_all | solution.py:24
  258.1 26.7 %copy-start.9 = (f32[64,576]{1,0:T(8,128)}, f32[64,576]{1,0:T(8,128)S(1)}, u32[]{:S(2)}) copy-start(f32[64,576]{1,0:T(8,128)S(1)} %convert_reduce_fusion.1) | copy-start | bytes 442372
  270.3 14.5 %all-to-all-start.9 = ((bf16[8,64,192]{2,1,0:T(8,128)(2,1)}), bf16[8,64,192]{2,1,0:T(8,128)(2,1)S(1)}, u32[]{:S(2)}, u32[]{:S(2)}) async-start(bf16[8,64,192]{2,1,0:T(8,128)(2,1)} %broadcast_in_dim.27), calls=%async_computation.9 | async-start | bytes 524288 | tf_op jit(solution)/shard_map/all_to_all | solution.py:24
  284.8 4.2 %copy-start.10 = (f32[64,576]{1,0:T(8,128)S(1)}, f32[64,576]{1,0:T(8,128)}, u32[]{:S(2)}) copy-start(f32[64,576]{1,0:T(8,128)} %copy-done.9) | copy-start | bytes 442372
  284.8 22.6 %all-to-all-start.5 = ((bf16[2,128,3072]{2,1,0:T(8,128)(2,1)}), bf16[2,128,3072]{2,1,0:T(8,128)(2,1)S(1)}, u32[]{:S(2)}, u32[]{:S(2)}) async-start(bf16[2,128,3072]{2,1,0:T(8,128)(2,1)} %bitcast.130), calls=%async_computation.5 | async-start | bytes 3145728 | tf_op jit(solution)/shard_map/all_to_all | solution.py:24
  307.7 11.1 %copy-start.16 = (f32[192]{0:T(256)S(1)}, f32[192]{0:T(256)}, u32[]{:S(2)}) copy-start(f32[192]{0:T(256)} %copy-done.15) | copy-start | bytes 2308
  307.7 21.1 %copy-start.18 = (f32[192]{0:T(256)S(1)}, f32[192]{0:T(256)}, u32[]{:S(2)}) copy-start(f32[192]{0:T(256)} %param.36) | copy-start | bytes 2308
  309.7 18.9 %all-to-all-start.10 = ((bf16[128,1,192]{2,1,0:T(2,128)(2,1)}), bf16[128,1,192]{2,1,0:T(2,128)(2,1)S(1)}, u32[]{:S(2)}, u32[]{:S(2)}) async-start(bf16[128,1,192]{2,1,0:T(2,128)(2,1)} %copy.73), calls=%async_computation.10 | async-start | bytes 262144 | tf_op jit(solution)/shard_map/all_to_all | solution.py:24
Sparse Core Ops, SparseCore 0:
  9.7 71.1 all-gather.3
  82.6 49.5 all-gather.5
  133.9 71.0 all-gather.7

commit v2 on v1

v2 whole, which is shorter than its diff:
```python
import math

import jax
import jax.numpy as jnp
from jax import lax
from jax.experimental import pallas as pl
from jax.experimental.pallas import tpu as pltpu
from jax.sharding import PartitionSpec as P

HD = 128
BLK = 128
EPSILON = 1e-06
F32 = jnp.float32
BF16 = jnp.bfloat16
Y_GROUPS = [[0, 2, 4, 6], [1, 3, 5, 7]]
QUERY_SCALE = math.log2(math.e) / math.sqrt(HD)


def rms_scale(values, gain):
    return values * lax.rsqrt(jnp.mean(values * values, -1, keepdims=True) + EPSILON) * gain


def swap(values, axes, groups=None):
    return lax.all_to_all(values, axes, 0, 0, tiled=True, axis_index_groups=groups)


def dot_t(left, right):
    return lax.dot_general(left, right, (((1,), (1,)), ((), ())), preferred_element_type=F32)


def pack_kernel(_, in_ref, out_ref):
    out_ref[0, 0] = in_ref[...].reshape(out_ref.shape[2:])


def pack_heads(rows, pair, n_seq):
    kinds, count, model = rows.shape
    width = model // n_seq
    return pl.pallas_call(
        pack_kernel,
        grid_spec=pltpu.PrefetchScalarGridSpec(
            num_scalar_prefetch=1,
            grid=(n_seq // 2, 2),
            in_specs=[
                pl.BlockSpec((kinds, count, width), lambda y, k, z: (0, 0, 2 * y + (z[0] + k) % 2))
            ],
            out_specs=pl.BlockSpec((1, 1, kinds * count, width), lambda y, k, z: (y, k, 0, 0)),
        ),
        out_shape=jax.ShapeDtypeStruct((n_seq // 2, 2, kinds * count, width), rows.dtype),
        compiler_params=pltpu.CompilerParams(vmem_limit_bytes=16 * 1024 * 1024),
        cost_estimate=pl.CostEstimate(flops=0, bytes_accessed=4 * rows.size, transcendentals=0),
    )(pair.reshape(1), rows)


def image_kernel(
    q_own, q_other, k_own, k_other, v_own, v_other, gain_ref, num_ref, den_ref, keys, values
):
    half = keys.shape[0] // 2

    @pl.when(pl.program_id(1) == 0)
    def _():
        for at, k_ref, v_ref in ((0, k_own, v_own), (half, k_other, v_other)):
            k = k_ref[...].reshape(-1, HD).astype(F32)
            keys[at : at + half, :] = rms_scale(k, gain_ref[1:2, :]).astype(BF16)
            values[at : at + half, :HD] = v_ref[...].reshape(-1, HD)
        values[:, HD:] = jnp.ones((2 * half, HD), BF16)

    q = jnp.concatenate([q_own[...].reshape(-1, HD), q_other[...].reshape(-1, HD)], 0)
    q = rms_scale(q.astype(F32), gain_ref[0:1, :] * QUERY_SCALE).astype(BF16)
    weight = jnp.exp2(dot_t(q, keys[...])).astype(BF16)
    both = jnp.dot(weight, values[...], preferred_element_type=F32)
    num_ref[...] = both[:, :HD]
    den_ref[...] = both[:, HD:]


def image_attention(own, other, gains):
    n_y, _, _, width = own.shape
    heads = width // HD
    rows = 2 * BLK
    image_len = n_y * rows

    def own_spec(count, kind):
        if count == 1:
            return pl.BlockSpec((1, 1, BLK, HD), lambda h, b: (b, 0, kind, h))
        return pl.BlockSpec((count, 1, BLK, HD), lambda h, b: (0, 0, kind, h))

    def other_spec(count, kind):
        if count == 1:
            return pl.BlockSpec((1, BLK, HD), lambda h, b: (b, kind, h))
        return pl.BlockSpec((count, BLK, HD), lambda h, b: (0, kind, h))

    return pl.pallas_call(
        image_kernel,
        grid=(heads, n_y),
        in_specs=[
            own_spec(1, 0),
            other_spec(1, 0),
            own_spec(n_y, 1),
            other_spec(n_y, 1),
            own_spec(n_y, 2),
            other_spec(n_y, 2),
            pl.BlockSpec((2, HD), lambda h, b: (0, 0)),
        ],
        out_specs=[
            pl.BlockSpec((rows, HD), lambda h, b: (b, h)),
            pl.BlockSpec((rows, HD), lambda h, b: (b, h)),
        ],
        out_shape=[jax.ShapeDtypeStruct((image_len, width), F32)] * 2,
        scratch_shapes=[pltpu.VMEM((image_len, HD), BF16), pltpu.VMEM((image_len, 2 * HD), BF16)],
        compiler_params=pltpu.CompilerParams(vmem_limit_bytes=24 * 1024 * 1024),
        cost_estimate=pl.CostEstimate(
            flops=6 * image_len * image_len * width,
            bytes_accessed=14 * image_len * width,
            transcendentals=heads * image_len * image_len,
        ),
    )(own, other, own, other, own, other, gains)


def text_kernel(
    length_ref, q_own, q_other, k_ref, v_ref, gain_ref, text_gain_ref, num_ref, den_ref, out_ref
):
    k = rms_scale(k_ref[...], text_gain_ref[...]).astype(BF16)
    v = v_ref[...].astype(BF16)
    stacked = jnp.concatenate([v, jnp.ones_like(v)], axis=1)
    for b in range(q_other.shape[0]):
        q = jnp.concatenate([q_own[b, 0], q_other[b]], 0).astype(F32)
        q = rms_scale(q, gain_ref[0:1, :] * QUERY_SCALE).astype(BF16)
        weight = jnp.exp2(dot_t(q, k))
        valid = lax.broadcasted_iota(jnp.int32, weight.shape, 1) < length_ref[0]
        weight = jnp.where(valid, weight, 0.0).astype(BF16)
        both = jnp.dot(weight, stacked, preferred_element_type=F32)
        rows = slice(b * q.shape[0], (b + 1) * q.shape[0])
        total = num_ref[rows, :] + both[:, :HD]
        out_ref[rows, :] = (total / (den_ref[rows, :] + both[:, HD:])).astype(BF16)


def text_attention(length, own, other, key_value, gains, text_gain, num, den):
    n_y, _, _, width = own.shape
    heads = width // HD
    image_len = n_y * 2 * BLK
    step = n_y // 2
    rows = step * 2 * BLK
    return pl.pallas_call(
        text_kernel,
        grid=(heads, n_y // step),
        in_specs=[
            pl.BlockSpec(memory_space=pltpu.SMEM),
            pl.BlockSpec((step, 1, BLK, HD), lambda h, b: (b, 0, 0, h)),
            pl.BlockSpec((step, BLK, HD), lambda h, b: (b, 0, h)),
            pl.BlockSpec((BLK, HD), lambda h, b: (0, h)),
            pl.BlockSpec((BLK, HD), lambda h, b: (0, heads + h)),
            pl.BlockSpec((2, HD), lambda h, b: (0, 0)),
            pl.BlockSpec((1, HD), lambda h, b: (0, 0)),
            pl.BlockSpec((rows, HD), lambda h, b: (b, h)),
            pl.BlockSpec((rows, HD), lambda h, b: (b, h)),
        ],
        out_specs=pl.BlockSpec((rows, HD), lambda h, b: (b, h)),
        out_shape=jax.ShapeDtypeStruct((image_len, width), BF16),
        compiler_params=pltpu.CompilerParams(vmem_limit_bytes=24 * 1024 * 1024),
        cost_estimate=pl.CostEstimate(
            flops=6 * image_len * BLK * width,
            bytes_accessed=12 * image_len * width,
            transcendentals=heads * image_len * BLK,
        ),
    )(length, own, other, key_value, key_value, gains, text_gain, num, den)


def on_device(
    enc_states,
    lengths,
    prompt_owner_sample,
    t5_gain,
    t5_in_weight,
    t5_out_weight,
    t5_final_gain,
    context_weight,
    text_shift,
    text_scale,
    kv_weight,
    text_key_gain,
    image_query_key_value,
    image_qk_gain,
    proj_weight,
    dora_a,
    dora_b,
    magnitude,
    grad_out,
):
    seq_rank = lax.axis_index("seq")
    data_rank = lax.axis_index("dp")
    n_seq = lax.axis_size("seq")
    n_dp = lax.axis_size("dp")
    n_all = n_seq * n_dp
    both = ("dp", "seq")
    rank, own_cols = dora_b.shape
    own_rows = dora_a.shape[0]
    model = own_cols * n_dp
    lanes = 128
    rows_of = model // lanes
    cotangent = grad_out[0]

    pair = seq_rank % 2
    flip_z = [(i, i ^ 1) for i in range(n_seq)]
    n_y = n_seq // 2

    weights = jnp.concatenate(
        [context_weight.T, kv_weight.reshape(kv_weight.shape[0], -1)], 1
    )
    weights = lax.all_gather(weights, "dp", axis=0, tiled=True)
    depth = context_weight.shape[0]
    context_all, kv_all = weights[:, :depth], weights[:, depth:]

    direction_t = proj_weight.T.astype(F32) + lax.dot_general(
        dora_b, dora_a, (((0,), (1,)), ((), ())), precision=lax.Precision.HIGHEST
    )
    direction_t = direction_t.astype(BF16)
    rows_y = swap(jnp.broadcast_to(direction_t[None], (n_y, own_cols, own_rows)), "seq", Y_GROUPS)

    tokens = enc_states[0, :BLK]
    feat = tokens.shape[1] // n_seq
    normed = rms_scale(tokens.astype(F32), t5_gain).astype(BF16)
    gate_proj = jnp.dot(normed, t5_in_weight[0], preferred_element_type=F32)
    upward = jnp.dot(normed, t5_in_weight[1], preferred_element_type=F32)
    hidden = (jax.nn.gelu(gate_proj, approximate=True) * upward).astype(BF16)
    ffn = jnp.dot(hidden, t5_out_weight, preferred_element_type=F32).astype(BF16)
    ffn = ffn.reshape(BLK, n_seq, feat).transpose(1, 0, 2)
    packed = pack_heads(image_query_key_value[0].transpose(1, 0, 2), pair, n_seq)
    rows_y, ffn, packed = lax.optimization_barrier((rows_y, ffn, packed))
    ffn = swap(ffn, "seq")
    ffn, packed = lax.optimization_barrier((ffn, packed))
    ffn_sum = jnp.sum(ffn.astype(F32), 0)

    own_heads = swap(packed, "seq", Y_GROUPS)

    rows_f = rows_y.astype(F32)
    column_sq = jnp.sum(rows_f * rows_f, (0, 2))
    column_sq = column_sq + lax.ppermute(column_sq, "seq", flip_z)
    ratio = magnitude / jnp.sqrt(column_sq + EPSILON)
    scaled_t = (rows_f * ratio[None, :, None]).astype(BF16)
    scaled_t = scaled_t.transpose(1, 0, 2).reshape(own_cols, -1)
    reach = scaled_t.shape[1]
    up = jnp.pad((dora_b * ratio).astype(BF16).T, ((0, 0), (0, lanes - rank)))
    scaled_all = lax.all_gather(jnp.concatenate([scaled_t, up], 1), "dp", axis=0, tiled=True)
    up_all = scaled_all[:, reach:]

    own_tokens = lax.dynamic_slice_in_dim(tokens, seq_rank * feat, feat, 1).astype(F32)
    own_final = lax.dynamic_slice_in_dim(t5_final_gain, seq_rank * feat, feat, 0)
    encoded = ((own_tokens + ffn_sum) * own_final).astype(BF16)
    context = dot_t(encoded, context_all).astype(BF16).reshape(BLK, rows_of, lanes)
    context, own_heads = lax.optimization_barrier((context, own_heads))
    other_heads = lax.ppermute(own_heads[:, 1], "seq", flip_z)
    arrived = swap(context, both)
    token_of = jnp.sum(arrived.reshape(n_dp, n_seq, rows_of, lanes).astype(F32), 1).astype(BF16)
    values = token_of.astype(F32)
    centre = jnp.mean(values, (1, 2), keepdims=True)
    spread = jnp.mean((values - centre) * (values - centre), (1, 2), keepdims=True)
    layer_normed = ((values - centre) * lax.rsqrt(spread + EPSILON)).astype(BF16)
    target = jnp.arange(n_all, dtype=jnp.int32) // n_seq
    one_hot = (target[:, None] == prompt_owner_sample[None, :]).astype(BF16)
    outgoing = jnp.einsum("sp,pab->sab", one_hot, layer_normed, preferred_element_type=F32)
    text = swap(outgoing.astype(BF16), both).reshape(BLK, model)
    modulated = ((1.0 + text_scale) * text.astype(F32) + text_shift).astype(BF16)
    length = jnp.sum(jnp.where(prompt_owner_sample == data_rank, lengths, 0))
    key_value = jnp.dot(modulated, kv_all, preferred_element_type=F32)

    num, den = image_attention(own_heads, other_heads, image_qk_gain)
    num, den, key_value = lax.optimization_barrier((num, den, key_value))
    attended = text_attention(
        length.reshape(1),
        own_heads,
        other_heads,
        key_value,
        image_qk_gain,
        text_key_gain.reshape(1, HD),
        num,
        den,
    )

    lowered = jnp.dot(attended, dora_a.astype(BF16), preferred_element_type=F32).astype(BF16)
    outgoing = jnp.concatenate([attended, lowered], 1).reshape(n_y, 2 * BLK, own_rows + rank)
    gathered = swap(outgoing, "seq", Y_GROUPS)
    lowered = jnp.sum(gathered[:, :, own_rows:].astype(F32), 0)
    gathered = gathered[:, :, :own_rows].transpose(1, 0, 2).reshape(2 * BLK, -1)
    scaled_z = scaled_all[:, :reach]
    sent = dot_t(gathered[BLK:], scaled_z)
    sent = jnp.concatenate([sent, lowered[BLK:]], 1).astype(BF16)
    landed = lax.ppermute(sent, "seq", flip_z).astype(F32)
    kept = lax.optimization_barrier(dot_t(gathered[:BLK], scaled_z))
    out = kept + landed[:, :model]
    image_out = out.astype(BF16)[None]
    lowered = (lowered[:BLK] + landed[:, model:]).astype(BF16)

    down = jnp.dot(cotangent, up_all, preferred_element_type=F32).astype(BF16)
    down = jnp.concatenate([down, lax.ppermute(down, "seq", flip_z)], 0)
    down_all = swap(jnp.broadcast_to(down[None], (n_y,) + down.shape), "seq", Y_GROUPS)
    down_all = down_all.reshape(-1, lanes)[:, :rank]
    grad_a = lax.dot_general(
        down_all, attended, (((0,), (0,)), ((), ())), preferred_element_type=F32
    )
    for bit in (1, 2, 4, 8):
        grad_a = grad_a.astype(BF16)
        moved = lax.ppermute(grad_a, "dp", [(i, i ^ bit) for i in range(n_dp)])
        grad_a = grad_a.astype(F32) + moved.astype(F32)
    grad_a = grad_a.T
    up_part = lax.dot_general(
        lowered, cotangent, (((0,), (0,)), ((), ())), preferred_element_type=F32
    ).astype(BF16)
    magnitude_part = jnp.sum(out * cotangent.astype(F32), 0).astype(BF16)
    parts = jnp.concatenate([up_part, jnp.pad(magnitude_part[None], ((0, 7), (0, 0)))], 0)
    parts = parts.reshape(rank + 8, n_dp, own_cols).transpose(1, 0, 2)
    parts = jnp.sum(swap(parts, "dp").astype(F32), 0).astype(BF16)
    parts = swap(jnp.broadcast_to(parts[None], (n_seq,) + parts.shape), "seq")
    parts = jnp.sum(parts.astype(F32), 0)
    grad_b = parts[:rank] * ratio
    grad_magnitude = parts[rank] / magnitude
    return (image_out, grad_a, grad_b, grad_magnitude)


def solution(mesh):
    return jax.shard_map(
        on_device,
        mesh=mesh,
        in_specs=(
            P("dp", None, None),
            P(),
            P(),
            P(),
            P(None, None, "seq"),
            P("seq", None),
            P(),
            P("seq", "dp"),
            P("dp", None),
            P("dp", None),
            P("dp", None, "seq"),
            P(),
            P("dp", "seq", None, None),
            P(),
            P("seq", "dp"),
            P("seq", None),
            P(None, "dp"),
            P("dp"),
            P("dp", "seq", None),
        ),
        out_specs=(P("dp", "seq", None), P("seq", None), P(None, "dp"), P("dp")),
        check_vma=False,
    )
```

time: 338 us -> 302 us (0.89)
  waiting for transfers between devices: 149 us -> 93.8 us
  blocking collectives: 0 us -> 40.1 us
  starting transfers between devices: 70.9 us -> 60.2 us
  local copies, waits for them, and re-layouts: 33.8 us -> 26.2 us
  other arithmetic: 18 us -> 13.3 us
    all_to_all x11 -> x7, waiting for transfers between devices: 148 us -> 41.9 us  [swap(): lax.all_to_all(values, axes, 0, 0, tiled=True, axis_index_groups=groups)]
    ppermute x0 -> x8, waiting for transfers between devices: none -> 48.7 us  [the longest x1 37 us: on_device(): other_heads = lax.ppermute(own_heads[:, 1], 'seq', flip_z)]
    all_to_all x0 -> x2, blocking collectives: none -> 40.1 us  [swap(): lax.all_to_all(values, axes, 0, 0, tiled=True, axis_index_groups=groups)]
    all_to_all x11 -> x7, starting transfers between devices: 70.8 us -> 41.5 us  [swap(): lax.all_to_all(values, axes, 0, 0, tiled=True, axis_index_groups=groups)]
    ppermute x0 -> x8, starting transfers between devices: none -> 18.7 us  [the longest x4 8.63 us: on_device(): moved = lax.ppermute(grad_a, 'dp', [(i, i ^ bit) for i in range(n_dp)])]
    reshape x6 -> x4, local copies, waits for them, and re-layouts: 7.26 us -> 2.25 us  [the longest x2 1.66 us: on_device(): parts = parts.reshape(rank + 8, n_dp, own_cols).transpose(1, 0, 2)]
    unnamed x44 -> x46, local copies, waits for them, and re-layouts: 8.67 us -> 7.11 us
    pallas_call x2 -> x3, Pallas kernels: 13.6 us -> 14.5 us  [the longest x1 9.46 us: image_attention(): pl.pallas_call(image_kernel, grid=(heads, n_y), in_specs=[own_spec(1, 0),...]
  transfers between devices with their start and end apart: 14 -> 17, of which waited for: 8 -> 9; matrix products, arithmetic and copies ran while one was open for 24% -> 22% of each run, Pallas kernels for 4% -> 5%
where the time goes in v2:
time: 302 us; the launch traced here: 300 us
  waiting for transfers between devices  93.8 us (31%)
  starting transfers between devices  60.2 us (20%)
  blocking collectives  40.1 us (13%)
  matrix products  37.1 us (12%)
  local copies, waits for them, and re-layouts  26.2 us (9%)
  between operations  14.6 us (5%)
  Pallas kernels  14.5 us (5%)
  other arithmetic  13.3 us (4%)
    all_to_all x7, waiting for transfers between devices, swap(): lax.all_to_all(values, axes, 0, 0, tiled=True, axis_index_groups=groups)  41.9 us
    all_to_all x7, starting transfers between devices, swap(): lax.all_to_all(values, axes, 0, 0, tiled=True, axis_index_groups=groups)  41.5 us
    all_to_all x2, blocking collectives, swap(): lax.all_to_all(values, axes, 0, 0, tiled=True, axis_index_groups=groups)  40.1 us
    ppermute x1, waiting for transfers between devices, on_device(): other_heads = lax.ppermute(own_heads[:, 1], 'seq', flip_z)  37 us
    dot_general x3, matrix products, dot_t(): lax.dot_general(left, right, (((1,), (1,)), ((), ())), preferred_element_...  17.1 us
    pallas_call x1, Pallas kernels, image_attention(): pl.pallas_call(image_kernel, grid=(heads, n_y), in_specs=[own_spec(1, 0),...  9.46 us
    ppermute x4, starting transfers between devices, on_device(): moved = lax.ppermute(grad_a, 'dp', [(i, i ^ bit) for i in range(n_dp)])  8.63 us
    ppermute x4, waiting for transfers between devices, on_device(): moved = lax.ppermute(grad_a, 'dp', [(i, i ^ bit) for i in range(n_dp)])  8.24 us
  transfers between devices with their start and end apart: 17, of which 9 were waited for; matrix products, arithmetic and copies ran while one was open for 22% of the time, Pallas kernels for 5%

profile of v2, /device:TPU:1, one launch (start us, length us, event | category | flops | bytes accessed | tf_op | source)
XLA Modules:
  0.0 299.7 jit_solution(11725448132485606454)
XLA Ops:
  7.3 1.1 copy.97
  8.4 1.8 pad_maximum_fusion.2
  10.7 0.9 broadcast_in_dim.12
  11.5 5.0 %all-to-all-start = ((bf16[4,192,384]{2,1,0:T(8,128)(2,1)}), bf16[4,192,384]{2,1,0:T(8,128)(2,1)S(1)}, u32[]{:S(2)}, u32[]{:S(2)}) async-start(bf16[4,192,384]{2,1,0:T(8,128)(2,1)} %broadcast_in_dim.12), calls=%async_computation | async-start | bytes 1179648 | tf_op jit(solution)/shard_map/all_to_all | solution.py:24
  16.9 3.5 %fusion.54 = f32[128,640]{1,0:T(8,128)S(1)} fusion(bf16[2,4096,640]{2,1,0:T(8,128)(2,1)} %param.23, f32[4096]{0:T(1024)S(1)} %copy-done.20, f32[128]{0:T(128)S(1)} %add_rsqrt_fusion.1, bf16[1,256,4096]{2,1,0:T(8,128)(2,1)S(1)} %copy-done.12), kind=kOutput, calls=%fused_computation.72 | convolution fusion | flops 673841152 | bytes 6636032 | tf_op jit(solution)/shard_map/dot_general | solution.py:221
  20.4 7.7 %convolution_convert_fusion = bf16[128,4096]{1,0:T(8,128)(2,1)} fusion(bf16[640,4096]{1,0:T(8,128)(2,1)} %param.24, f32[128,640]{1,0:T(8,128)S(1)} %fusion.54, bf16[2,4096,640]{2,1,0:T(8,128)(2,1)} %param.23, f32[4096]{0:T(1024)S(1)} %copy-done.20, f32[128]{0:T(128)S(1)} %add_rsqrt_fusion.1, bf16[1,256,4096]{2,1,0:T(8,128)(2,1)} %param.19), kind=kOutput, calls=%fused_computation.10 | convolution fusion | flops 1344962560 | bytes 12927488 | tf_op jit(solution)/shard_map/dot_general | solution.py:224
  28.1 2.3 copy.105
  30.4 0.7 shard_map.210
  31.2 1.4 copy-done.2
  32.8 3.7 %collective-permute-start.1 = (f32[192]{0:T(256)S(1)}, f32[192]{0:T(256)S(1)}, u32[]{:S(2)}, u32[]{:S(2)}) collective-permute-start(f32[192]{0:T(256)S(1)} %fusion.25), channel_id=1, source_target_pairs={{0,1},{1,0},{2,3},{3,2},{4,5},{5,4},{6,7},{7,6},{8,9},{9,8},{10,11... | collective-permute-start | bytes 2312 | tf_op jit(solution)/shard_map/ppermute | solution.py:236
  36.5 1.0 collective-permute-done.1
  37.8 0.9 fusion.45
  38.8 24.6 %all_to_all.45 = bf16[8,128,512]{2,1,0:T(8,128)(2,1)S(1)} all-to-all(bf16[8,128,512]{2,1,0:T(8,128)(2,1)S(1)} %bitcast.94), channel_id=1, replica_groups=mesh['dp'=16,'seq'=8] {'seq'}, dimensions={0} | all-to-all | bytes 2097152 | tf_op jit(solution)/shard_map/all_to_all | solution.py:24
  63.4 4.4 %all-to-all-start.2 = ((bf16[4,2,384,384]{3,2,1,0:T(8,128)(2,1)}), bf16[4,2,384,384]{3,2,1,0:T(8,128)(2,1)S(1)}, u32[]{:S(2)}, u32[]{:S(2)}) async-start(bf16[4,2,384,384]{3,2,1,0:T(8,128)(2,1)} %copy-done.2), calls=%async_computation.2 | async-start | bytes 4718592 | tf_op jit(solution)/shard_map/all_to_all | solution.py:24
  67.7 2.3 slice.64
  70.1 0.8 dynamic_slice.7
  70.9 0.8 convert_reduce_fusion
  71.7 3.2 %all-gather.3.cloned.1.call-done = bf16[3072,1280]{1,0:T(8,128)(2,1)} async-done(((bf16[192,1280]{1,0:T(8,128)(2,1)}), bf16[3072,1280]{1,0:T(8,128)(2,1)}) %all-gather.3.cloned.1.call-update) | async-done | bytes 7864336 | tf_op jit(solution)/shard_map/all_gather | solution.py:208
  74.9 3.2 %fusion.21 = bf16[16,8,24,128]{3,1,2,0:T(8,128)(2,1)S(1)} fusion(bf16[3072,1280]{1,0:T(8,128)(2,1)} %all-gather.3.cloned.1.call-done, f32[128,512]{1,0:T(8,128)} %convert_reduce_fusion, f32[512]{0:T(512)S(1)} %dynamic_slice.7, bf16[1,128,4096]{2,1,0:T(8,128)(2,1)} %slice.64, s32[]{:T(128)S(6)} %select_n.25), kind=kOutput, calls=%fused_computation.31 | convolution fusion | flops 403308544 | bytes 4327428 | tf_op jit(solution)/shard_map/dot_general | solution.py:28
  78.1 1.0 copy.98
  79.2 16.0 %all-to-all-done.2.q_own.k_own.v_own = bf16[4,2,384,384]{3,2,1,0:T(8,128)(2,1)S(1)} async-done(((bf16[4,2,384,384]{3,2,1,0:T(8,128)(2,1)}), bf16[4,2,384,384]{3,2,1,0:T(8,128)(2,1)S(1)}, u32[]{:S(2)}, u32[]{:S(2)}) %all-to-all-start.2) | async-done | bytes 2359328 | tf_op jit(solution)/shard_map/all_to_all | solution.py:24
  95.2 7.7 %all-to-all-start.3 = ((bf16[128,24,128]{2,1,0:T(8,128)(2,1)}), bf16[128,24,128]{2,1,0:T(8,128)(2,1)}, u32[]{:S(2)}, u32[]{:S(2)}) async-start(bf16[128,24,128]{2,1,0:T(8,128)(2,1)} %bitcast.41), calls=%async_computation.3 | async-start | bytes 1572864 | tf_op jit(solution)/shard_map/all_to_all | solution.py:24
  104.0 1.1 slice_bitcast_fusion
  105.1 3.3 %collective-permute-start = (bf16[4,384,384]{2,1,0:T(8,128)(2,1)}, bf16[4,384,384]{2,1,0:T(8,128)(2,1)S(1)}, u32[]{:S(2)}, u32[]{:S(2)}) collective-permute-start(bf16[4,384,384]{2,1,0:T(8,128)(2,1)} %slice_bitcast_fusion), channel_id=1, source_target_pairs={{0,1},{1,0},{2,3},{3,2},{4,5},{5,4},{6,7},{7,6},{8,9},{9,8},{10,11... | collective-permute-start | bytes 3538952 | tf_op jit(solution)/shard_map/ppermute | solution.py:250
  108.4 17.8 %all-to-all-done.3 = bf16[128,24,128]{2,1,0:T(8,128)(2,1)} async-done(((bf16[128,24,128]{2,1,0:T(8,128)(2,1)}), bf16[128,24,128]{2,1,0:T(8,128)(2,1)}, u32[]{:S(2)}, u32[]{:S(2)}) %all-to-all-start.3) | async-done | bytes 786464 | tf_op jit(solution)/shard_map/all_to_all | solution.py:24
  126.1 1.3 bitcast_reduce_fusion
  128.0 1.1 convolution_convert_fusion.3
  129.2 1.4 copy.82
  130.6 5.9 %all-to-all-start.4 = ((bf16[128,24,128]{2,1,0:T(8,128)(2,1)}), bf16[128,24,128]{2,1,0:T(8,128)(2,1)}, u32[]{:S(2)}, u32[]{:S(2)}) async-start(bf16[128,24,128]{2,1,0:T(8,128)(2,1)} %copy.82), calls=%async_computation.4 | async-start | bytes 1572864 | tf_op jit(solution)/shard_map/all_to_all | solution.py:24
  136.5 1.3 broadcast_add_fusion
  137.8 37.0 %collective-permute-done.q_other.k_other.v_other = bf16[4,384,384]{2,1,0:T(8,128)(2,1)S(1)} collective-permute-done((bf16[4,384,384]{2,1,0:T(8,128)(2,1)}, bf16[4,384,384]{2,1,0:T(8,128)(2,1)S(1)}, u32[]{:S(2)}, u32[]{:S(2)}) %collective-permute-start) | collective-permute-done | bytes 1179680 | tf_op jit(solution)/shard_map/ppermute | solution.py:250
  174.8 9.5 %shard_map.211 = (f32[1024,384]{1,0:T(8,128)S(1)}, f32[1024,384]{1,0:T(8,128)S(1)}) custom-call(bf16[4,2,384,384]{3,2,1,0:T(8,128)(2,1)S(1)} %all-to-all-done.2.q_own.k_own.v_own, bf16[4,384,384]{2,1,0:T(8,128)(2,1)S(1)} %collective-permute-done.q_other.k_other.v_other, bf16[4,2,384,384]{3,2,1,0:T(8,128)(2,1)S(1)} %all-to-all-done.2.q_own.k_own.v_own, ...), custom_call_target="tpu_custom_call" | custom-call | flops 2415919104 | bytes 5505024 | tf_op jit(solution)/shard_map/pallas_call | solution.py:91
  184.2 1.1 copy-done.4
  185.4 1.1 copy-done.6
  186.5 2.4 copy.83
  189.0 4.8 %fusion.10.k_ref.v_ref = f32[128,768]{1,0:T(8,128)S(1)} fusion(bf16[3072,1280]{1,0:T(8,128)(2,1)} %all-gather.3.cloned.1.call-done, bf16[128,3072]{0,1:T(8,128)(2,1)} %bitcast.100, f32[3072]{0:T(1024)} %bitcast.107, f32[3072]{0:T(1024)} %bitcast.105), kind=kOutput, calls=%fused_computation.11 | convolution fusion | flops 605552640 | bytes 5922816 | tf_op jit(solution)/shard_map/dot_general | solution.py:263
  193.8 4.3 %shard_map.212 = bf16[1024,384]{1,0:T(8,128)(2,1)S(1)} custom-call(s32[1]{0:T(128)} %bitcast.length_ref, bf16[4,2,384,384]{3,2,1,0:T(8,128)(2,1)S(1)} %all-to-all-done.2.q_own.k_own.v_own, bf16[4,384,384]{2,1,0:T(8,128)(2,1)S(1)} %collective-permute-done.q_other.k_other.v_other, f32[128,768]{1,0:T(8,128)S(1)} %fusion.10.k_ref.v_ref, ...), custom_call_target="tpu_custom_call" | custom-call | flops 301989888 | bytes 4718592 | tf_op jit(solution)/shard_map/pallas_call | solution.py:142
  198.1 0.9 copy-done
  199.6 1.3 pad_maximum_fusion
  201.3 15.6 %all_to_all.46 = bf16[4,256,448]{1,2,0:T(8,128)(2,1)S(1)} all-to-all(bf16[4,256,448]{1,2,0:T(8,128)(2,1)S(1)} %copy.85), channel_id=1, replica_groups={{0,2,4,6},{1,3,5,7},{8,10,12,14},{9,11,13,15},{16,18,20,22},{17,19,21,2..., dimensions={0} | all-to-all | bytes 1835008 | tf_op jit(solution)/shard_map/all_to_all | solution.py:24
  217.2 0.9 fusion.85
  218.1 1.5 fusion.34
  219.9 6.9 %fusion.12 = bf16[128,3072]{1,0:T(8,128)(2,1)S(1)} fusion(bf16[128,1536]{0,1:T(8,128)(2,1)S(1)} %bitcast.102, bf16[3072,1664]{1,0:T(8,128)(2,1)} %all-gather.5.cloned.1.call-done), kind=kOutput, calls=%fused_computation.14 | convolution fusion | flops 1208352768 | bytes 10616832 | tf_op jit(solution)/shard_map/dot_general | solution.py:28
  226.8 0.7 broadcast_in_dim.15
  227.6 3.4 %all-to-all-start.6 = ((bf16[4,256,128]{2,1,0:T(8,128)(2,1)}), bf16[4,256,128]{2,1,0:T(8,128)(2,1)S(1)}, u32[]{:S(2)}, u32[]{:S(2)}) async-start(bf16[4,256,128]{2,1,0:T(8,128)(2,1)} %broadcast_in_dim.15), calls=%async_computation.6 | async-start | bytes 524288 | tf_op jit(solution)/shard_map/all_to_all | solution.py:24
  231.0 1.3 copy.89
  232.3 2.8 collective-permute-start.2
  235.1 1.4 all-to-all-done.6
  236.8 4.1 %collective-permute-start.4 = (bf16[64,384]{1,0:T(8,128)(2,1)S(1)}, bf16[64,384]{1,0:T(8,128)(2,1)S(1)}, u32[]{:S(2)}, u32[]{:S(2)}) collective-permute-start(bf16[64,384]{1,0:T(8,128)(2,1)S(1)} %convolution_convert_fusion.5), channel_id=1, source_target_pairs={{0,8},{8,0},{16,24},{24,16},{32,40},{40,32},{48,56},{56,48},{64,72... | collective-permute-start | bytes 147464 | tf_op jit(solution)/shard_map/ppermute | solution.py:301
  240.8 7.0 %fusion.2 = f32[128,3072]{1,0:T(8,128)S(1)} fusion(bf16[128,1536]{0,1:T(8,128)(2,1)} %bitcast.101, bf16[3072,1664]{1,0:T(8,128)(2,1)} %all-gather.5.cloned.1.call-done), kind=kOutput, calls=%fused_computation.2 | convolution fusion | flops 1207959552 | bytes 11403264 | tf_op jit(solution)/shard_map/dot_general | solution.py:28
  248.2 2.5 collective-permute-done.2
  250.7 1.5 copy.90
  252.4 1.2 multiply_reduce_fusion
  253.9 0.7 reshape.138
  254.6 1.0 copy.106
  255.6 7.7 %all-to-all-start.7 = ((bf16[16,72,192]{2,1,0:T(8,128)(2,1)}), bf16[16,72,192]{2,1,0:T(8,128)(2,1)S(1)}, u32[]{:S(2)}, u32[]{:S(2)}) async-start(bf16[16,72,192]{2,1,0:T(8,128)(2,1)} %bitcast.91), calls=%async_computation.7 | async-start | bytes 1179648 | tf_op jit(solution)/shard_map/all_to_all | solution.py:24
  263.4 3.0 collective-permute-start.6
  266.3 8.2 %collective-permute-done.6 = bf16[64,384]{1,0:T(8,128)(2,1)S(1)} collective-permute-done((bf16[64,384]{1,0:T(8,128)(2,1)S(1)}, bf16[64,384]{1,0:T(8,128)(2,1)S(1)}, u32[]{:S(2)}, u32[]{:S(2)}) %collective-permute-start.6) | collective-permute-done | bytes 49184 | tf_op jit(solution)/shard_map/ppermute | solution.py:301
  274.6 1.3 collective-permute-start.7
  276.0 0.7 broadcast_in_dim.16
  276.7 7.5 %all-to-all-start.8 = ((bf16[8,72,192]{2,1,0:T(8,128)(2,1)}), bf16[8,72,192]{2,1,0:T(8,128)(2,1)S(1)}, u32[]{:S(2)}, u32[]{:S(2)}) async-start(bf16[8,72,192]{2,1,0:T(8,128)(2,1)} %broadcast_in_dim.16), calls=%async_computation.8 | async-start | bytes 589824 | tf_op jit(solution)/shard_map/all_to_all | solution.py:24
  284.2 0.7 add_bitcast_fusion
  284.8 6.8 %all-to-all-done.8 = bf16[8,72,192]{2,1,0:T(8,128)(2,1)S(1)} async-done(((bf16[8,72,192]{2,1,0:T(8,128)(2,1)}), bf16[8,72,192]{2,1,0:T(8,128)(2,1)S(1)}, u32[]{:S(2)}, u32[]{:S(2)}) %all-to-all-start.8) | async-done | bytes 221216 | tf_op jit(solution)/shard_map/all_to_all | solution.py:24
  291.6 0.6 slice_multiply_fusion
  (91 shorter events, 6.9 us)
Async XLA Ops:
  7.2 3.0 %copy-start.15 = (f32[64,192]{1,0:T(8,128)S(1)}, f32[64,192]{1,0:T(8,128)}, u32[]{:S(2)}) copy-start(f32[64,192]{1,0:T(8,128)} %param.35) | copy-start | bytes 147460
  7.2 3.0 %copy-start.13 = (f32[384,64]{0,1:T(8,128)S(1)}, f32[384,64]{0,1:T(8,128)}, u32[]{:S(2)}) copy-start(f32[384,64]{0,1:T(8,128)} %param.34) | copy-start | bytes 294916
  7.2 3.0 %copy-start.16 = (bf16[384,192]{0,1:T(8,128)(2,1)S(1)}, bf16[384,192]{0,1:T(8,128)(2,1)}, u32[]{:S(2)}) copy-start(bf16[384,192]{0,1:T(8,128)(2,1)} %param.33) | copy-start | bytes 442372
  7.2 67.7 %all-gather.3.cloned.1.call-start = ((), (), s32[]{:S(2)}) async-start(), calls=%async_computation.9 | async-start | bytes 8355840 | tf_op jit(solution)/shard_map/all_gather | solution.py:208
  7.2 9.3 %copy-start.12 = (bf16[1,256,4096]{2,1,0:T(8,128)(2,1)S(1)}, bf16[1,256,4096]{2,1,0:T(8,128)(2,1)}, u32[]{:S(2)}) copy-start(bf16[1,256,4096]{2,1,0:T(8,128)(2,1)} %param.19) | copy-start | bytes 6291460
  10.2 6.7 %copy-start.20 = (f32[4096]{0:T(1024)S(1)}, f32[4096]{0:T(1024)}, u32[]{:S(2)}) copy-start(f32[4096]{0:T(1024)} %param.22) | copy-start | bytes 49156
  11.5 21.0 %all-to-all-start = ((bf16[4,192,384]{2,1,0:T(8,128)(2,1)}), bf16[4,192,384]{2,1,0:T(8,128)(2,1)S(1)}, u32[]{:S(2)}, u32[]{:S(2)}) async-start(bf16[4,192,384]{2,1,0:T(8,128)(2,1)} %broadcast_in_dim.12), calls=%async_computation | async-start | bytes 1179648 | tf_op jit(solution)/shard_map/all_to_all | solution.py:24
  16.6 201.6 %all-gather.5.cloned.1.call-start = ((), (), s32[]{:S(2)}) async-start(), calls=%async_computation.10 | async-start | bytes 10862592 | tf_op jit(solution)/shard_map/all_gather | solution.py:242
  20.4 10.0 %copy-start.3 = (bf16[1,128,3,3072]{3,1,2,0:T(8,128)(2,1)S(1)}, bf16[1,128,3,3072]{3,1,2,0:T(8,128)(2,1)}, u32[]{:S(2)}) copy-start(bf16[1,128,3,3072]{3,1,2,0:T(8,128)(2,1)} %param.31) | copy-start | bytes 7077892
  30.4 7.0 %copy-start.17 = (f32[192]{0:T(256)S(1)}, f32[192]{0:T(256)}, u32[]{:S(2)}) copy-start(f32[192]{0:T(256)} %param.36) | copy-start | bytes 2308
  31.2 1.4 copy-start.2
  32.8 4.7 %collective-permute-start.1 = (f32[192]{0:T(256)S(1)}, f32[192]{0:T(256)S(1)}, u32[]{:S(2)}, u32[]{:S(2)}) collective-permute-start(f32[192]{0:T(256)S(1)} %fusion.25), channel_id=1, source_target_pairs={{0,1},{1,0},{2,3},{3,2},{4,5},{5,4},{6,7},{7,6},{8,9},{9,8},{10,11... | collective-permute-start | bytes 2312 | tf_op jit(solution)/shard_map/ppermute | solution.py:236
  37.6 1.3 copy-start.10
  63.4 31.8 %all-to-all-start.2 = ((bf16[4,2,384,384]{3,2,1,0:T(8,128)(2,1)}), bf16[4,2,384,384]{3,2,1,0:T(8,128)(2,1)S(1)}, u32[]{:S(2)}, u32[]{:S(2)}) async-start(bf16[4,2,384,384]{3,2,1,0:T(8,128)(2,1)} %copy-done.2), calls=%async_computation.2 | async-start | bytes 4718592 | tf_op jit(solution)/shard_map/all_to_all | solution.py:24
  78.1 25.2 %copy-start.18 = (s32[16]{0:T(128)S(1)}, s32[16]{0:T(128)}, u32[]{:S(2)}) copy-start(s32[16]{0:T(128)} %param.21) | copy-start | bytes 196
  78.1 25.2 %copy-start.19 = (s32[16]{0:T(128)S(1)}, s32[16]{0:T(128)}, u32[]{:S(2)}) copy-start(s32[16]{0:T(128)} %param.20) | copy-start | bytes 196
  95.2 31.0 %all-to-all-start.3 = ((bf16[128,24,128]{2,1,0:T(8,128)(2,1)}), bf16[128,24,128]{2,1,0:T(8,128)(2,1)}, u32[]{:S(2)}, u32[]{:S(2)}) async-start(bf16[128,24,128]{2,1,0:T(8,128)(2,1)} %bitcast.41), calls=%async_computation.3 | async-start | bytes 1572864 | tf_op jit(solution)/shard_map/all_to_all | solution.py:24
  105.1 69.7 %collective-permute-start = (bf16[4,384,384]{2,1,0:T(8,128)(2,1)}, bf16[4,384,384]{2,1,0:T(8,128)(2,1)S(1)}, u32[]{:S(2)}, u32[]{:S(2)}) collective-permute-start(bf16[4,384,384]{2,1,0:T(8,128)(2,1)} %slice_bitcast_fusion), channel_id=1, source_target_pairs={{0,1},{1,0},{2,3},{3,2},{4,5},{5,4},{6,7},{7,6},{8,9},{9,8},{10,11... | collective-permute-start | bytes 3538952 | tf_op jit(solution)/shard_map/ppermute | solution.py:250
  127.9 46.9 %copy-start.8 = (f32[2,128]{1,0:T(2,128)S(1)}, f32[2,128]{1,0:T(2,128)}, u32[]{:S(2)}) copy-start(f32[2,128]{1,0:T(2,128)} %gain_ref.3) | copy-start | bytes 3076
  130.6 56.0 %all-to-all-start.4 = ((bf16[128,24,128]{2,1,0:T(8,128)(2,1)}), bf16[128,24,128]{2,1,0:T(8,128)(2,1)}, u32[]{:S(2)}, u32[]{:S(2)}) async-start(bf16[128,24,128]{2,1,0:T(8,128)(2,1)} %copy.82), calls=%async_computation.4 | async-start | bytes 1572864 | tf_op jit(solution)/shard_map/all_to_all | solution.py:24
  184.2 1.2 copy-start.4
  185.4 1.2 copy-start.6
  188.9 4.8 %copy-start.5 = (f32[1024,384]{1,0:T(8,128)S(1)}, f32[1024,384]{1,0:T(8,128)}, u32[]{:S(2)}) copy-start(f32[1024,384]{1,0:T(8,128)} %copy-done.4) | copy-start | bytes 4718596
  189.0 4.8 %copy-start.7 = (f32[1024,384]{1,0:T(8,128)S(1)}, f32[1024,384]{1,0:T(8,128)}, u32[]{:S(2)}) copy-start(f32[1024,384]{1,0:T(8,128)} %copy-done.6) | copy-start | bytes 4718596
  189.0 4.8 %copy-start.9 = (f32[128]{0:T(128)S(1)}, f32[128]{0:T(128)}, u32[]{:S(2)}) copy-start(f32[128]{0:T(128)} %param.30) | copy-start | bytes 1540
  193.8 5.2 %copy-start.14 = (f32[384,64]{0,1:T(8,128)S(1)}, f32[384,64]{0,1:T(8,128)}, u32[]{:S(2)}) copy-start(f32[384,64]{0,1:T(8,128)} %param.34) | copy-start | bytes 294916
  198.1 0.9 copy-start
  216.9 1.2 copy-start.11
  219.6 7.2 %collective-permute-start.3 = (bf16[128,128]{1,0:T(8,128)(2,1)S(1)}, bf16[128,128]{1,0:T(8,128)(2,1)S(1)}, u32[]{:S(2)}, u32[]{:S(2)}) collective-permute-start(bf16[128,128]{1,0:T(8,128)(2,1)S(1)} %fusion.34), channel_id=1, source_target_pairs={{0,1},{1,0},{2,3},{3,2},{4,5},{5,4},{6,7},{7,6},{8,9},{9,8},{10,11... | collective-permute-start | bytes 98312 | tf_op jit(solution)/shard_map/ppermute | solution.py:293
  226.8 9.7 %copy-start.1 = (bf16[1024,384]{1,0:T(8,128)(2,1)S(1)}, bf16[1024,384]{1,0:T(8,128)(2,1)}, u32[]{:S(2)}) copy-start(bf16[1024,384]{1,0:T(8,128)(2,1)} %copy-done) | copy-start | bytes 2359300
  227.6 8.9 %all-to-all-start.6 = ((bf16[4,256,128]{2,1,0:T(8,128)(2,1)}), bf16[4,256,128]{2,1,0:T(8,128)(2,1)S(1)}, u32[]{:S(2)}, u32[]{:S(2)}) async-start(bf16[4,256,128]{2,1,0:T(8,128)(2,1)} %broadcast_in_dim.15), calls=%async_computation.6 | async-start | bytes 524288 | tf_op jit(solution)/shard_map/all_to_all | solution.py:24
  232.3 18.3 %collective-permute-start.2 = (bf16[128,3136]{0,1:T(8,128)(2,1)}, bf16[128,3136]{0,1:T(8,128)(2,1)}, u32[]{:S(2)}, u32[]{:S(2)}) collective-permute-start(bf16[128,3136]{0,1:T(8,128)(2,1)} %copy.89), channel_id=1, source_target_pairs={{0,1},{1,0},{2,3},{3,2},{4,5},{5,4},{6,7},{7,6},{8,9},{9,8},{10,11... | collective-permute-start | bytes 2408456 | tf_op jit(solution)/shard_map/ppermute | solution.py:286
  236.8 11.1 %collective-permute-start.4 = (bf16[64,384]{1,0:T(8,128)(2,1)S(1)}, bf16[64,384]{1,0:T(8,128)(2,1)S(1)}, u32[]{:S(2)}, u32[]{:S(2)}) collective-permute-start(bf16[64,384]{1,0:T(8,128)(2,1)S(1)} %convolution_convert_fusion.5), channel_id=1, source_target_pairs={{0,8},{8,0},{16,24},{24,16},{32,40},{40,32},{48,56},{56,48},{64,72... | collective-permute-start | bytes 147464 | tf_op jit(solution)/shard_map/ppermute | solution.py:301
  247.9 15.4 %collective-permute-start.5 = (bf16[64,384]{1,0:T(8,128)(2,1)S(1)}, bf16[64,384]{1,0:T(8,128)(2,1)S(1)}, u32[]{:S(2)}, u32[]{:S(2)}) collective-permute-start(bf16[64,384]{1,0:T(8,128)(2,1)S(1)} %add_convert_fusion.2), channel_id=1, source_target_pairs={{0,16},{8,24},{16,0},{24,8},{32,48},{40,56},{48,32},{56,40},{64,80... | collective-permute-start | bytes 147464 | tf_op jit(solution)/shard_map/ppermute | solution.py:301
  255.6 20.3 %all-to-all-start.7 = ((bf16[16,72,192]{2,1,0:T(8,128)(2,1)}), bf16[16,72,192]{2,1,0:T(8,128)(2,1)S(1)}, u32[]{:S(2)}, u32[]{:S(2)}) async-start(bf16[16,72,192]{2,1,0:T(8,128)(2,1)} %bitcast.91), calls=%async_computation.7 | async-start | bytes 1179648 | tf_op jit(solution)/shard_map/all_to_all | solution.py:24
  263.4 11.2 %collective-permute-start.6 = (bf16[64,384]{1,0:T(8,128)(2,1)S(1)}, bf16[64,384]{1,0:T(8,128)(2,1)S(1)}, u32[]{:S(2)}, u32[]{:S(2)}) collective-permute-start(bf16[64,384]{1,0:T(8,128)(2,1)S(1)} %add_convert_fusion.1), channel_id=1, source_target_pairs={{0,32},{8,40},{16,48},{24,56},{32,0},{40,8},{48,16},{56,24},{64,96... | collective-permute-start | bytes 147464 | tf_op jit(solution)/shard_map/ppermute | solution.py:301
  274.6 9.6 %collective-permute-start.7 = (bf16[64,384]{1,0:T(8,128)(2,1)S(1)}, bf16[64,384]{1,0:T(8,128)(2,1)S(1)}, u32[]{:S(2)}, u32[]{:S(2)}) collective-permute-start(bf16[64,384]{1,0:T(8,128)(2,1)S(1)} %add_convert_fusion), channel_id=1, source_target_pairs={{0,64},{8,72},{16,80},{24,88},{32,96},{40,104},{48,112},{56,120},{... | collective-permute-start | bytes 147464 | tf_op jit(solution)/shard_map/ppermute | solution.py:301
  276.7 14.9 %all-to-all-start.8 = ((bf16[8,72,192]{2,1,0:T(8,128)(2,1)}), bf16[8,72,192]{2,1,0:T(8,128)(2,1)S(1)}, u32[]{:S(2)}, u32[]{:S(2)}) async-start(bf16[8,72,192]{2,1,0:T(8,128)(2,1)} %broadcast_in_dim.16), calls=%async_computation.8 | async-start | bytes 589824 | tf_op jit(solution)/shard_map/all_to_all | solution.py:24
Sparse Core Ops, SparseCore 0:
  10.3 64.5 all-gather.2
  76.6 103.5 all-gather.4

commit v3 on v2

--- a/solution.py
+++ b/solution.py
@@ -22,6 +22,29 @@
 
 def swap(values, axes, groups=None):
     return lax.all_to_all(values, axes, 0, 0, tiled=True, axis_index_groups=groups)
+
+
+def gather_columns(values):
+    n_dp = lax.axis_size("dp")
+    near = n_dp // 2
+    other = lax.ppermute(values, "dp", [(i, (i + near) % n_dp) for i in range(n_dp)])
+    low = lax.axis_index("dp") < near
+    halves = jnp.stack([jnp.where(low, values, other), jnp.where(low, other, values)])
+    groups = [list(range(near)), list(range(near, n_dp))]
+    gathered = lax.all_gather(halves, "dp", axis=0, axis_index_groups=groups)
+    return gathered.reshape(n_dp * values.shape[0], values.shape[1])
+
+
+def to_gathered(values, n_dp):
+    rows = values.shape[0]
+    cut = values.reshape(rows, 2, n_dp // 2, -1)
+    return cut.transpose(0, 2, 1, 3).reshape(rows, -1)
+
+
+def from_gathered(values, n_dp):
+    rows = values.shape[0]
+    cut = values.reshape(rows, n_dp // 2, 2, -1)
+    return cut.transpose(0, 2, 1, 3).reshape(rows, -1)
 
 
 def dot_t(left, right):
@@ -196,7 +219,7 @@
     model = own_cols * n_dp
     lanes = 128
     rows_of = model // lanes
-    cotangent = grad_out[0]
+    cotangent = to_gathered(grad_out[0], n_dp)
 
     pair = seq_rank % 2
     flip_z = [(i, i ^ 1) for i in range(n_seq)]
@@ -205,7 +228,7 @@
     weights = jnp.concatenate(
         [context_weight.T, kv_weight.reshape(kv_weight.shape[0], -1)], 1
     )
-    weights = lax.all_gather(weights, "dp", axis=0, tiled=True)
+    weights = gather_columns(weights)
     depth = context_weight.shape[0]
     context_all, kv_all = weights[:, :depth], weights[:, depth:]
 
@@ -239,7 +262,7 @@
     scaled_t = scaled_t.transpose(1, 0, 2).reshape(own_cols, -1)
     reach = scaled_t.shape[1]
     up = jnp.pad((dora_b * ratio).astype(BF16).T, ((0, 0), (0, lanes - rank)))
-    scaled_all = lax.all_gather(jnp.concatenate([scaled_t, up], 1), "dp", axis=0, tiled=True)
+    scaled_all = gather_columns(jnp.concatenate([scaled_t, up], 1))
     up_all = scaled_all[:, reach:]
 
     own_tokens = lax.dynamic_slice_in_dim(tokens, seq_rank * feat, feat, 1).astype(F32)
@@ -258,7 +281,8 @@
     one_hot = (target[:, None] == prompt_owner_sample[None, :]).astype(BF16)
     outgoing = jnp.einsum("sp,pab->sab", one_hot, layer_normed, preferred_element_type=F32)
     text = swap(outgoing.astype(BF16), both).reshape(BLK, model)
-    modulated = ((1.0 + text_scale) * text.astype(F32) + text_shift).astype(BF16)
+    scale, shift = to_gathered(text_scale, n_dp), to_gathered(text_shift, n_dp)
+    modulated = ((1.0 + scale) * text.astype(F32) + shift).astype(BF16)
     length = jnp.sum(jnp.where(prompt_owner_sample == data_rank, lengths, 0))
     key_value = jnp.dot(modulated, kv_all, preferred_element_type=F32)
 
@@ -286,7 +310,7 @@
     landed = lax.ppermute(sent, "seq", flip_z).astype(F32)
     kept = lax.optimization_barrier(dot_t(gathered[:BLK], scaled_z))
     out = kept + landed[:, :model]
-    image_out = out.astype(BF16)[None]
+    image_out = from_gathered(out.astype(BF16), n_dp)[None]
     lowered = (lowered[:BLK] + landed[:, model:]).astype(BF16)
 
     down = jnp.dot(cotangent, up_all, preferred_element_type=F32).astype(BF16)
@@ -306,7 +330,8 @@
     ).astype(BF16)
     magnitude_part = jnp.sum(out * cotangent.astype(F32), 0).astype(BF16)
     parts = jnp.concatenate([up_part, jnp.pad(magnitude_part[None], ((0, 7), (0, 0)))], 0)
-    parts = parts.reshape(rank + 8, n_dp, own_cols).transpose(1, 0, 2)
+    parts = parts.reshape(rank + 8, n_dp // 2, 2, own_cols).transpose(2, 1, 0, 3)
+    parts = parts.reshape(n_dp, rank + 8, own_cols)
     parts = jnp.sum(swap(parts, "dp").astype(F32), 0).astype(BF16)
     parts = swap(jnp.broadcast_to(parts[None], (n_seq,) + parts.shape), "seq")
     parts = jnp.sum(parts.astype(F32), 0)

time: 302 us -> 305 us (level)
  blocking collectives: 40.1 us -> 19.4 us
  local copies, waits for them, and re-layouts: 26.2 us -> 38.3 us
  starting transfers between devices: 60.2 us -> 70.4 us
  waiting for transfers between devices: 93.8 us -> 89.2 us
  other arithmetic: 13.3 us -> 16.4 us
    ppermute x1, waiting for transfers between devices: 37 us -> 5.43 us  [on_device(): other_heads = lax.ppermute(own_heads[:, 1], 'seq', flip_z)]
    ppermute x0 -> x2, waiting for transfers between devices: none -> 22.4 us  [gather_columns(): lax.ppermute(values, 'dp', [(i, (i + near) % n_dp) for i in range(n_dp)])]
    all_to_all x2 -> x1, blocking collectives: 40.1 us -> 19.4 us  [swap(): lax.all_to_all(values, axes, 0, 0, tiled=True, axis_index_groups=groups)]
    all_to_all x7 -> x8, waiting for transfers between devices: 41.9 us -> 49.9 us  [swap(): lax.all_to_all(values, axes, 0, 0, tiled=True, axis_index_groups=groups)]
    all_to_all x7 -> x8, starting transfers between devices: 41.5 us -> 47.6 us  [swap(): lax.all_to_all(values, axes, 0, 0, tiled=True, axis_index_groups=groups)]
    add x0 -> x4, local copies, waits for them, and re-layouts: none -> 4.82 us  [on_device(): modulated = ((1.0 + scale) * text.astype(F32) + shift).astype(BF16)]
    ppermute x0 -> x2, starting transfers between devices: none -> 3.89 us  [gather_columns(): lax.ppermute(values, 'dp', [(i, (i + near) % n_dp) for i in range(n_dp)])]
    unnamed x46 -> x57, local copies, waits for them, and re-layouts: 7.11 us -> 10.7 us
  transfers between devices with their start and end apart: 17 -> 20, of which waited for: 9 -> 11; matrix products, arithmetic and copies ran while one was open for 22% -> 26% of each run, Pallas kernels for 5% -> 5%
where the time goes in v3:
time: 305 us; the launch traced here: 302 us
  waiting for transfers between devices  89.2 us (29%)
  starting transfers between devices  70.4 us (23%)
  matrix products  39 us (13%)
  local copies, waits for them, and re-layouts  38.3 us (13%)
  blocking collectives  19.4 us (6%)
  other arithmetic  16.4 us (5%)
  between operations  14.6 us (5%)
  Pallas kernels  14.5 us (5%)
    all_to_all x8, waiting for transfers between devices, swap(): lax.all_to_all(values, axes, 0, 0, tiled=True, axis_index_groups=groups)  49.9 us
    all_to_all x8, starting transfers between devices, swap(): lax.all_to_all(values, axes, 0, 0, tiled=True, axis_index_groups=groups)  47.6 us
    ppermute x2, waiting for transfers between devices, gather_columns(): lax.ppermute(values, 'dp', [(i, (i + near) % n_dp) for i in range(n_dp)])  22.4 us
    all_to_all x1, blocking collectives, swap(): lax.all_to_all(values, axes, 0, 0, tiled=True, axis_index_groups=groups)  19.4 us
    dot_general x3, matrix products, dot_t(): lax.dot_general(left, right, (((1,), (1,)), ((), ())), preferred_element_...  19.1 us
    unnamed x57, local copies, waits for them, and re-layouts  10.7 us
    pallas_call x1, Pallas kernels, image_attention(): pl.pallas_call(image_kernel, grid=(heads, n_y), in_specs=[own_spec(1, 0),...  9.45 us
    ppermute x4, starting transfers between devices, on_device(): moved = lax.ppermute(grad_a, 'dp', [(i, i ^ bit) for i in range(n_dp)])  9.26 us
  transfers between devices with their start and end apart: 20, of which 11 were waited for; matrix products, arithmetic and copies ran while one was open for 26% of the time, Pallas kernels for 5%

profile of v3, /device:TPU:1, one launch (start us, length us, event | category | flops | bytes accessed | tf_op | source)
XLA Modules:
  0.0 301.8 jit_solution(11916434202158055171)
XLA Ops:
  9.2 2.5 collective-permute-start
  11.7 10.9 %collective-permute-done = bf16[192,1280]{1,0:T(8,128)(2,1)S(1)} collective-permute-done((bf16[192,1280]{1,0:T(8,128)(2,1)S(1)}, bf16[192,1280]{1,0:T(8,128)(2,1)S(1)}, u32[]{:S(2)}, u32[]{:S(2)}) %collective-permute-start) | collective-permute-done | bytes 491552 | tf_op jit(solution)/shard_map/ppermute | solution.py:30
  22.6 1.1 select_bitcast_fusion.3
  23.7 1.0 pad_maximum_fusion.2
  26.2 4.1 %all-to-all-start = ((bf16[4,192,384]{2,1,0:T(8,128)(2,1)}), bf16[4,192,384]{2,1,0:T(8,128)(2,1)S(1)}, u32[]{:S(2)}, u32[]{:S(2)}) async-start(bf16[4,192,384]{2,1,0:T(8,128)(2,1)} %broadcast_in_dim.10), calls=%async_computation | async-start | bytes 1179648 | tf_op jit(solution)/shard_map/all_to_all | solution.py:24
  30.6 3.5 %fusion.53 = f32[128,640]{1,0:T(8,128)S(1)} fusion(bf16[2,4096,640]{2,1,0:T(8,128)(2,1)} %param.23, f32[4096]{0:T(1024)S(1)} %copy-done.24, f32[128]{0:T(128)S(1)} %add_rsqrt_fusion.1, bf16[1,256,4096]{2,1,0:T(8,128)(2,1)S(1)} %copy-done.11), kind=kOutput, calls=%fused_computation.75 | convolution fusion | flops 673841152 | bytes 6636032 | tf_op jit(solution)/shard_map/dot_general | solution.py:244
  34.1 8.0 %convolution_convert_fusion = bf16[128,4096]{1,0:T(8,128)(2,1)} fusion(bf16[640,4096]{1,0:T(8,128)(2,1)} %param.24, f32[128,640]{1,0:T(8,128)S(1)} %fusion.53, bf16[2,4096,640]{2,1,0:T(8,128)(2,1)} %param.23, f32[4096]{0:T(1024)S(1)} %copy-done.24, f32[128]{0:T(128)S(1)} %add_rsqrt_fusion.1, bf16[1,256,4096]{2,1,0:T(8,128)(2,1)} %param.19), kind=kOutput, calls=%fused_computation.10 | convolution fusion | flops 1344962560 | bytes 12927488 | tf_op jit(solution)/shard_map/dot_general | solution.py:247
  42.1 2.3 copy.150
  45.2 1.4 copy-done.2
  46.8 3.3 %collective-permute-start.2 = (f32[192]{0:T(256)S(1)}, f32[192]{0:T(256)S(1)}, u32[]{:S(2)}, u32[]{:S(2)}) collective-permute-start(f32[192]{0:T(256)S(1)} %fusion.25), channel_id=1, source_target_pairs={{0,1},{1,0},{2,3},{3,2},{4,5},{5,4},{6,7},{7,6},{8,9},{9,8},{10,11... | collective-permute-start | bytes 2312 | tf_op jit(solution)/shard_map/ppermute | solution.py:259
  51.6 1.3 collective-permute-start.3
  52.9 11.5 %collective-permute-done.3 = bf16[192,1664]{1,0:T(8,128)(2,1)S(1)} collective-permute-done((bf16[192,1664]{1,0:T(8,128)(2,1)S(1)}, bf16[192,1664]{1,0:T(8,128)(2,1)S(1)}, u32[]{:S(2)}, u32[]{:S(2)}) %collective-permute-start.3) | collective-permute-done | bytes 639008 | tf_op jit(solution)/shard_map/ppermute | solution.py:30
  64.6 1.2 pad_maximum_fusion
  66.2 19.4 %all_to_all.45 = bf16[8,128,512]{2,1,0:T(8,128)(2,1)S(1)} all-to-all(bf16[8,128,512]{2,1,0:T(8,128)(2,1)S(1)} %bitcast.115), channel_id=1, replica_groups=mesh['dp'=16,'seq'=8] {'seq'}, dimensions={0} | all-to-all | bytes 2097152 | tf_op jit(solution)/shard_map/all_to_all | solution.py:24
  85.7 3.7 %all-to-all-start.2 = ((bf16[4,2,384,384]{3,2,1,0:T(8,128)(2,1)}), bf16[4,2,384,384]{3,2,1,0:T(8,128)(2,1)S(1)}, u32[]{:S(2)}, u32[]{:S(2)}) async-start(bf16[4,2,384,384]{3,2,1,0:T(8,128)(2,1)} %copy-done.2), calls=%async_computation.2 | async-start | bytes 4718592 | tf_op jit(solution)/shard_map/all_to_all | solution.py:24
  89.4 2.4 slice.64
  93.4 3.2 %fusion.21 = bf16[16,8,24,128]{3,1,2,0:T(8,128)(2,1)S(1)} fusion(bf16[3072,1280]{1,0:T(8,128)(2,1)} %bitcast.122, f32[128,512]{1,0:T(8,128)} %convert_reduce_fusion, f32[512]{0:T(512)S(1)} %dynamic_slice.7, bf16[1,128,4096]{2,1,0:T(8,128)(2,1)} %slice.64, s32[]{:T(128)S(6)} %select_n.49), kind=kOutput, calls=%fused_computation.31 | convolution fusion | flops 403308544 | bytes 4327428 | tf_op jit(solution)/shard_map/dot_general | solution.py:51
  96.6 1.0 copy.142
  97.6 15.5 %all-to-all-done.2.q_own.k_own.v_own = bf16[4,2,384,384]{3,2,1,0:T(8,128)(2,1)S(1)} async-done(((bf16[4,2,384,384]{3,2,1,0:T(8,128)(2,1)}), bf16[4,2,384,384]{3,2,1,0:T(8,128)(2,1)S(1)}, u32[]{:S(2)}, u32[]{:S(2)}) %all-to-all-start.2) | async-done | bytes 2359328 | tf_op jit(solution)/shard_map/all_to_all | solution.py:24
  113.1 12.0 %all-to-all-start.3 = ((bf16[128,24,128]{2,1,0:T(8,128)(2,1)}), bf16[128,24,128]{2,1,0:T(8,128)(2,1)}, u32[]{:S(2)}, u32[]{:S(2)}) async-start(bf16[128,24,128]{2,1,0:T(8,128)(2,1)} %bitcast.55), calls=%async_computation.3 | async-start | bytes 1572864 | tf_op jit(solution)/shard_map/all_to_all | solution.py:24
  125.1 1.1 slice_bitcast_fusion
  126.2 3.3 %collective-permute-start.1 = (bf16[4,384,384]{2,1,0:T(8,128)(2,1)}, bf16[4,384,384]{2,1,0:T(8,128)(2,1)S(1)}, u32[]{:S(2)}, u32[]{:S(2)}) collective-permute-start(bf16[4,384,384]{2,1,0:T(8,128)(2,1)} %slice_bitcast_fusion), channel_id=1, source_target_pairs={{0,1},{1,0},{2,3},{3,2},{4,5},{5,4},{6,7},{7,6},{8,9},{9,8},{10,11... | collective-permute-start | bytes 3538952 | tf_op jit(solution)/shard_map/ppermute | solution.py:273
  129.5 16.0 %all-to-all-done.3 = bf16[128,24,128]{2,1,0:T(8,128)(2,1)} async-done(((bf16[128,24,128]{2,1,0:T(8,128)(2,1)}), bf16[128,24,128]{2,1,0:T(8,128)(2,1)}, u32[]{:S(2)}, u32[]{:S(2)}) %all-to-all-start.3) | async-done | bytes 786464 | tf_op jit(solution)/shard_map/all_to_all | solution.py:24
  145.5 1.2 bitcast_reduce_fusion
  147.9 1.4 copy.119
  149.3 5.7 %all-to-all-start.4 = ((bf16[128,24,128]{2,1,0:T(8,128)(2,1)}), bf16[128,24,128]{2,1,0:T(8,128)(2,1)}, u32[]{:S(2)}, u32[]{:S(2)}) async-start(bf16[128,24,128]{2,1,0:T(8,128)(2,1)} %copy.119), calls=%async_computation.4 | async-start | bytes 1572864 | tf_op jit(solution)/shard_map/all_to_all | solution.py:24
  155.5 1.4 reduce.10
  157.5 1.3 copy.151
  158.9 1.4 add.123
  161.7 1.3 copy.152
  163.0 1.4 add.121
  164.4 1.3 fusion.79
  165.7 5.4 %collective-permute-done.1.q_other.k_other.v_other = bf16[4,384,384]{2,1,0:T(8,128)(2,1)S(1)} collective-permute-done((bf16[4,384,384]{2,1,0:T(8,128)(2,1)}, bf16[4,384,384]{2,1,0:T(8,128)(2,1)S(1)}, u32[]{:S(2)}, u32[]{:S(2)}) %collective-permute-start.1) | collective-permute-done | bytes 1179680 | tf_op jit(solution)/shard_map/ppermute | solution.py:273
  171.2 9.5 %shard_map.211 = (f32[1024,384]{1,0:T(8,128)S(1)}, f32[1024,384]{1,0:T(8,128)S(1)}) custom-call(bf16[4,2,384,384]{3,2,1,0:T(8,128)(2,1)S(1)} %all-to-all-done.2.q_own.k_own.v_own, bf16[4,384,384]{2,1,0:T(8,128)(2,1)S(1)} %collective-permute-done.1.q_other.k_other.v_other, bf16[4,2,384,384]{3,2,1,0:T(8,128)(2,1)S(1)} %all-to-all-done.2.q_own.k_own.v_own, ...), custom_call_target="tpu_custom_call" | custom-call | flops 2415919104 | bytes 5505024 | tf_op jit(solution)/shard_map/pallas_call | solution.py:114
  180.6 1.1 copy-done.4
  181.8 1.2 copy-done.6
  183.0 2.4 copy.120
  185.4 4.8 %fusion.10.k_ref.v_ref = f32[128,768]{1,0:T(8,128)S(1)} fusion(bf16[3072,1280]{1,0:T(8,128)(2,1)} %bitcast.123, bf16[128,3072]{0,1:T(8,128)(2,1)} %bitcast.126, f32[3072]{0:T(1024)S(1)} %copy-done.20, f32[3072]{0:T(1024)} %add.121), kind=kOutput, calls=%fused_computation.11 | convolution fusion | flops 605552640 | bytes 5922816 | tf_op jit(solution)/shard_map/dot_general | solution.py:287
  190.2 4.3 %shard_map.212 = bf16[1024,384]{1,0:T(8,128)(2,1)S(1)} custom-call(s32[1]{0:T(128)} %bitcast.length_ref, bf16[4,2,384,384]{3,2,1,0:T(8,128)(2,1)S(1)} %all-to-all-done.2.q_own.k_own.v_own, bf16[4,384,384]{2,1,0:T(8,128)(2,1)S(1)} %collective-permute-done.1.q_other.k_other.v_other, f32[128,768]{1,0:T(8,128)S(1)} %fusion.10.k_ref.v_ref, ...), custom_call_target="tpu_custom_call" | custom-call | flops 301989888 | bytes 4718592 | tf_op jit(solution)/shard_map/pallas_call | solution.py:165
  196.0 1.3 pad_maximum_fusion.1
  197.3 1.3 copy.123
  198.5 3.6 %all-to-all-start.5 = ((bf16[4,256,448]{1,2,0:T(8,128)(2,1)}), bf16[4,256,448]{1,2,0:T(8,128)(2,1)S(1)}, u32[]{:S(2)}, u32[]{:S(2)}) async-start(bf16[4,256,448]{1,2,0:T(8,128)(2,1)} %copy.123), calls=%async_computation.5 | async-start | bytes 1835008 | tf_op jit(solution)/shard_map/all_to_all | solution.py:24
  202.9 11.9 %all-to-all-done.5 = bf16[4,256,448]{1,2,0:T(8,128)(2,1)S(1)} async-done(((bf16[4,256,448]{1,2,0:T(8,128)(2,1)}), bf16[4,256,448]{1,2,0:T(8,128)(2,1)S(1)}, u32[]{:S(2)}, u32[]{:S(2)}) %all-to-all-start.5) | async-done | bytes 917536 | tf_op jit(solution)/shard_map/all_to_all | solution.py:24
  216.0 1.5 fusion.34
  217.5 1.5 collective-permute-start.5
  219.0 7.7 %fusion.12 = bf16[128,3072]{1,0:T(8,128)(2,1)} fusion(bf16[128,1536]{0,1:T(8,128)(2,1)S(1)} %bitcast.130, bf16[3072,1664]{1,0:T(8,128)(2,1)} %bitcast.136), kind=kOutput, calls=%fused_computation.14 | convolution fusion | flops 1208352768 | bytes 10616832 | tf_op jit(solution)/shard_map/dot_general | solution.py:51
  227.5 3.4 %all-to-all-start.6 = ((bf16[4,256,128]{2,1,0:T(8,128)(2,1)}), bf16[4,256,128]{2,1,0:T(8,128)(2,1)S(1)}, u32[]{:S(2)}, u32[]{:S(2)}) async-start(bf16[4,256,128]{2,1,0:T(8,128)(2,1)} %broadcast_in_dim.11), calls=%async_computation.6 | async-start | bytes 524288 | tf_op jit(solution)/shard_map/all_to_all | solution.py:24
  230.9 1.2 pad_maximum_fusion.3
  232.1 1.3 copy.127
  233.4 1.5 collective-permute-start.4
  235.0 1.4 all-to-all-done.6
  236.7 3.7 %collective-permute-start.6 = (bf16[64,384]{1,0:T(8,128)(2,1)S(1)}, bf16[64,384]{1,0:T(8,128)(2,1)S(1)}, u32[]{:S(2)}, u32[]{:S(2)}) collective-permute-start(bf16[64,384]{1,0:T(8,128)(2,1)S(1)} %convolution_convert_fusion.5), channel_id=1, source_target_pairs={{0,8},{8,0},{16,24},{24,16},{32,40},{40,32},{48,56},{56,48},{64,72... | collective-permute-start | bytes 147464 | tf_op jit(solution)/shard_map/ppermute | solution.py:325
  240.4 8.2 %fusion.2 = f32[128,3072]{1,0:T(8,128)} fusion(bf16[128,1536]{0,1:T(8,128)(2,1)} %bitcast.129, bf16[3072,1664]{1,0:T(8,128)(2,1)} %bitcast.137), kind=kOutput, calls=%fused_computation.2 | convolution fusion | flops 1207959552 | bytes 11403264 | tf_op jit(solution)/shard_map/dot_general | solution.py:51
  248.6 1.3 collective-permute-start.7
  250.0 2.3 collective-permute-done.4
  252.2 1.5 copy.128
  253.9 1.3 copy-done.12
  257.7 8.1 %all-to-all-start.7 = ((bf16[16,72,192]{2,1,0:T(8,128)(2,1)}), bf16[16,72,192]{2,1,0:T(8,128)(2,1)S(1)}, u32[]{:S(2)}, u32[]{:S(2)}) async-start(bf16[16,72,192]{2,1,0:T(8,128)(2,1)} %bitcast.40), calls=%async_computation.7 | async-start | bytes 1179648 | tf_op jit(solution)/shard_map/all_to_all | solution.py:24
  265.8 3.0 collective-permute-start.8
  268.8 8.2 %collective-permute-done.8 = bf16[64,384]{1,0:T(8,128)(2,1)S(1)} collective-permute-done((bf16[64,384]{1,0:T(8,128)(2,1)S(1)}, bf16[64,384]{1,0:T(8,128)(2,1)S(1)}, u32[]{:S(2)}, u32[]{:S(2)}) %collective-permute-start.8) | collective-permute-done | bytes 49184 | tf_op jit(solution)/shard_map/ppermute | solution.py:325
  277.0 1.3 collective-permute-start.9
  279.2 7.1 %all-to-all-start.8 = ((bf16[8,72,192]{2,1,0:T(8,128)(2,1)}), bf16[8,72,192]{2,1,0:T(8,128)(2,1)S(1)}, u32[]{:S(2)}, u32[]{:S(2)}) async-start(bf16[8,72,192]{2,1,0:T(8,128)(2,1)} %broadcast_in_dim.12), calls=%async_computation.8 | async-start | bytes 589824 | tf_op jit(solution)/shard_map/all_to_all | solution.py:24
  287.3 1.2 copy.136
  288.5 5.1 %all-to-all-done.8 = bf16[8,72,192]{2,1,0:T(8,128)(2,1)S(1)} async-done(((bf16[8,72,192]{2,1,0:T(8,128)(2,1)}), bf16[8,72,192]{2,1,0:T(8,128)(2,1)S(1)}, u32[]{:S(2)}, u32[]{:S(2)}) %all-to-all-start.8) | async-done | bytes 221216 | tf_op jit(solution)/shard_map/all_to_all | solution.py:24
  (122 shorter events, 22.3 us)
Async XLA Ops:
  7.2 86.2 %all-gather.5.cloned.1.call-start = ((), (), s32[]{:S(2)}) async-start(), calls=%async_computation.9 | async-start | bytes 8847360 | tf_op jit(solution)/shard_map/all_gather | solution.py:34
  9.2 13.5 %collective-permute-start = (bf16[192,1280]{1,0:T(8,128)(2,1)S(1)}, bf16[192,1280]{1,0:T(8,128)(2,1)S(1)}, u32[]{:S(2)}, u32[]{:S(2)}) collective-permute-start(bf16[192,1280]{1,0:T(8,128)(2,1)S(1)} %pad_maximum_fusion.4), channel_id=1, source_target_pairs={{0,64},{8,72},{16,80},{24,88},{32,96},{40,104},{48,112},{56,120},{... | collective-permute-start | bytes 1474568 | tf_op jit(solution)/shard_map/ppermute | solution.py:30
  11.7 13.1 %copy-start.14 = (f32[384,64]{0,1:T(8,128)S(1)}, f32[384,64]{0,1:T(8,128)}, u32[]{:S(2)}) copy-start(f32[384,64]{0,1:T(8,128)} %param.34) | copy-start | bytes 294916
  11.7 13.1 %copy-start.16 = (f32[64,192]{1,0:T(8,128)S(1)}, f32[64,192]{1,0:T(8,128)}, u32[]{:S(2)}) copy-start(f32[64,192]{1,0:T(8,128)} %param.35) | copy-start | bytes 147460
  11.7 13.1 %copy-start.17 = (bf16[384,192]{0,1:T(8,128)(2,1)S(1)}, bf16[384,192]{0,1:T(8,128)(2,1)}, u32[]{:S(2)}) copy-start(bf16[384,192]{0,1:T(8,128)(2,1)} %param.33) | copy-start | bytes 442372
  24.8 5.5 %copy-start.11 = (bf16[1,256,4096]{2,1,0:T(8,128)(2,1)S(1)}, bf16[1,256,4096]{2,1,0:T(8,128)(2,1)}, u32[]{:S(2)}) copy-start(bf16[1,256,4096]{2,1,0:T(8,128)(2,1)} %param.19) | copy-start | bytes 6291460
  24.8 5.8 %copy-start.24 = (f32[4096]{0:T(1024)S(1)}, f32[4096]{0:T(1024)}, u32[]{:S(2)}) copy-start(f32[4096]{0:T(1024)} %param.22) | copy-start | bytes 49156
  26.2 20.4 %all-to-all-start = ((bf16[4,192,384]{2,1,0:T(8,128)(2,1)}), bf16[4,192,384]{2,1,0:T(8,128)(2,1)S(1)}, u32[]{:S(2)}, u32[]{:S(2)}) async-start(bf16[4,192,384]{2,1,0:T(8,128)(2,1)} %broadcast_in_dim.10), calls=%async_computation | async-start | bytes 1179648 | tf_op jit(solution)/shard_map/all_to_all | solution.py:24
  30.2 185.7 %all-gather.7.cloned.1.call-start = ((), (), s32[]{:S(2)}) async-start(), calls=%async_computation.10 | async-start | bytes 11501568 | tf_op jit(solution)/shard_map/all_gather | solution.py:34
  34.1 10.3 %copy-start.3 = (bf16[1,128,3,3072]{3,1,2,0:T(8,128)(2,1)S(1)}, bf16[1,128,3,3072]{3,1,2,0:T(8,128)(2,1)}, u32[]{:S(2)}) copy-start(bf16[1,128,3,3072]{3,1,2,0:T(8,128)(2,1)} %param.31) | copy-start | bytes 7077892
  44.4 6.7 %copy-start.21 = (f32[192]{0:T(256)S(1)}, f32[192]{0:T(256)}, u32[]{:S(2)}) copy-start(f32[192]{0:T(256)} %param.36) | copy-start | bytes 2308
  45.2 1.4 copy-start.2
  46.8 4.3 %collective-permute-start.2 = (f32[192]{0:T(256)S(1)}, f32[192]{0:T(256)S(1)}, u32[]{:S(2)}, u32[]{:S(2)}) collective-permute-start(f32[192]{0:T(256)S(1)} %fusion.25), channel_id=1, source_target_pairs={{0,1},{1,0},{2,3},{3,2},{4,5},{5,4},{6,7},{7,6},{8,9},{9,8},{10,11... | collective-permute-start | bytes 2312 | tf_op jit(solution)/shard_map/ppermute | solution.py:259
  51.1 13.2 %copy-start.18 = (f32[192]{0:T(256)}, f32[192]{0:T(256)S(1)}, u32[]{:S(2)}) copy-start(f32[192]{0:T(256)S(1)} %rsqrt_multiply_fusion) | copy-start | bytes 2308
  51.6 12.8 %collective-permute-start.3 = (bf16[192,1664]{1,0:T(8,128)(2,1)S(1)}, bf16[192,1664]{1,0:T(8,128)(2,1)S(1)}, u32[]{:S(2)}, u32[]{:S(2)}) collective-permute-start(bf16[192,1664]{1,0:T(8,128)(2,1)S(1)} %fusion.43), channel_id=1, source_target_pairs={{0,64},{8,72},{16,80},{24,88},{32,96},{40,104},{48,112},{56,120},{... | collective-permute-start | bytes 1916936 | tf_op jit(solution)/shard_map/ppermute | solution.py:30
  64.6 1.7 copy-start.10
  85.7 27.4 %all-to-all-start.2 = ((bf16[4,2,384,384]{3,2,1,0:T(8,128)(2,1)}), bf16[4,2,384,384]{3,2,1,0:T(8,128)(2,1)S(1)}, u32[]{:S(2)}, u32[]{:S(2)}) async-start(bf16[4,2,384,384]{3,2,1,0:T(8,128)(2,1)} %copy-done.2), calls=%async_computation.2 | async-start | bytes 4718592 | tf_op jit(solution)/shard_map/all_to_all | solution.py:24
  113.1 32.4 %all-to-all-start.3 = ((bf16[128,24,128]{2,1,0:T(8,128)(2,1)}), bf16[128,24,128]{2,1,0:T(8,128)(2,1)}, u32[]{:S(2)}, u32[]{:S(2)}) async-start(bf16[128,24,128]{2,1,0:T(8,128)(2,1)} %bitcast.55), calls=%async_computation.3 | async-start | bytes 1572864 | tf_op jit(solution)/shard_map/all_to_all | solution.py:24
  125.1 22.3 %copy-start.23 = (s32[16]{0:T(128)S(1)}, s32[16]{0:T(128)}, u32[]{:S(2)}) copy-start(s32[16]{0:T(128)} %param.21) | copy-start | bytes 196
  126.2 44.9 %collective-permute-start.1 = (bf16[4,384,384]{2,1,0:T(8,128)(2,1)}, bf16[4,384,384]{2,1,0:T(8,128)(2,1)S(1)}, u32[]{:S(2)}, u32[]{:S(2)}) collective-permute-start(bf16[4,384,384]{2,1,0:T(8,128)(2,1)} %slice_bitcast_fusion), channel_id=1, source_target_pairs={{0,1},{1,0},{2,3},{3,2},{4,5},{5,4},{6,7},{7,6},{8,9},{9,8},{10,11... | collective-permute-start | bytes 3538952 | tf_op jit(solution)/shard_map/ppermute | solution.py:273
  147.4 23.8 %copy-start.8 = (f32[2,128]{1,0:T(2,128)S(1)}, f32[2,128]{1,0:T(2,128)}, u32[]{:S(2)}) copy-start(f32[2,128]{1,0:T(2,128)} %gain_ref.3) | copy-start | bytes 3076
  149.3 33.7 %all-to-all-start.4 = ((bf16[128,24,128]{2,1,0:T(8,128)(2,1)}), bf16[128,24,128]{2,1,0:T(8,128)(2,1)}, u32[]{:S(2)}, u32[]{:S(2)}) async-start(bf16[128,24,128]{2,1,0:T(8,128)(2,1)} %copy.119), calls=%async_computation.4 | async-start | bytes 1572864 | tf_op jit(solution)/shard_map/all_to_all | solution.py:24
  165.7 19.6 %copy-start.20 = (f32[3072]{0:T(1024)S(1)}, f32[3072]{0:T(1024)}, u32[]{:S(2)}) copy-start(f32[3072]{0:T(1024)} %add.123) | copy-start | bytes 36868
  180.6 1.1 copy-start.4
  181.8 1.2 copy-start.6
  185.4 4.8 %copy-start.5 = (f32[1024,384]{1,0:T(8,128)S(1)}, f32[1024,384]{1,0:T(8,128)}, u32[]{:S(2)}) copy-start(f32[1024,384]{1,0:T(8,128)} %copy-done.4) | copy-start | bytes 4718596
  185.4 4.8 %copy-start.7 = (f32[1024,384]{1,0:T(8,128)S(1)}, f32[1024,384]{1,0:T(8,128)}, u32[]{:S(2)}) copy-start(f32[1024,384]{1,0:T(8,128)} %copy-done.6) | copy-start | bytes 4718596
  185.4 4.8 %copy-start.9 = (f32[128]{0:T(128)S(1)}, f32[128]{0:T(128)}, u32[]{:S(2)}) copy-start(f32[128]{0:T(128)} %param.30) | copy-start | bytes 1540
  190.2 5.2 %copy-start.15 = (f32[384,64]{0,1:T(8,128)S(1)}, f32[384,64]{0,1:T(8,128)}, u32[]{:S(2)}) copy-start(f32[384,64]{0,1:T(8,128)} %param.34) | copy-start | bytes 294916
  194.6 0.9 copy-start
  197.2 4.9 %copy-start.13 = (bf16[1,128,3072]{2,1,0:T(8,128)(2,1)S(1)}, bf16[1,128,3072]{2,1,0:T(8,128)(2,1)}, u32[]{:S(2)}) copy-start(bf16[1,128,3072]{2,1,0:T(8,128)(2,1)} %param.37) | copy-start | bytes 2359300
  198.5 16.2 %all-to-all-start.5 = ((bf16[4,256,448]{1,2,0:T(8,128)(2,1)}), bf16[4,256,448]{1,2,0:T(8,128)(2,1)S(1)}, u32[]{:S(2)}, u32[]{:S(2)}) async-start(bf16[4,256,448]{1,2,0:T(8,128)(2,1)} %copy.123), calls=%async_computation.5 | async-start | bytes 1835008 | tf_op jit(solution)/shard_map/all_to_all | solution.py:24
  217.5 9.3 %collective-permute-start.5 = (bf16[128,128]{1,0:T(8,128)(2,1)S(1)}, bf16[128,128]{1,0:T(8,128)(2,1)S(1)}, u32[]{:S(2)}, u32[]{:S(2)}) collective-permute-start(bf16[128,128]{1,0:T(8,128)(2,1)S(1)} %fusion.34), channel_id=1, source_target_pairs={{0,1},{1,0},{2,3},{3,2},{4,5},{5,4},{6,7},{7,6},{8,9},{9,8},{10,11... | collective-permute-start | bytes 98312 | tf_op jit(solution)/shard_map/ppermute | solution.py:317
  226.8 9.7 %copy-start.1 = (bf16[1024,384]{1,0:T(8,128)(2,1)S(1)}, bf16[1024,384]{1,0:T(8,128)(2,1)}, u32[]{:S(2)}) copy-start(bf16[1024,384]{1,0:T(8,128)(2,1)} %copy-done) | copy-start | bytes 2359300
  227.5 8.9 %all-to-all-start.6 = ((bf16[4,256,128]{2,1,0:T(8,128)(2,1)}), bf16[4,256,128]{2,1,0:T(8,128)(2,1)S(1)}, u32[]{:S(2)}, u32[]{:S(2)}) async-start(bf16[4,256,128]{2,1,0:T(8,128)(2,1)} %broadcast_in_dim.11), calls=%async_computation.6 | async-start | bytes 524288 | tf_op jit(solution)/shard_map/all_to_all | solution.py:24
  233.4 18.8 %collective-permute-start.4 = (bf16[128,3136]{0,1:T(8,128)(2,1)}, bf16[128,3136]{0,1:T(8,128)(2,1)}, u32[]{:S(2)}, u32[]{:S(2)}) collective-permute-start(bf16[128,3136]{0,1:T(8,128)(2,1)} %copy.127), channel_id=1, source_target_pairs={{0,1},{1,0},{2,3},{3,2},{4,5},{5,4},{6,7},{7,6},{8,9},{9,8},{10,11... | collective-permute-start | bytes 2408456 | tf_op jit(solution)/shard_map/ppermute | solution.py:310
  236.7 11.9 %collective-permute-start.6 = (bf16[64,384]{1,0:T(8,128)(2,1)S(1)}, bf16[64,384]{1,0:T(8,128)(2,1)S(1)}, u32[]{:S(2)}, u32[]{:S(2)}) collective-permute-start(bf16[64,384]{1,0:T(8,128)(2,1)S(1)} %convolution_convert_fusion.5), channel_id=1, source_target_pairs={{0,8},{8,0},{16,24},{24,16},{32,40},{40,32},{48,56},{56,48},{64,72... | collective-permute-start | bytes 147464 | tf_op jit(solution)/shard_map/ppermute | solution.py:325
  248.6 17.2 %collective-permute-start.7 = (bf16[64,384]{1,0:T(8,128)(2,1)S(1)}, bf16[64,384]{1,0:T(8,128)(2,1)S(1)}, u32[]{:S(2)}, u32[]{:S(2)}) collective-permute-start(bf16[64,384]{1,0:T(8,128)(2,1)S(1)} %add_convert_fusion.2), channel_id=1, source_target_pairs={{0,16},{8,24},{16,0},{24,8},{32,48},{40,56},{48,32},{56,40},{64,80... | collective-permute-start | bytes 147464 | tf_op jit(solution)/shard_map/ppermute | solution.py:325
  253.8 1.4 copy-start.12
  257.7 20.6 %all-to-all-start.7 = ((bf16[16,72,192]{2,1,0:T(8,128)(2,1)}), bf16[16,72,192]{2,1,0:T(8,128)(2,1)S(1)}, u32[]{:S(2)}, u32[]{:S(2)}) async-start(bf16[16,72,192]{2,1,0:T(8,128)(2,1)} %bitcast.40), calls=%async_computation.7 | async-start | bytes 1179648 | tf_op jit(solution)/shard_map/all_to_all | solution.py:24
  265.8 11.2 %collective-permute-start.8 = (bf16[64,384]{1,0:T(8,128)(2,1)S(1)}, bf16[64,384]{1,0:T(8,128)(2,1)S(1)}, u32[]{:S(2)}, u32[]{:S(2)}) collective-permute-start(bf16[64,384]{1,0:T(8,128)(2,1)S(1)} %add_convert_fusion.1), channel_id=1, source_target_pairs={{0,32},{8,40},{16,48},{24,56},{32,0},{40,8},{48,16},{56,24},{64,96... | collective-permute-start | bytes 147464 | tf_op jit(solution)/shard_map/ppermute | solution.py:325
  277.0 9.2 %collective-permute-start.9 = (bf16[64,384]{1,0:T(8,128)(2,1)S(1)}, bf16[64,384]{1,0:T(8,128)(2,1)S(1)}, u32[]{:S(2)}, u32[]{:S(2)}) collective-permute-start(bf16[64,384]{1,0:T(8,128)(2,1)S(1)} %add_convert_fusion), channel_id=1, source_target_pairs={{0,64},{8,72},{16,80},{24,88},{32,96},{40,104},{48,112},{56,120},{... | collective-permute-start | bytes 147464 | tf_op jit(solution)/shard_map/ppermute | solution.py:325
  279.2 14.5 %all-to-all-start.8 = ((bf16[8,72,192]{2,1,0:T(8,128)(2,1)}), bf16[8,72,192]{2,1,0:T(8,128)(2,1)S(1)}, u32[]{:S(2)}, u32[]{:S(2)}) async-start(bf16[8,72,192]{2,1,0:T(8,128)(2,1)} %broadcast_in_dim.12), calls=%async_computation.8 | async-start | bytes 589824 | tf_op jit(solution)/shard_map/all_to_all | solution.py:24
  287.3 6.4 %copy-start.19 = (f32[192]{0:T(256)S(1)}, f32[192]{0:T(256)}, u32[]{:S(2)}) copy-start(f32[192]{0:T(256)} %copy-done.18) | copy-start | bytes 2308
  287.3 7.1 %copy-start.22 = (f32[192]{0:T(256)S(1)}, f32[192]{0:T(256)}, u32[]{:S(2)}) copy-start(f32[192]{0:T(256)} %param.36) | copy-start | bytes 2308
Sparse Core Ops, SparseCore 0:
  24.9 50.7 all-gather.4
  77.4 65.7 all-gather.6

commit v4 on v3

--- a/solution.py
+++ b/solution.py
@@ -24,10 +24,14 @@
     return lax.all_to_all(values, axes, 0, 0, tiled=True, axis_index_groups=groups)
 
 
-def gather_columns(values):
+def near_shard(values):
+    n_dp = lax.axis_size("dp")
+    return lax.ppermute(values, "dp", [(i, (i + n_dp // 2) % n_dp) for i in range(n_dp)])
+
+
+def gather_columns(values, other):
     n_dp = lax.axis_size("dp")
     near = n_dp // 2
-    other = lax.ppermute(values, "dp", [(i, (i + near) % n_dp) for i in range(n_dp)])
     low = lax.axis_index("dp") < near
     halves = jnp.stack([jnp.where(low, values, other), jnp.where(low, other, values)])
     groups = [list(range(near)), list(range(near, n_dp))]
@@ -51,76 +55,64 @@
     return lax.dot_general(left, right, (((1,), (1,)), ((), ())), preferred_element_type=F32)
 
 
-def pack_kernel(_, in_ref, out_ref):
-    out_ref[0, 0] = in_ref[...].reshape(out_ref.shape[2:])
+def pack_kernel(_, own_in, other_in, own_ref, other_ref):
+    own_ref[0] = own_in[...].reshape(own_ref.shape[1:])
+    other_ref[0] = other_in[...].reshape(other_ref.shape[1:])
 
 
 def pack_heads(rows, pair, n_seq):
     kinds, count, model = rows.shape
     width = model // n_seq
+    n_y = n_seq // 2
+    block = (kinds, count, width)
+    shape = jax.ShapeDtypeStruct((n_y, kinds * count, width), rows.dtype)
+    out_spec = pl.BlockSpec((1, kinds * count, width), lambda y, z: (y, 0, 0))
     return pl.pallas_call(
         pack_kernel,
         grid_spec=pltpu.PrefetchScalarGridSpec(
             num_scalar_prefetch=1,
-            grid=(n_seq // 2, 2),
+            grid=(n_y,),
             in_specs=[
-                pl.BlockSpec((kinds, count, width), lambda y, k, z: (0, 0, 2 * y + (z[0] + k) % 2))
+                pl.BlockSpec(block, lambda y, z: (0, 0, 2 * y + z[0])),
+                pl.BlockSpec(block, lambda y, z: (0, 0, 2 * y + 1 - z[0])),
             ],
-            out_specs=pl.BlockSpec((1, 1, kinds * count, width), lambda y, k, z: (y, k, 0, 0)),
+            out_specs=[out_spec, out_spec],
         ),
-        out_shape=jax.ShapeDtypeStruct((n_seq // 2, 2, kinds * count, width), rows.dtype),
+        out_shape=[shape, shape],
         compiler_params=pltpu.CompilerParams(vmem_limit_bytes=16 * 1024 * 1024),
         cost_estimate=pl.CostEstimate(flops=0, bytes_accessed=4 * rows.size, transcendentals=0),
-    )(pair.reshape(1), rows)
-
-
-def image_kernel(
-    q_own, q_other, k_own, k_other, v_own, v_other, gain_ref, num_ref, den_ref, keys, values
-):
-    half = keys.shape[0] // 2
-
+    )(pair.reshape(1), rows, rows)
+
+
+def image_kernel(q_ref, k_ref, v_ref, gain_ref, num_ref, den_ref, keys, values):
     @pl.when(pl.program_id(1) == 0)
     def _():
-        for at, k_ref, v_ref in ((0, k_own, v_own), (half, k_other, v_other)):
-            k = k_ref[...].reshape(-1, HD).astype(F32)
-            keys[at : at + half, :] = rms_scale(k, gain_ref[1:2, :]).astype(BF16)
-            values[at : at + half, :HD] = v_ref[...].reshape(-1, HD)
-        values[:, HD:] = jnp.ones((2 * half, HD), BF16)
-
-    q = jnp.concatenate([q_own[...].reshape(-1, HD), q_other[...].reshape(-1, HD)], 0)
-    q = rms_scale(q.astype(F32), gain_ref[0:1, :] * QUERY_SCALE).astype(BF16)
+        k = k_ref[...].reshape(-1, HD).astype(F32)
+        keys[...] = rms_scale(k, gain_ref[1:2, :]).astype(BF16)
+        values[:, :HD] = v_ref[...].reshape(-1, HD)
+        values[:, HD:] = jnp.ones((values.shape[0], HD), BF16)
+
+    q = q_ref[...].reshape(-1, HD).astype(F32)
+    q = rms_scale(q, gain_ref[0:1, :] * QUERY_SCALE).astype(BF16)
     weight = jnp.exp2(dot_t(q, keys[...])).astype(BF16)
     both = jnp.dot(weight, values[...], preferred_element_type=F32)
     num_ref[...] = both[:, :HD]
     den_ref[...] = both[:, HD:]
 
 
-def image_attention(own, other, gains):
-    n_y, _, _, width = own.shape
+def image_attention(received, gains):
+    sources, _, width = received.shape
     heads = width // HD
-    rows = 2 * BLK
-    image_len = n_y * rows
-
-    def own_spec(count, kind):
-        if count == 1:
-            return pl.BlockSpec((1, 1, BLK, HD), lambda h, b: (b, 0, kind, h))
-        return pl.BlockSpec((count, 1, BLK, HD), lambda h, b: (0, 0, kind, h))
-
-    def other_spec(count, kind):
-        if count == 1:
-            return pl.BlockSpec((1, BLK, HD), lambda h, b: (b, kind, h))
-        return pl.BlockSpec((count, BLK, HD), lambda h, b: (0, kind, h))
-
+    image_len = sources * BLK
+    step = 2
+    rows = step * BLK
     return pl.pallas_call(
         image_kernel,
-        grid=(heads, n_y),
+        grid=(heads, sources // step),
         in_specs=[
-            own_spec(1, 0),
-            other_spec(1, 0),
-            own_spec(n_y, 1),
-            other_spec(n_y, 1),
-            own_spec(n_y, 2),
-            other_spec(n_y, 2),
+            pl.BlockSpec((step, BLK, HD), lambda h, b: (b, 0, h)),
+            pl.BlockSpec((sources, BLK, HD), lambda h, b: (0, 1, h)),
+            pl.BlockSpec((sources, BLK, HD), lambda h, b: (0, 2, h)),
             pl.BlockSpec((2, HD), lambda h, b: (0, 0)),
         ],
         out_specs=[
@@ -135,39 +127,34 @@
             bytes_accessed=14 * image_len * width,
             transcendentals=heads * image_len * image_len,
         ),
-    )(own, other, own, other, own, other, gains)
-
-
-def text_kernel(
-    length_ref, q_own, q_other, k_ref, v_ref, gain_ref, text_gain_ref, num_ref, den_ref, out_ref
-):
+    )(received, received, received, gains)
+
+
+def text_kernel(length_ref, q_ref, k_ref, v_ref, gain_ref, text_gain_ref, num_ref, den_ref, out_ref):
     k = rms_scale(k_ref[...], text_gain_ref[...]).astype(BF16)
     v = v_ref[...].astype(BF16)
+    q = q_ref[...].reshape(-1, HD).astype(F32)
+    q = rms_scale(q, gain_ref[0:1, :] * QUERY_SCALE).astype(BF16)
+    weight = jnp.exp2(dot_t(q, k))
+    valid = lax.broadcasted_iota(jnp.int32, weight.shape, 1) < length_ref[0]
+    weight = jnp.where(valid, weight, 0.0).astype(BF16)
     stacked = jnp.concatenate([v, jnp.ones_like(v)], axis=1)
-    for b in range(q_other.shape[0]):
-        q = jnp.concatenate([q_own[b, 0], q_other[b]], 0).astype(F32)
-        q = rms_scale(q, gain_ref[0:1, :] * QUERY_SCALE).astype(BF16)
-        weight = jnp.exp2(dot_t(q, k))
-        valid = lax.broadcasted_iota(jnp.int32, weight.shape, 1) < length_ref[0]
-        weight = jnp.where(valid, weight, 0.0).astype(BF16)
-        both = jnp.dot(weight, stacked, preferred_element_type=F32)
-        rows = slice(b * q.shape[0], (b + 1) * q.shape[0])
-        total = num_ref[rows, :] + both[:, :HD]
-        out_ref[rows, :] = (total / (den_ref[rows, :] + both[:, HD:])).astype(BF16)
-
-
-def text_attention(length, own, other, key_value, gains, text_gain, num, den):
-    n_y, _, _, width = own.shape
+    both = jnp.dot(weight, stacked, preferred_element_type=F32)
+    total = num_ref[...] + both[:, :HD]
+    out_ref[...] = (total / (den_ref[...] + both[:, HD:])).astype(BF16)
+
+
+def text_attention(length, received, key_value, gains, text_gain, num, den):
+    sources, _, width = received.shape
     heads = width // HD
-    image_len = n_y * 2 * BLK
-    step = n_y // 2
-    rows = step * 2 * BLK
+    image_len = sources * BLK
+    step = sources // 2
+    rows = step * BLK
     return pl.pallas_call(
         text_kernel,
-        grid=(heads, n_y // step),
+        grid=(heads, sources // step),
         in_specs=[
             pl.BlockSpec(memory_space=pltpu.SMEM),
-            pl.BlockSpec((step, 1, BLK, HD), lambda h, b: (b, 0, 0, h)),
             pl.BlockSpec((step, BLK, HD), lambda h, b: (b, 0, h)),
             pl.BlockSpec((BLK, HD), lambda h, b: (0, h)),
             pl.BlockSpec((BLK, HD), lambda h, b: (0, heads + h)),
@@ -184,7 +171,7 @@
             bytes_accessed=12 * image_len * width,
             transcendentals=heads * image_len * BLK,
         ),
-    )(length, own, other, key_value, key_value, gains, text_gain, num, den)
+    )(length, received, key_value, key_value, gains, text_gain, num, den)
 
 
 def on_device(
@@ -228,10 +215,9 @@
     weights = jnp.concatenate(
         [context_weight.T, kv_weight.reshape(kv_weight.shape[0], -1)], 1
     )
-    weights = gather_columns(weights)
-    depth = context_weight.shape[0]
-    context_all, kv_all = weights[:, :depth], weights[:, depth:]
-
+    near_weights = near_shard(weights)
+    own_heads, other_heads = pack_heads(image_query_key_value[0].transpose(1, 0, 2), pair, n_seq)
+    other_heads = lax.ppermute(other_heads, "seq", flip_z)
     direction_t = proj_weight.T.astype(F32) + lax.dot_general(
         dora_b, dora_a, (((0,), (1,)), ((), ())), precision=lax.Precision.HIGHEST
     )
@@ -246,13 +232,11 @@
     hidden = (jax.nn.gelu(gate_proj, approximate=True) * upward).astype(BF16)
     ffn = jnp.dot(hidden, t5_out_weight, preferred_element_type=F32).astype(BF16)
     ffn = ffn.reshape(BLK, n_seq, feat).transpose(1, 0, 2)
-    packed = pack_heads(image_query_key_value[0].transpose(1, 0, 2), pair, n_seq)
-    rows_y, ffn, packed = lax.optimization_barrier((rows_y, ffn, packed))
-    ffn = swap(ffn, "seq")
-    ffn, packed = lax.optimization_barrier((ffn, packed))
-    ffn_sum = jnp.sum(ffn.astype(F32), 0)
-
-    own_heads = swap(packed, "seq", Y_GROUPS)
+    rows_y, ffn, near_weights = lax.optimization_barrier((rows_y, ffn, near_weights))
+
+    weights = gather_columns(weights, near_weights)
+    depth = context_weight.shape[0]
+    context_all, kv_all = weights[:, :depth], weights[:, depth:]
 
     rows_f = rows_y.astype(F32)
     column_sq = jnp.sum(rows_f * rows_f, (0, 2))
@@ -262,15 +246,23 @@
     scaled_t = scaled_t.transpose(1, 0, 2).reshape(own_cols, -1)
     reach = scaled_t.shape[1]
     up = jnp.pad((dora_b * ratio).astype(BF16).T, ((0, 0), (0, lanes - rank)))
-    scaled_all = gather_columns(jnp.concatenate([scaled_t, up], 1))
+    scaled_t = jnp.concatenate([scaled_t, up], 1)
+    near_scaled = near_shard(scaled_t)
+
+    ffn = swap(ffn, "seq")
+    ffn, near_scaled, other_heads = lax.optimization_barrier((ffn, near_scaled, other_heads))
+    scaled_all = gather_columns(scaled_t, near_scaled)
     up_all = scaled_all[:, reach:]
+    ffn_sum = jnp.sum(ffn.astype(F32), 0)
+
+    received = swap(jnp.stack([own_heads, other_heads], 1), "seq", Y_GROUPS)
+    received = received.reshape(n_seq, 3 * BLK, own_rows)
 
     own_tokens = lax.dynamic_slice_in_dim(tokens, seq_rank * feat, feat, 1).astype(F32)
     own_final = lax.dynamic_slice_in_dim(t5_final_gain, seq_rank * feat, feat, 0)
     encoded = ((own_tokens + ffn_sum) * own_final).astype(BF16)
     context = dot_t(encoded, context_all).astype(BF16).reshape(BLK, rows_of, lanes)
-    context, own_heads = lax.optimization_barrier((context, own_heads))
-    other_heads = lax.ppermute(own_heads[:, 1], "seq", flip_z)
+    context, received = lax.optimization_barrier((context, received))
     arrived = swap(context, both)
     token_of = jnp.sum(arrived.reshape(n_dp, n_seq, rows_of, lanes).astype(F32), 1).astype(BF16)
     values = token_of.astype(F32)
@@ -286,36 +278,30 @@
     length = jnp.sum(jnp.where(prompt_owner_sample == data_rank, lengths, 0))
     key_value = jnp.dot(modulated, kv_all, preferred_element_type=F32)
 
-    num, den = image_attention(own_heads, other_heads, image_qk_gain)
-    num, den, key_value = lax.optimization_barrier((num, den, key_value))
+    num, den = image_attention(received, image_qk_gain)
     attended = text_attention(
-        length.reshape(1),
-        own_heads,
-        other_heads,
-        key_value,
-        image_qk_gain,
-        text_key_gain.reshape(1, HD),
-        num,
-        den,
+        length.reshape(1), received, key_value, image_qk_gain, text_key_gain.reshape(1, HD), num, den
     )
 
     lowered = jnp.dot(attended, dora_a.astype(BF16), preferred_element_type=F32).astype(BF16)
     outgoing = jnp.concatenate([attended, lowered], 1).reshape(n_y, 2 * BLK, own_rows + rank)
     gathered = swap(outgoing, "seq", Y_GROUPS)
-    lowered = jnp.sum(gathered[:, :, own_rows:].astype(F32), 0)
-    gathered = gathered[:, :, :own_rows].transpose(1, 0, 2).reshape(2 * BLK, -1)
-    scaled_z = scaled_all[:, :reach]
-    sent = dot_t(gathered[BLK:], scaled_z)
-    sent = jnp.concatenate([sent, lowered[BLK:]], 1).astype(BF16)
-    landed = lax.ppermute(sent, "seq", flip_z).astype(F32)
-    kept = lax.optimization_barrier(dot_t(gathered[:BLK], scaled_z))
-    out = kept + landed[:, :model]
-    image_out = from_gathered(out.astype(BF16), n_dp)[None]
-    lowered = (lowered[:BLK] + landed[:, model:]).astype(BF16)
-
     down = jnp.dot(cotangent, up_all, preferred_element_type=F32).astype(BF16)
     down = jnp.concatenate([down, lax.ppermute(down, "seq", flip_z)], 0)
+    gathered, down = lax.optimization_barrier((gathered, down))
     down_all = swap(jnp.broadcast_to(down[None], (n_y,) + down.shape), "seq", Y_GROUPS)
+    lowered = jnp.sum(gathered[:, :, own_rows:].astype(F32), 0)
+    lowered_other = lax.ppermute(lowered[BLK:].astype(BF16), "seq", flip_z)
+    gathered = gathered[:, :, :own_rows].transpose(1, 0, 2).reshape(2 * BLK, -1)
+    landed = []
+    for at in range(0, model, model // 2):
+        part = dot_t(gathered[BLK:], scaled_all[at : at + model // 2, :reach]).astype(BF16)
+        landed.append(lax.ppermute(part, "seq", flip_z))
+    kept = lax.optimization_barrier(dot_t(gathered[:BLK], scaled_all[:, :reach]))
+    out = kept + jnp.concatenate(landed, 1).astype(F32)
+    image_out = from_gathered(out.astype(BF16), n_dp)[None]
+    lowered = (lowered[:BLK] + lowered_other.astype(F32)).astype(BF16)
+
     down_all = down_all.reshape(-1, lanes)[:, :rank]
     grad_a = lax.dot_general(
         down_all, attended, (((0,), (0,)), ((), ())), preferred_element_type=F32

time: 305 us -> 308 us (level)
  waiting for transfers between devices: 89.2 us -> 114 us
  blocking collectives: 19.4 us -> 0 us
  local copies, waits for them, and re-layouts: 38.3 us -> 27.7 us
  starting transfers between devices: 70.4 us -> 76.2 us
  matrix products: 39 us -> 42.5 us
    ppermute x4 -> x6, waiting for transfers between devices: 30.1 us -> 52.4 us  [the longest x2 42.5 us: near_shard(): lax.ppermute(values, 'dp', [(i, (i + n_dp // 2) % n_dp) for i in range(n_...]
    all_to_all x1 -> x0, blocking collectives: 19.4 us -> none  [swap(): lax.all_to_all(values, axes, 0, 0, tiled=True, axis_index_groups=groups)]
    all_to_all x8 -> x9, starting transfers between devices: 47.6 us -> 52.7 us  [swap(): lax.all_to_all(values, axes, 0, 0, tiled=True, axis_index_groups=groups)]
    add x4, local copies, waits for them, and re-layouts: 4.82 us -> 0.26 us  [on_device(): modulated = ((1.0 + scale) * text.astype(F32) + shift).astype(BF16)]
    all_to_all x8 -> x9, waiting for transfers between devices: 49.9 us -> 52.5 us  [swap(): lax.all_to_all(values, axes, 0, 0, tiled=True, axis_index_groups=groups)]
    dot_general x3 -> x4, matrix products: 19.1 us -> 21.1 us  [dot_t(): lax.dot_general(left, right, (((1,), (1,)), ((), ())), preferred_element_...]
    unnamed x57 -> x50, local copies, waits for them, and re-layouts: 10.7 us -> 8.98 us
    ppermute x4 -> x6, starting transfers between devices: 8.72 us -> 8.86 us  [the longest x2 3.51 us: on_device(): landed.append(lax.ppermute(part, 'seq', flip_z))]
  transfers between devices with their start and end apart: 20 -> 23, of which waited for: 11 -> 9; matrix products, arithmetic and copies ran while one was open for 26% -> 20% of each run, Pallas kernels for 5% -> 5%
where the time goes in v4:
time: 308 us; the launch traced here: 305 us
  waiting for transfers between devices  114 us (37%)
  starting transfers between devices  76.2 us (25%)
  matrix products  42.5 us (14%)
  local copies, waits for them, and re-layouts  27.7 us (9%)
  Pallas kernels  15.4 us (5%)
  other arithmetic  15.1 us (5%)
  between operations  14.6 us (5%)
    all_to_all x9, starting transfers between devices, swap(): lax.all_to_all(values, axes, 0, 0, tiled=True, axis_index_groups=groups)  52.7 us
    all_to_all x9, waiting for transfers between devices, swap(): lax.all_to_all(values, axes, 0, 0, tiled=True, axis_index_groups=groups)  52.5 us
    ppermute x2, waiting for transfers between devices, near_shard(): lax.ppermute(values, 'dp', [(i, (i + n_dp // 2) % n_dp) for i in range(n_...  42.5 us
    dot_general x4, matrix products, dot_t(): lax.dot_general(left, right, (((1,), (1,)), ((), ())), preferred_element_...  21.1 us
    ppermute x1, waiting for transfers between devices, on_device(): lowered_other = lax.ppermute(lowered[BLK:].astype(BF16), 'seq', flip_z)  9.87 us
    pallas_call x1, Pallas kernels, image_attention(): pl.pallas_call(image_kernel, grid=(heads, sources // step), in_specs=[pl....  9.27 us
    unnamed x50, local copies, waits for them, and re-layouts  8.98 us
    ppermute x4, starting transfers between devices, on_device(): moved = lax.ppermute(grad_a, 'dp', [(i, i ^ bit) for i in range(n_dp)])  8.64 us
  transfers between devices with their start and end apart: 23, of which 9 were waited for; matrix products, arithmetic and copies ran while one was open for 20% of the time, Pallas kernels for 5%

profile of v4, /device:TPU:1, one launch (start us, length us, event | category | flops | bytes accessed | tf_op | source)
XLA Modules:
  0.0 305.3 jit_solution(8260567744280240212)
XLA Ops:
  7.2 1.6 fusion.38
  8.8 0.9 broadcast_in_dim.10
  9.7 5.0 %all-to-all-start = ((bf16[4,192,384]{2,1,0:T(8,128)(2,1)}), bf16[4,192,384]{2,1,0:T(8,128)(2,1)S(1)}, u32[]{:S(2)}, u32[]{:S(2)}) async-start(bf16[4,192,384]{2,1,0:T(8,128)(2,1)} %broadcast_in_dim.10), calls=%async_computation | async-start | bytes 1179648 | tf_op jit(solution)/shard_map/all_to_all | solution.py:24
  14.7 0.8 pad_maximum_fusion.5
  15.6 1.6 collective-permute-start
  17.5 4.3 %fusion.58 = f32[128,640]{1,0:T(8,128)} fusion(bf16[2,4096,640]{2,1,0:T(8,128)(2,1)} %param.23, f32[4096]{0:T(1024)S(1)} %copy-done.21, f32[128]{0:T(128)S(1)} %add_rsqrt_fusion.1, bf16[1,256,4096]{2,1,0:T(8,128)(2,1)S(1)} %copy-done.9), kind=kOutput, calls=%fused_computation.78 | convolution fusion | flops 673841152 | bytes 6636032 | tf_op jit(solution)/shard_map/dot_general | solution.py:230
  21.8 7.0 %convolution_convert_fusion = bf16[128,4096]{1,0:T(8,128)(2,1)} fusion(bf16[640,4096]{1,0:T(8,128)(2,1)} %param.24, f32[128,640]{1,0:T(8,128)} %fusion.58, bf16[2,4096,640]{2,1,0:T(8,128)(2,1)} %param.23, f32[4096]{0:T(1024)S(1)} %copy-done.21, f32[128]{0:T(128)S(1)} %add_rsqrt_fusion.1, bf16[1,256,4096]{2,1,0:T(8,128)(2,1)S(1)} %copy-done.9), kind=kOutput, calls=%fused_computation.8 | convolution fusion | flops 1344962560 | bytes 12927488 | tf_op jit(solution)/shard_map/dot_general | solution.py:233
  28.8 2.3 copy.123
  31.1 1.4 select_bitcast_fusion.3
  32.5 1.0 pad_maximum_fusion.3
  33.8 3.4 %collective-permute-start.1 = (f32[192]{0:T(256)S(1)}, f32[192]{0:T(256)S(1)}, u32[]{:S(2)}, u32[]{:S(2)}) collective-permute-start(f32[192]{0:T(256)S(1)} %fusion.30), channel_id=1, source_target_pairs={{0,1},{1,0},{2,3},{3,2},{4,5},{5,4},{6,7},{7,6},{8,9},{9,8},{10,11... | collective-permute-start | bytes 2312 | tf_op jit(solution)/shard_map/ppermute | solution.py:243
  37.2 1.8 shard_map.210
  39.7 6.3 %all-to-all-start.1 = ((bf16[8,128,512]{2,1,0:T(8,128)(2,1)}), bf16[8,128,512]{2,1,0:T(8,128)(2,1)S(1)}, u32[]{:S(2)}, u32[]{:S(2)}) async-start(bf16[8,128,512]{2,1,0:T(8,128)(2,1)} %bitcast.123), calls=%async_computation.1 | async-start | bytes 2097152 | tf_op jit(solution)/shard_map/all_to_all | solution.py:24
  46.6 42.5 %collective-permute-done.2 = bf16[192,1664]{1,0:T(8,128)(2,1)S(1)} collective-permute-done((bf16[192,1664]{1,0:T(8,128)(2,1)S(1)}, bf16[192,1664]{1,0:T(8,128)(2,1)S(1)}, u32[]{:S(2)}, u32[]{:S(2)}) %collective-permute-start.2) | collective-permute-done | bytes 639008 | tf_op jit(solution)/shard_map/ppermute | solution.py:29
  89.1 0.8 copy-done.11
  90.0 1.3 select_bitcast_fusion.1
  91.3 1.2 pad_maximum_fusion.1
  92.5 1.5 pad_maximum_fusion
  94.0 1.7 copy.98
  95.6 4.0 %all-to-all-start.2 = ((bf16[4,2,384,384]{3,2,1,0:T(8,128)(2,1)}), bf16[4,2,384,384]{3,2,1,0:T(8,128)(2,1)S(1)}, u32[]{:S(2)}, u32[]{:S(2)}) async-start(bf16[4,2,384,384]{3,2,1,0:T(8,128)(2,1)} %copy.98), calls=%async_computation.2 | async-start | bytes 4718592 | tf_op jit(solution)/shard_map/all_to_all | solution.py:24
  99.6 2.3 slice.62
  101.9 0.8 dynamic_slice.7
  102.7 0.8 convert_reduce_fusion
  103.5 3.5 %fusion.26 = bf16[16,8,24,128]{3,1,2,0:T(8,128)(2,1)S(1)} fusion(bf16[3072,1280]{1,0:T(8,128)(2,1)} %bitcast.130, f32[128,512]{1,0:T(8,128)} %convert_reduce_fusion, f32[512]{0:T(512)S(1)} %dynamic_slice.7, bf16[1,128,4096]{2,1,0:T(8,128)(2,1)} %slice.62, s32[]{:T(128)S(6)} %select_n.49), kind=kOutput, calls=%fused_computation.35 | convolution fusion | flops 403308544 | bytes 4327428 | tf_op jit(solution)/shard_map/dot_general | solution.py:55
  107.1 1.0 copy.117
  108.1 18.0 %all-to-all-done.2 = bf16[4,2,384,384]{3,2,1,0:T(8,128)(2,1)S(1)} async-done(((bf16[4,2,384,384]{3,2,1,0:T(8,128)(2,1)}), bf16[4,2,384,384]{3,2,1,0:T(8,128)(2,1)S(1)}, u32[]{:S(2)}, u32[]{:S(2)}) %all-to-all-start.2) | async-done | bytes 2359328 | tf_op jit(solution)/shard_map/all_to_all | solution.py:24
  126.1 10.6 %all-to-all-start.3 = ((bf16[128,24,128]{2,1,0:T(8,128)(2,1)}), bf16[128,24,128]{2,1,0:T(8,128)(2,1)S(1)}, u32[]{:S(2)}, u32[]{:S(2)}) async-start(bf16[128,24,128]{2,1,0:T(8,128)(2,1)} %bitcast.57), calls=%async_computation.3 | async-start | bytes 1572864 | tf_op jit(solution)/shard_map/all_to_all | solution.py:24
  136.7 23.6 %all-to-all-done.3 = bf16[128,24,128]{2,1,0:T(8,128)(2,1)S(1)} async-done(((bf16[128,24,128]{2,1,0:T(8,128)(2,1)}), bf16[128,24,128]{2,1,0:T(8,128)(2,1)S(1)}, u32[]{:S(2)}, u32[]{:S(2)}) %all-to-all-start.3) | async-done | bytes 786464 | tf_op jit(solution)/shard_map/all_to_all | solution.py:24
  161.6 1.4 copy.101
  163.0 5.5 %all-to-all-start.4 = ((bf16[128,24,128]{2,1,0:T(8,128)(2,1)}), bf16[128,24,128]{2,1,0:T(8,128)(2,1)S(1)}, u32[]{:S(2)}, u32[]{:S(2)}) async-start(bf16[128,24,128]{2,1,0:T(8,128)(2,1)} %copy.101), calls=%async_computation.4 | async-start | bytes 1572864 | tf_op jit(solution)/shard_map/all_to_all | solution.py:24
  170.7 9.3 %shard_map.211 = (f32[1024,384]{1,0:T(8,128)S(1)}, f32[1024,384]{1,0:T(8,128)S(1)}) custom-call(bf16[8,384,384]{2,1,0:T(8,128)(2,1)S(1)} %bitcast.112, bf16[8,384,384]{2,1,0:T(8,128)(2,1)S(1)} %bitcast.113, bf16[8,384,384]{2,1,0:T(8,128)(2,1)S(1)} %bitcast.114, f32[2,128]{1,0:T(2,128)S(1)} %copy-done.5), custom_call_target="tpu_custom_call" | custom-call | flops 2415919104 | bytes 5505024 | tf_op jit(solution)/shard_map/pallas_call | solution.py:109
  180.0 1.1 copy-done.1
  181.1 1.2 copy-done.3
  182.3 1.3 all-to-all-done.4
  183.7 1.3 copy.102
  185.0 4.8 %fusion.12.k_ref.v_ref = f32[128,768]{1,0:T(8,128)S(1)} fusion(bf16[3072,1280]{1,0:T(8,128)(2,1)} %bitcast.131, bf16[128,3072]{0,1:T(8,128)(2,1)} %bitcast.134, f32[3072]{0:T(1024)S(1)} %add.126, f32[3072]{0:T(1024)S(1)} %add.124), kind=kOutput, calls=%fused_computation.13 | convolution fusion | flops 605552640 | bytes 5922816 | tf_op jit(solution)/shard_map/dot_general | solution.py:279
  189.8 4.3 %shard_map.212 = bf16[1024,384]{1,0:T(8,128)(2,1)S(1)} custom-call(s32[1]{0:T(128)} %bitcast.length_ref, bf16[8,384,384]{2,1,0:T(8,128)(2,1)S(1)} %bitcast.115, f32[128,768]{1,0:T(8,128)S(1)} %fusion.12.k_ref.v_ref, f32[128,768]{1,0:T(8,128)S(1)} %fusion.12.k_ref.v_ref, f32[2,128]{1,0:T(2,128)S(1)} %copy-done.5, f32[1,128]{1,0:T(1,128)S(1)} %bitcast.117, ...), custom_call_target="tpu_custom_call" | custom-call | flops 301989888 | bytes 4718592 | tf_op jit(solution)/shard_map/pallas_call | solution.py:153
  194.8 1.3 copy.105
  196.1 3.5 %all-to-all-start.5 = ((bf16[4,256,448]{1,2,0:T(8,128)(2,1)}), bf16[4,256,448]{1,2,0:T(8,128)(2,1)S(1)}, u32[]{:S(2)}, u32[]{:S(2)}) async-start(bf16[4,256,448]{1,2,0:T(8,128)(2,1)} %copy.105), calls=%async_computation.5 | async-start | bytes 1835008 | tf_op jit(solution)/shard_map/all_to_all | solution.py:24
  199.6 2.3 copy.106
  201.9 1.2 copy.107
  203.1 1.5 fusion.39
  204.7 2.6 collective-permute-start.4
  207.3 1.2 copy.110
  209.1 2.8 all-to-all-done.5
  212.0 8.0 %fusion = f32[128,3072]{1,0:T(8,128)} fusion(bf16[128,1536]{0,1:T(8,128)(2,1)S(1)} %bitcast.139, bf16[3072,1664]{1,0:T(8,128)(2,1)} %bitcast.145), kind=kOutput, calls=%fused_computation | convolution fusion | flops 1207959552 | bytes 11403264 | tf_op jit(solution)/shard_map/dot_general | solution.py:55
  220.1 4.8 %fusion.18 = bf16[128,1536]{1,0:T(8,128)(2,1)} fusion(bf16[128,1536]{0,1:T(8,128)(2,1)S(1)} %bitcast.137, bf16[3072,1664]{1,0:T(8,128)(2,1)} %bitcast.146), kind=kOutput, calls=%fused_computation.21 | convolution fusion | flops 604176384 | bytes 5505024 | tf_op jit(solution)/shard_map/dot_general | solution.py:55
  225.6 3.4 %all-to-all-start.6 = ((bf16[4,256,128]{2,1,0:T(8,128)(2,1)}), bf16[4,256,128]{2,1,0:T(8,128)(2,1)S(1)}, u32[]{:S(2)}, u32[]{:S(2)}) async-start(bf16[4,256,128]{2,1,0:T(8,128)(2,1)} %broadcast_in_dim.11), calls=%async_computation.6 | async-start | bytes 524288 | tf_op jit(solution)/shard_map/all_to_all | solution.py:24
  229.0 4.8 %fusion.15 = bf16[128,1536]{1,0:T(8,128)(2,1)} fusion(bf16[128,1536]{0,1:T(8,128)(2,1)S(1)} %bitcast.138, bf16[3072,1664]{1,0:T(8,128)(2,1)} %bitcast.147), kind=kOutput, calls=%fused_computation.20 | convolution fusion | flops 604176384 | bytes 5505024 | tf_op jit(solution)/shard_map/dot_general | solution.py:55
  233.7 3.5 %collective-permute-start.6 = (bf16[128,1536]{1,0:T(8,128)(2,1)}, bf16[128,1536]{1,0:T(8,128)(2,1)S(1)}, u32[]{:S(2)}, u32[]{:S(2)}) collective-permute-start(bf16[128,1536]{1,0:T(8,128)(2,1)} %fusion.18), channel_id=1, source_target_pairs={{0,1},{1,0},{2,3},{3,2},{4,5},{5,4},{6,7},{7,6},{8,9},{9,8},{10,11... | collective-permute-start | bytes 1179656 | tf_op jit(solution)/shard_map/ppermute | solution.py:299
  237.9 2.9 collective-permute-start.11
  241.1 2.4 collective-permute-start.7
  243.6 9.9 %collective-permute-done.11 = bf16[128,64]{0,1:T(8,128)(2,1)S(1)} collective-permute-done((bf16[128,64]{0,1:T(8,128)(2,1)S(1)}, bf16[128,64]{0,1:T(8,128)(2,1)S(1)}, u32[]{:S(2)}, u32[]{:S(2)}) %collective-permute-start.11) | collective-permute-done | bytes 16416 | tf_op jit(solution)/shard_map/ppermute | solution.py:294
  253.4 1.1 convolution_convert_fusion.2
  254.6 2.0 collective-permute-start.8
  256.6 2.0 multiply_reduce_fusion
  259.4 1.0 copy.111
  260.4 7.6 %all-to-all-start.7 = ((bf16[16,72,192]{2,1,0:T(8,128)(2,1)}), bf16[16,72,192]{2,1,0:T(8,128)(2,1)S(1)}, u32[]{:S(2)}, u32[]{:S(2)}) async-start(bf16[16,72,192]{2,1,0:T(8,128)(2,1)} %bitcast.42), calls=%async_computation.7 | async-start | bytes 1179648 | tf_op jit(solution)/shard_map/all_to_all | solution.py:24
  268.0 3.0 collective-permute-start.9
  271.0 8.2 %collective-permute-done.9 = bf16[64,384]{1,0:T(8,128)(2,1)S(1)} collective-permute-done((bf16[64,384]{1,0:T(8,128)(2,1)S(1)}, bf16[64,384]{1,0:T(8,128)(2,1)S(1)}, u32[]{:S(2)}, u32[]{:S(2)}) %collective-permute-start.9) | collective-permute-done | bytes 49184 | tf_op jit(solution)/shard_map/ppermute | solution.py:311
  279.2 1.3 collective-permute-start.10
  280.9 1.2 copy.112
  282.9 6.8 %all-to-all-start.8 = ((bf16[8,72,192]{2,1,0:T(8,128)(2,1)}), bf16[8,72,192]{2,1,0:T(8,128)(2,1)S(1)}, u32[]{:S(2)}, u32[]{:S(2)}) async-start(bf16[8,72,192]{2,1,0:T(8,128)(2,1)} %broadcast_in_dim.12), calls=%async_computation.8 | async-start | bytes 589824 | tf_op jit(solution)/shard_map/all_to_all | solution.py:24
  290.4 6.8 %all-to-all-done.8 = bf16[8,72,192]{2,1,0:T(8,128)(2,1)S(1)} async-done(((bf16[8,72,192]{2,1,0:T(8,128)(2,1)}), bf16[8,72,192]{2,1,0:T(8,128)(2,1)S(1)}, u32[]{:S(2)}, u32[]{:S(2)}) %all-to-all-start.8) | async-done | bytes 221216 | tf_op jit(solution)/shard_map/all_to_all | solution.py:24
  (116 shorter events, 12.5 us)
Async XLA Ops:
  7.2 7.5 %copy-start.13 = (bf16[192,2,384]{2,1,0:T(2,128)(2,1)S(1)}, bf16[192,2,384]{2,1,0:T(2,128)(2,1)}, u32[]{:S(2)}) copy-start(bf16[192,2,384]{2,1,0:T(2,128)(2,1)} %param.29) | copy-start | bytes 884740
  7.2 7.6 %copy-start.10 = (bf16[512,192]{0,1:T(8,128)(2,1)S(1)}, bf16[512,192]{0,1:T(8,128)(2,1)}, u32[]{:S(2)}) copy-start(bf16[512,192]{0,1:T(8,128)(2,1)} %param.26) | copy-start | bytes 589828
  7.2 10.0 %copy-start.9 = (bf16[1,256,4096]{2,1,0:T(8,128)(2,1)S(1)}, bf16[1,256,4096]{2,1,0:T(8,128)(2,1)}, u32[]{:S(2)}) copy-start(bf16[1,256,4096]{2,1,0:T(8,128)(2,1)} %param.19) | copy-start | bytes 6291460
  8.8 8.7 %copy-start.21 = (f32[4096]{0:T(1024)S(1)}, f32[4096]{0:T(1024)}, u32[]{:S(2)}) copy-start(f32[4096]{0:T(1024)} %param.22) | copy-start | bytes 49156
  9.7 21.4 %all-to-all-start = ((bf16[4,192,384]{2,1,0:T(8,128)(2,1)}), bf16[4,192,384]{2,1,0:T(8,128)(2,1)S(1)}, u32[]{:S(2)}, u32[]{:S(2)}) async-start(bf16[4,192,384]{2,1,0:T(8,128)(2,1)} %broadcast_in_dim.10), calls=%async_computation | async-start | bytes 1179648 | tf_op jit(solution)/shard_map/all_to_all | solution.py:24
  14.7 88.8 %all-gather.5.cloned.1.call-start = ((), (), s32[]{:S(2)}) async-start(), calls=%async_computation.9 | async-start | bytes 8847360 | tf_op jit(solution)/shard_map/all_gather | solution.py:38
  15.6 15.5 %collective-permute-start = (bf16[192,1280]{1,0:T(8,128)(2,1)}, bf16[192,1280]{1,0:T(8,128)(2,1)}, u32[]{:S(2)}, u32[]{:S(2)}) collective-permute-start(bf16[192,1280]{1,0:T(8,128)(2,1)} %pad_maximum_fusion.5), channel_id=1, source_target_pairs={{0,64},{8,72},{16,80},{24,88},{32,96},{40,104},{48,112},{56,120},{... | collective-permute-start | bytes 1474568 | tf_op jit(solution)/shard_map/ppermute | solution.py:29
  31.1 2.5 copy-start.7
  32.5 4.7 %copy-start = (bf16[1,128,3,3072]{3,1,2,0:T(8,128)(2,1)S(1)}, bf16[1,128,3,3072]{3,1,2,0:T(8,128)(2,1)}, u32[]{:S(2)}) copy-start(bf16[1,128,3,3072]{3,1,2,0:T(8,128)(2,1)} %param.31) | copy-start | bytes 7077892
  33.8 12.2 %collective-permute-start.1 = (f32[192]{0:T(256)S(1)}, f32[192]{0:T(256)S(1)}, u32[]{:S(2)}, u32[]{:S(2)}) collective-permute-start(f32[192]{0:T(256)S(1)} %fusion.30), channel_id=1, source_target_pairs={{0,1},{1,0},{2,3},{3,2},{4,5},{5,4},{6,7},{7,6},{8,9},{9,8},{10,11... | collective-permute-start | bytes 2312 | tf_op jit(solution)/shard_map/ppermute | solution.py:243
  39.0 7.0 %copy-start.18 = (f32[192]{0:T(256)S(1)}, f32[192]{0:T(256)}, u32[]{:S(2)}) copy-start(f32[192]{0:T(256)} %param.36) | copy-start | bytes 2308
  39.0 7.0 %copy-start.8 = (bf16[4,192,384]{2,1,0:T(8,128)(2,1)S(1)}, bf16[4,192,384]{2,1,0:T(8,128)(2,1)}, u32[]{:S(2)}) copy-start(bf16[4,192,384]{2,1,0:T(8,128)(2,1)} %copy-done.7) | copy-start | bytes 1769476
  39.0 7.2 %copy-start.14 = (f32[64,192]{1,0:T(8,128)S(1)}, f32[64,192]{1,0:T(8,128)}, u32[]{:S(2)}) copy-start(f32[64,192]{1,0:T(8,128)} %param.35) | copy-start | bytes 147460
  39.0 50.9 %collective-permute-start.3 = (bf16[4,384,384]{2,1,0:T(8,128)(2,1)}, bf16[4,384,384]{2,1,0:T(8,128)(2,1)}, u32[]{:S(2)}, u32[]{:S(2)}) collective-permute-start(bf16[4,384,384]{2,1,0:T(8,128)(2,1)} %get-tuple-element.20), channel_id=1, source_target_pairs={{0,1},{1,0},{2,3},{3,2},{4,5},{5,4},{6,7},{7,6},{8,9},{9,8},{10,11... | collective-permute-start | bytes 3538952 | tf_op jit(solution)/shard_map/ppermute | solution.py:220
  39.7 50.3 %all-to-all-start.1 = ((bf16[8,128,512]{2,1,0:T(8,128)(2,1)}), bf16[8,128,512]{2,1,0:T(8,128)(2,1)S(1)}, u32[]{:S(2)}, u32[]{:S(2)}) async-start(bf16[8,128,512]{2,1,0:T(8,128)(2,1)} %bitcast.123), calls=%async_computation.1 | async-start | bytes 2097152 | tf_op jit(solution)/shard_map/all_to_all | solution.py:24
  46.0 157.2 %all-gather.7.cloned.1.call-start = ((), (), s32[]{:S(2)}) async-start(), calls=%async_computation.10 | async-start | bytes 11501568 | tf_op jit(solution)/shard_map/all_gather | solution.py:38
  46.5 42.6 %collective-permute-start.2 = (bf16[192,1664]{1,0:T(8,128)(2,1)S(1)}, bf16[192,1664]{1,0:T(8,128)(2,1)S(1)}, u32[]{:S(2)}, u32[]{:S(2)}) collective-permute-start(bf16[192,1664]{1,0:T(8,128)(2,1)S(1)} %fusion.49), channel_id=1, source_target_pairs={{0,64},{8,72},{16,80},{24,88},{32,96},{40,104},{48,112},{56,120},{... | collective-permute-start | bytes 1916936 | tf_op jit(solution)/shard_map/ppermute | solution.py:29
  89.1 0.8 copy-start.11
  95.6 30.4 %all-to-all-start.2 = ((bf16[4,2,384,384]{3,2,1,0:T(8,128)(2,1)}), bf16[4,2,384,384]{3,2,1,0:T(8,128)(2,1)S(1)}, u32[]{:S(2)}, u32[]{:S(2)}) async-start(bf16[4,2,384,384]{3,2,1,0:T(8,128)(2,1)} %copy.98), calls=%async_computation.2 | async-start | bytes 4718592 | tf_op jit(solution)/shard_map/all_to_all | solution.py:24
  107.1 54.0 %copy-start.19 = (s32[16]{0:T(128)S(1)}, s32[16]{0:T(128)}, u32[]{:S(2)}) copy-start(s32[16]{0:T(128)} %param.21) | copy-start | bytes 196
  126.1 34.3 %all-to-all-start.3 = ((bf16[128,24,128]{2,1,0:T(8,128)(2,1)}), bf16[128,24,128]{2,1,0:T(8,128)(2,1)S(1)}, u32[]{:S(2)}, u32[]{:S(2)}) async-start(bf16[128,24,128]{2,1,0:T(8,128)(2,1)} %bitcast.57), calls=%async_computation.3 | async-start | bytes 1572864 | tf_op jit(solution)/shard_map/all_to_all | solution.py:24
  160.9 8.1 %copy-start.16 = (f32[1,3072]{1,0:T(1,128)S(1)}, f32[1,3072]{1,0:T(1,128)}, u32[]{:S(2)}) copy-start(f32[1,3072]{1,0:T(1,128)} %param.27) | copy-start | bytes 36868
  161.1 8.8 %copy-start.17 = (f32[1,3072]{1,0:T(1,128)S(1)}, f32[1,3072]{1,0:T(1,128)}, u32[]{:S(2)}) copy-start(f32[1,3072]{1,0:T(1,128)} %param.28) | copy-start | bytes 36868
  161.1 9.0 %copy-start.20 = (s32[16]{0:T(128)S(1)}, s32[16]{0:T(128)}, u32[]{:S(2)}) copy-start(s32[16]{0:T(128)} %param.20) | copy-start | bytes 196
  161.1 9.6 %copy-start.5 = (f32[2,128]{1,0:T(2,128)S(1)}, f32[2,128]{1,0:T(2,128)}, u32[]{:S(2)}) copy-start(f32[2,128]{1,0:T(2,128)} %gain_ref.3) | copy-start | bytes 3076
  163.0 20.7 %all-to-all-start.4 = ((bf16[128,24,128]{2,1,0:T(8,128)(2,1)}), bf16[128,24,128]{2,1,0:T(8,128)(2,1)S(1)}, u32[]{:S(2)}, u32[]{:S(2)}) async-start(bf16[128,24,128]{2,1,0:T(8,128)(2,1)} %copy.101), calls=%async_computation.4 | async-start | bytes 1572864 | tf_op jit(solution)/shard_map/all_to_all | solution.py:24
  180.0 1.1 copy-start.1
  181.1 1.2 copy-start.3
  185.0 4.8 %copy-start.2 = (f32[1024,384]{1,0:T(8,128)S(1)}, f32[1024,384]{1,0:T(8,128)}, u32[]{:S(2)}) copy-start(f32[1024,384]{1,0:T(8,128)} %copy-done.1) | copy-start | bytes 4718596
  185.0 4.8 %copy-start.4 = (f32[1024,384]{1,0:T(8,128)S(1)}, f32[1024,384]{1,0:T(8,128)}, u32[]{:S(2)}) copy-start(f32[1024,384]{1,0:T(8,128)} %copy-done.3) | copy-start | bytes 4718596
  185.0 4.8 %copy-start.6 = (f32[128]{0:T(128)S(1)}, f32[128]{0:T(128)}, u32[]{:S(2)}) copy-start(f32[128]{0:T(128)} %param.30) | copy-start | bytes 1540
  189.8 4.3 %copy-start.12 = (f32[384,64]{0,1:T(8,128)S(1)}, f32[384,64]{0,1:T(8,128)}, u32[]{:S(2)}) copy-start(f32[384,64]{0,1:T(8,128)} %param.34) | copy-start | bytes 294916
  196.1 15.7 %all-to-all-start.5 = ((bf16[4,256,448]{1,2,0:T(8,128)(2,1)}), bf16[4,256,448]{1,2,0:T(8,128)(2,1)S(1)}, u32[]{:S(2)}, u32[]{:S(2)}) async-start(bf16[4,256,448]{1,2,0:T(8,128)(2,1)} %copy.105), calls=%async_computation.5 | async-start | bytes 1835008 | tf_op jit(solution)/shard_map/all_to_all | solution.py:24
  204.7 4.3 %collective-permute-start.4 = (bf16[128,128]{1,0:T(8,128)(2,1)S(1)}, bf16[128,128]{1,0:T(8,128)(2,1)S(1)}, u32[]{:S(2)}, u32[]{:S(2)}) collective-permute-start(bf16[128,128]{1,0:T(8,128)(2,1)S(1)} %fusion.39), channel_id=1, source_target_pairs={{0,1},{1,0},{2,3},{3,2},{4,5},{5,4},{6,7},{7,6},{8,9},{9,8},{10,11... | collective-permute-start | bytes 98312 | tf_op jit(solution)/shard_map/ppermute | solution.py:290
  225.6 15.3 %all-to-all-start.6 = ((bf16[4,256,128]{2,1,0:T(8,128)(2,1)}), bf16[4,256,128]{2,1,0:T(8,128)(2,1)S(1)}, u32[]{:S(2)}, u32[]{:S(2)}) async-start(bf16[4,256,128]{2,1,0:T(8,128)(2,1)} %broadcast_in_dim.11), calls=%async_computation.6 | async-start | bytes 524288 | tf_op jit(solution)/shard_map/all_to_all | solution.py:24
  233.7 22.8 %collective-permute-start.6 = (bf16[128,1536]{1,0:T(8,128)(2,1)}, bf16[128,1536]{1,0:T(8,128)(2,1)S(1)}, u32[]{:S(2)}, u32[]{:S(2)}) collective-permute-start(bf16[128,1536]{1,0:T(8,128)(2,1)} %fusion.18), channel_id=1, source_target_pairs={{0,1},{1,0},{2,3},{3,2},{4,5},{5,4},{6,7},{7,6},{8,9},{9,8},{10,11... | collective-permute-start | bytes 1179656 | tf_op jit(solution)/shard_map/ppermute | solution.py:299
  237.2 19.4 %collective-permute-start.5 = (bf16[128,1536]{1,0:T(8,128)(2,1)}, bf16[128,1536]{1,0:T(8,128)(2,1)S(1)}, u32[]{:S(2)}, u32[]{:S(2)}) collective-permute-start(bf16[128,1536]{1,0:T(8,128)(2,1)} %fusion.15), channel_id=1, source_target_pairs={{0,1},{1,0},{2,3},{3,2},{4,5},{5,4},{6,7},{7,6},{8,9},{9,8},{10,11... | collective-permute-start | bytes 1179656 | tf_op jit(solution)/shard_map/ppermute | solution.py:299
  237.3 0.6 copy-start.15
  237.9 15.5 %collective-permute-start.11 = (bf16[128,64]{0,1:T(8,128)(2,1)S(1)}, bf16[128,64]{0,1:T(8,128)(2,1)S(1)}, u32[]{:S(2)}, u32[]{:S(2)}) collective-permute-start(bf16[128,64]{0,1:T(8,128)(2,1)S(1)} %slice.149), channel_id=1, source_target_pairs={{0,1},{1,0},{2,3},{3,2},{4,5},{5,4},{6,7},{7,6},{8,9},{9,8},{10,11... | collective-permute-start | bytes 49160 | tf_op jit(solution)/shard_map/ppermute | solution.py:294
  241.1 13.4 %collective-permute-start.7 = (bf16[64,384]{1,0:T(8,128)(2,1)S(1)}, bf16[64,384]{1,0:T(8,128)(2,1)S(1)}, u32[]{:S(2)}, u32[]{:S(2)}) collective-permute-start(bf16[64,384]{1,0:T(8,128)(2,1)S(1)} %convolution_convert_fusion.5), channel_id=1, source_target_pairs={{0,8},{8,0},{16,24},{24,16},{32,40},{40,32},{48,56},{56,48},{64,72... | collective-permute-start | bytes 147464 | tf_op jit(solution)/shard_map/ppermute | solution.py:311
  254.6 13.3 %collective-permute-start.8 = (bf16[64,384]{1,0:T(8,128)(2,1)S(1)}, bf16[64,384]{1,0:T(8,128)(2,1)S(1)}, u32[]{:S(2)}, u32[]{:S(2)}) collective-permute-start(bf16[64,384]{1,0:T(8,128)(2,1)S(1)} %add_convert_fusion.2), channel_id=1, source_target_pairs={{0,16},{8,24},{16,0},{24,8},{32,48},{40,56},{48,32},{56,40},{64,80... | collective-permute-start | bytes 147464 | tf_op jit(solution)/shard_map/ppermute | solution.py:311
  260.4 21.7 %all-to-all-start.7 = ((bf16[16,72,192]{2,1,0:T(8,128)(2,1)}), bf16[16,72,192]{2,1,0:T(8,128)(2,1)S(1)}, u32[]{:S(2)}, u32[]{:S(2)}) async-start(bf16[16,72,192]{2,1,0:T(8,128)(2,1)} %bitcast.42), calls=%async_computation.7 | async-start | bytes 1179648 | tf_op jit(solution)/shard_map/all_to_all | solution.py:24
  268.0 11.2 %collective-permute-start.9 = (bf16[64,384]{1,0:T(8,128)(2,1)S(1)}, bf16[64,384]{1,0:T(8,128)(2,1)S(1)}, u32[]{:S(2)}, u32[]{:S(2)}) collective-permute-start(bf16[64,384]{1,0:T(8,128)(2,1)S(1)} %add_convert_fusion.1), channel_id=1, source_target_pairs={{0,32},{8,40},{16,48},{24,56},{32,0},{40,8},{48,16},{56,24},{64,96... | collective-permute-start | bytes 147464 | tf_op jit(solution)/shard_map/ppermute | solution.py:311
  279.2 10.5 %collective-permute-start.10 = (bf16[64,384]{1,0:T(8,128)(2,1)S(1)}, bf16[64,384]{1,0:T(8,128)(2,1)S(1)}, u32[]{:S(2)}, u32[]{:S(2)}) collective-permute-start(bf16[64,384]{1,0:T(8,128)(2,1)S(1)} %add_convert_fusion), channel_id=1, source_target_pairs={{0,64},{8,72},{16,80},{24,88},{32,96},{40,104},{48,112},{56,120},{... | collective-permute-start | bytes 147464 | tf_op jit(solution)/shard_map/ppermute | solution.py:311
  282.9 14.2 %all-to-all-start.8 = ((bf16[8,72,192]{2,1,0:T(8,128)(2,1)}), bf16[8,72,192]{2,1,0:T(8,128)(2,1)S(1)}, u32[]{:S(2)}, u32[]{:S(2)}) async-start(bf16[8,72,192]{2,1,0:T(8,128)(2,1)} %broadcast_in_dim.12), calls=%async_computation.8 | async-start | bytes 589824 | tf_op jit(solution)/shard_map/all_to_all | solution.py:24
Sparse Core Ops, SparseCore 0:
  33.7 50.7 all-gather.4
  92.6 69.4 all-gather.6

commit v5 on v4

--- a/solution.py
+++ b/solution.py
@@ -130,48 +130,143 @@
     )(received, received, received, gains)
 
 
-def text_kernel(length_ref, q_ref, k_ref, v_ref, gain_ref, text_gain_ref, num_ref, den_ref, out_ref):
-    k = rms_scale(k_ref[...], text_gain_ref[...]).astype(BF16)
-    v = v_ref[...].astype(BF16)
-    q = q_ref[...].reshape(-1, HD).astype(F32)
-    q = rms_scale(q, gain_ref[0:1, :] * QUERY_SCALE).astype(BF16)
-    weight = jnp.exp2(dot_t(q, k))
-    valid = lax.broadcasted_iota(jnp.int32, weight.shape, 1) < length_ref[0]
-    weight = jnp.where(valid, weight, 0.0).astype(BF16)
-    stacked = jnp.concatenate([v, jnp.ones_like(v)], axis=1)
-    both = jnp.dot(weight, stacked, preferred_element_type=F32)
-    total = num_ref[...] + both[:, :HD]
-    out_ref[...] = (total / (den_ref[...] + both[:, HD:])).astype(BF16)
-
-
-def text_attention(length, received, key_value, gains, text_gain, num, den):
+def prompt_kernel(
+    length_ref,
+    q_ref,
+    text_ref,
+    k_weight,
+    v_weight,
+    down_ref,
+    gain_ref,
+    text_gain_ref,
+    num_ref,
+    den_ref,
+    out_ref,
+    lowered,
+):
+    head = pl.program_id(0)
+    heads = pl.num_programs(0) - 1
+
+    @pl.when(head == 0)
+    def _():
+        lowered[...] = jnp.zeros_like(lowered)
+
+    @pl.when(head < heads)
+    def _():
+        text = text_ref[...]
+        k = jnp.dot(text, k_weight[...], preferred_element_type=F32)
+        k = rms_scale(k, text_gain_ref[...]).astype(BF16)
+        v = jnp.dot(text, v_weight[...], preferred_element_type=F32).astype(BF16)
+        stacked = jnp.concatenate([v, jnp.ones_like(v)], axis=1)
+        groups, rows, _ = out_ref.shape
+        for b in range(groups):
+            q = q_ref[2 * b : 2 * b + 2].reshape(rows, HD).astype(F32)
+            q = rms_scale(q, gain_ref[0:1, :] * QUERY_SCALE).astype(BF16)
+            weight = jnp.exp2(dot_t(q, k))
+            valid = lax.broadcasted_iota(jnp.int32, weight.shape, 1) < length_ref[0]
+            weight = jnp.where(valid, weight, 0.0).astype(BF16)
+            both = jnp.dot(weight, stacked, preferred_element_type=F32)
+            at = slice(b * rows, (b + 1) * rows)
+            total = num_ref[at, :] + both[:, :HD]
+            attended = (total / (den_ref[at, :] + both[:, HD:])).astype(BF16)
+            out_ref[b] = attended
+            lowered[at, :] += jnp.dot(attended, down_ref[...], preferred_element_type=F32)
+
+    @pl.when(head == heads)
+    def _():
+        out_ref[...] = lowered[...].reshape(out_ref.shape).astype(BF16)
+
+
+def prompt_attention(length, received, text, weights, first, down, gains, text_gain, num, den):
     sources, _, width = received.shape
     heads = width // HD
     image_len = sources * BLK
-    step = sources // 2
-    rows = step * BLK
+    model = text.shape[1]
+    groups = sources // 2
+
+    def last(h):
+        return jnp.minimum(h, heads - 1)
+
     return pl.pallas_call(
-        text_kernel,
-        grid=(heads, sources // step),
+        prompt_kernel,
+        grid=(heads + 1,),
         in_specs=[
             pl.BlockSpec(memory_space=pltpu.SMEM),
-            pl.BlockSpec((step, BLK, HD), lambda h, b: (b, 0, h)),
-            pl.BlockSpec((BLK, HD), lambda h, b: (0, h)),
-            pl.BlockSpec((BLK, HD), lambda h, b: (0, heads + h)),
-            pl.BlockSpec((2, HD), lambda h, b: (0, 0)),
-            pl.BlockSpec((1, HD), lambda h, b: (0, 0)),
-            pl.BlockSpec((rows, HD), lambda h, b: (b, h)),
-            pl.BlockSpec((rows, HD), lambda h, b: (b, h)),
+            pl.BlockSpec((sources, BLK, HD), lambda h: (0, 0, last(h))),
+            pl.BlockSpec((BLK, model), lambda h: (0, 0)),
+            pl.BlockSpec((model, HD), lambda h: (0, first + last(h))),
+            pl.BlockSpec((model, HD), lambda h: (0, first + heads + last(h))),
+            pl.BlockSpec((HD, down.shape[1]), lambda h: (last(h), 0)),
+            pl.BlockSpec((2, HD), lambda h: (0, 0)),
+            pl.BlockSpec((1, HD), lambda h: (0, 0)),
+            pl.BlockSpec((image_len, HD), lambda h: (0, last(h))),
+            pl.BlockSpec((image_len, HD), lambda h: (0, last(h))),
         ],
-        out_specs=pl.BlockSpec((rows, HD), lambda h, b: (b, h)),
-        out_shape=jax.ShapeDtypeStruct((image_len, width), BF16),
+        out_specs=pl.BlockSpec((groups, 2 * BLK, HD), lambda h: (0, 0, h)),
+        out_shape=jax.ShapeDtypeStruct((groups, 2 * BLK, width + HD), BF16),
+        scratch_shapes=[pltpu.VMEM((image_len, HD), F32)],
         compiler_params=pltpu.CompilerParams(vmem_limit_bytes=24 * 1024 * 1024),
         cost_estimate=pl.CostEstimate(
-            flops=6 * image_len * BLK * width,
-            bytes_accessed=12 * image_len * width,
+            flops=6 * image_len * BLK * width + 4 * BLK * model * width,
+            bytes_accessed=12 * image_len * width + 4 * model * width,
             transcendentals=heads * image_len * BLK,
         ),
-    )(length, received, key_value, key_value, gains, text_gain, num, den)
+    )(length, received, text, weights, weights, down, gains, text_gain, num, den)
+
+
+def t5_kernel(x_ref, gain_ref, gate_w, up_w, out_w, out_ref, normed, hidden):
+    step = pl.program_id(0)
+    cuts = hidden.shape[0]
+
+    @pl.when(step == 0)
+    def _():
+        normed[...] = rms_scale(x_ref[0].astype(F32), gain_ref[...]).astype(BF16)
+
+    @pl.when(step < cuts)
+    def _():
+        gate = jnp.dot(normed[...], gate_w[0], preferred_element_type=F32)
+        upward = jnp.dot(normed[...], up_w[0], preferred_element_type=F32)
+        hidden[step] = (jax.nn.gelu(gate, approximate=True) * upward).astype(BF16)
+
+    @pl.when(step >= cuts)
+    def _():
+        joined = jnp.concatenate([hidden[c] for c in range(cuts)], 1)
+        total = jnp.dot(joined, out_w[...], preferred_element_type=F32)
+        out_ref[0] = total.astype(BF16)
+
+
+def t5_ffn(states, gain, in_weight, out_weight, n_seq):
+    _, features, units = in_weight.shape
+    cut = 128
+    cuts = units // cut
+    feat = features // n_seq
+
+    def unit(i):
+        return jnp.minimum(i, cuts - 1)
+
+    def share(i):
+        return jnp.maximum(i - cuts, 0)
+
+    return pl.pallas_call(
+        t5_kernel,
+        grid=(cuts + n_seq,),
+        in_specs=[
+            pl.BlockSpec((1, BLK, features), lambda i: (0, 0, 0)),
+            pl.BlockSpec((1, features), lambda i: (0, 0)),
+            pl.BlockSpec((1, features, cut), lambda i: (0, 0, unit(i))),
+            pl.BlockSpec((1, features, cut), lambda i: (1, 0, unit(i))),
+            pl.BlockSpec((units, feat), lambda i: (0, share(i))),
+        ],
+        out_specs=pl.BlockSpec((1, BLK, feat), lambda i: (share(i), 0, 0)),
+        out_shape=jax.ShapeDtypeStruct((n_seq, BLK, feat), BF16),
+        scratch_shapes=[pltpu.VMEM((BLK, features), BF16), pltpu.VMEM((cuts, BLK, cut), BF16)],
+        compiler_params=pltpu.CompilerParams(vmem_limit_bytes=24 * 1024 * 1024),
+        cost_estimate=pl.CostEstimate(
+            flops=6 * BLK * features * units,
+            bytes_accessed=6 * features * units,
+            transcendentals=BLK * units,
+        ),
+    )(states, gain.reshape(1, features), in_weight, in_weight, out_weight)
 
 
 def on_device(
@@ -217,6 +312,7 @@
     )
     near_weights = near_shard(weights)
     own_heads, other_heads = pack_heads(image_query_key_value[0].transpose(1, 0, 2), pair, n_seq)
+    t5_gain, other_heads = lax.optimization_barrier((t5_gain, other_heads))
     other_heads = lax.ppermute(other_heads, "seq", flip_z)
     direction_t = proj_weight.T.astype(F32) + lax.dot_general(
         dora_b, dora_a, (((0,), (1,)), ((), ())), precision=lax.Precision.HIGHEST
@@ -226,17 +322,12 @@
 
     tokens = enc_states[0, :BLK]
     feat = tokens.shape[1] // n_seq
-    normed = rms_scale(tokens.astype(F32), t5_gain).astype(BF16)
-    gate_proj = jnp.dot(normed, t5_in_weight[0], preferred_element_type=F32)
-    upward = jnp.dot(normed, t5_in_weight[1], preferred_element_type=F32)
-    hidden = (jax.nn.gelu(gate_proj, approximate=True) * upward).astype(BF16)
-    ffn = jnp.dot(hidden, t5_out_weight, preferred_element_type=F32).astype(BF16)
-    ffn = ffn.reshape(BLK, n_seq, feat).transpose(1, 0, 2)
+    ffn = t5_ffn(enc_states, t5_gain, t5_in_weight, t5_out_weight, n_seq)
     rows_y, ffn, near_weights = lax.optimization_barrier((rows_y, ffn, near_weights))
 
     weights = gather_columns(weights, near_weights)
     depth = context_weight.shape[0]
-    context_all, kv_all = weights[:, :depth], weights[:, depth:]
+    context_all = weights[:, :depth]
 
     rows_f = rows_y.astype(F32)
     column_sq = jnp.sum(rows_f * rows_f, (0, 2))
@@ -276,53 +367,77 @@
     scale, shift = to_gathered(text_scale, n_dp), to_gathered(text_shift, n_dp)
     modulated = ((1.0 + scale) * text.astype(F32) + shift).astype(BF16)
     length = jnp.sum(jnp.where(prompt_owner_sample == data_rank, lengths, 0))
-    key_value = jnp.dot(modulated, kv_all, preferred_element_type=F32)
 
     num, den = image_attention(received, image_qk_gain)
-    attended = text_attention(
-        length.reshape(1), received, key_value, image_qk_gain, text_key_gain.reshape(1, HD), num, den
-    )
-
-    lowered = jnp.dot(attended, dora_a.astype(BF16), preferred_element_type=F32).astype(BF16)
-    outgoing = jnp.concatenate([attended, lowered], 1).reshape(n_y, 2 * BLK, own_rows + rank)
-    gathered = swap(outgoing, "seq", Y_GROUPS)
+    down_factor = jnp.pad(dora_a.astype(BF16), ((0, 0), (0, lanes - rank)))
+    attended = prompt_attention(
+        length.reshape(1),
+        received,
+        modulated,
+        weights,
+        depth // HD,
+        down_factor,
+        image_qk_gain,
+        text_key_gain.reshape(1, HD),
+        num,
+        den,
+    )
+
+    gathered = swap(attended, "seq", Y_GROUPS)
     down = jnp.dot(cotangent, up_all, preferred_element_type=F32).astype(BF16)
     down = jnp.concatenate([down, lax.ppermute(down, "seq", flip_z)], 0)
     gathered, down = lax.optimization_barrier((gathered, down))
-    down_all = swap(jnp.broadcast_to(down[None], (n_y,) + down.shape), "seq", Y_GROUPS)
     lowered = jnp.sum(gathered[:, :, own_rows:].astype(F32), 0)
     lowered_other = lax.ppermute(lowered[BLK:].astype(BF16), "seq", flip_z)
     gathered = gathered[:, :, :own_rows].transpose(1, 0, 2).reshape(2 * BLK, -1)
+    kept_rows = gathered[:BLK]
     landed = []
     for at in range(0, model, model // 2):
         part = dot_t(gathered[BLK:], scaled_all[at : at + model // 2, :reach]).astype(BF16)
+        kept_rows, part = lax.optimization_barrier((kept_rows, part))
         landed.append(lax.ppermute(part, "seq", flip_z))
-    kept = lax.optimization_barrier(dot_t(gathered[:BLK], scaled_all[:, :reach]))
-    out = kept + jnp.concatenate(landed, 1).astype(F32)
-    image_out = from_gathered(out.astype(BF16), n_dp)[None]
-    lowered = (lowered[:BLK] + lowered_other.astype(F32)).astype(BF16)
-
-    down_all = down_all.reshape(-1, lanes)[:, :rank]
+
+    lowered = (lowered[:BLK] + lowered_other.astype(F32)).astype(BF16)[:, :rank]
+    up_part = lax.dot_general(
+        lowered, cotangent, (((0,), (0,)), ((), ())), preferred_element_type=F32
+    ).astype(BF16)
+    up_part = up_part.reshape(rank, n_dp // 2, 2, own_cols).transpose(2, 1, 0, 3)
+    up_part = swap(up_part.reshape(n_dp, rank, own_cols), "dp")
+
+    for bit in (2, 4):
+        moved = lax.ppermute(down, "seq", [(i, i ^ bit) for i in range(n_seq)])
+        first = (seq_rank & bit) == 0
+        down = jnp.concatenate([jnp.where(first, down, moved), jnp.where(first, moved, down)], 0)
+    rows_all = attended.reshape(-1, own_rows + lanes)[:, :own_rows]
     grad_a = lax.dot_general(
-        down_all, attended, (((0,), (0,)), ((), ())), preferred_element_type=F32
-    )
-    for bit in (1, 2, 4, 8):
+        down[:, :rank], rows_all, (((0,), (0,)), ((), ())), preferred_element_type=F32
+    )
+    for bit in (1, 2, 4):
         grad_a = grad_a.astype(BF16)
         moved = lax.ppermute(grad_a, "dp", [(i, i ^ bit) for i in range(n_dp)])
         grad_a = grad_a.astype(F32) + moved.astype(F32)
-    grad_a = grad_a.T
-    up_part = lax.dot_general(
-        lowered, cotangent, (((0,), (0,)), ((), ())), preferred_element_type=F32
-    ).astype(BF16)
+    grad_a = grad_a.astype(BF16)
+
+    kept = dot_t(kept_rows, scaled_all[:, :reach])
+    kept, up_part, grad_a = lax.optimization_barrier((kept, up_part, grad_a))
+    out = kept + jnp.concatenate(landed, 1).astype(F32)
+    image_out = from_gathered(out.astype(BF16), n_dp)[None]
     magnitude_part = jnp.sum(out * cotangent.astype(F32), 0).astype(BF16)
-    parts = jnp.concatenate([up_part, jnp.pad(magnitude_part[None], ((0, 7), (0, 0)))], 0)
-    parts = parts.reshape(rank + 8, n_dp // 2, 2, own_cols).transpose(2, 1, 0, 3)
-    parts = parts.reshape(n_dp, rank + 8, own_cols)
-    parts = jnp.sum(swap(parts, "dp").astype(F32), 0).astype(BF16)
-    parts = swap(jnp.broadcast_to(parts[None], (n_seq,) + parts.shape), "seq")
-    parts = jnp.sum(parts.astype(F32), 0)
-    grad_b = parts[:rank] * ratio
-    grad_magnitude = parts[rank] / magnitude
+    magnitude_part = magnitude_part.reshape(n_dp // 2, 2, own_cols).transpose(1, 0, 2)
+    magnitude_part = jnp.broadcast_to(
+        magnitude_part.reshape(n_dp, 1, own_cols), (n_dp, n_seq, own_cols)
+    )
+    magnitude_part = swap(magnitude_part.reshape(n_all, own_cols), both)
+    grad_magnitude = jnp.sum(magnitude_part.astype(F32), 0) / magnitude
+
+    moved = lax.ppermute(grad_a, "dp", [(i, i ^ 8) for i in range(n_dp)])
+    grad_a = (grad_a.astype(F32) + moved.astype(F32)).T
+    grad_b = jnp.sum(up_part.astype(F32), 0)
+    for bit in (2, 4, 1):
+        grad_b = grad_b.astype(BF16)
+        moved = lax.ppermute(grad_b, "seq", [(i, i ^ bit) for i in range(n_seq)])
+        grad_b = grad_b.astype(F32) + moved.astype(F32)
+    grad_b = grad_b * ratio
     return (image_out, grad_a, grad_b, grad_magnitude)
 
 

time: 308 us -> 305 us (level)
  matrix products: 42.5 us -> 25.2 us
  Pallas kernels: 15.4 us -> 28.6 us
  waiting for transfers between devices: 114 us -> 103 us
  other arithmetic: 15.1 us -> 21.2 us
  local copies, waits for them, and re-layouts: 27.7 us -> 31.7 us
  starting transfers between devices: 76.2 us -> 79.3 us
    dot_general x5 -> x1, matrix products: 16.7 us -> 1.42 us  [on_device(): lax.dot_general(down[:, :rank], rows_all, (((0,), (0,)), ((), ())), prefe...]
    pallas_call x1 -> x2, Pallas kernels: 4.31 us -> 18.8 us  [the longest x1 10.4 us: t5_ffn(): pl.pallas_call(t5_kernel, grid=(cuts + n_seq,), in_specs=[pl.BlockSpec((1...]
    unnamed x50 -> x64, local copies, waits for them, and re-layouts: 8.98 us -> 21.8 us
    ppermute x1, waiting for transfers between devices: 9.87 us -> 0.01 us  [on_device(): lowered_other = lax.ppermute(lowered[BLK:].astype(BF16), 'seq', flip_z)]
    ppermute x4 -> x3, waiting for transfers between devices: 8.24 us -> 0.01 us  [on_device(): moved = lax.ppermute(grad_a, 'dp', [(i, i ^ bit) for i in range(n_dp)])]
    ppermute x0 -> x6, starting transfers between devices: none -> 7.8 us  [the longest x3 4.87 us: on_device(): moved = lax.ppermute(grad_b, 'seq', [(i, i ^ bit) for i in range(n_seq)])]
    all_to_all x9 -> x8, waiting for transfers between devices: 52.5 us -> 59.3 us  [swap(): lax.all_to_all(values, axes, 0, 0, tiled=True, axis_index_groups=groups)]
    reshape x4 -> x2, local copies, waits for them, and re-layouts: 5.33 us -> 1.61 us  [on_device(): up_part.reshape(rank, n_dp // 2, 2, own_cols).transpose(2, 1, 0, 3)]
  transfers between devices with their start and end apart: 23 -> 27, of which waited for: 9 -> 9; matrix products, arithmetic and copies ran while one was open for 20% -> 16% of each run, Pallas kernels for 5% -> 9%
where the time goes in v5:
time: 305 us; the launch traced here: 303 us
  waiting for transfers between devices  103 us (34%)
  starting transfers between devices  79.3 us (26%)
  local copies, waits for them, and re-layouts  31.7 us (10%)
  Pallas kernels  28.6 us (9%)
  matrix products  25.2 us (8%)
  other arithmetic  21.2 us (7%)
  between operations  14.7 us (5%)
    all_to_all x8, waiting for transfers between devices, swap(): lax.all_to_all(values, axes, 0, 0, tiled=True, axis_index_groups=groups)  59.3 us
    all_to_all x8, starting transfers between devices, swap(): lax.all_to_all(values, axes, 0, 0, tiled=True, axis_index_groups=groups)  49.1 us
    ppermute x2, waiting for transfers between devices, near_shard(): lax.ppermute(values, 'dp', [(i, (i + n_dp // 2) % n_dp) for i in range(n_...  39.4 us
    unnamed x64, local copies, waits for them, and re-layouts  21.8 us
    dot_general x4, matrix products, dot_t(): lax.dot_general(left, right, (((1,), (1,)), ((), ())), preferred_element_...  20.9 us
    pallas_call x1, Pallas kernels, t5_ffn(): pl.pallas_call(t5_kernel, grid=(cuts + n_seq,), in_specs=[pl.BlockSpec((1...  10.4 us
    pallas_call x1, Pallas kernels, image_attention(): pl.pallas_call(image_kernel, grid=(heads, sources // step), in_specs=[pl....  9.27 us
    pallas_call x1, Pallas kernels, prompt_attention(): pl.pallas_call(prompt_kernel, grid=(heads + 1,), in_specs=[pl.BlockSpec(m...  8.38 us
  transfers between devices with their start and end apart: 27, of which 9 were waited for; matrix products, arithmetic and copies ran while one was open for 16% of the time, Pallas kernels for 9%

profile of v5, /device:TPU:1, one launch (start us, length us, event | category | flops | bytes accessed | tf_op | source)
XLA Modules:
  0.0 303.4 jit_solution(9544594822863116757)
XLA Ops:
  7.2 1.0 copy.120
  9.0 1.9 pad_maximum_fusion.4
  10.9 2.5 collective-permute-start
  13.8 0.9 broadcast_in_dim.10
  14.7 4.2 %all-to-all-start = ((bf16[4,192,384]{2,1,0:T(8,128)(2,1)}), bf16[4,192,384]{2,1,0:T(8,128)(2,1)}, u32[]{:S(2)}, u32[]{:S(2)}) async-start(bf16[4,192,384]{2,1,0:T(8,128)(2,1)} %broadcast_in_dim.10), calls=%async_computation | async-start | bytes 1179648 | tf_op jit(solution)/shard_map/all_to_all | solution.py:24
  19.5 1.0 copy-done.12
  20.5 4.0 %copy-done.1 = bf16[2,4096,640]{2,1,0:T(8,128)(2,1)S(1)} copy-done((bf16[2,4096,640]{2,1,0:T(8,128)(2,1)S(1)}, bf16[2,4096,640]{2,1,0:T(8,128)(2,1)}, u32[]{:S(2)}) %copy-start.1) | copy-done | bytes 10485784
  24.5 2.5 copy-done.3
  27.0 1.6 copy-done.4
  28.6 10.4 %shard_map.211 = bf16[8,128,512]{2,1,0:T(8,128)(2,1)} custom-call(bf16[1,256,4096]{2,1,0:T(8,128)(2,1)S(1)} %copy-done.4, f32[1,4096]{1,0:T(1,128)S(1)} %bitcast.102, bf16[2,4096,640]{2,1,0:T(8,128)(2,1)S(1)} %copy-done.1, bf16[2,4096,640]{2,1,0:T(8,128)(2,1)S(1)} %copy-done.1, bf16[640,4096]{1,0:T(8,128)(2,1)S(1)} %copy-done.3), custom_call_target="tpu_custom_call" | custom-call | flops 2013265920 | bytes 15728640 | tf_op jit(solution)/shard_map/pallas_call | solution.py:250
  39.0 1.2 select_bitcast_fusion.3
  40.2 1.0 pad_maximum_fusion.2
  41.3 1.3 fusion.19
  42.6 3.4 %collective-permute-start.1 = (f32[192]{0:T(256)S(1)}, f32[192]{0:T(256)S(1)}, u32[]{:S(2)}, u32[]{:S(2)}) collective-permute-start(f32[192]{0:T(256)S(1)} %fusion.19), channel_id=1, source_target_pairs={{0,1},{1,0},{2,3},{3,2},{4,5},{5,4},{6,7},{7,6},{8,9},{9,8},{10,11... | collective-permute-start | bytes 2312 | tf_op jit(solution)/shard_map/ppermute | solution.py:334
  46.0 6.8 %all-to-all-start.1 = ((bf16[8,128,512]{2,1,0:T(8,128)(2,1)}), bf16[8,128,512]{2,1,0:T(8,128)(2,1)}, u32[]{:S(2)}, u32[]{:S(2)}) async-start(bf16[8,128,512]{2,1,0:T(8,128)(2,1)} %shard_map.211), calls=%async_computation.1 | async-start | bytes 2097152 | tf_op jit(solution)/shard_map/all_to_all | solution.py:24
  52.9 1.3 fusion.27
  56.0 39.4 %collective-permute-done.2 = bf16[192,1664]{1,0:T(8,128)(2,1)} collective-permute-done((bf16[192,1664]{1,0:T(8,128)(2,1)S(1)}, bf16[192,1664]{1,0:T(8,128)(2,1)}, u32[]{:S(2)}, u32[]{:S(2)}) %collective-permute-start.2) | collective-permute-done | bytes 639008 | tf_op jit(solution)/shard_map/ppermute | solution.py:29
  95.4 1.3 select_bitcast_fusion.1
  96.7 1.2 pad_maximum_fusion.1
  97.9 1.5 pad_maximum_fusion
  99.5 1.7 copy.101
  101.2 3.8 %all-to-all-start.2 = ((bf16[4,2,384,384]{3,2,1,0:T(8,128)(2,1)}), bf16[4,2,384,384]{3,2,1,0:T(8,128)(2,1)S(1)}, u32[]{:S(2)}, u32[]{:S(2)}) async-start(bf16[4,2,384,384]{3,2,1,0:T(8,128)(2,1)} %copy.101), calls=%async_computation.2 | async-start | bytes 4718592 | tf_op jit(solution)/shard_map/all_to_all | solution.py:24
  105.9 2.1 convert_reduce_fusion
  108.0 3.1 %fusion.15 = bf16[16,8,24,128]{3,1,2,0:T(8,128)(2,1)S(1)} fusion(bf16[3072,1280]{1,0:T(8,128)(2,1)} %bitcast.92, f32[128,512]{1,0:T(8,128)} %convert_reduce_fusion, f32[512]{0:T(512)S(1)} %dynamic_slice.7, bf16[1,128,4096]{2,1,0:T(8,128)(2,1)S(1)} %slice-done, s32[]{:T(128)S(6)} %select_n.73), kind=kOutput, calls=%fused_computation.21 | convolution fusion | flops 403308544 | bytes 4327428 | tf_op jit(solution)/shard_map/dot_general | solution.py:55
  111.1 1.0 copy.121
  112.1 19.3 %all-to-all-done.2 = bf16[4,2,384,384]{3,2,1,0:T(8,128)(2,1)S(1)} async-done(((bf16[4,2,384,384]{3,2,1,0:T(8,128)(2,1)}), bf16[4,2,384,384]{3,2,1,0:T(8,128)(2,1)S(1)}, u32[]{:S(2)}, u32[]{:S(2)}) %all-to-all-start.2) | async-done | bytes 2359328 | tf_op jit(solution)/shard_map/all_to_all | solution.py:24
  131.4 11.3 %all-to-all-start.3 = ((bf16[128,24,128]{2,1,0:T(8,128)(2,1)}), bf16[128,24,128]{2,1,0:T(8,128)(2,1)S(1)}, u32[]{:S(2)}, u32[]{:S(2)}) async-start(bf16[128,24,128]{2,1,0:T(8,128)(2,1)} %bitcast.51), calls=%async_computation.3 | async-start | bytes 1572864 | tf_op jit(solution)/shard_map/all_to_all | solution.py:24
  142.7 23.6 %all-to-all-done.3 = bf16[128,24,128]{2,1,0:T(8,128)(2,1)S(1)} async-done(((bf16[128,24,128]{2,1,0:T(8,128)(2,1)}), bf16[128,24,128]{2,1,0:T(8,128)(2,1)S(1)}, u32[]{:S(2)}, u32[]{:S(2)}) %all-to-all-start.3) | async-done | bytes 786464 | tf_op jit(solution)/shard_map/all_to_all | solution.py:24
  167.6 1.4 copy.104
  169.0 5.5 %all-to-all-start.4 = ((bf16[128,24,128]{2,1,0:T(8,128)(2,1)}), bf16[128,24,128]{2,1,0:T(8,128)(2,1)S(1)}, u32[]{:S(2)}, u32[]{:S(2)}) async-start(bf16[128,24,128]{2,1,0:T(8,128)(2,1)} %copy.104), calls=%async_computation.4 | async-start | bytes 1572864 | tf_op jit(solution)/shard_map/all_to_all | solution.py:24
  176.9 9.3 %shard_map.212 = (f32[1024,384]{1,0:T(8,128)S(1)}, f32[1024,384]{1,0:T(8,128)S(1)}) custom-call(bf16[8,384,384]{2,1,0:T(8,128)(2,1)S(1)} %bitcast.95, bf16[8,384,384]{2,1,0:T(8,128)(2,1)S(1)} %bitcast.96, bf16[8,384,384]{2,1,0:T(8,128)(2,1)S(1)} %bitcast.97, f32[2,128]{1,0:T(2,128)S(1)} %copy-done.10), custom_call_target="tpu_custom_call" | custom-call | flops 2415919104 | bytes 5505024 | tf_op jit(solution)/shard_map/pallas_call | solution.py:109
  186.2 1.2 copy-done.5
  187.4 1.2 copy-done.7
  188.6 1.1 all-to-all-done.4
  190.1 0.9 copy-done.8
  191.6 3.2 %copy-done = bf16[16,192,1280]{2,1,0:T(8,128)(2,1)S(1)} copy-done((bf16[16,192,1280]{2,1,0:T(8,128)(2,1)S(1)}, bf16[16,192,1280]{2,1,0:T(8,128)(2,1)}, u32[]{:S(2)}) %copy-start) | copy-done | bytes 7864344
  194.8 8.4 %shard_map.213 = bf16[4,256,512]{2,1,0:T(8,128)(2,1)} custom-call(s32[1]{0:T(128)} %bitcast.length_ref, bf16[8,384,384]{2,1,0:T(8,128)(2,1)S(1)} %bitcast.98, bf16[128,3072]{1,0:T(8,128)(2,1)S(1)} %fusion.14.text_ref, bf16[3072,1280]{1,0:T(8,128)(2,1)S(1)} %bitcast.93, bf16[3072,1280]{1,0:T(8,128)(2,1)S(1)} %bitcast.94, bf16[384,128]{1,0:T(8,128)(2,1)S(1)} %pad.9.down_ref, ...), custom_call_target="tpu_custom_call" | custom-call | flops 905969664 | bytes 9437184 | tf_op jit(solution)/shard_map/pallas_call | solution.py:190
  203.2 3.6 %all-to-all-start.5 = ((bf16[4,256,512]{2,1,0:T(8,128)(2,1)}), bf16[4,256,512]{2,1,0:T(8,128)(2,1)S(1)}, u32[]{:S(2)}, u32[]{:S(2)}) async-start(bf16[4,256,512]{2,1,0:T(8,128)(2,1)} %shard_map.213), calls=%async_computation.5 | async-start | bytes 2097152 | tf_op jit(solution)/shard_map/all_to_all | solution.py:24
  207.4 1.5 fusion.22
  208.9 2.8 collective-permute-start.4
  212.0 1.2 collective-permute-done.4
  213.3 7.2 %all-to-all-done.5 = bf16[4,256,512]{2,1,0:T(8,128)(2,1)S(1)} async-done(((bf16[4,256,512]{2,1,0:T(8,128)(2,1)}), bf16[4,256,512]{2,1,0:T(8,128)(2,1)S(1)}, u32[]{:S(2)}, u32[]{:S(2)}) %all-to-all-start.5) | async-done | bytes 1048608 | tf_op jit(solution)/shard_map/all_to_all | solution.py:24
  220.6 0.9 copy.110
  221.9 4.9 %fusion.7 = bf16[128,1536]{1,0:T(8,128)(2,1)} fusion(bf16[128,1536]{0,1:T(8,128)(2,1)} %bitcast.118, bf16[3072,1664]{1,0:T(8,128)(2,1)} %bitcast.126), kind=kOutput, calls=%fused_computation.9 | convolution fusion | flops 604176384 | bytes 5505024 | tf_op jit(solution)/shard_map/dot_general | solution.py:55
  226.8 1.9 collective-permute-start.7
  228.7 4.8 %fusion.10 = bf16[128,1536]{1,0:T(8,128)(2,1)} fusion(bf16[128,1536]{0,1:T(8,128)(2,1)S(1)} %bitcast.119, bf16[3072,1664]{1,0:T(8,128)(2,1)} %bitcast.127), kind=kOutput, calls=%fused_computation.10 | convolution fusion | flops 604176384 | bytes 5505024 | tf_op jit(solution)/shard_map/dot_general | solution.py:55
  233.6 1.4 convolution_convert_fusion.3
  235.0 3.1 %collective-permute-start.8 = (bf16[64,384]{1,0:T(8,128)(2,1)S(1)}, bf16[64,384]{1,0:T(8,128)(2,1)}, u32[]{:S(2)}, u32[]{:S(2)}) collective-permute-start(bf16[64,384]{1,0:T(8,128)(2,1)S(1)} %convolution_convert_fusion.3), channel_id=1, source_target_pairs={{0,8},{8,0},{16,24},{24,16},{32,40},{40,32},{48,56},{56,48},{64,72... | collective-permute-start | bytes 147464 | tf_op jit(solution)/shard_map/ppermute | solution.py:417
  238.4 2.9 collective-permute-start.5
  241.4 2.8 collective-permute-start.11
  245.0 1.3 collective-permute-start.9
  247.4 1.0 copy.111
  248.4 5.4 %all-to-all-start.6 = ((bf16[16,64,192]{2,1,0:T(8,128)(2,1)}), bf16[16,64,192]{2,1,0:T(8,128)(2,1)S(1)}, u32[]{:S(2)}, u32[]{:S(2)}) async-start(bf16[16,64,192]{2,1,0:T(8,128)(2,1)} %bitcast.32), calls=%async_computation.6 | async-start | bytes 1048576 | tf_op jit(solution)/shard_map/all_to_all | solution.py:24
  253.8 3.2 %collective-permute-start.10 = (bf16[64,384]{1,0:T(8,128)(2,1)S(1)}, bf16[64,384]{1,0:T(8,128)(2,1)S(1)}, u32[]{:S(2)}, u32[]{:S(2)}) collective-permute-start(bf16[64,384]{1,0:T(8,128)(2,1)S(1)} %add_convert_fusion.1), channel_id=1, source_target_pairs={{0,32},{8,40},{16,48},{24,56},{32,0},{40,8},{48,16},{56,24},{64,96... | collective-permute-start | bytes 147464 | tf_op jit(solution)/shard_map/ppermute | solution.py:417
  257.0 8.1 %fusion = f32[128,3072]{1,0:T(8,128)} fusion(bf16[128,1536]{0,1:T(8,128)(2,1)S(1)} %bitcast.117, bf16[3072,1664]{1,0:T(8,128)(2,1)} %bitcast.128), kind=kOutput, calls=%fused_computation | convolution fusion | flops 1207959552 | bytes 11403264 | tf_op jit(solution)/shard_map/dot_general | solution.py:55
  265.1 1.4 all-to-all-done.6
  266.5 1.8 multiply_reduce_fusion
  268.7 1.2 copy.117
  270.7 0.9 collective-permute-start.14
  272.5 8.5 %all-to-all-start.7 = ((bf16[128,1,192]{2,1,0:T(2,128)(2,1)}), bf16[128,1,192]{2,1,0:T(2,128)(2,1)S(1)}, u32[]{:S(2)}, u32[]{:S(2)}) async-start(bf16[128,1,192]{2,1,0:T(2,128)(2,1)} %copy.116), calls=%async_computation.7 | async-start | bytes 262144 | tf_op jit(solution)/shard_map/all_to_all | solution.py:24
  281.0 3.0 collective-permute-start.15
  284.0 6.8 %all-to-all-done.7 = bf16[128,1,192]{2,1,0:T(2,128)(2,1)S(1)} async-done(((bf16[128,1,192]{2,1,0:T(2,128)(2,1)}), bf16[128,1,192]{2,1,0:T(2,128)(2,1)S(1)}, u32[]{:S(2)}, u32[]{:S(2)}) %all-to-all-start.7) | async-done | bytes 49184 | tf_op jit(solution)/shard_map/all_to_all | solution.py:24
  291.6 1.0 collective-permute-start.16
  293.3 2.7 collective-permute-done.16
  (141 shorter events, 17.1 us)
Async XLA Ops:
  7.2 6.2 %copy-start.21 = (f32[64,192]{1,0:T(8,128)S(1)}, f32[64,192]{1,0:T(8,128)}, u32[]{:S(2)}) copy-start(f32[64,192]{1,0:T(8,128)} %param.35) | copy-start | bytes 147460
  7.2 6.2 %copy-start.19 = (f32[384,64]{0,1:T(8,128)S(1)}, f32[384,64]{0,1:T(8,128)}, u32[]{:S(2)}) copy-start(f32[384,64]{0,1:T(8,128)} %param.34) | copy-start | bytes 294916
  7.2 6.2 %copy-start.23 = (bf16[384,192]{0,1:T(8,128)(2,1)S(1)}, bf16[384,192]{0,1:T(8,128)(2,1)}, u32[]{:S(2)}) copy-start(bf16[384,192]{0,1:T(8,128)(2,1)} %param.33) | copy-start | bytes 442372
  8.2 0.7 copy-start.14
  9.0 9.9 %copy-start.2 = (bf16[1,128,3,3072]{3,1,2,0:T(8,128)(2,1)S(1)}, bf16[1,128,3,3072]{3,1,2,0:T(8,128)(2,1)}, u32[]{:S(2)}) copy-start(bf16[1,128,3,3072]{3,1,2,0:T(8,128)(2,1)} %param.31) | copy-start | bytes 7077892
  10.9 28.1 %collective-permute-start = (bf16[192,1280]{1,0:T(8,128)(2,1)}, bf16[192,1280]{1,0:T(8,128)(2,1)}, u32[]{:S(2)}, u32[]{:S(2)}) collective-permute-start(bf16[192,1280]{1,0:T(8,128)(2,1)} %pad_maximum_fusion.4), channel_id=1, source_target_pairs={{0,64},{8,72},{16,80},{24,88},{32,96},{40,104},{48,112},{56,120},{... | collective-permute-start | bytes 1474568 | tf_op jit(solution)/shard_map/ppermute | solution.py:29
  14.7 24.3 %all-to-all-start = ((bf16[4,192,384]{2,1,0:T(8,128)(2,1)}), bf16[4,192,384]{2,1,0:T(8,128)(2,1)}, u32[]{:S(2)}, u32[]{:S(2)}) async-start(bf16[4,192,384]{2,1,0:T(8,128)(2,1)} %broadcast_in_dim.10), calls=%async_computation | async-start | bytes 1179648 | tf_op jit(solution)/shard_map/all_to_all | solution.py:24
  18.9 89.1 %all-gather.5.cloned.1.call-start = ((), (), s32[]{:S(2)}) async-start(), calls=%async_computation.8 | async-start | bytes 8847360 | tf_op jit(solution)/shard_map/all_gather | solution.py:38
  18.9 1.6 copy-start.9
  19.5 1.0 copy-start.12
  20.5 4.0 %copy-start.1 = (bf16[2,4096,640]{2,1,0:T(8,128)(2,1)S(1)}, bf16[2,4096,640]{2,1,0:T(8,128)(2,1)}, u32[]{:S(2)}) copy-start(bf16[2,4096,640]{2,1,0:T(8,128)(2,1)} %up_w.1) | copy-start | bytes 31457284
  24.5 2.5 copy-start.3
  27.0 1.6 copy-start.4
  28.6 10.4 %copy-start.15 = (bf16[24,8,2,384]{3,1,2,0:T(8,128)(2,1)S(1)}, bf16[24,8,2,384]{3,1,2,0:T(8,128)(2,1)}, u32[]{:S(2)}) copy-start(bf16[24,8,2,384]{3,1,2,0:T(8,128)(2,1)} %copy-done.14) | copy-start | bytes 884740
  28.6 10.4 %copy-start.17 = (bf16[512,192]{0,1:T(8,128)(2,1)S(1)}, bf16[512,192]{0,1:T(8,128)(2,1)}, u32[]{:S(2)}) copy-start(bf16[512,192]{0,1:T(8,128)(2,1)} %param.26) | copy-start | bytes 589828
  40.2 5.7 %copy-start.13 = (bf16[4,384,384]{2,1,0:T(8,128)(2,1)S(1)}, bf16[4,384,384]{2,1,0:T(8,128)(2,1)}, u32[]{:S(2)}) copy-start(bf16[4,384,384]{2,1,0:T(8,128)(2,1)} %copy-done.12) | copy-start | bytes 3538948
  41.3 11.6 %copy-start.26 = (f32[192]{0:T(256)S(1)}, f32[192]{0:T(256)}, u32[]{:S(2)}) copy-start(f32[192]{0:T(256)} %param.36) | copy-start | bytes 2308
  42.6 11.6 %copy-start.22 = (f32[64,192]{1,0:T(8,128)S(1)}, f32[64,192]{1,0:T(8,128)}, u32[]{:S(2)}) copy-start(f32[64,192]{1,0:T(8,128)} %param.35) | copy-start | bytes 147460
  42.6 10.3 %collective-permute-start.1 = (f32[192]{0:T(256)S(1)}, f32[192]{0:T(256)S(1)}, u32[]{:S(2)}, u32[]{:S(2)}) collective-permute-start(f32[192]{0:T(256)S(1)} %fusion.19), channel_id=1, source_target_pairs={{0,1},{1,0},{2,3},{3,2},{4,5},{5,4},{6,7},{7,6},{8,9},{9,8},{10,11... | collective-permute-start | bytes 2312 | tf_op jit(solution)/shard_map/ppermute | solution.py:334
  45.9 49.5 %collective-permute-start.3 = (bf16[4,384,384]{2,1,0:T(8,128)(2,1)S(1)}, bf16[4,384,384]{2,1,0:T(8,128)(2,1)}, u32[]{:S(2)}, u32[]{:S(2)}) collective-permute-start(bf16[4,384,384]{2,1,0:T(8,128)(2,1)S(1)} %copy-done.13), channel_id=1, source_target_pairs={{0,1},{1,0},{2,3},{3,2},{4,5},{5,4},{6,7},{7,6},{8,9},{9,8},{10,11... | collective-permute-start | bytes 3538952 | tf_op jit(solution)/shard_map/ppermute | solution.py:316
  46.0 49.4 %all-to-all-start.1 = ((bf16[8,128,512]{2,1,0:T(8,128)(2,1)}), bf16[8,128,512]{2,1,0:T(8,128)(2,1)}, u32[]{:S(2)}, u32[]{:S(2)}) async-start(bf16[8,128,512]{2,1,0:T(8,128)(2,1)} %shard_map.211), calls=%async_computation.1 | async-start | bytes 2097152 | tf_op jit(solution)/shard_map/all_to_all | solution.py:24
  52.8 154.5 %all-gather.7.cloned.1.call-start = ((), (), s32[]{:S(2)}) async-start(), calls=%async_computation.9 | async-start | bytes 11501568 | tf_op jit(solution)/shard_map/all_gather | solution.py:38
  55.9 39.5 %collective-permute-start.2 = (bf16[192,1664]{1,0:T(8,128)(2,1)S(1)}, bf16[192,1664]{1,0:T(8,128)(2,1)}, u32[]{:S(2)}, u32[]{:S(2)}) collective-permute-start(bf16[192,1664]{1,0:T(8,128)(2,1)S(1)} %fusion.26), channel_id=1, source_target_pairs={{0,64},{8,72},{16,80},{24,88},{32,96},{40,104},{48,112},{56,120},{... | collective-permute-start | bytes 1916936 | tf_op jit(solution)/shard_map/ppermute | solution.py:29
  101.2 30.2 %all-to-all-start.2 = ((bf16[4,2,384,384]{3,2,1,0:T(8,128)(2,1)}), bf16[4,2,384,384]{3,2,1,0:T(8,128)(2,1)S(1)}, u32[]{:S(2)}, u32[]{:S(2)}) async-start(bf16[4,2,384,384]{3,2,1,0:T(8,128)(2,1)} %copy.101), calls=%async_computation.2 | async-start | bytes 4718592 | tf_op jit(solution)/shard_map/all_to_all | solution.py:24
  105.0 2.9 slice-start
  112.1 54.9 %copy-start.27 = (s32[16]{0:T(128)S(1)}, s32[16]{0:T(128)}, u32[]{:S(2)}) copy-start(s32[16]{0:T(128)} %param.21) | copy-start | bytes 196
  131.4 34.9 %all-to-all-start.3 = ((bf16[128,24,128]{2,1,0:T(8,128)(2,1)}), bf16[128,24,128]{2,1,0:T(8,128)(2,1)S(1)}, u32[]{:S(2)}, u32[]{:S(2)}) async-start(bf16[128,24,128]{2,1,0:T(8,128)(2,1)} %bitcast.51), calls=%async_computation.3 | async-start | bytes 1572864 | tf_op jit(solution)/shard_map/all_to_all | solution.py:24
  167.5 7.0 %copy-start.20 = (f32[384,64]{0,1:T(8,128)S(1)}, f32[384,64]{0,1:T(8,128)}, u32[]{:S(2)}) copy-start(f32[384,64]{0,1:T(8,128)} %param.34) | copy-start | bytes 294916
  167.6 7.5 %copy-start.24 = (f32[1,3072]{1,0:T(1,128)S(1)}, f32[1,3072]{1,0:T(1,128)}, u32[]{:S(2)}) copy-start(f32[1,3072]{1,0:T(1,128)} %param.27) | copy-start | bytes 36868
  167.6 8.3 %copy-start.25 = (f32[1,3072]{1,0:T(1,128)S(1)}, f32[1,3072]{1,0:T(1,128)}, u32[]{:S(2)}) copy-start(f32[1,3072]{1,0:T(1,128)} %param.28) | copy-start | bytes 36868
  167.6 8.7 %copy-start.28 = (s32[16]{0:T(128)S(1)}, s32[16]{0:T(128)}, u32[]{:S(2)}) copy-start(s32[16]{0:T(128)} %param.20) | copy-start | bytes 196
  167.6 9.3 %copy-start.10 = (f32[2,128]{1,0:T(2,128)S(1)}, f32[2,128]{1,0:T(2,128)}, u32[]{:S(2)}) copy-start(f32[2,128]{1,0:T(2,128)} %gain_ref.3) | copy-start | bytes 3076
  169.0 20.7 %all-to-all-start.4 = ((bf16[128,24,128]{2,1,0:T(8,128)(2,1)}), bf16[128,24,128]{2,1,0:T(8,128)(2,1)S(1)}, u32[]{:S(2)}, u32[]{:S(2)}) async-start(bf16[128,24,128]{2,1,0:T(8,128)(2,1)} %copy.104), calls=%async_computation.4 | async-start | bytes 1572864 | tf_op jit(solution)/shard_map/all_to_all | solution.py:24
  186.2 1.2 copy-start.5
  187.4 1.2 copy-start.7
  189.7 1.4 copy-start.8
  189.8 1.8 copy-start.6
  189.9 1.7 copy-start.11
  191.6 3.2 %copy-start = (bf16[16,192,1280]{2,1,0:T(8,128)(2,1)S(1)}, bf16[16,192,1280]{2,1,0:T(8,128)(2,1)}, u32[]{:S(2)}) copy-start(bf16[16,192,1280]{2,1,0:T(8,128)(2,1)} %all-gather.5.cloned.1.call-done) | copy-start | bytes 23592964
  203.2 3.7 %copy-start.16 = (bf16[1,128,3072]{2,1,0:T(8,128)(2,1)S(1)}, bf16[1,128,3072]{2,1,0:T(8,128)(2,1)}, u32[]{:S(2)}) copy-start(bf16[1,128,3072]{2,1,0:T(8,128)(2,1)} %param.37) | copy-start | bytes 2359300
  203.2 17.2 %all-to-all-start.5 = ((bf16[4,256,512]{2,1,0:T(8,128)(2,1)}), bf16[4,256,512]{2,1,0:T(8,128)(2,1)S(1)}, u32[]{:S(2)}, u32[]{:S(2)}) async-start(bf16[4,256,512]{2,1,0:T(8,128)(2,1)} %shard_map.213), calls=%async_computation.5 | async-start | bytes 2097152 | tf_op jit(solution)/shard_map/all_to_all | solution.py:24
  208.9 4.3 %collective-permute-start.4 = (bf16[128,128]{1,0:T(8,128)(2,1)S(1)}, bf16[128,128]{1,0:T(8,128)(2,1)S(1)}, u32[]{:S(2)}, u32[]{:S(2)}) collective-permute-start(bf16[128,128]{1,0:T(8,128)(2,1)S(1)} %fusion.22), channel_id=1, source_target_pairs={{0,1},{1,0},{2,3},{3,2},{4,5},{5,4},{6,7},{7,6},{8,9},{9,8},{10,11... | collective-permute-start | bytes 98312 | tf_op jit(solution)/shard_map/ppermute | solution.py:388
  221.6 5.2 %collective-permute-start.6 = (bf16[256,128]{1,0:T(8,128)(2,1)S(1)}, bf16[256,128]{1,0:T(8,128)(2,1)S(1)}, u32[]{:S(2)}, u32[]{:S(2)}) collective-permute-start(bf16[256,128]{1,0:T(8,128)(2,1)S(1)} %pad_maximum_fusion.8), channel_id=1, source_target_pairs={{0,2},{1,3},{2,0},{3,1},{4,6},{5,7},{6,4},{7,5},{8,10},{9,11},{10,... | collective-permute-start | bytes 196616 | tf_op jit(solution)/shard_map/ppermute | solution.py:408
  221.9 6.8 %copy-start.18 = (bf16[128,4,384]{0,2,1:T(8,128)(2,1)S(1)}, bf16[128,4,384]{0,2,1:T(8,128)(2,1)}, u32[]{:S(2)}) copy-start(bf16[128,4,384]{0,2,1:T(8,128)(2,1)} %copy.110) | copy-start | bytes 1179652
  226.8 6.6 %collective-permute-start.7 = (bf16[512,128]{1,0:T(8,128)(2,1)S(1)}, bf16[512,128]{1,0:T(8,128)(2,1)S(1)}, u32[]{:S(2)}, u32[]{:S(2)}) collective-permute-start(bf16[512,128]{1,0:T(8,128)(2,1)S(1)} %pad_maximum_fusion.7), channel_id=1, source_target_pairs={{0,4},{1,5},{2,6},{3,7},{4,0},{5,1},{6,2},{7,3},{8,12},{9,13},{10,... | collective-permute-start | bytes 393224 | tf_op jit(solution)/shard_map/ppermute | solution.py:408
  235.0 9.2 %collective-permute-start.8 = (bf16[64,384]{1,0:T(8,128)(2,1)S(1)}, bf16[64,384]{1,0:T(8,128)(2,1)}, u32[]{:S(2)}, u32[]{:S(2)}) collective-permute-start(bf16[64,384]{1,0:T(8,128)(2,1)S(1)} %convolution_convert_fusion.3), channel_id=1, source_target_pairs={{0,8},{8,0},{16,24},{24,16},{32,40},{40,32},{48,56},{56,48},{64,72... | collective-permute-start | bytes 147464 | tf_op jit(solution)/shard_map/ppermute | solution.py:417
  238.4 8.0 %collective-permute-start.5 = (bf16[128,128]{1,0:T(8,128)(2,1)S(1)}, bf16[128,128]{1,0:T(8,128)(2,1)S(1)}, u32[]{:S(2)}, u32[]{:S(2)}) collective-permute-start(bf16[128,128]{1,0:T(8,128)(2,1)S(1)} %slice.111), channel_id=1, source_target_pairs={{0,1},{1,0},{2,3},{3,2},{4,5},{5,4},{6,7},{7,6},{8,9},{9,8},{10,11... | collective-permute-start | bytes 98312 | tf_op jit(solution)/shard_map/ppermute | solution.py:391
  241.2 25.2 %collective-permute-start.12 = (bf16[128,1536]{1,0:T(8,128)(2,1)}, bf16[128,1536]{1,0:T(8,128)(2,1)S(1)}, u32[]{:S(2)}, u32[]{:S(2)}) collective-permute-start(bf16[128,1536]{1,0:T(8,128)(2,1)} %fusion.10), channel_id=1, source_target_pairs={{0,1},{1,0},{2,3},{3,2},{4,5},{5,4},{6,7},{7,6},{8,9},{9,8},{10,11... | collective-permute-start | bytes 1179656 | tf_op jit(solution)/shard_map/ppermute | solution.py:398
  241.4 25.1 %collective-permute-start.11 = (bf16[128,1536]{1,0:T(8,128)(2,1)}, bf16[128,1536]{1,0:T(8,128)(2,1)}, u32[]{:S(2)}, u32[]{:S(2)}) collective-permute-start(bf16[128,1536]{1,0:T(8,128)(2,1)} %fusion.7), channel_id=1, source_target_pairs={{0,1},{1,0},{2,3},{3,2},{4,5},{5,4},{6,7},{7,6},{8,9},{9,8},{10,11... | collective-permute-start | bytes 1179656 | tf_op jit(solution)/shard_map/ppermute | solution.py:398
  245.0 8.7 %collective-permute-start.9 = (bf16[64,384]{1,0:T(8,128)(2,1)S(1)}, bf16[64,384]{1,0:T(8,128)(2,1)S(1)}, u32[]{:S(2)}, u32[]{:S(2)}) collective-permute-start(bf16[64,384]{1,0:T(8,128)(2,1)S(1)} %add_convert_fusion.2), channel_id=1, source_target_pairs={{0,16},{8,24},{16,0},{24,8},{32,48},{40,56},{48,32},{56,40},{64,80... | collective-permute-start | bytes 147464 | tf_op jit(solution)/shard_map/ppermute | solution.py:417
  248.4 18.1 %all-to-all-start.6 = ((bf16[16,64,192]{2,1,0:T(8,128)(2,1)}), bf16[16,64,192]{2,1,0:T(8,128)(2,1)S(1)}, u32[]{:S(2)}, u32[]{:S(2)}) async-start(bf16[16,64,192]{2,1,0:T(8,128)(2,1)} %bitcast.32), calls=%async_computation.6 | async-start | bytes 1048576 | tf_op jit(solution)/shard_map/all_to_all | solution.py:24
  253.8 11.3 %collective-permute-start.10 = (bf16[64,384]{1,0:T(8,128)(2,1)S(1)}, bf16[64,384]{1,0:T(8,128)(2,1)S(1)}, u32[]{:S(2)}, u32[]{:S(2)}) collective-permute-start(bf16[64,384]{1,0:T(8,128)(2,1)S(1)} %add_convert_fusion.1), channel_id=1, source_target_pairs={{0,32},{8,40},{16,48},{24,56},{32,0},{40,8},{48,16},{56,24},{64,96... | collective-permute-start | bytes 147464 | tf_op jit(solution)/shard_map/ppermute | solution.py:417
  269.9 22.8 %collective-permute-start.13 = (bf16[64,384]{1,0:T(8,128)(2,1)S(1)}, bf16[64,384]{1,0:T(8,128)(2,1)S(1)}, u32[]{:S(2)}, u32[]{:S(2)}) collective-permute-start(bf16[64,384]{1,0:T(8,128)(2,1)S(1)} %add_convert_fusion), channel_id=1, source_target_pairs={{0,64},{8,72},{16,80},{24,88},{32,96},{40,104},{48,112},{56,120},{... | collective-permute-start | bytes 147464 | tf_op jit(solution)/shard_map/ppermute | solution.py:433
  270.7 10.2 %collective-permute-start.14 = (bf16[64,192]{1,0:T(8,128)(2,1)S(1)}, bf16[64,192]{1,0:T(8,128)(2,1)S(1)}, u32[]{:S(2)}, u32[]{:S(2)}) collective-permute-start(bf16[64,192]{1,0:T(8,128)(2,1)S(1)} %reduce_sum.103), channel_id=1, source_target_pairs={{0,2},{1,3},{2,0},{3,1},{4,6},{5,7},{6,4},{7,5},{8,10},{9,11},{10,... | collective-permute-start | bytes 73736 | tf_op jit(solution)/shard_map/ppermute | solution.py:438
  272.5 18.3 %all-to-all-start.7 = ((bf16[128,1,192]{2,1,0:T(2,128)(2,1)}), bf16[128,1,192]{2,1,0:T(2,128)(2,1)S(1)}, u32[]{:S(2)}, u32[]{:S(2)}) async-start(bf16[128,1,192]{2,1,0:T(2,128)(2,1)} %copy.116), calls=%async_computation.7 | async-start | bytes 262144 | tf_op jit(solution)/shard_map/all_to_all | solution.py:24
  281.0 10.6 %collective-permute-start.15 = (bf16[64,192]{1,0:T(8,128)(2,1)S(1)}, bf16[64,192]{1,0:T(8,128)(2,1)S(1)}, u32[]{:S(2)}, u32[]{:S(2)}) collective-permute-start(bf16[64,192]{1,0:T(8,128)(2,1)S(1)} %add_convert_fusion.4), channel_id=1, source_target_pairs={{0,4},{1,5},{2,6},{3,7},{4,0},{5,1},{6,2},{7,3},{8,12},{9,13},{10,... | collective-permute-start | bytes 73736 | tf_op jit(solution)/shard_map/ppermute | solution.py:438
  291.6 4.3 %collective-permute-start.16 = (bf16[64,192]{1,0:T(8,128)(2,1)S(1)}, bf16[64,192]{1,0:T(8,128)(2,1)S(1)}, u32[]{:S(2)}, u32[]{:S(2)}) collective-permute-start(bf16[64,192]{1,0:T(8,128)(2,1)S(1)} %add_convert_fusion.3), channel_id=1, source_target_pairs={{0,1},{1,0},{2,3},{3,2},{4,5},{5,4},{6,7},{7,6},{8,9},{9,8},{10,11... | collective-permute-start | bytes 73736 | tf_op jit(solution)/shard_map/ppermute | solution.py:438
Sparse Core Ops, SparseCore 0:
  41.4 50.6 all-gather.4
  98.0 69.9 all-gather.6

commit v6 on v5

--- a/solution.py
+++ b/solution.py
@@ -10,6 +10,7 @@
 HD = 128
 BLK = 128
 EPSILON = 1e-06
+VMEM_LIMIT = 56 * 1024 * 1024
 F32 = jnp.float32
 BF16 = jnp.bfloat16
 Y_GROUPS = [[0, 2, 4, 6], [1, 3, 5, 7]]
@@ -55,9 +56,12 @@
     return lax.dot_general(left, right, (((1,), (1,)), ((), ())), preferred_element_type=F32)
 
 
-def pack_kernel(_, own_in, other_in, own_ref, other_ref):
+def pack_kernel(_, own_in, other_in, own_ref, first_ref, second_ref):
     own_ref[0] = own_in[...].reshape(own_ref.shape[1:])
-    other_ref[0] = other_in[...].reshape(other_ref.shape[1:])
+    other = other_in[...].reshape(own_ref.shape[1:])
+    half = first_ref.shape[1]
+    first_ref[0] = other[:half]
+    second_ref[0] = other[half:]
 
 
 def pack_heads(rows, pair, n_seq):
@@ -65,8 +69,14 @@
     width = model // n_seq
     n_y = n_seq // 2
     block = (kinds, count, width)
-    shape = jax.ShapeDtypeStruct((n_y, kinds * count, width), rows.dtype)
-    out_spec = pl.BlockSpec((1, kinds * count, width), lambda y, z: (y, 0, 0))
+    total = kinds * count
+
+    def spec(size):
+        return pl.BlockSpec((1, size, width), lambda y, z: (y, 0, 0))
+
+    def shape(size):
+        return jax.ShapeDtypeStruct((n_y, size, width), rows.dtype)
+
     return pl.pallas_call(
         pack_kernel,
         grid_spec=pltpu.PrefetchScalarGridSpec(
@@ -76,23 +86,28 @@
                 pl.BlockSpec(block, lambda y, z: (0, 0, 2 * y + z[0])),
                 pl.BlockSpec(block, lambda y, z: (0, 0, 2 * y + 1 - z[0])),
             ],
-            out_specs=[out_spec, out_spec],
+            out_specs=[spec(total), spec(total // 2), spec(total // 2)],
         ),
-        out_shape=[shape, shape],
-        compiler_params=pltpu.CompilerParams(vmem_limit_bytes=16 * 1024 * 1024),
+        out_shape=[shape(total), shape(total // 2), shape(total // 2)],
+        compiler_params=pltpu.CompilerParams(vmem_limit_bytes=VMEM_LIMIT),
         cost_estimate=pl.CostEstimate(flops=0, bytes_accessed=4 * rows.size, transcendentals=0),
     )(pair.reshape(1), rows, rows)
 
 
-def image_kernel(q_ref, k_ref, v_ref, gain_ref, num_ref, den_ref, keys, values):
+def image_kernel(
+    q_own, q_other, k_own, k_other, v_own, v_other, gain_ref, num_ref, den_ref, keys, values
+):
+    half = keys.shape[0] // 2
+
     @pl.when(pl.program_id(1) == 0)
     def _():
-        k = k_ref[...].reshape(-1, HD).astype(F32)
-        keys[...] = rms_scale(k, gain_ref[1:2, :]).astype(BF16)
-        values[:, :HD] = v_ref[...].reshape(-1, HD)
-        values[:, HD:] = jnp.ones((values.shape[0], HD), BF16)
-
-    q = q_ref[...].reshape(-1, HD).astype(F32)
+        for at, k_ref, v_ref in ((0, k_own, v_own), (half, k_other, v_other)):
+            k = k_ref[...].reshape(-1, HD).astype(F32)
+            keys[at : at + half, :] = rms_scale(k, gain_ref[1:2, :]).astype(BF16)
+            values[at : at + half, :HD] = v_ref[...].reshape(-1, HD)
+        values[:, HD:] = jnp.ones((2 * half, HD), BF16)
+
+    q = jnp.concatenate([q_own[0], q_other[0]], 0).astype(F32)
     q = rms_scale(q, gain_ref[0:1, :] * QUERY_SCALE).astype(BF16)
     weight = jnp.exp2(dot_t(q, keys[...])).astype(BF16)
     both = jnp.dot(weight, values[...], preferred_element_type=F32)
@@ -100,19 +115,28 @@
     den_ref[...] = both[:, HD:]
 
 
-def image_attention(received, gains):
-    sources, _, width = received.shape
+def image_attention(own, other, gains):
+    n_y, _, width = own.shape
     heads = width // HD
-    image_len = sources * BLK
-    step = 2
-    rows = step * BLK
+    rows = 2 * BLK
+    image_len = n_y * rows
+
+    def queries():
+        return pl.BlockSpec((1, BLK, HD), lambda h, b: (b, 0, h))
+
+    def whole(kind):
+        return pl.BlockSpec((n_y, BLK, HD), lambda h, b: (0, kind, h))
+
     return pl.pallas_call(
         image_kernel,
-        grid=(heads, sources // step),
+        grid=(heads, n_y),
         in_specs=[
-            pl.BlockSpec((step, BLK, HD), lambda h, b: (b, 0, h)),
-            pl.BlockSpec((sources, BLK, HD), lambda h, b: (0, 1, h)),
-            pl.BlockSpec((sources, BLK, HD), lambda h, b: (0, 2, h)),
+            queries(),
+            queries(),
+            whole(1),
+            whole(1),
+            whole(2),
+            whole(2),
             pl.BlockSpec((2, HD), lambda h, b: (0, 0)),
         ],
         out_specs=[
@@ -121,18 +145,19 @@
         ],
         out_shape=[jax.ShapeDtypeStruct((image_len, width), F32)] * 2,
         scratch_shapes=[pltpu.VMEM((image_len, HD), BF16), pltpu.VMEM((image_len, 2 * HD), BF16)],
-        compiler_params=pltpu.CompilerParams(vmem_limit_bytes=24 * 1024 * 1024),
+        compiler_params=pltpu.CompilerParams(vmem_limit_bytes=VMEM_LIMIT),
         cost_estimate=pl.CostEstimate(
             flops=6 * image_len * image_len * width,
             bytes_accessed=14 * image_len * width,
             transcendentals=heads * image_len * image_len,
         ),
-    )(received, received, received, gains)
+    )(own, other, own, other, own, other, gains)
 
 
 def prompt_kernel(
     length_ref,
-    q_ref,
+    q_own,
+    q_other,
     text_ref,
     k_weight,
     v_weight,
@@ -160,7 +185,7 @@
         stacked = jnp.concatenate([v, jnp.ones_like(v)], axis=1)
         groups, rows, _ = out_ref.shape
         for b in range(groups):
-            q = q_ref[2 * b : 2 * b + 2].reshape(rows, HD).astype(F32)
+            q = jnp.concatenate([q_own[b], q_other[b]], 0).astype(F32)
             q = rms_scale(q, gain_ref[0:1, :] * QUERY_SCALE).astype(BF16)
             weight = jnp.exp2(dot_t(q, k))
             valid = lax.broadcasted_iota(jnp.int32, weight.shape, 1) < length_ref[0]
@@ -177,12 +202,11 @@
         out_ref[...] = lowered[...].reshape(out_ref.shape).astype(BF16)
 
 
-def prompt_attention(length, received, text, weights, first, down, gains, text_gain, num, den):
-    sources, _, width = received.shape
+def prompt_attention(length, own, other, text, weights, first, down, gains, text_gain, num, den):
+    groups, _, width = own.shape
     heads = width // HD
-    image_len = sources * BLK
+    image_len = groups * 2 * BLK
     model = text.shape[1]
-    groups = sources // 2
 
     def last(h):
         return jnp.minimum(h, heads - 1)
@@ -192,7 +216,8 @@
         grid=(heads + 1,),
         in_specs=[
             pl.BlockSpec(memory_space=pltpu.SMEM),
-            pl.BlockSpec((sources, BLK, HD), lambda h: (0, 0, last(h))),
+            pl.BlockSpec((groups, BLK, HD), lambda h: (0, 0, last(h))),
+            pl.BlockSpec((groups, BLK, HD), lambda h: (0, 0, last(h))),
             pl.BlockSpec((BLK, model), lambda h: (0, 0)),
             pl.BlockSpec((model, HD), lambda h: (0, first + last(h))),
             pl.BlockSpec((model, HD), lambda h: (0, first + heads + last(h))),
@@ -205,68 +230,73 @@
         out_specs=pl.BlockSpec((groups, 2 * BLK, HD), lambda h: (0, 0, h)),
         out_shape=jax.ShapeDtypeStruct((groups, 2 * BLK, width + HD), BF16),
         scratch_shapes=[pltpu.VMEM((image_len, HD), F32)],
-        compiler_params=pltpu.CompilerParams(vmem_limit_bytes=24 * 1024 * 1024),
+        compiler_params=pltpu.CompilerParams(vmem_limit_bytes=VMEM_LIMIT),
         cost_estimate=pl.CostEstimate(
             flops=6 * image_len * BLK * width + 4 * BLK * model * width,
             bytes_accessed=12 * image_len * width + 4 * model * width,
             transcendentals=heads * image_len * BLK,
         ),
-    )(length, received, text, weights, weights, down, gains, text_gain, num, den)
-
-
-def t5_kernel(x_ref, gain_ref, gate_w, up_w, out_w, out_ref, normed, hidden):
-    step = pl.program_id(0)
-    cuts = hidden.shape[0]
-
-    @pl.when(step == 0)
+    )(length, own, other, text, weights, weights, down, gains, text_gain, num, den)
+
+
+def t5_in_kernel(x_ref, gain_ref, gate_w, up_w, out_ref, normed):
+    @pl.when(pl.program_id(0) == 0)
     def _():
         normed[...] = rms_scale(x_ref[0].astype(F32), gain_ref[...]).astype(BF16)
 
-    @pl.when(step < cuts)
-    def _():
-        gate = jnp.dot(normed[...], gate_w[0], preferred_element_type=F32)
-        upward = jnp.dot(normed[...], up_w[0], preferred_element_type=F32)
-        hidden[step] = (jax.nn.gelu(gate, approximate=True) * upward).astype(BF16)
-
-    @pl.when(step >= cuts)
-    def _():
-        joined = jnp.concatenate([hidden[c] for c in range(cuts)], 1)
-        total = jnp.dot(joined, out_w[...], preferred_element_type=F32)
-        out_ref[0] = total.astype(BF16)
-
-
-def t5_ffn(states, gain, in_weight, out_weight, n_seq):
+    gate = jnp.dot(normed[...], gate_w[0], preferred_element_type=F32)
+    upward = jnp.dot(normed[...], up_w[0], preferred_element_type=F32)
+    out_ref[...] = (jax.nn.gelu(gate, approximate=True) * upward).astype(BF16)
+
+
+def t5_in(states, gain, in_weight):
     _, features, units = in_weight.shape
     cut = 128
-    cuts = units // cut
-    feat = features // n_seq
-
-    def unit(i):
-        return jnp.minimum(i, cuts - 1)
-
-    def share(i):
-        return jnp.maximum(i - cuts, 0)
-
     return pl.pallas_call(
-        t5_kernel,
-        grid=(cuts + n_seq,),
+        t5_in_kernel,
+        grid=(units // cut,),
         in_specs=[
             pl.BlockSpec((1, BLK, features), lambda i: (0, 0, 0)),
             pl.BlockSpec((1, features), lambda i: (0, 0)),
-            pl.BlockSpec((1, features, cut), lambda i: (0, 0, unit(i))),
-            pl.BlockSpec((1, features, cut), lambda i: (1, 0, unit(i))),
-            pl.BlockSpec((units, feat), lambda i: (0, share(i))),
+            pl.BlockSpec((1, features, cut), lambda i: (0, 0, i)),
+            pl.BlockSpec((1, features, cut), lambda i: (1, 0, i)),
         ],
-        out_specs=pl.BlockSpec((1, BLK, feat), lambda i: (share(i), 0, 0)),
-        out_shape=jax.ShapeDtypeStruct((n_seq, BLK, feat), BF16),
-        scratch_shapes=[pltpu.VMEM((BLK, features), BF16), pltpu.VMEM((cuts, BLK, cut), BF16)],
-        compiler_params=pltpu.CompilerParams(vmem_limit_bytes=24 * 1024 * 1024),
+        out_specs=pl.BlockSpec((BLK, cut), lambda i: (0, i)),
+        out_shape=jax.ShapeDtypeStruct((BLK, units), BF16),
+        scratch_shapes=[pltpu.VMEM((BLK, features), BF16)],
+        compiler_params=pltpu.CompilerParams(vmem_limit_bytes=VMEM_LIMIT),
         cost_estimate=pl.CostEstimate(
-            flops=6 * BLK * features * units,
-            bytes_accessed=6 * features * units,
+            flops=4 * BLK * features * units,
+            bytes_accessed=4 * features * units,
             transcendentals=BLK * units,
         ),
-    )(states, gain.reshape(1, features), in_weight, in_weight, out_weight)
+    )(states, gain.reshape(1, features), in_weight, in_weight)
+
+
+def t5_out_kernel(hidden_ref, out_w, out_ref):
+    total = jnp.dot(hidden_ref[...], out_w[...], preferred_element_type=F32)
+    out_ref[0] = total.astype(BF16)
+
+
+def t5_out(hidden, out_weight, n_seq):
+    units, features = out_weight.shape
+    feat = features // n_seq
+    return pl.pallas_call(
+        t5_out_kernel,
+        grid=(n_seq,),
+        in_specs=[
+            pl.BlockSpec((BLK, units), lambda i: (0, 0)),
+            pl.BlockSpec((units, feat), lambda i: (0, i)),
+        ],
+        out_specs=pl.BlockSpec((1, BLK, feat), lambda i: (i, 0, 0)),
+        out_shape=jax.ShapeDtypeStruct((n_seq, BLK, feat), BF16),
+        compiler_params=pltpu.CompilerParams(vmem_limit_bytes=VMEM_LIMIT),
+        cost_estimate=pl.CostEstimate(
+            flops=2 * BLK * features * units,
+            bytes_accessed=2 * features * units,
+            transcendentals=0,
+        ),
+    )(hidden, out_weight)
 
 
 def on_device(
@@ -311,23 +341,31 @@
         [context_weight.T, kv_weight.reshape(kv_weight.shape[0], -1)], 1
     )
     near_weights = near_shard(weights)
-    own_heads, other_heads = pack_heads(image_query_key_value[0].transpose(1, 0, 2), pair, n_seq)
-    t5_gain, other_heads = lax.optimization_barrier((t5_gain, other_heads))
-    other_heads = lax.ppermute(other_heads, "seq", flip_z)
+    own_heads, first_heads, second_heads = pack_heads(
+        image_query_key_value[0].transpose(1, 0, 2), pair, n_seq
+    )
+    t5_gain, first_heads = lax.optimization_barrier((t5_gain, first_heads))
+    first_heads = lax.ppermute(first_heads, "seq", flip_z)
     direction_t = proj_weight.T.astype(F32) + lax.dot_general(
         dora_b, dora_a, (((0,), (1,)), ((), ())), precision=lax.Precision.HIGHEST
     )
     direction_t = direction_t.astype(BF16)
     rows_y = swap(jnp.broadcast_to(direction_t[None], (n_y, own_cols, own_rows)), "seq", Y_GROUPS)
+    rows_y, own_heads = lax.optimization_barrier((rows_y, own_heads))
+    own_heads = swap(own_heads, "seq", Y_GROUPS)
 
     tokens = enc_states[0, :BLK]
     feat = tokens.shape[1] // n_seq
-    ffn = t5_ffn(enc_states, t5_gain, t5_in_weight, t5_out_weight, n_seq)
-    rows_y, ffn, near_weights = lax.optimization_barrier((rows_y, ffn, near_weights))
-
+    hidden = t5_in(enc_states, t5_gain, t5_in_weight)
+    hidden, near_weights = lax.optimization_barrier((hidden, near_weights))
     weights = gather_columns(weights, near_weights)
     depth = context_weight.shape[0]
     context_all = weights[:, :depth]
+    ffn = t5_out(hidden, t5_out_weight, n_seq)
+    own_heads, ffn, first_heads, second_heads = lax.optimization_barrier(
+        (own_heads, ffn, first_heads, second_heads)
+    )
+    second_heads = lax.ppermute(second_heads, "seq", flip_z)
 
     rows_f = rows_y.astype(F32)
     column_sq = jnp.sum(rows_f * rows_f, (0, 2))
@@ -341,19 +379,20 @@
     near_scaled = near_shard(scaled_t)
 
     ffn = swap(ffn, "seq")
-    ffn, near_scaled, other_heads = lax.optimization_barrier((ffn, near_scaled, other_heads))
-    scaled_all = gather_columns(scaled_t, near_scaled)
-    up_all = scaled_all[:, reach:]
+    ffn, second_heads = lax.optimization_barrier((ffn, second_heads))
     ffn_sum = jnp.sum(ffn.astype(F32), 0)
 
-    received = swap(jnp.stack([own_heads, other_heads], 1), "seq", Y_GROUPS)
-    received = received.reshape(n_seq, 3 * BLK, own_rows)
+    other_heads = swap(jnp.concatenate([first_heads, second_heads], 1), "seq", Y_GROUPS)
 
     own_tokens = lax.dynamic_slice_in_dim(tokens, seq_rank * feat, feat, 1).astype(F32)
     own_final = lax.dynamic_slice_in_dim(t5_final_gain, seq_rank * feat, feat, 0)
     encoded = ((own_tokens + ffn_sum) * own_final).astype(BF16)
     context = dot_t(encoded, context_all).astype(BF16).reshape(BLK, rows_of, lanes)
-    context, received = lax.optimization_barrier((context, received))
+    context, other_heads, near_scaled = lax.optimization_barrier(
+        (context, other_heads, near_scaled)
+    )
+    scaled_all = gather_columns(scaled_t, near_scaled)
+    up_all = scaled_all[:, reach:]
     arrived = swap(context, both)
     token_of = jnp.sum(arrived.reshape(n_dp, n_seq, rows_of, lanes).astype(F32), 1).astype(BF16)
     values = token_of.astype(F32)
@@ -368,11 +407,12 @@
     modulated = ((1.0 + scale) * text.astype(F32) + shift).astype(BF16)
     length = jnp.sum(jnp.where(prompt_owner_sample == data_rank, lengths, 0))
 
-    num, den = image_attention(received, image_qk_gain)
+    num, den = image_attention(own_heads, other_heads, image_qk_gain)
     down_factor = jnp.pad(dora_a.astype(BF16), ((0, 0), (0, lanes - rank)))
     attended = prompt_attention(
         length.reshape(1),
-        received,
+        own_heads,
+        other_heads,
         modulated,
         weights,
         depth // HD,
@@ -386,23 +426,33 @@
     gathered = swap(attended, "seq", Y_GROUPS)
     down = jnp.dot(cotangent, up_all, preferred_element_type=F32).astype(BF16)
     down = jnp.concatenate([down, lax.ppermute(down, "seq", flip_z)], 0)
-    gathered, down = lax.optimization_barrier((gathered, down))
+    cotangent_other = lax.ppermute(cotangent, "seq", flip_z)
+    gathered, down, cotangent_other = lax.optimization_barrier((gathered, down, cotangent_other))
     lowered = jnp.sum(gathered[:, :, own_rows:].astype(F32), 0)
     lowered_other = lax.ppermute(lowered[BLK:].astype(BF16), "seq", flip_z)
     gathered = gathered[:, :, :own_rows].transpose(1, 0, 2).reshape(2 * BLK, -1)
-    kept_rows = gathered[:BLK]
-    landed = []
-    for at in range(0, model, model // 2):
-        part = dot_t(gathered[BLK:], scaled_all[at : at + model // 2, :reach]).astype(BF16)
-        kept_rows, part = lax.optimization_barrier((kept_rows, part))
-        landed.append(lax.ppermute(part, "seq", flip_z))
+    sent_rows, kept_rows = gathered[BLK:], gathered[:BLK]
+    half = model // 2
+    part = dot_t(sent_rows, scaled_all[:half, :reach])
+    sum_first = jnp.sum(part * cotangent_other[:, :half].astype(F32), 0)
+    part = part.astype(BF16)
 
     lowered = (lowered[:BLK] + lowered_other.astype(F32)).astype(BF16)[:, :rank]
     up_part = lax.dot_general(
         lowered, cotangent, (((0,), (0,)), ((), ())), preferred_element_type=F32
     ).astype(BF16)
     up_part = up_part.reshape(rank, n_dp // 2, 2, own_cols).transpose(2, 1, 0, 3)
-    up_part = swap(up_part.reshape(n_dp, rank, own_cols), "dp")
+    up_part = up_part.reshape(n_dp, rank, own_cols)
+    sent_rows, part, up_part = lax.optimization_barrier((sent_rows, part, up_part))
+    landed_first = lax.ppermute(part, "seq", flip_z)
+    up_part = swap(up_part, "dp")
+    part = dot_t(sent_rows, scaled_all[half:, :reach])
+    sum_second = jnp.sum(part * cotangent_other[:, half:].astype(F32), 0)
+    kept_rows, part, landed_first = lax.optimization_barrier(
+        (kept_rows, part.astype(BF16), landed_first)
+    )
+    landed_second = lax.ppermute(part, "seq", flip_z)
+    kept = dot_t(kept_rows, scaled_all[:, :reach])
 
     for bit in (2, 4):
         moved = lax.ppermute(down, "seq", [(i, i ^ bit) for i in range(n_seq)])
@@ -418,18 +468,18 @@
         grad_a = grad_a.astype(F32) + moved.astype(F32)
     grad_a = grad_a.astype(BF16)
 
-    kept = dot_t(kept_rows, scaled_all[:, :reach])
-    kept, up_part, grad_a = lax.optimization_barrier((kept, up_part, grad_a))
-    out = kept + jnp.concatenate(landed, 1).astype(F32)
-    image_out = from_gathered(out.astype(BF16), n_dp)[None]
-    magnitude_part = jnp.sum(out * cotangent.astype(F32), 0).astype(BF16)
-    magnitude_part = magnitude_part.reshape(n_dp // 2, 2, own_cols).transpose(1, 0, 2)
+    magnitude_part = jnp.concatenate([sum_first, sum_second])
+    magnitude_part = magnitude_part + jnp.sum(kept * cotangent.astype(F32), 0)
+    magnitude_part = magnitude_part.astype(BF16).reshape(n_dp // 2, 2, own_cols).transpose(1, 0, 2)
     magnitude_part = jnp.broadcast_to(
         magnitude_part.reshape(n_dp, 1, own_cols), (n_dp, n_seq, own_cols)
     )
+    magnitude_part, up_part, grad_a = lax.optimization_barrier((magnitude_part, up_part, grad_a))
     magnitude_part = swap(magnitude_part.reshape(n_all, own_cols), both)
     grad_magnitude = jnp.sum(magnitude_part.astype(F32), 0) / magnitude
 
+    out = kept + jnp.concatenate([landed_first, landed_second], 1).astype(F32)
+    image_out = from_gathered(out.astype(BF16), n_dp)[None]
     moved = lax.ppermute(grad_a, "dp", [(i, i ^ 8) for i in range(n_dp)])
     grad_a = (grad_a.astype(F32) + moved.astype(F32)).T
     grad_b = jnp.sum(up_part.astype(F32), 0)

time: 305 us -> 293 us (0.961)
  waiting for transfers between devices: 103 us -> 83.5 us
  local copies, waits for them, and re-layouts: 31.7 us -> 14.7 us
  blocking collectives: 0 us -> 13.1 us
  Pallas kernels: 28.6 us -> 41.2 us
  other arithmetic: 21.2 us -> 17.7 us
    ppermute x2, waiting for transfers between devices: 39.4 us -> 7.59 us  [near_shard(): lax.ppermute(values, 'dp', [(i, (i + n_dp // 2) % n_dp) for i in range(n_...]
    ppermute x1, waiting for transfers between devices: 0.01 us -> 22.6 us  [on_device(): column_sq = column_sq + lax.ppermute(column_sq, 'seq', flip_z)]
    all_to_all x8, waiting for transfers between devices: 59.3 us -> 41.1 us  [swap(): lax.all_to_all(values, axes, 0, 0, tiled=True, axis_index_groups=groups)]
    unnamed x64 -> x46, local copies, waits for them, and re-layouts: 21.8 us -> 4.28 us
    all_to_all x0 -> x1, blocking collectives: none -> 13.1 us  [swap(): lax.all_to_all(values, axes, 0, 0, tiled=True, axis_index_groups=groups)]
    ppermute x3 -> x5, starting transfers between devices: 3.07 us -> 13.9 us  [the longest x1 3.54 us: on_device(): cotangent_other = lax.ppermute(cotangent, 'seq', flip_z)]
    pallas_call x2 -> x3, Pallas kernels: 19.6 us -> 27.7 us  [the longest x1 12.2 us: image_attention(): pl.pallas_call(image_kernel, grid=(heads, n_y), in_specs=[queries(), quer...]
    ppermute x3 -> x5, waiting for transfers between devices: 0.01 us -> 5.67 us  [the longest x1 4.47 us: on_device(): first_heads = lax.ppermute(first_heads, 'seq', flip_z)]
  transfers between devices with their start and end apart: 27 -> 29, of which waited for: 9 -> 12; matrix products, arithmetic and copies ran while one was open for 16% -> 17% of each run, Pallas kernels for 9% -> 14%
where the time goes in v6:
time: 293 us; the launch traced here: 290 us
  waiting for transfers between devices  83.5 us (28%)
  starting transfers between devices  82 us (28%)
  Pallas kernels  41.2 us (14%)
  matrix products  23.5 us (8%)
  other arithmetic  17.7 us (6%)
  local copies, waits for them, and re-layouts  14.7 us (5%)
  between operations  14.6 us (5%)
  blocking collectives  13.1 us (4%)
    all_to_all x8, starting transfers between devices, swap(): lax.all_to_all(values, axes, 0, 0, tiled=True, axis_index_groups=groups)  49.8 us
    all_to_all x8, waiting for transfers between devices, swap(): lax.all_to_all(values, axes, 0, 0, tiled=True, axis_index_groups=groups)  41.1 us
    ppermute x1, waiting for transfers between devices, on_device(): column_sq = column_sq + lax.ppermute(column_sq, 'seq', flip_z)  22.6 us
    dot_general x4, matrix products, dot_t(): lax.dot_general(left, right, (((1,), (1,)), ((), ())), preferred_element_...  20.3 us
    all_to_all x1, blocking collectives, swap(): lax.all_to_all(values, axes, 0, 0, tiled=True, axis_index_groups=groups)  13.1 us
    pallas_call x1, Pallas kernels, image_attention(): pl.pallas_call(image_kernel, grid=(heads, n_y), in_specs=[queries(), quer...  12.2 us
    pallas_call x1, Pallas kernels, prompt_attention(): pl.pallas_call(prompt_kernel, grid=(heads + 1,), in_specs=[pl.BlockSpec(m...  9.59 us
    pallas_call x1, Pallas kernels, t5_in(): pl.pallas_call(t5_in_kernel, grid=(units // cut,), in_specs=[pl.BlockSpec...  8.45 us
  transfers between devices with their start and end apart: 29, of which 12 were waited for; matrix products, arithmetic and copies ran while one was open for 17% of the time, Pallas kernels for 14%

profile of v6, /device:TPU:1, one launch (start us, length us, event | category | flops | bytes accessed | tf_op | source)
XLA Modules:
  0.0 290.3 jit_solution(949570043926157180)
XLA Ops:
  7.2 1.0 copy.119
  8.2 1.0 pad_maximum_fusion.3
  9.2 2.5 collective-permute-start
  11.7 3.9 %shard_map.210 = (bf16[4,384,384]{2,1,0:T(8,128)(2,1)}, bf16[4,192,384]{2,1,0:T(8,128)(2,1)}, bf16[4,192,384]{2,1,0:T(8,128)(2,1)}) custom-call(s32[1]{0:T(128)} %bitcast.2._, bf16[3,128,3072]{2,1,0:T(8,128)(2,1)} %bitcast.92, bf16[3,128,3072]{2,1,0:T(8,128)(2,1)} %bitcast.93), custom_call_target="tpu_custom_call" | custom-call | bytes 4718592 | tf_op jit(solution)/shard_map/pallas_call | solution.py:80
  15.6 8.4 %shard_map.211.hidden_ref = bf16[128,640]{1,0:T(8,128)(2,1)} custom-call(bf16[1,256,4096]{2,1,0:T(8,128)(2,1)} %x_ref.1, f32[1,4096]{1,0:T(1,128)} %bitcast.116, bf16[2,4096,640]{2,1,0:T(8,128)(2,1)} %up_w.1, bf16[2,4096,640]{2,1,0:T(8,128)(2,1)} %up_w.1), custom_call_target="tpu_custom_call" | custom-call | flops 1342177280 | bytes 10485760 | tf_op jit(solution)/shard_map/pallas_call | solution.py:255
  24.2 1.0 pad_maximum_fusion.2
  25.9 13.1 %all_to_all.49 = bf16[4,192,384]{2,1,0:T(8,128)(2,1)S(1)} all-to-all(bf16[4,192,384]{2,1,0:T(8,128)(2,1)S(1)} %broadcast_in_dim.10), channel_id=1, replica_groups={{0,2,4,6},{1,3,5,7},{8,10,12,14},{9,11,13,15},{16,18,20,22},{17,19,21,2..., dimensions={0} | all-to-all | bytes 1179648 | tf_op jit(solution)/shard_map/all_to_all | solution.py:25
  38.9 3.5 %all-to-all-start.1 = ((bf16[4,384,384]{2,1,0:T(8,128)(2,1)}), bf16[4,384,384]{2,1,0:T(8,128)(2,1)S(1)}, u32[]{:S(2)}, u32[]{:S(2)}) async-start(bf16[4,384,384]{2,1,0:T(8,128)(2,1)} %get-tuple-element.37), calls=%async_computation.1 | async-start | bytes 2359296 | tf_op jit(solution)/shard_map/all_to_all | solution.py:25
  42.5 3.4 %collective-permute-start.1 = (bf16[4,192,384]{2,1,0:T(8,128)(2,1)S(1)}, bf16[4,192,384]{2,1,0:T(8,128)(2,1)}, u32[]{:S(2)}, u32[]{:S(2)}) collective-permute-start(bf16[4,192,384]{2,1,0:T(8,128)(2,1)S(1)} %copy-done.18), channel_id=1, source_target_pairs={{0,1},{1,0},{2,3},{3,2},{4,5},{5,4},{6,7},{7,6},{8,9},{9,8},{10,11... | collective-permute-start | bytes 1769480 | tf_op jit(solution)/shard_map/ppermute | solution.py:348
  45.9 7.1 %shard_map.212 = bf16[8,128,512]{2,1,0:T(8,128)(2,1)} custom-call(bf16[128,640]{1,0:T(8,128)(2,1)} %shard_map.211.hidden_ref, bf16[640,4096]{1,0:T(8,128)(2,1)} %out_w.1), custom_call_target="tpu_custom_call" | custom-call | flops 671088640 | bytes 5242880 | tf_op jit(solution)/shard_map/pallas_call | solution.py:284
  53.0 4.5 %collective-permute-done.1 = bf16[4,192,384]{2,1,0:T(8,128)(2,1)} collective-permute-done((bf16[4,192,384]{2,1,0:T(8,128)(2,1)S(1)}, bf16[4,192,384]{2,1,0:T(8,128)(2,1)}, u32[]{:S(2)}, u32[]{:S(2)}) %collective-permute-start.1) | collective-permute-done | bytes 589856 | tf_op jit(solution)/shard_map/ppermute | solution.py:348
  57.5 6.2 %all-to-all-start.2 = ((bf16[8,128,512]{2,1,0:T(8,128)(2,1)}), bf16[8,128,512]{2,1,0:T(8,128)(2,1)S(1)}, u32[]{:S(2)}, u32[]{:S(2)}) async-start(bf16[8,128,512]{2,1,0:T(8,128)(2,1)} %shard_map.212), calls=%async_computation.2 | async-start | bytes 2097152 | tf_op jit(solution)/shard_map/all_to_all | solution.py:25
  63.7 3.0 %collective-permute-start.2 = (bf16[4,192,384]{2,1,0:T(8,128)(2,1)}, bf16[4,192,384]{2,1,0:T(8,128)(2,1)}, u32[]{:S(2)}, u32[]{:S(2)}) collective-permute-start(bf16[4,192,384]{2,1,0:T(8,128)(2,1)} %get-tuple-element.45), channel_id=1, source_target_pairs={{0,1},{1,0},{2,3},{3,2},{4,5},{5,4},{6,7},{7,6},{8,9},{9,8},{10,11... | collective-permute-start | bytes 1769480 | tf_op jit(solution)/shard_map/ppermute | solution.py:368
  67.0 22.6 %collective-permute-done.3 = f32[192]{0:T(256)S(1)} collective-permute-done((f32[192]{0:T(256)S(1)}, f32[192]{0:T(256)S(1)}, u32[]{:S(2)}, u32[]{:S(2)}) %collective-permute-start.3) | collective-permute-done | bytes 800 | tf_op jit(solution)/shard_map/ppermute | solution.py:372
  89.6 1.0 fusion.20
  90.6 2.8 pad_maximum_fusion.1
  93.3 5.0 %all-to-all-start.3 = ((bf16[4,384,384]{2,1,0:T(8,128)(2,1)}), bf16[4,384,384]{2,1,0:T(8,128)(2,1)S(1)}, u32[]{:S(2)}, u32[]{:S(2)}) async-start(bf16[4,384,384]{2,1,0:T(8,128)(2,1)} %pad_maximum_fusion.1), calls=%async_computation.3 | async-start | bytes 2359296 | tf_op jit(solution)/shard_map/all_to_all | solution.py:25
  98.4 1.1 copy.118
  99.6 0.9 fusion.19
  100.4 0.8 dynamic_slice.7
  101.3 1.4 convert_reduce_fusion
  102.7 3.0 %fusion.9 = bf16[16,8,24,128]{3,1,2,0:T(8,128)(2,1)S(1)} fusion(bf16[3072,1280]{1,0:T(8,128)(2,1)} %bitcast.89, f32[128,512]{1,0:T(8,128)S(1)} %convert_reduce_fusion, f32[512]{0:T(512)S(1)} %dynamic_slice.7, bf16[1,128,4096]{2,1,0:T(8,128)(2,1)S(1)} %slice-done, s32[]{:T(128)S(6)} %select_n.74), kind=kOutput, calls=%fused_computation.18 | convolution fusion | flops 403308544 | bytes 4327428 | tf_op jit(solution)/shard_map/dot_general | solution.py:56
  105.8 1.0 copy.120
  106.8 7.6 %collective-permute-done.4 = bf16[192,1664]{1,0:T(8,128)(2,1)} collective-permute-done((bf16[192,1664]{1,0:T(8,128)(2,1)}, bf16[192,1664]{1,0:T(8,128)(2,1)}, u32[]{:S(2)}, u32[]{:S(2)}) %collective-permute-start.4) | collective-permute-done | bytes 639008 | tf_op jit(solution)/shard_map/ppermute | solution.py:30
  114.4 1.7 select_bitcast_fusion.1
  116.1 1.2 pad_maximum_fusion
  117.4 11.2 %all-to-all-start.4 = ((bf16[128,24,128]{2,1,0:T(8,128)(2,1)}), bf16[128,24,128]{2,1,0:T(8,128)(2,1)S(1)}, u32[]{:S(2)}, u32[]{:S(2)}) async-start(bf16[128,24,128]{2,1,0:T(8,128)(2,1)} %bitcast.48), calls=%async_computation.4 | async-start | bytes 1572864 | tf_op jit(solution)/shard_map/all_to_all | solution.py:25
  128.6 19.9 %all-to-all-done.4 = bf16[128,24,128]{2,1,0:T(8,128)(2,1)S(1)} async-done(((bf16[128,24,128]{2,1,0:T(8,128)(2,1)}), bf16[128,24,128]{2,1,0:T(8,128)(2,1)S(1)}, u32[]{:S(2)}, u32[]{:S(2)}) %all-to-all-start.4) | async-done | bytes 786464 | tf_op jit(solution)/shard_map/all_to_all | solution.py:25
  149.7 1.5 copy.102
  151.2 5.9 %all-to-all-start.5 = ((bf16[128,24,128]{2,1,0:T(8,128)(2,1)}), bf16[128,24,128]{2,1,0:T(8,128)(2,1)S(1)}, u32[]{:S(2)}, u32[]{:S(2)}) async-start(bf16[128,24,128]{2,1,0:T(8,128)(2,1)} %copy.102), calls=%async_computation.5 | async-start | bytes 1572864 | tf_op jit(solution)/shard_map/all_to_all | solution.py:25
  157.8 3.5 %collective-permute-start.6 = (bf16[128,3072]{1,0:T(8,128)(2,1)S(1)}, bf16[128,3072]{1,0:T(8,128)(2,1)}, u32[]{:S(2)}, u32[]{:S(2)}) collective-permute-start(bf16[128,3072]{1,0:T(8,128)(2,1)S(1)} %copy.107), channel_id=1, source_target_pairs={{0,1},{1,0},{2,3},{3,2},{4,5},{5,4},{6,7},{7,6},{8,9},{9,8},{10,11... | collective-permute-start | bytes 2359304 | tf_op jit(solution)/shard_map/ppermute | solution.py:429
  164.4 12.2 %shard_map.213 = (f32[1024,384]{1,0:T(8,128)}, f32[1024,384]{1,0:T(8,128)}) custom-call(bf16[4,384,384]{2,1,0:T(8,128)(2,1)} %copy-done, bf16[4,384,384]{2,1,0:T(8,128)(2,1)} %copy-done.1, bf16[4,384,384]{2,1,0:T(8,128)(2,1)} %copy-done, bf16[4,384,384]{2,1,0:T(8,128)(2,1)} %copy-done.1, bf16[4,384,384]{2,1,0:T(8,128)(2,1)} %copy-done, ...), custom_call_target="tpu_custom_call" | custom-call | flops 2415919104 | bytes 5505024 | tf_op jit(solution)/shard_map/pallas_call | solution.py:130
  176.6 4.1 %all-to-all-done.5 = bf16[128,24,128]{2,1,0:T(8,128)(2,1)S(1)} async-done(((bf16[128,24,128]{2,1,0:T(8,128)(2,1)}), bf16[128,24,128]{2,1,0:T(8,128)(2,1)S(1)}, u32[]{:S(2)}, u32[]{:S(2)}) %all-to-all-start.5) | async-done | bytes 786464 | tf_op jit(solution)/shard_map/all_to_all | solution.py:25
  180.8 1.2 fusion.8.text_ref
  182.0 9.6 %shard_map.214 = bf16[4,256,512]{2,1,0:T(8,128)(2,1)} custom-call(s32[1]{0:T(128)} %bitcast.length_ref, bf16[4,384,384]{2,1,0:T(8,128)(2,1)} %copy-done, bf16[4,384,384]{2,1,0:T(8,128)(2,1)} %copy-done.1, bf16[128,3072]{1,0:T(8,128)(2,1)} %fusion.8.text_ref, bf16[3072,1280]{1,0:T(8,128)(2,1)} %bitcast.90, bf16[3072,1280]{1,0:T(8,128)(2,1)} %bitcast.91, ...), custom_call_target="tpu_custom_call" | custom-call | flops 905969664 | bytes 9437184 | tf_op jit(solution)/shard_map/pallas_call | solution.py:214
  191.6 3.5 %all-to-all-start.6 = ((bf16[4,256,512]{2,1,0:T(8,128)(2,1)}), bf16[4,256,512]{2,1,0:T(8,128)(2,1)S(1)}, u32[]{:S(2)}, u32[]{:S(2)}) async-start(bf16[4,256,512]{2,1,0:T(8,128)(2,1)} %shard_map.214), calls=%async_computation.6 | async-start | bytes 2097152 | tf_op jit(solution)/shard_map/all_to_all | solution.py:25
  195.1 1.5 fusion.16
  196.7 1.2 collective-permute-start.5
  197.9 3.1 %collective-permute-done.5 = bf16[128,128]{1,0:T(8,128)(2,1)S(1)} collective-permute-done((bf16[128,128]{1,0:T(8,128)(2,1)S(1)}, bf16[128,128]{1,0:T(8,128)(2,1)S(1)}, u32[]{:S(2)}, u32[]{:S(2)}) %collective-permute-start.5) | collective-permute-done | bytes 32800 | tf_op jit(solution)/shard_map/ppermute | solution.py:428
  201.1 7.5 %all-to-all-done.6 = bf16[4,256,512]{2,1,0:T(8,128)(2,1)S(1)} async-done(((bf16[4,256,512]{2,1,0:T(8,128)(2,1)}), bf16[4,256,512]{2,1,0:T(8,128)(2,1)S(1)}, u32[]{:S(2)}, u32[]{:S(2)}) %all-to-all-start.6) | async-done | bytes 1048608 | tf_op jit(solution)/shard_map/all_to_all | solution.py:25
  209.0 0.9 fusion.46
  209.8 1.2 copy.109
  212.5 1.1 collective-permute-start.11
  213.6 5.0 %fusion.47 = (bf16[128,1536]{1,0:T(8,128)(2,1)}, f32[128,1536]{1,0:T(8,128)}) fusion(bf16[128,1536]{0,1:T(8,128)(2,1)S(1)} %bitcast.109, bf16[3072,1664]{1,0:T(8,128)(2,1)} %bitcast.119), kind=kOutput, calls=%fused_computation.103 | convolution fusion | flops 604176384 | bytes 6291456 | tf_op jit(solution)/shard_map/dot_general | solution.py:56
  218.9 1.8 collective-permute-start.7
  221.1 3.1 %collective-permute-start.12 = (bf16[64,384]{1,0:T(8,128)(2,1)S(1)}, bf16[64,384]{1,0:T(8,128)(2,1)S(1)}, u32[]{:S(2)}, u32[]{:S(2)}) collective-permute-start(bf16[64,384]{1,0:T(8,128)(2,1)S(1)} %convolution_convert_fusion.3), channel_id=1, source_target_pairs={{0,8},{8,0},{16,24},{24,16},{32,40},{40,32},{48,56},{56,48},{64,72... | collective-permute-start | bytes 147464 | tf_op jit(solution)/shard_map/ppermute | solution.py:467
  225.3 1.0 copy.110
  226.3 1.7 collective-permute-start.8
  228.5 5.3 %multiply_reduce_fusion.2 = (f32[1536]{0:T(1024)S(1)}, f32[1536]{0:T(1024)S(1)}, bf16[128,1536]{1,0:T(8,128)(2,1)}) fusion(f32[128,1536]{1,0:T(8,128)} %get-tuple-element.104, bf16[128,3072]{1,0:T(8,128)(2,1)} %collective-permute-done.6, bf16[128,1536]{0,1:T(8,128)(2,1)S(1)} %bitcast.110, bf16[3072,1664]{1,0:T(8,128)(2,1)} %bitcast.120), kind=kOutput, calls=%fused_computation.35 | convolution fusion | flops 605352960 | bytes 7090176 | tf_op jit(solution)/shard_map/dot_general | solution.py:56
  233.7 1.2 collective-permute-done.8
  234.9 2.2 collective-permute-start.9
  237.2 1.4 collective-permute-start.14
  238.8 8.2 %all-to-all-start.7 = ((bf16[16,64,192]{2,1,0:T(8,128)(2,1)}), bf16[16,64,192]{2,1,0:T(8,128)(2,1)S(1)}, u32[]{:S(2)}, u32[]{:S(2)}) async-start(bf16[16,64,192]{2,1,0:T(8,128)(2,1)} %bitcast.29), calls=%async_computation.7 | async-start | bytes 1048576 | tf_op jit(solution)/shard_map/all_to_all | solution.py:25
  247.0 7.0 %multiply_reduce_fusion = (f32[3072]{0:T(1024)S(1)}, bf16[128,3072]{1,0:T(8,128)(2,1)S(1)}) fusion(bf16[128,3072]{1,0:T(8,128)(2,1)S(1)} %copy-done.6, bf16[128,1536]{1,0:T(8,128)(2,1)S(1)} %collective-permute-done.9, bf16[128,1536]{1,0:T(8,128)(2,1)S(1)} %collective-permute-done.8, bf16[128,1536]{0,1:T(8,128)(2,1)S(1)} %bitcast.108, ...), kind=kOutput, calls=%fused_computation.13 | convolution fusion | flops 1211495424 | bytes 12201984 | tf_op jit(solution)/shard_map/dot_general | solution.py:56
  254.1 2.8 all-to-all-done.7
  257.1 1.2 collective-permute-start.16
  258.7 1.2 copy.116
  259.9 0.9 collective-permute-start.15
  260.8 0.8 copy.115
  261.5 6.4 %all-to-all-start.8 = ((bf16[128,1,192]{2,1,0:T(2,128)(2,1)}), bf16[128,1,192]{2,1,0:T(2,128)(2,1)S(1)}, u32[]{:S(2)}, u32[]{:S(2)}) async-start(bf16[128,1,192]{2,1,0:T(2,128)(2,1)} %copy.115), calls=%async_computation.8 | async-start | bytes 262144 | tf_op jit(solution)/shard_map/all_to_all | solution.py:25
  267.9 3.0 %collective-permute-start.17 = (bf16[64,192]{1,0:T(8,128)(2,1)S(1)}, bf16[64,192]{1,0:T(8,128)(2,1)S(1)}, u32[]{:S(2)}, u32[]{:S(2)}) collective-permute-start(bf16[64,192]{1,0:T(8,128)(2,1)S(1)} %add_convert_fusion.5), channel_id=1, source_target_pairs={{0,4},{1,5},{2,6},{3,7},{4,0},{5,1},{6,2},{7,3},{8,12},{9,13},{10,... | collective-permute-start | bytes 73736 | tf_op jit(solution)/shard_map/ppermute | solution.py:488
  270.9 6.8 %all-to-all-done.8 = bf16[128,1,192]{2,1,0:T(2,128)(2,1)S(1)} async-done(((bf16[128,1,192]{2,1,0:T(2,128)(2,1)}), bf16[128,1,192]{2,1,0:T(2,128)(2,1)S(1)}, u32[]{:S(2)}, u32[]{:S(2)}) %all-to-all-start.8) | async-done | bytes 49184 | tf_op jit(solution)/shard_map/all_to_all | solution.py:25
  278.5 1.0 collective-permute-start.18
  280.2 2.7 collective-permute-done.18
  (130 shorter events, 13.4 us)
Async XLA Ops:
  7.2 95.5 %all-gather.5.cloned.1.call-start = ((), (), s32[]{:S(2)}) async-start(), calls=%async_computation.9 | async-start | bytes 8847360 | tf_op jit(solution)/shard_map/all_gather | solution.py:39
  9.2 14.9 %collective-permute-start = (bf16[192,1280]{1,0:T(8,128)(2,1)S(1)}, bf16[192,1280]{1,0:T(8,128)(2,1)S(1)}, u32[]{:S(2)}, u32[]{:S(2)}) collective-permute-start(bf16[192,1280]{1,0:T(8,128)(2,1)S(1)} %pad_maximum_fusion.3), channel_id=1, source_target_pairs={{0,64},{8,72},{16,80},{24,88},{32,96},{40,104},{48,112},{56,120},{... | collective-permute-start | bytes 1474568 | tf_op jit(solution)/shard_map/ppermute | solution.py:30
  15.6 8.5 %copy-start.7 = (bf16[512,192]{0,1:T(8,128)(2,1)S(1)}, bf16[512,192]{0,1:T(8,128)(2,1)}, u32[]{:S(2)}) copy-start(bf16[512,192]{0,1:T(8,128)(2,1)} %param.26) | copy-start | bytes 589828
  24.2 1.1 copy-start.10
  24.2 1.1 copy-start.11
  24.2 1.1 copy-start.12
  25.8 16.6 %copy-start.18 = (bf16[4,192,384]{2,1,0:T(8,128)(2,1)S(1)}, bf16[4,192,384]{2,1,0:T(8,128)(2,1)}, u32[]{:S(2)}) copy-start(bf16[4,192,384]{2,1,0:T(8,128)(2,1)} %get-tuple-element.41) | copy-start | bytes 1769476
  38.9 18.5 %all-to-all-start.1 = ((bf16[4,384,384]{2,1,0:T(8,128)(2,1)}), bf16[4,384,384]{2,1,0:T(8,128)(2,1)S(1)}, u32[]{:S(2)}, u32[]{:S(2)}) async-start(bf16[4,384,384]{2,1,0:T(8,128)(2,1)} %get-tuple-element.37), calls=%async_computation.1 | async-start | bytes 2359296 | tf_op jit(solution)/shard_map/all_to_all | solution.py:25
  42.5 15.0 %collective-permute-start.1 = (bf16[4,192,384]{2,1,0:T(8,128)(2,1)S(1)}, bf16[4,192,384]{2,1,0:T(8,128)(2,1)}, u32[]{:S(2)}, u32[]{:S(2)}) collective-permute-start(bf16[4,192,384]{2,1,0:T(8,128)(2,1)S(1)} %copy-done.18), channel_id=1, source_target_pairs={{0,1},{1,0},{2,3},{3,2},{4,5},{5,4},{6,7},{7,6},{8,9},{9,8},{10,11... | collective-permute-start | bytes 1769480 | tf_op jit(solution)/shard_map/ppermute | solution.py:348
  53.0 36.6 %copy-start.15 = (f32[192]{0:T(256)S(1)}, f32[192]{0:T(256)}, u32[]{:S(2)}) copy-start(f32[192]{0:T(256)} %param.36) | copy-start | bytes 2308
  57.5 33.1 %copy-start = (bf16[4,384,384]{2,1,0:T(8,128)(2,1)}, bf16[4,384,384]{2,1,0:T(8,128)(2,1)S(1)}, u32[]{:S(2)}) copy-start(bf16[4,384,384]{2,1,0:T(8,128)(2,1)S(1)} %all-to-all-done.1.q_own.k_own.v_own) | copy-start | bytes 3538948
  57.5 33.1 %all-to-all-start.2 = ((bf16[8,128,512]{2,1,0:T(8,128)(2,1)}), bf16[8,128,512]{2,1,0:T(8,128)(2,1)S(1)}, u32[]{:S(2)}, u32[]{:S(2)}) async-start(bf16[8,128,512]{2,1,0:T(8,128)(2,1)} %shard_map.212), calls=%async_computation.2 | async-start | bytes 2097152 | tf_op jit(solution)/shard_map/all_to_all | solution.py:25
  63.7 26.8 %collective-permute-start.2 = (bf16[4,192,384]{2,1,0:T(8,128)(2,1)}, bf16[4,192,384]{2,1,0:T(8,128)(2,1)}, u32[]{:S(2)}, u32[]{:S(2)}) collective-permute-start(bf16[4,192,384]{2,1,0:T(8,128)(2,1)} %get-tuple-element.45), channel_id=1, source_target_pairs={{0,1},{1,0},{2,3},{3,2},{4,5},{5,4},{6,7},{7,6},{8,9},{9,8},{10,11... | collective-permute-start | bytes 1769480 | tf_op jit(solution)/shard_map/ppermute | solution.py:368
  66.9 22.7 %collective-permute-start.3 = (f32[192]{0:T(256)S(1)}, f32[192]{0:T(256)S(1)}, u32[]{:S(2)}, u32[]{:S(2)}) collective-permute-start(f32[192]{0:T(256)S(1)} %fusion.13), channel_id=1, source_target_pairs={{0,1},{1,0},{2,3},{3,2},{4,5},{5,4},{6,7},{7,6},{8,9},{9,8},{10,11... | collective-permute-start | bytes 2312 | tf_op jit(solution)/shard_map/ppermute | solution.py:372
  90.6 2.8 copy-start.3
  93.3 21.1 %all-to-all-start.3 = ((bf16[4,384,384]{2,1,0:T(8,128)(2,1)}), bf16[4,384,384]{2,1,0:T(8,128)(2,1)S(1)}, u32[]{:S(2)}, u32[]{:S(2)}) async-start(bf16[4,384,384]{2,1,0:T(8,128)(2,1)} %pad_maximum_fusion.1), calls=%async_computation.3 | async-start | bytes 2359296 | tf_op jit(solution)/shard_map/all_to_all | solution.py:25
  98.3 96.8 %all-gather.7.cloned.1.call-start = ((), (), s32[]{:S(2)}) async-start(), calls=%async_computation.10 | async-start | bytes 11501568 | tf_op jit(solution)/shard_map/all_gather | solution.py:39
  100.4 2.3 slice-start
  100.4 14.0 %collective-permute-start.4 = (bf16[192,1664]{1,0:T(8,128)(2,1)}, bf16[192,1664]{1,0:T(8,128)(2,1)}, u32[]{:S(2)}, u32[]{:S(2)}) collective-permute-start(bf16[192,1664]{1,0:T(8,128)(2,1)} %fusion.19), channel_id=1, source_target_pairs={{0,64},{8,72},{16,80},{24,88},{32,96},{40,104},{48,112},{56,120},{... | collective-permute-start | bytes 1916936 | tf_op jit(solution)/shard_map/ppermute | solution.py:30
  114.4 2.9 %copy-start.1 = (bf16[4,384,384]{2,1,0:T(8,128)(2,1)}, bf16[4,384,384]{2,1,0:T(8,128)(2,1)S(1)}, u32[]{:S(2)}) copy-start(bf16[4,384,384]{2,1,0:T(8,128)(2,1)S(1)} %all-to-all-done.3.q_other.k_other.v_other) | copy-start | bytes 3538948
  117.4 31.8 %copy-start.16 = (s32[16]{0:T(128)S(1)}, s32[16]{0:T(128)}, u32[]{:S(2)}) copy-start(s32[16]{0:T(128)} %param.21) | copy-start | bytes 196
  117.4 31.1 %all-to-all-start.4 = ((bf16[128,24,128]{2,1,0:T(8,128)(2,1)}), bf16[128,24,128]{2,1,0:T(8,128)(2,1)S(1)}, u32[]{:S(2)}, u32[]{:S(2)}) async-start(bf16[128,24,128]{2,1,0:T(8,128)(2,1)} %bitcast.48), calls=%async_computation.4 | async-start | bytes 1572864 | tf_op jit(solution)/shard_map/all_to_all | solution.py:25
  149.7 7.4 %copy-start.4 = (bf16[1,128,3072]{2,1,0:T(8,128)(2,1)S(1)}, bf16[1,128,3072]{2,1,0:T(8,128)(2,1)}, u32[]{:S(2)}) copy-start(bf16[1,128,3072]{2,1,0:T(8,128)(2,1)} %param.37) | copy-start | bytes 2359300
  151.2 29.5 %all-to-all-start.5 = ((bf16[128,24,128]{2,1,0:T(8,128)(2,1)}), bf16[128,24,128]{2,1,0:T(8,128)(2,1)S(1)}, u32[]{:S(2)}, u32[]{:S(2)}) async-start(bf16[128,24,128]{2,1,0:T(8,128)(2,1)} %copy.102), calls=%async_computation.5 | async-start | bytes 1572864 | tf_op jit(solution)/shard_map/all_to_all | solution.py:25
  157.4 4.5 %copy-start.13 = (f32[1,3072]{1,0:T(1,128)S(1)}, f32[1,3072]{1,0:T(1,128)}, u32[]{:S(2)}) copy-start(f32[1,3072]{1,0:T(1,128)} %param.27) | copy-start | bytes 36868
  157.4 5.3 %copy-start.14 = (f32[1,3072]{1,0:T(1,128)S(1)}, f32[1,3072]{1,0:T(1,128)}, u32[]{:S(2)}) copy-start(f32[1,3072]{1,0:T(1,128)} %param.28) | copy-start | bytes 36868
  157.5 6.3 %copy-start.17 = (s32[16]{0:T(128)S(1)}, s32[16]{0:T(128)}, u32[]{:S(2)}) copy-start(s32[16]{0:T(128)} %param.20) | copy-start | bytes 196
  157.8 18.8 %copy-start.5 = (bf16[128,3072]{1,0:T(8,128)(2,1)}, bf16[128,3072]{1,0:T(8,128)(2,1)S(1)}, u32[]{:S(2)}) copy-start(bf16[128,3072]{1,0:T(8,128)(2,1)S(1)} %copy.107) | copy-start | bytes 2359300
  157.8 43.2 %collective-permute-start.6 = (bf16[128,3072]{1,0:T(8,128)(2,1)S(1)}, bf16[128,3072]{1,0:T(8,128)(2,1)}, u32[]{:S(2)}, u32[]{:S(2)}) collective-permute-start(bf16[128,3072]{1,0:T(8,128)(2,1)S(1)} %copy.107), channel_id=1, source_target_pairs={{0,1},{1,0},{2,3},{3,2},{4,5},{5,4},{6,7},{7,6},{8,9},{9,8},{10,11... | collective-permute-start | bytes 2359304 | tf_op jit(solution)/shard_map/ppermute | solution.py:429
  191.6 16.9 %all-to-all-start.6 = ((bf16[4,256,512]{2,1,0:T(8,128)(2,1)}), bf16[4,256,512]{2,1,0:T(8,128)(2,1)S(1)}, u32[]{:S(2)}, u32[]{:S(2)}) async-start(bf16[4,256,512]{2,1,0:T(8,128)(2,1)} %shard_map.214), calls=%async_computation.6 | async-start | bytes 2097152 | tf_op jit(solution)/shard_map/all_to_all | solution.py:25
  196.7 4.3 %collective-permute-start.5 = (bf16[128,128]{1,0:T(8,128)(2,1)S(1)}, bf16[128,128]{1,0:T(8,128)(2,1)S(1)}, u32[]{:S(2)}, u32[]{:S(2)}) collective-permute-start(bf16[128,128]{1,0:T(8,128)(2,1)S(1)} %fusion.16), channel_id=1, source_target_pairs={{0,1},{1,0},{2,3},{3,2},{4,5},{5,4},{6,7},{7,6},{8,9},{9,8},{10,11... | collective-permute-start | bytes 98312 | tf_op jit(solution)/shard_map/ppermute | solution.py:428
  208.6 3.2 %collective-permute-start.10 = (bf16[256,128]{1,0:T(8,128)(2,1)S(1)}, bf16[256,128]{1,0:T(8,128)(2,1)S(1)}, u32[]{:S(2)}, u32[]{:S(2)}) collective-permute-start(bf16[256,128]{1,0:T(8,128)(2,1)S(1)} %pad_maximum_fusion.7), channel_id=1, source_target_pairs={{0,2},{1,3},{2,0},{3,1},{4,6},{5,7},{6,4},{7,5},{8,10},{9,11},{10,... | collective-permute-start | bytes 196616 | tf_op jit(solution)/shard_map/ppermute | solution.py:458
  211.0 2.6 copy-start.8
  212.5 8.3 %collective-permute-start.11 = (bf16[512,128]{1,0:T(8,128)(2,1)}, bf16[512,128]{1,0:T(8,128)(2,1)S(1)}, u32[]{:S(2)}, u32[]{:S(2)}) collective-permute-start(bf16[512,128]{1,0:T(8,128)(2,1)} %pad_maximum_fusion.6), channel_id=1, source_target_pairs={{0,4},{1,5},{2,6},{3,7},{4,0},{5,1},{6,2},{7,3},{8,12},{9,13},{10,... | collective-permute-start | bytes 393224 | tf_op jit(solution)/shard_map/ppermute | solution.py:458
  218.6 2.1 copy-start.2
  218.9 5.3 %collective-permute-start.7 = (bf16[128,128]{1,0:T(8,128)(2,1)S(1)}, bf16[128,128]{1,0:T(8,128)(2,1)S(1)}, u32[]{:S(2)}, u32[]{:S(2)}) collective-permute-start(bf16[128,128]{1,0:T(8,128)(2,1)S(1)} %slice.116), channel_id=1, source_target_pairs={{0,1},{1,0},{2,3},{3,2},{4,5},{5,4},{6,7},{7,6},{8,9},{9,8},{10,11... | collective-permute-start | bytes 98312 | tf_op jit(solution)/shard_map/ppermute | solution.py:432
  221.1 5.2 %copy-start.19 = (bf16[128,1536]{1,0:T(8,128)(2,1)S(1)}, bf16[128,1536]{1,0:T(8,128)(2,1)}, u32[]{:S(2)}) copy-start(bf16[128,1536]{1,0:T(8,128)(2,1)} %get-tuple-element.58) | copy-start | bytes 1179652
  221.1 7.4 %copy-start.9 = (bf16[128,4,384]{0,2,1:T(8,128)(2,1)S(1)}, bf16[128,4,384]{0,2,1:T(8,128)(2,1)}, u32[]{:S(2)}) copy-start(bf16[128,4,384]{0,2,1:T(8,128)(2,1)} %copy-done.8) | copy-start | bytes 1179652
  221.1 6.9 %collective-permute-start.12 = (bf16[64,384]{1,0:T(8,128)(2,1)S(1)}, bf16[64,384]{1,0:T(8,128)(2,1)S(1)}, u32[]{:S(2)}, u32[]{:S(2)}) collective-permute-start(bf16[64,384]{1,0:T(8,128)(2,1)S(1)} %convolution_convert_fusion.3), channel_id=1, source_target_pairs={{0,8},{8,0},{16,24},{24,16},{32,40},{40,32},{48,56},{56,48},{64,72... | collective-permute-start | bytes 147464 | tf_op jit(solution)/shard_map/ppermute | solution.py:467
  226.3 8.7 %collective-permute-start.8 = (bf16[128,1536]{1,0:T(8,128)(2,1)S(1)}, bf16[128,1536]{1,0:T(8,128)(2,1)S(1)}, u32[]{:S(2)}, u32[]{:S(2)}) collective-permute-start(bf16[128,1536]{1,0:T(8,128)(2,1)S(1)} %copy-done.19), channel_id=1, source_target_pairs={{0,1},{1,0},{2,3},{3,2},{4,5},{5,4},{6,7},{7,6},{8,9},{9,8},{10,11... | collective-permute-start | bytes 1179656 | tf_op jit(solution)/shard_map/ppermute | solution.py:447
  228.0 9.2 %collective-permute-start.13 = (bf16[64,384]{1,0:T(8,128)(2,1)S(1)}, bf16[64,384]{1,0:T(8,128)(2,1)S(1)}, u32[]{:S(2)}, u32[]{:S(2)}) collective-permute-start(bf16[64,384]{1,0:T(8,128)(2,1)S(1)} %add_convert_fusion.3), channel_id=1, source_target_pairs={{0,16},{8,24},{16,0},{24,8},{32,48},{40,56},{48,32},{56,40},{64,80... | collective-permute-start | bytes 147464 | tf_op jit(solution)/shard_map/ppermute | solution.py:467
  228.5 18.5 %copy-start.6 = (bf16[128,3072]{1,0:T(8,128)(2,1)S(1)}, bf16[128,3072]{1,0:T(8,128)(2,1)}, u32[]{:S(2)}) copy-start(bf16[128,3072]{1,0:T(8,128)(2,1)} %copy-done.5) | copy-start | bytes 2359300
  234.9 12.1 %collective-permute-start.9 = (bf16[128,1536]{1,0:T(8,128)(2,1)}, bf16[128,1536]{1,0:T(8,128)(2,1)S(1)}, u32[]{:S(2)}, u32[]{:S(2)}) collective-permute-start(bf16[128,1536]{1,0:T(8,128)(2,1)} %get-tuple-element.61), channel_id=1, source_target_pairs={{0,1},{1,0},{2,3},{3,2},{4,5},{5,4},{6,7},{7,6},{8,9},{9,8},{10,11... | collective-permute-start | bytes 1179656 | tf_op jit(solution)/shard_map/ppermute | solution.py:454
  237.2 9.8 %collective-permute-start.14 = (bf16[64,384]{1,0:T(8,128)(2,1)S(1)}, bf16[64,384]{1,0:T(8,128)(2,1)S(1)}, u32[]{:S(2)}, u32[]{:S(2)}) collective-permute-start(bf16[64,384]{1,0:T(8,128)(2,1)S(1)} %add_convert_fusion.2), channel_id=1, source_target_pairs={{0,32},{8,40},{16,48},{24,56},{32,0},{40,8},{48,16},{56,24},{64,96... | collective-permute-start | bytes 147464 | tf_op jit(solution)/shard_map/ppermute | solution.py:467
  238.8 18.2 %all-to-all-start.7 = ((bf16[16,64,192]{2,1,0:T(8,128)(2,1)}), bf16[16,64,192]{2,1,0:T(8,128)(2,1)S(1)}, u32[]{:S(2)}, u32[]{:S(2)}) async-start(bf16[16,64,192]{2,1,0:T(8,128)(2,1)} %bitcast.29), calls=%async_computation.7 | async-start | bytes 1048576 | tf_op jit(solution)/shard_map/all_to_all | solution.py:25
  257.1 10.8 %collective-permute-start.16 = (bf16[64,192]{1,0:T(8,128)(2,1)S(1)}, bf16[64,192]{1,0:T(8,128)(2,1)S(1)}, u32[]{:S(2)}, u32[]{:S(2)}) collective-permute-start(bf16[64,192]{1,0:T(8,128)(2,1)S(1)} %reduce_sum.127), channel_id=1, source_target_pairs={{0,2},{1,3},{2,0},{3,1},{4,6},{5,7},{6,4},{7,5},{8,10},{9,11},{10,... | collective-permute-start | bytes 73736 | tf_op jit(solution)/shard_map/ppermute | solution.py:488
  259.9 19.6 %collective-permute-start.15 = (bf16[64,384]{1,0:T(8,128)(2,1)S(1)}, bf16[64,384]{1,0:T(8,128)(2,1)S(1)}, u32[]{:S(2)}, u32[]{:S(2)}) collective-permute-start(bf16[64,384]{1,0:T(8,128)(2,1)S(1)} %add_convert_fusion.1), channel_id=1, source_target_pairs={{0,64},{8,72},{16,80},{24,88},{32,96},{40,104},{48,112},{56,120},{... | collective-permute-start | bytes 147464 | tf_op jit(solution)/shard_map/ppermute | solution.py:483
  261.5 16.2 %all-to-all-start.8 = ((bf16[128,1,192]{2,1,0:T(2,128)(2,1)}), bf16[128,1,192]{2,1,0:T(2,128)(2,1)S(1)}, u32[]{:S(2)}, u32[]{:S(2)}) async-start(bf16[128,1,192]{2,1,0:T(2,128)(2,1)} %copy.115), calls=%async_computation.8 | async-start | bytes 262144 | tf_op jit(solution)/shard_map/all_to_all | solution.py:25
  267.9 10.6 %collective-permute-start.17 = (bf16[64,192]{1,0:T(8,128)(2,1)S(1)}, bf16[64,192]{1,0:T(8,128)(2,1)S(1)}, u32[]{:S(2)}, u32[]{:S(2)}) collective-permute-start(bf16[64,192]{1,0:T(8,128)(2,1)S(1)} %add_convert_fusion.5), channel_id=1, source_target_pairs={{0,4},{1,5},{2,6},{3,7},{4,0},{5,1},{6,2},{7,3},{8,12},{9,13},{10,... | collective-permute-start | bytes 73736 | tf_op jit(solution)/shard_map/ppermute | solution.py:488
  278.5 4.3 %collective-permute-start.18 = (bf16[64,192]{1,0:T(8,128)(2,1)S(1)}, bf16[64,192]{1,0:T(8,128)(2,1)S(1)}, u32[]{:S(2)}, u32[]{:S(2)}) collective-permute-start(bf16[64,192]{1,0:T(8,128)(2,1)S(1)} %add_convert_fusion.4), channel_id=1, source_target_pairs={{0,1},{1,0},{2,3},{3,2},{4,5},{5,4},{6,7},{7,6},{8,9},{9,8},{10,11... | collective-permute-start | bytes 73736 | tf_op jit(solution)/shard_map/ppermute | solution.py:488
Sparse Core Ops, SparseCore 0:
  25.4 50.0 all-gather.4
  117.5 74.1 all-gather.6

commit v7 on v6

--- a/solution.py
+++ b/solution.py
@@ -350,27 +350,31 @@
         dora_b, dora_a, (((0,), (1,)), ((), ())), precision=lax.Precision.HIGHEST
     )
     direction_t = direction_t.astype(BF16)
-    rows_y = swap(jnp.broadcast_to(direction_t[None], (n_y, own_cols, own_rows)), "seq", Y_GROUPS)
-    rows_y, own_heads = lax.optimization_barrier((rows_y, own_heads))
+    shifted = [direction_t]
+    for step in range(1, n_y):
+        ahead = [(i, (i + 2 * step) % n_seq) for i in range(n_seq)]
+        shifted.insert(0, lax.ppermute(direction_t, "seq", ahead))
     own_heads = swap(own_heads, "seq", Y_GROUPS)
 
     tokens = enc_states[0, :BLK]
     feat = tokens.shape[1] // n_seq
     hidden = t5_in(enc_states, t5_gain, t5_in_weight)
-    hidden, near_weights = lax.optimization_barrier((hidden, near_weights))
+    hidden, near_weights, shifted = lax.optimization_barrier((hidden, near_weights, shifted))
     weights = gather_columns(weights, near_weights)
     depth = context_weight.shape[0]
     context_all = weights[:, :depth]
+    rows_y = jnp.stack(shifted + shifted[:-1])
+    rows_y = lax.dynamic_slice_in_dim(rows_y, n_y - 1 - seq_rank // 2, n_y, 0)
+    column_sq = jnp.sum(jnp.square(jnp.stack(shifted).astype(F32)), (0, 2))
+    column_other = lax.ppermute(column_sq, "seq", flip_z)
     ffn = t5_out(hidden, t5_out_weight, n_seq)
-    own_heads, ffn, first_heads, second_heads = lax.optimization_barrier(
-        (own_heads, ffn, first_heads, second_heads)
+    own_heads, ffn, first_heads, second_heads, column_other = lax.optimization_barrier(
+        (own_heads, ffn, first_heads, second_heads, column_other)
     )
     second_heads = lax.ppermute(second_heads, "seq", flip_z)
 
     rows_f = rows_y.astype(F32)
-    column_sq = jnp.sum(rows_f * rows_f, (0, 2))
-    column_sq = column_sq + lax.ppermute(column_sq, "seq", flip_z)
-    ratio = magnitude / jnp.sqrt(column_sq + EPSILON)
+    ratio = magnitude / jnp.sqrt(column_sq + column_other + EPSILON)
     scaled_t = (rows_f * ratio[None, :, None]).astype(BF16)
     scaled_t = scaled_t.transpose(1, 0, 2).reshape(own_cols, -1)
     reach = scaled_t.shape[1]
@@ -402,12 +406,13 @@
     target = jnp.arange(n_all, dtype=jnp.int32) // n_seq
     one_hot = (target[:, None] == prompt_owner_sample[None, :]).astype(BF16)
     outgoing = jnp.einsum("sp,pab->sab", one_hot, layer_normed, preferred_element_type=F32)
-    text = swap(outgoing.astype(BF16), both).reshape(BLK, model)
+    num, den = image_attention(own_heads, other_heads, image_qk_gain)
+    outgoing, num, den = lax.optimization_barrier((outgoing.astype(BF16), num, den))
+    text = swap(outgoing, both).reshape(BLK, model)
     scale, shift = to_gathered(text_scale, n_dp), to_gathered(text_shift, n_dp)
     modulated = ((1.0 + scale) * text.astype(F32) + shift).astype(BF16)
     length = jnp.sum(jnp.where(prompt_owner_sample == data_rank, lengths, 0))
 
-    num, den = image_attention(own_heads, other_heads, image_qk_gain)
     down_factor = jnp.pad(dora_a.astype(BF16), ((0, 0), (0, lanes - rank)))
     attended = prompt_attention(
         length.reshape(1),
@@ -431,11 +436,17 @@
     lowered = jnp.sum(gathered[:, :, own_rows:].astype(F32), 0)
     lowered_other = lax.ppermute(lowered[BLK:].astype(BF16), "seq", flip_z)
     gathered = gathered[:, :, :own_rows].transpose(1, 0, 2).reshape(2 * BLK, -1)
-    sent_rows, kept_rows = gathered[BLK:], gathered[:BLK]
     half = model // 2
-    part = dot_t(sent_rows, scaled_all[:half, :reach])
-    sum_first = jnp.sum(part * cotangent_other[:, :half].astype(F32), 0)
-    part = part.astype(BF16)
+
+    def project(rows, at):
+        product = dot_t(rows, scaled_all[at : at + half, :reach])
+        sums = jnp.sum(product[:BLK] * cotangent[:, at : at + half].astype(F32), 0)
+        sums = sums + jnp.sum(product[BLK:] * cotangent_other[:, at : at + half].astype(F32), 0)
+        return product[:BLK], product[BLK:].astype(BF16), sums
+
+    kept_first, sent, sum_first = project(gathered, 0)
+    gathered, sent = lax.optimization_barrier((gathered, sent))
+    landed_first = lax.ppermute(sent, "seq", flip_z)
 
     lowered = (lowered[:BLK] + lowered_other.astype(F32)).astype(BF16)[:, :rank]
     up_part = lax.dot_general(
@@ -443,16 +454,11 @@
     ).astype(BF16)
     up_part = up_part.reshape(rank, n_dp // 2, 2, own_cols).transpose(2, 1, 0, 3)
     up_part = up_part.reshape(n_dp, rank, own_cols)
-    sent_rows, part, up_part = lax.optimization_barrier((sent_rows, part, up_part))
-    landed_first = lax.ppermute(part, "seq", flip_z)
+    gathered, up_part = lax.optimization_barrier((gathered, up_part))
     up_part = swap(up_part, "dp")
-    part = dot_t(sent_rows, scaled_all[half:, :reach])
-    sum_second = jnp.sum(part * cotangent_other[:, half:].astype(F32), 0)
-    kept_rows, part, landed_first = lax.optimization_barrier(
-        (kept_rows, part.astype(BF16), landed_first)
-    )
-    landed_second = lax.ppermute(part, "seq", flip_z)
-    kept = dot_t(kept_rows, scaled_all[:, :reach])
+    kept_second, sent, sum_second = project(gathered, half)
+    sent, landed_first = lax.optimization_barrier((sent, landed_first))
+    landed_second = lax.ppermute(sent, "seq", flip_z)
 
     for bit in (2, 4):
         moved = lax.ppermute(down, "seq", [(i, i ^ bit) for i in range(n_seq)])
@@ -469,17 +475,16 @@
     grad_a = grad_a.astype(BF16)
 
     magnitude_part = jnp.concatenate([sum_first, sum_second])
-    magnitude_part = magnitude_part + jnp.sum(kept * cotangent.astype(F32), 0)
     magnitude_part = magnitude_part.astype(BF16).reshape(n_dp // 2, 2, own_cols).transpose(1, 0, 2)
     magnitude_part = jnp.broadcast_to(
         magnitude_part.reshape(n_dp, 1, own_cols), (n_dp, n_seq, own_cols)
     )
-    magnitude_part, up_part, grad_a = lax.optimization_barrier((magnitude_part, up_part, grad_a))
+    magnitude_part, up_part = lax.optimization_barrier((magnitude_part, up_part))
     magnitude_part = swap(magnitude_part.reshape(n_all, own_cols), both)
     grad_magnitude = jnp.sum(magnitude_part.astype(F32), 0) / magnitude
 
-    out = kept + jnp.concatenate([landed_first, landed_second], 1).astype(F32)
-    image_out = from_gathered(out.astype(BF16), n_dp)[None]
+    out = [kept_first + landed_first.astype(F32), kept_second + landed_second.astype(F32)]
+    image_out = from_gathered(jnp.concatenate(out, 1).astype(BF16), n_dp)[None]
     moved = lax.ppermute(grad_a, "dp", [(i, i ^ 8) for i in range(n_dp)])
     grad_a = (grad_a.astype(F32) + moved.astype(F32)).T
     grad_b = jnp.sum(up_part.astype(F32), 0)

time: 293 us -> 277 us (0.945)
  blocking collectives: 13.1 us -> 0 us
  matrix products: 23.5 us -> 14 us
  waiting for transfers between devices: 83.5 us -> 75.3 us
  local copies, waits for them, and re-layouts: 14.7 us -> 22 us
  starting transfers between devices: 82 us -> 86.2 us
  other arithmetic: 17.7 us -> 21.3 us
    ppermute x3 -> x6, waiting for transfers between devices: 23.8 us -> 1.11 us  [the longest x1 1.1 us: on_device(): column_other = lax.ppermute(column_sq, 'seq', flip_z)]
    ppermute x1, waiting for transfers between devices: 0.01 us -> 19.3 us  [on_device(): second_heads = lax.ppermute(second_heads, 'seq', flip_z)]
    all_to_all x1 -> x0, blocking collectives: 13.1 us -> none  [swap(): lax.all_to_all(values, axes, 0, 0, tiled=True, axis_index_groups=groups)]
    dot_general x4 -> x3, matrix products: 20.3 us -> 10.8 us  [dot_t(): lax.dot_general(left, right, (((1,), (1,)), ((), ())), preferred_element_...]
    unnamed x46 -> x52, local copies, waits for them, and re-layouts: 4.28 us -> 10.3 us
    ppermute x1, waiting for transfers between devices: 4.47 us -> 0.01 us  [on_device(): first_heads = lax.ppermute(first_heads, 'seq', flip_z)]
    reduce_sum x1 -> x2, other arithmetic: 0.2 us -> 3.32 us  [the longest x1 3.12 us: project(): jnp.sum(product[BLK:] * cotangent_other[:, at:at + half].astype(F32), 0)]
    ppermute x3 -> x6, starting transfers between devices: 4.09 us -> 6.79 us  [the longest x3 3.84 us: on_device(): shifted.insert(0, lax.ppermute(direction_t, 'seq', ahead))]
  transfers between devices with their start and end apart: 29 -> 32, of which waited for: 12 -> 10; matrix products, arithmetic and copies ran while one was open for 17% -> 18% of each run, Pallas kernels for 14% -> 15%
where the time goes in v7:
time: 277 us; the launch traced here: 275 us
  starting transfers between devices  86.2 us (31%)
  waiting for transfers between devices  75.3 us (27%)
  Pallas kernels  41.8 us (15%)
  local copies, waits for them, and re-layouts  22 us (8%)
  other arithmetic  21.3 us (8%)
  between operations  14.6 us (5%)
  matrix products  14 us (5%)
    all_to_all x8, starting transfers between devices, swap(): lax.all_to_all(values, axes, 0, 0, tiled=True, axis_index_groups=groups)  47 us
    all_to_all x8, waiting for transfers between devices, swap(): lax.all_to_all(values, axes, 0, 0, tiled=True, axis_index_groups=groups)  42.5 us
    ppermute x1, waiting for transfers between devices, on_device(): second_heads = lax.ppermute(second_heads, 'seq', flip_z)  19.3 us
    pallas_call x1, Pallas kernels, image_attention(): pl.pallas_call(image_kernel, grid=(heads, n_y), in_specs=[queries(), quer...  12.6 us
    dot_general x3, matrix products, dot_t(): lax.dot_general(left, right, (((1,), (1,)), ((), ())), preferred_element_...  10.8 us
    unnamed x52, local copies, waits for them, and re-layouts  10.3 us
    pallas_call x1, Pallas kernels, prompt_attention(): pl.pallas_call(prompt_kernel, grid=(heads + 1,), in_specs=[pl.BlockSpec(m...  9.58 us
    pallas_call x1, Pallas kernels, t5_in(): pl.pallas_call(t5_in_kernel, grid=(units // cut,), in_specs=[pl.BlockSpec...  8.45 us
  transfers between devices with their start and end apart: 32, of which 10 were waited for; matrix products, arithmetic and copies ran while one was open for 18% of the time, Pallas kernels for 15%

profile of v7, /device:TPU:1, one launch (start us, length us, event | category | flops | bytes accessed | tf_op | source)
XLA Modules:
  0.0 275.3 jit_solution(9066418866107003034)
XLA Ops:
  7.2 1.1 copy.126
  8.3 1.0 pad_maximum_fusion.3
  9.3 2.5 collective-permute-start
  12.3 2.8 %collective-permute-start.1 = (bf16[192,384]{1,0:T(8,128)(2,1)S(1)}, bf16[192,384]{1,0:T(8,128)(2,1)S(1)}, u32[]{:S(2)}, u32[]{:S(2)}) collective-permute-start(bf16[192,384]{1,0:T(8,128)(2,1)S(1)} %fusion.11), channel_id=1, source_target_pairs={{0,6},{1,7},{2,0},{3,1},{4,2},{5,3},{6,4},{7,5},{8,14},{9,15},{10,... | collective-permute-start | bytes 442376 | tf_op jit(solution)/shard_map/ppermute | solution.py:356
  16.1 3.9 %shard_map.210 = (bf16[4,384,384]{2,1,0:T(8,128)(2,1)}, bf16[4,192,384]{2,1,0:T(8,128)(2,1)}, bf16[4,192,384]{2,1,0:T(8,128)(2,1)}) custom-call(s32[1]{0:T(128)} %bitcast.1._, bf16[3,128,3072]{2,1,0:T(8,128)(2,1)} %bitcast.102, bf16[3,128,3072]{2,1,0:T(8,128)(2,1)} %bitcast.103), custom_call_target="tpu_custom_call" | custom-call | bytes 4718592 | tf_op jit(solution)/shard_map/pallas_call | solution.py:80
  20.0 8.4 %shard_map.211.hidden_ref = bf16[128,640]{1,0:T(8,128)(2,1)} custom-call(bf16[1,256,4096]{2,1,0:T(8,128)(2,1)} %x_ref.1, f32[1,4096]{1,0:T(1,128)} %bitcast.131, bf16[2,4096,640]{2,1,0:T(8,128)(2,1)} %up_w.1, bf16[2,4096,640]{2,1,0:T(8,128)(2,1)} %up_w.1), custom_call_target="tpu_custom_call" | custom-call | flops 1342177280 | bytes 10485760 | tf_op jit(solution)/shard_map/pallas_call | solution.py:255
  28.7 1.0 pad_maximum_fusion.2
  29.7 3.5 %all-to-all-start = ((bf16[4,384,384]{2,1,0:T(8,128)(2,1)}), bf16[4,384,384]{2,1,0:T(8,128)(2,1)S(1)}, u32[]{:S(2)}, u32[]{:S(2)}) async-start(bf16[4,384,384]{2,1,0:T(8,128)(2,1)} %get-tuple-element.41), calls=%async_computation | async-start | bytes 2359296 | tf_op jit(solution)/shard_map/all_to_all | solution.py:25
  33.3 3.4 %collective-permute-start.4 = (bf16[4,192,384]{2,1,0:T(8,128)(2,1)}, bf16[4,192,384]{2,1,0:T(8,128)(2,1)S(1)}, u32[]{:S(2)}, u32[]{:S(2)}) collective-permute-start(bf16[4,192,384]{2,1,0:T(8,128)(2,1)} %get-tuple-element.45), channel_id=1, source_target_pairs={{0,1},{1,0},{2,3},{3,2},{4,5},{5,4},{6,7},{7,6},{8,9},{9,8},{10,11... | collective-permute-start | bytes 1769480 | tf_op jit(solution)/shard_map/ppermute | solution.py:348
  40.3 7.3 %shard_map.212 = bf16[8,128,512]{2,1,0:T(8,128)(2,1)} custom-call(bf16[128,640]{1,0:T(8,128)(2,1)} %shard_map.211.hidden_ref, bf16[640,4096]{1,0:T(8,128)(2,1)} %out_w.1), custom_call_target="tpu_custom_call" | custom-call | flops 671088640 | bytes 5242880 | tf_op jit(solution)/shard_map/pallas_call | solution.py:284
  47.6 1.1 collective-permute-done.5
  48.7 0.8 copy-done.10
  49.5 6.3 %all-to-all-start.1 = ((bf16[8,128,512]{2,1,0:T(8,128)(2,1)}), bf16[8,128,512]{2,1,0:T(8,128)(2,1)S(1)}, u32[]{:S(2)}, u32[]{:S(2)}) async-start(bf16[8,128,512]{2,1,0:T(8,128)(2,1)} %shard_map.212), calls=%async_computation.1 | async-start | bytes 2097152 | tf_op jit(solution)/shard_map/all_to_all | solution.py:25
  56.5 3.0 %collective-permute-start.6 = (bf16[4,192,384]{2,1,0:T(8,128)(2,1)}, bf16[4,192,384]{2,1,0:T(8,128)(2,1)}, u32[]{:S(2)}, u32[]{:S(2)}) collective-permute-start(bf16[4,192,384]{2,1,0:T(8,128)(2,1)} %get-tuple-element.53), channel_id=1, source_target_pairs={{0,1},{1,0},{2,3},{3,2},{4,5},{5,4},{6,7},{7,6},{8,9},{9,8},{10,11... | collective-permute-start | bytes 1769480 | tf_op jit(solution)/shard_map/ppermute | solution.py:374
  60.2 2.1 fusion.16
  62.3 19.3 %collective-permute-done.6 = bf16[4,192,384]{2,1,0:T(8,128)(2,1)} collective-permute-done((bf16[4,192,384]{2,1,0:T(8,128)(2,1)}, bf16[4,192,384]{2,1,0:T(8,128)(2,1)}, u32[]{:S(2)}, u32[]{:S(2)}) %collective-permute-start.6) | collective-permute-done | bytes 589856 | tf_op jit(solution)/shard_map/ppermute | solution.py:374
  81.7 2.6 pad_maximum_fusion.1
  84.3 5.0 %all-to-all-start.2 = ((bf16[4,384,384]{2,1,0:T(8,128)(2,1)}), bf16[4,384,384]{2,1,0:T(8,128)(2,1)S(1)}, u32[]{:S(2)}, u32[]{:S(2)}) async-start(bf16[4,384,384]{2,1,0:T(8,128)(2,1)} %pad_maximum_fusion.1), calls=%async_computation.2 | async-start | bytes 2359296 | tf_op jit(solution)/shard_map/all_to_all | solution.py:25
  89.4 1.1 copy.125
  90.5 0.9 fusion.15
  91.4 0.8 dynamic_slice.10
  92.3 1.4 convert_reduce_fusion
  93.7 3.0 %fusion.7 = bf16[16,8,24,128]{3,1,2,0:T(8,128)(2,1)S(1)} fusion(bf16[3072,1280]{1,0:T(8,128)(2,1)} %bitcast.99, f32[128,512]{1,0:T(8,128)S(1)} %convert_reduce_fusion, f32[512]{0:T(512)S(1)} %dynamic_slice.10, bf16[1,128,4096]{2,1,0:T(8,128)(2,1)S(1)} %slice-done, s32[]{:T(128)S(6)} %select_n.81), kind=kOutput, calls=%fused_computation.12 | convolution fusion | flops 403308544 | bytes 4327428 | tf_op jit(solution)/shard_map/dot_general | solution.py:56
  96.7 1.0 copy.127
  97.8 7.6 %collective-permute-done.7 = bf16[192,1664]{1,0:T(8,128)(2,1)} collective-permute-done((bf16[192,1664]{1,0:T(8,128)(2,1)}, bf16[192,1664]{1,0:T(8,128)(2,1)}, u32[]{:S(2)}, u32[]{:S(2)}) %collective-permute-start.7) | collective-permute-done | bytes 639008 | tf_op jit(solution)/shard_map/ppermute | solution.py:30
  105.4 1.7 select_bitcast_fusion.1
  107.1 1.2 pad_maximum_fusion
  108.3 11.1 %all-to-all-start.3 = ((bf16[128,24,128]{2,1,0:T(8,128)(2,1)}), bf16[128,24,128]{2,1,0:T(8,128)(2,1)S(1)}, u32[]{:S(2)}, u32[]{:S(2)}) async-start(bf16[128,24,128]{2,1,0:T(8,128)(2,1)} %bitcast.51), calls=%async_computation.3 | async-start | bytes 1572864 | tf_op jit(solution)/shard_map/all_to_all | solution.py:25
  119.5 12.6 %shard_map.213 = (f32[1024,384]{1,0:T(8,128)}, f32[1024,384]{1,0:T(8,128)}) custom-call(bf16[4,384,384]{2,1,0:T(8,128)(2,1)} %copy-done, bf16[4,384,384]{2,1,0:T(8,128)(2,1)} %copy-done.1, bf16[4,384,384]{2,1,0:T(8,128)(2,1)} %copy-done, bf16[4,384,384]{2,1,0:T(8,128)(2,1)} %copy-done.1, bf16[4,384,384]{2,1,0:T(8,128)(2,1)} %copy-done, ...), custom_call_target="tpu_custom_call" | custom-call | flops 2415919104 | bytes 5505024 | tf_op jit(solution)/shard_map/pallas_call | solution.py:130
  132.1 7.2 %all-to-all-done.3 = bf16[128,24,128]{2,1,0:T(8,128)(2,1)S(1)} async-done(((bf16[128,24,128]{2,1,0:T(8,128)(2,1)}), bf16[128,24,128]{2,1,0:T(8,128)(2,1)S(1)}, u32[]{:S(2)}, u32[]{:S(2)}) %all-to-all-start.3) | async-done | bytes 786464 | tf_op jit(solution)/shard_map/all_to_all | solution.py:25
  140.6 1.4 copy.108
  141.9 5.9 %all-to-all-start.4 = ((bf16[128,24,128]{2,1,0:T(8,128)(2,1)}), bf16[128,24,128]{2,1,0:T(8,128)(2,1)S(1)}, u32[]{:S(2)}, u32[]{:S(2)}) async-start(bf16[128,24,128]{2,1,0:T(8,128)(2,1)} %copy.108), calls=%async_computation.4 | async-start | bytes 1572864 | tf_op jit(solution)/shard_map/all_to_all | solution.py:25
  148.6 3.5 %collective-permute-start.9 = (bf16[128,3072]{1,0:T(8,128)(2,1)S(1)}, bf16[128,3072]{1,0:T(8,128)(2,1)}, u32[]{:S(2)}, u32[]{:S(2)}) collective-permute-start(bf16[128,3072]{1,0:T(8,128)(2,1)S(1)} %copy.113), channel_id=1, source_target_pairs={{0,1},{1,0},{2,3},{3,2},{4,5},{5,4},{6,7},{7,6},{8,9},{9,8},{10,11... | collective-permute-start | bytes 2359304 | tf_op jit(solution)/shard_map/ppermute | solution.py:434
  155.2 16.3 %all-to-all-done.4 = bf16[128,24,128]{2,1,0:T(8,128)(2,1)S(1)} async-done(((bf16[128,24,128]{2,1,0:T(8,128)(2,1)}), bf16[128,24,128]{2,1,0:T(8,128)(2,1)S(1)}, u32[]{:S(2)}, u32[]{:S(2)}) %all-to-all-start.4) | async-done | bytes 786464 | tf_op jit(solution)/shard_map/all_to_all | solution.py:25
  171.6 1.1 fusion.6.text_ref
  172.8 9.6 %shard_map.214 = bf16[4,256,512]{2,1,0:T(8,128)(2,1)} custom-call(s32[1]{0:T(128)} %bitcast.length_ref, bf16[4,384,384]{2,1,0:T(8,128)(2,1)} %copy-done, bf16[4,384,384]{2,1,0:T(8,128)(2,1)} %copy-done.1, bf16[128,3072]{1,0:T(8,128)(2,1)} %fusion.6.text_ref, bf16[3072,1280]{1,0:T(8,128)(2,1)} %bitcast.100, bf16[3072,1280]{1,0:T(8,128)(2,1)} %bitcast.101, ...), custom_call_target="tpu_custom_call" | custom-call | flops 905969664 | bytes 9437184 | tf_op jit(solution)/shard_map/pallas_call | solution.py:214
  182.3 3.5 %all-to-all-start.5 = ((bf16[4,256,512]{2,1,0:T(8,128)(2,1)}), bf16[4,256,512]{2,1,0:T(8,128)(2,1)S(1)}, u32[]{:S(2)}, u32[]{:S(2)}) async-start(bf16[4,256,512]{2,1,0:T(8,128)(2,1)} %shard_map.214), calls=%async_computation.5 | async-start | bytes 2097152 | tf_op jit(solution)/shard_map/all_to_all | solution.py:25
  185.9 1.5 fusion.12
  187.5 1.2 collective-permute-start.8
  188.7 3.1 %collective-permute-done.8 = bf16[128,128]{1,0:T(8,128)(2,1)S(1)} collective-permute-done((bf16[128,128]{1,0:T(8,128)(2,1)S(1)}, bf16[128,128]{1,0:T(8,128)(2,1)S(1)}, u32[]{:S(2)}, u32[]{:S(2)}) %collective-permute-start.8) | collective-permute-done | bytes 32800 | tf_op jit(solution)/shard_map/ppermute | solution.py:433
  191.8 7.4 %all-to-all-done.5 = bf16[4,256,512]{2,1,0:T(8,128)(2,1)S(1)} async-done(((bf16[4,256,512]{2,1,0:T(8,128)(2,1)}), bf16[4,256,512]{2,1,0:T(8,128)(2,1)S(1)}, u32[]{:S(2)}, u32[]{:S(2)}) %all-to-all-start.5) | async-done | bytes 1048608 | tf_op jit(solution)/shard_map/all_to_all | solution.py:25
  199.6 1.2 copy.114
  200.8 1.6 collective-permute-done.13
  203.1 4.0 %fusion.2 = f32[256,1536]{1,0:T(8,128)S(1)} fusion(bf16[256,1536]{0,1:T(8,128)(2,1)} %bitcast.122, bf16[3072,1664]{1,0:T(8,128)(2,1)} %bitcast.134), kind=kOutput, calls=%fused_computation.2 | convolution fusion | flops 1207959552 | bytes 7077888 | tf_op jit(solution)/shard_map/dot_general | solution.py:56
  207.2 0.8 slice.136
  208.0 1.7 collective-permute-start.10
  209.8 1.2 collective-permute-start.11
  211.4 4.4 %collective-permute-start.15 = (bf16[64,384]{1,0:T(8,128)(2,1)S(1)}, bf16[64,384]{1,0:T(8,128)(2,1)S(1)}, u32[]{:S(2)}, u32[]{:S(2)}) collective-permute-start(bf16[64,384]{1,0:T(8,128)(2,1)S(1)} %convolution_convert_fusion.3), channel_id=1, source_target_pairs={{0,8},{8,0},{16,24},{24,16},{32,40},{40,32},{48,56},{56,48},{64,72... | collective-permute-start | bytes 147464 | tf_op jit(solution)/shard_map/ppermute | solution.py:473
  216.9 1.0 copy.115
  218.3 3.8 %fusion = f32[256,1536]{1,0:T(8,128)S(1)} fusion(bf16[256,1536]{0,1:T(8,128)(2,1)S(1)} %bitcast.123, bf16[3072,1664]{1,0:T(8,128)(2,1)} %bitcast.135), kind=kOutput, calls=%fused_computation | convolution fusion | flops 1207959552 | bytes 7077888 | tf_op jit(solution)/shard_map/dot_general | solution.py:56
  222.1 1.2 copy-done.6
  223.3 1.6 collective-permute-start.12
  225.0 2.5 collective-permute-start.17
  227.4 6.0 %all-to-all-start.6 = ((bf16[16,64,192]{2,1,0:T(8,128)(2,1)}), bf16[16,64,192]{2,1,0:T(8,128)(2,1)S(1)}, u32[]{:S(2)}, u32[]{:S(2)}) async-start(bf16[16,64,192]{2,1,0:T(8,128)(2,1)} %bitcast.115), calls=%async_computation.6 | async-start | bytes 1048576 | tf_op jit(solution)/shard_map/all_to_all | solution.py:25
  233.5 1.5 collective-permute-start.18
  235.0 3.1 %multiply_reduce_fusion.1 = (f32[1536]{0:T(1024)S(1)}, f32[1536]{0:T(1024)S(1)}, f32[1536]{0:T(1024)S(1)}, f32[1536]{0:T(1024)S(1)}, bf16[128,1536]{1,0:T(8,128)(2,1)S(1)}, /*index=5*/bf16[128,1536]{1,0:T(8,128)(2,1)}) fusion(f32[256,1536]{1,0:T(8,128)} %copy-done.6, bf16[128,3072]{1,0:T(8,128)(2,1)} %collective-permute-done.9, ...), kind=kLoop, calls=%fused_computation.29 | loop fusion | flops 3532800 | bytes 6316032 | tf_op jit(solution)/shard_map/reduce_sum | solution.py:444
  238.3 5.1 %all-to-all-done.6 = bf16[16,64,192]{2,1,0:T(8,128)(2,1)S(1)} async-done(((bf16[16,64,192]{2,1,0:T(8,128)(2,1)}), bf16[16,64,192]{2,1,0:T(8,128)(2,1)S(1)}, u32[]{:S(2)}, u32[]{:S(2)}) %all-to-all-start.6) | async-done | bytes 393248 | tf_op jit(solution)/shard_map/all_to_all | solution.py:25
  243.6 1.2 collective-permute-start.19
  245.4 1.2 copy.117
  246.9 2.5 collective-permute-start.20
  249.5 1.2 copy.123
  251.4 5.6 %all-to-all-start.7 = ((bf16[128,1,192]{2,1,0:T(2,128)(2,1)}), bf16[128,1,192]{2,1,0:T(2,128)(2,1)S(1)}, u32[]{:S(2)}, u32[]{:S(2)}) async-start(bf16[128,1,192]{2,1,0:T(2,128)(2,1)} %copy.122), calls=%async_computation.7 | async-start | bytes 262144 | tf_op jit(solution)/shard_map/all_to_all | solution.py:25
  257.1 3.5 %collective-permute-start.21 = (bf16[64,192]{1,0:T(8,128)(2,1)S(1)}, bf16[64,192]{1,0:T(8,128)(2,1)S(1)}, u32[]{:S(2)}, u32[]{:S(2)}) collective-permute-start(bf16[64,192]{1,0:T(8,128)(2,1)S(1)} %add_convert_fusion.5), channel_id=1, source_target_pairs={{0,1},{1,0},{2,3},{3,2},{4,5},{5,4},{6,7},{7,6},{8,9},{9,8},{10,11... | collective-permute-start | bytes 73736 | tf_op jit(solution)/shard_map/ppermute | solution.py:493
  260.6 6.4 %all-to-all-done.7 = bf16[128,1,192]{2,1,0:T(2,128)(2,1)S(1)} async-done(((bf16[128,1,192]{2,1,0:T(2,128)(2,1)}), bf16[128,1,192]{2,1,0:T(2,128)(2,1)S(1)}, u32[]{:S(2)}, u32[]{:S(2)}) %all-to-all-start.7) | async-done | bytes 49184 | tf_op jit(solution)/shard_map/all_to_all | solution.py:25
  (143 shorter events, 18.7 us)
Async XLA Ops:
  7.2 4.7 %copy-start.13 = (f32[64,192]{1,0:T(8,128)S(1)}, f32[64,192]{1,0:T(8,128)}, u32[]{:S(2)}) copy-start(f32[64,192]{1,0:T(8,128)} %param.35) | copy-start | bytes 147460
  7.2 4.7 %copy-start.12 = (f32[384,64]{0,1:T(8,128)S(1)}, f32[384,64]{0,1:T(8,128)}, u32[]{:S(2)}) copy-start(f32[384,64]{0,1:T(8,128)} %param.34) | copy-start | bytes 294916
  7.2 4.6 %copy-start.14 = (bf16[384,192]{0,1:T(8,128)(2,1)S(1)}, bf16[384,192]{0,1:T(8,128)(2,1)}, u32[]{:S(2)}) copy-start(bf16[384,192]{0,1:T(8,128)(2,1)} %param.33) | copy-start | bytes 442372
  7.2 86.5 %all-gather.5.cloned.1.call-start = ((), (), s32[]{:S(2)}) async-start(), calls=%async_computation.8 | async-start | bytes 8847360 | tf_op jit(solution)/shard_map/all_gather | solution.py:39
  9.3 19.2 %collective-permute-start = (bf16[192,1280]{1,0:T(8,128)(2,1)S(1)}, bf16[192,1280]{1,0:T(8,128)(2,1)S(1)}, u32[]{:S(2)}, u32[]{:S(2)}) collective-permute-start(bf16[192,1280]{1,0:T(8,128)(2,1)S(1)} %pad_maximum_fusion.3), channel_id=1, source_target_pairs={{0,64},{8,72},{16,80},{24,88},{32,96},{40,104},{48,112},{56,120},{... | collective-permute-start | bytes 1474568 | tf_op jit(solution)/shard_map/ppermute | solution.py:30
  12.3 16.2 %collective-permute-start.1 = (bf16[192,384]{1,0:T(8,128)(2,1)S(1)}, bf16[192,384]{1,0:T(8,128)(2,1)S(1)}, u32[]{:S(2)}, u32[]{:S(2)}) collective-permute-start(bf16[192,384]{1,0:T(8,128)(2,1)S(1)} %fusion.11), channel_id=1, source_target_pairs={{0,6},{1,7},{2,0},{3,1},{4,2},{5,3},{6,4},{7,5},{8,14},{9,15},{10,... | collective-permute-start | bytes 442376 | tf_op jit(solution)/shard_map/ppermute | solution.py:356
  15.1 13.4 %collective-permute-start.2 = (bf16[192,384]{1,0:T(8,128)(2,1)S(1)}, bf16[192,384]{1,0:T(8,128)(2,1)S(1)}, u32[]{:S(2)}, u32[]{:S(2)}) collective-permute-start(bf16[192,384]{1,0:T(8,128)(2,1)S(1)} %fusion.11), channel_id=1, source_target_pairs={{0,4},{1,5},{2,6},{3,7},{4,0},{5,1},{6,2},{7,3},{8,12},{9,13},{10,... | collective-permute-start | bytes 442376 | tf_op jit(solution)/shard_map/ppermute | solution.py:356
  15.4 13.0 %collective-permute-start.3 = (bf16[192,384]{1,0:T(8,128)(2,1)S(1)}, bf16[192,384]{1,0:T(8,128)(2,1)S(1)}, u32[]{:S(2)}, u32[]{:S(2)}) collective-permute-start(bf16[192,384]{1,0:T(8,128)(2,1)S(1)} %fusion.11), channel_id=1, source_target_pairs={{0,2},{1,3},{2,4},{3,5},{4,6},{5,7},{6,0},{7,1},{8,10},{9,11},{10,... | collective-permute-start | bytes 442376 | tf_op jit(solution)/shard_map/ppermute | solution.py:356
  20.0 8.5 %copy-start.9 = (bf16[512,192]{0,1:T(8,128)(2,1)S(1)}, bf16[512,192]{0,1:T(8,128)(2,1)}, u32[]{:S(2)}) copy-start(bf16[512,192]{0,1:T(8,128)(2,1)} %param.26) | copy-start | bytes 589828
  29.7 19.0 %all-to-all-start = ((bf16[4,384,384]{2,1,0:T(8,128)(2,1)}), bf16[4,384,384]{2,1,0:T(8,128)(2,1)S(1)}, u32[]{:S(2)}, u32[]{:S(2)}) async-start(bf16[4,384,384]{2,1,0:T(8,128)(2,1)} %get-tuple-element.41), calls=%async_computation | async-start | bytes 2359296 | tf_op jit(solution)/shard_map/all_to_all | solution.py:25
  33.3 15.5 %collective-permute-start.4 = (bf16[4,192,384]{2,1,0:T(8,128)(2,1)}, bf16[4,192,384]{2,1,0:T(8,128)(2,1)S(1)}, u32[]{:S(2)}, u32[]{:S(2)}) collective-permute-start(bf16[4,192,384]{2,1,0:T(8,128)(2,1)} %get-tuple-element.45), channel_id=1, source_target_pairs={{0,1},{1,0},{2,3},{3,2},{4,5},{5,4},{6,7},{7,6},{8,9},{9,8},{10,11... | collective-permute-start | bytes 1769480 | tf_op jit(solution)/shard_map/ppermute | solution.py:348
  36.9 11.9 %collective-permute-start.5 = (f32[192]{0:T(256)S(1)}, f32[192]{0:T(256)S(1)}, u32[]{:S(2)}, u32[]{:S(2)}) collective-permute-start(f32[192]{0:T(256)S(1)} %multiply_reduce_fusion), channel_id=1, source_target_pairs={{0,1},{1,0},{2,3},{3,2},{4,5},{5,4},{6,7},{7,6},{8,9},{9,8},{10,11... | collective-permute-start | bytes 2312 | tf_op jit(solution)/shard_map/ppermute | solution.py:369
  47.6 12.6 %copy-start.17 = (f32[192]{0:T(256)S(1)}, f32[192]{0:T(256)}, u32[]{:S(2)}) copy-start(f32[192]{0:T(256)} %param.36) | copy-start | bytes 2308
  48.7 0.8 copy-start.10
  48.7 13.6 %copy-start = (bf16[4,384,384]{2,1,0:T(8,128)(2,1)}, bf16[4,384,384]{2,1,0:T(8,128)(2,1)S(1)}, u32[]{:S(2)}) copy-start(bf16[4,384,384]{2,1,0:T(8,128)(2,1)S(1)} %all-to-all-done.q_own.k_own.v_own) | copy-start | bytes 3538948
  49.5 32.1 %all-to-all-start.1 = ((bf16[8,128,512]{2,1,0:T(8,128)(2,1)}), bf16[8,128,512]{2,1,0:T(8,128)(2,1)S(1)}, u32[]{:S(2)}, u32[]{:S(2)}) async-start(bf16[8,128,512]{2,1,0:T(8,128)(2,1)} %shard_map.212), calls=%async_computation.1 | async-start | bytes 2097152 | tf_op jit(solution)/shard_map/all_to_all | solution.py:25
  56.5 25.1 %collective-permute-start.6 = (bf16[4,192,384]{2,1,0:T(8,128)(2,1)}, bf16[4,192,384]{2,1,0:T(8,128)(2,1)}, u32[]{:S(2)}, u32[]{:S(2)}) collective-permute-start(bf16[4,192,384]{2,1,0:T(8,128)(2,1)} %get-tuple-element.53), channel_id=1, source_target_pairs={{0,1},{1,0},{2,3},{3,2},{4,5},{5,4},{6,7},{7,6},{8,9},{9,8},{10,11... | collective-permute-start | bytes 1769480 | tf_op jit(solution)/shard_map/ppermute | solution.py:374
  60.2 21.5 %copy-start.11 = (bf16[4,192,384]{2,1,0:T(8,128)(2,1)S(1)}, bf16[4,192,384]{2,1,0:T(8,128)(2,1)}, u32[]{:S(2)}) copy-start(bf16[4,192,384]{2,1,0:T(8,128)(2,1)} %copy-done.10) | copy-start | bytes 1769476
  81.7 2.6 copy-start.3
  84.3 21.1 %all-to-all-start.2 = ((bf16[4,384,384]{2,1,0:T(8,128)(2,1)}), bf16[4,384,384]{2,1,0:T(8,128)(2,1)S(1)}, u32[]{:S(2)}, u32[]{:S(2)}) async-start(bf16[4,384,384]{2,1,0:T(8,128)(2,1)} %pad_maximum_fusion.1), calls=%async_computation.2 | async-start | bytes 2359296 | tf_op jit(solution)/shard_map/all_to_all | solution.py:25
  89.3 96.6 %all-gather.7.cloned.1.call-start = ((), (), s32[]{:S(2)}) async-start(), calls=%async_computation.9 | async-start | bytes 11501568 | tf_op jit(solution)/shard_map/all_gather | solution.py:39
  91.4 2.3 slice-start
  91.4 13.9 %collective-permute-start.7 = (bf16[192,1664]{1,0:T(8,128)(2,1)}, bf16[192,1664]{1,0:T(8,128)(2,1)}, u32[]{:S(2)}, u32[]{:S(2)}) collective-permute-start(bf16[192,1664]{1,0:T(8,128)(2,1)} %fusion.15), channel_id=1, source_target_pairs={{0,64},{8,72},{16,80},{24,88},{32,96},{40,104},{48,112},{56,120},{... | collective-permute-start | bytes 1916936 | tf_op jit(solution)/shard_map/ppermute | solution.py:30
  105.4 2.9 %copy-start.1 = (bf16[4,384,384]{2,1,0:T(8,128)(2,1)}, bf16[4,384,384]{2,1,0:T(8,128)(2,1)S(1)}, u32[]{:S(2)}) copy-start(bf16[4,384,384]{2,1,0:T(8,128)(2,1)S(1)} %all-to-all-done.2.q_other.k_other.v_other) | copy-start | bytes 3538948
  108.3 31.0 %all-to-all-start.3 = ((bf16[128,24,128]{2,1,0:T(8,128)(2,1)}), bf16[128,24,128]{2,1,0:T(8,128)(2,1)S(1)}, u32[]{:S(2)}, u32[]{:S(2)}) async-start(bf16[128,24,128]{2,1,0:T(8,128)(2,1)} %bitcast.51), calls=%async_computation.3 | async-start | bytes 1572864 | tf_op jit(solution)/shard_map/all_to_all | solution.py:25
  119.4 20.6 %copy-start.18 = (s32[16]{0:T(128)S(1)}, s32[16]{0:T(128)}, u32[]{:S(2)}) copy-start(s32[16]{0:T(128)} %param.21) | copy-start | bytes 196
  140.5 7.3 %copy-start.7 = (bf16[1,128,3072]{2,1,0:T(8,128)(2,1)S(1)}, bf16[1,128,3072]{2,1,0:T(8,128)(2,1)}, u32[]{:S(2)}) copy-start(bf16[1,128,3072]{2,1,0:T(8,128)(2,1)} %param.37) | copy-start | bytes 2359300
  141.9 29.5 %all-to-all-start.4 = ((bf16[128,24,128]{2,1,0:T(8,128)(2,1)}), bf16[128,24,128]{2,1,0:T(8,128)(2,1)S(1)}, u32[]{:S(2)}, u32[]{:S(2)}) async-start(bf16[128,24,128]{2,1,0:T(8,128)(2,1)} %copy.108), calls=%async_computation.4 | async-start | bytes 1572864 | tf_op jit(solution)/shard_map/all_to_all | solution.py:25
  148.2 4.5 %copy-start.15 = (f32[1,3072]{1,0:T(1,128)S(1)}, f32[1,3072]{1,0:T(1,128)}, u32[]{:S(2)}) copy-start(f32[1,3072]{1,0:T(1,128)} %param.27) | copy-start | bytes 36868
  148.2 5.3 %copy-start.16 = (f32[1,3072]{1,0:T(1,128)S(1)}, f32[1,3072]{1,0:T(1,128)}, u32[]{:S(2)}) copy-start(f32[1,3072]{1,0:T(1,128)} %param.28) | copy-start | bytes 36868
  148.3 6.3 %copy-start.19 = (s32[16]{0:T(128)S(1)}, s32[16]{0:T(128)}, u32[]{:S(2)}) copy-start(s32[16]{0:T(128)} %param.20) | copy-start | bytes 196
  148.6 43.2 %collective-permute-start.9 = (bf16[128,3072]{1,0:T(8,128)(2,1)S(1)}, bf16[128,3072]{1,0:T(8,128)(2,1)}, u32[]{:S(2)}, u32[]{:S(2)}) collective-permute-start(bf16[128,3072]{1,0:T(8,128)(2,1)S(1)} %copy.113), channel_id=1, source_target_pairs={{0,1},{1,0},{2,3},{3,2},{4,5},{5,4},{6,7},{7,6},{8,9},{9,8},{10,11... | collective-permute-start | bytes 2359304 | tf_op jit(solution)/shard_map/ppermute | solution.py:434
  182.3 16.9 %all-to-all-start.5 = ((bf16[4,256,512]{2,1,0:T(8,128)(2,1)}), bf16[4,256,512]{2,1,0:T(8,128)(2,1)S(1)}, u32[]{:S(2)}, u32[]{:S(2)}) async-start(bf16[4,256,512]{2,1,0:T(8,128)(2,1)} %shard_map.214), calls=%async_computation.5 | async-start | bytes 2097152 | tf_op jit(solution)/shard_map/all_to_all | solution.py:25
  187.5 4.3 %collective-permute-start.8 = (bf16[128,128]{1,0:T(8,128)(2,1)S(1)}, bf16[128,128]{1,0:T(8,128)(2,1)S(1)}, u32[]{:S(2)}, u32[]{:S(2)}) collective-permute-start(bf16[128,128]{1,0:T(8,128)(2,1)S(1)} %fusion.12), channel_id=1, source_target_pairs={{0,1},{1,0},{2,3},{3,2},{4,5},{5,4},{6,7},{7,6},{8,9},{9,8},{10,11... | collective-permute-start | bytes 98312 | tf_op jit(solution)/shard_map/ppermute | solution.py:433
  199.3 3.1 %collective-permute-start.13 = (bf16[256,128]{1,0:T(8,128)(2,1)S(1)}, bf16[256,128]{1,0:T(8,128)(2,1)S(1)}, u32[]{:S(2)}, u32[]{:S(2)}) collective-permute-start(bf16[256,128]{1,0:T(8,128)(2,1)S(1)} %pad_maximum_fusion.7), channel_id=1, source_target_pairs={{0,2},{1,3},{2,0},{3,1},{4,6},{5,7},{6,4},{7,5},{8,10},{9,11},{10,... | collective-permute-start | bytes 196616 | tf_op jit(solution)/shard_map/ppermute | solution.py:464
  202.4 8.6 %collective-permute-start.14 = (bf16[512,128]{1,0:T(8,128)(2,1)S(1)}, bf16[512,128]{1,0:T(8,128)(2,1)S(1)}, u32[]{:S(2)}, u32[]{:S(2)}) collective-permute-start(bf16[512,128]{1,0:T(8,128)(2,1)S(1)} %pad_maximum_fusion.6), channel_id=1, source_target_pairs={{0,4},{1,5},{2,6},{3,7},{4,0},{5,1},{6,2},{7,3},{8,12},{9,13},{10,... | collective-permute-start | bytes 393224 | tf_op jit(solution)/shard_map/ppermute | solution.py:464
  207.1 4.3 %copy-start.4 = (f32[256,1536]{1,0:T(8,128)}, f32[256,1536]{1,0:T(8,128)S(1)}, u32[]{:S(2)}) copy-start(f32[256,1536]{1,0:T(8,128)S(1)} %fusion.2) | copy-start | bytes 4718596
  207.1 3.9 %copy-start.2 = (bf16[4,256,512]{2,1,0:T(8,128)(2,1)S(1)}, bf16[4,256,512]{2,1,0:T(8,128)(2,1)}, u32[]{:S(2)}) copy-start(bf16[4,256,512]{2,1,0:T(8,128)(2,1)} %shard_map.214) | copy-start | bytes 3145732
  208.0 7.8 %collective-permute-start.10 = (bf16[128,128]{1,0:T(8,128)(2,1)S(1)}, bf16[128,128]{1,0:T(8,128)(2,1)S(1)}, u32[]{:S(2)}, u32[]{:S(2)}) collective-permute-start(bf16[128,128]{1,0:T(8,128)(2,1)S(1)} %slice.137), channel_id=1, source_target_pairs={{0,1},{1,0},{2,3},{3,2},{4,5},{5,4},{6,7},{7,6},{8,9},{9,8},{10,11... | collective-permute-start | bytes 98312 | tf_op jit(solution)/shard_map/ppermute | solution.py:437
  209.8 13.6 %collective-permute-start.11 = (bf16[128,1536]{1,0:T(8,128)(2,1)}, bf16[128,1536]{1,0:T(8,128)(2,1)}, u32[]{:S(2)}, u32[]{:S(2)}) collective-permute-start(bf16[128,1536]{1,0:T(8,128)(2,1)} %slice.136), channel_id=1, source_target_pairs={{0,1},{1,0},{2,3},{3,2},{4,5},{5,4},{6,7},{7,6},{8,9},{9,8},{10,11... | collective-permute-start | bytes 1179656 | tf_op jit(solution)/shard_map/ppermute | solution.py:449
  211.4 6.9 %copy-start.8 = (bf16[256,4,384]{0,2,1:T(8,128)(2,1)S(1)}, bf16[256,4,384]{0,2,1:T(8,128)(2,1)}, u32[]{:S(2)}) copy-start(bf16[256,4,384]{0,2,1:T(8,128)(2,1)} %copy.114) | copy-start | bytes 2359300
  211.4 6.5 %collective-permute-start.15 = (bf16[64,384]{1,0:T(8,128)(2,1)S(1)}, bf16[64,384]{1,0:T(8,128)(2,1)S(1)}, u32[]{:S(2)}, u32[]{:S(2)}) collective-permute-start(bf16[64,384]{1,0:T(8,128)(2,1)S(1)} %convolution_convert_fusion.3), channel_id=1, source_target_pairs={{0,8},{8,0},{16,24},{24,16},{32,40},{40,32},{48,56},{56,48},{64,72... | collective-permute-start | bytes 147464 | tf_op jit(solution)/shard_map/ppermute | solution.py:473
  217.9 7.1 %collective-permute-start.16 = (bf16[64,384]{1,0:T(8,128)(2,1)S(1)}, bf16[64,384]{1,0:T(8,128)(2,1)S(1)}, u32[]{:S(2)}, u32[]{:S(2)}) collective-permute-start(bf16[64,384]{1,0:T(8,128)(2,1)S(1)} %add_convert_fusion.4), channel_id=1, source_target_pairs={{0,16},{8,24},{16,0},{24,8},{32,48},{40,56},{48,32},{56,40},{64,80... | collective-permute-start | bytes 147464 | tf_op jit(solution)/shard_map/ppermute | solution.py:473
  222.1 1.2 copy-start.6
  223.3 11.7 %copy-start.5 = (f32[256,1536]{1,0:T(8,128)S(1)}, f32[256,1536]{1,0:T(8,128)}, u32[]{:S(2)}) copy-start(f32[256,1536]{1,0:T(8,128)} %copy-done.4) | copy-start | bytes 4718596
  223.3 11.7 %collective-permute-start.12 = (bf16[128,1536]{1,0:T(8,128)(2,1)S(1)}, bf16[128,1536]{1,0:T(8,128)(2,1)}, u32[]{:S(2)}, u32[]{:S(2)}) collective-permute-start(bf16[128,1536]{1,0:T(8,128)(2,1)S(1)} %slice.135), channel_id=1, source_target_pairs={{0,1},{1,0},{2,3},{3,2},{4,5},{5,4},{6,7},{7,6},{8,9},{9,8},{10,11... | collective-permute-start | bytes 1179656 | tf_op jit(solution)/shard_map/ppermute | solution.py:461
  225.0 8.5 %collective-permute-start.17 = (bf16[64,384]{1,0:T(8,128)(2,1)S(1)}, bf16[64,384]{1,0:T(8,128)(2,1)S(1)}, u32[]{:S(2)}, u32[]{:S(2)}) collective-permute-start(bf16[64,384]{1,0:T(8,128)(2,1)S(1)} %add_convert_fusion.3), channel_id=1, source_target_pairs={{0,32},{8,40},{16,48},{24,56},{32,0},{40,8},{48,16},{56,24},{64,96... | collective-permute-start | bytes 147464 | tf_op jit(solution)/shard_map/ppermute | solution.py:473
  227.4 16.0 %all-to-all-start.6 = ((bf16[16,64,192]{2,1,0:T(8,128)(2,1)}), bf16[16,64,192]{2,1,0:T(8,128)(2,1)S(1)}, u32[]{:S(2)}, u32[]{:S(2)}) async-start(bf16[16,64,192]{2,1,0:T(8,128)(2,1)} %bitcast.115), calls=%async_computation.6 | async-start | bytes 1048576 | tf_op jit(solution)/shard_map/all_to_all | solution.py:25
  233.5 11.3 %collective-permute-start.18 = (bf16[64,384]{1,0:T(8,128)(2,1)S(1)}, bf16[64,384]{1,0:T(8,128)(2,1)S(1)}, u32[]{:S(2)}, u32[]{:S(2)}) collective-permute-start(bf16[64,384]{1,0:T(8,128)(2,1)S(1)} %add_convert_fusion.2), channel_id=1, source_target_pairs={{0,64},{8,72},{16,80},{24,88},{32,96},{40,104},{48,112},{56,120},{... | collective-permute-start | bytes 147464 | tf_op jit(solution)/shard_map/ppermute | solution.py:488
  243.6 3.3 %collective-permute-start.19 = (bf16[64,192]{1,0:T(8,128)(2,1)S(1)}, bf16[64,192]{1,0:T(8,128)(2,1)S(1)}, u32[]{:S(2)}, u32[]{:S(2)}) collective-permute-start(bf16[64,192]{1,0:T(8,128)(2,1)S(1)} %reduce_sum.134), channel_id=1, source_target_pairs={{0,2},{1,3},{2,0},{3,1},{4,6},{5,7},{6,4},{7,5},{8,10},{9,11},{10,... | collective-permute-start | bytes 73736 | tf_op jit(solution)/shard_map/ppermute | solution.py:493
  246.9 10.1 %collective-permute-start.20 = (bf16[64,192]{1,0:T(8,128)(2,1)S(1)}, bf16[64,192]{1,0:T(8,128)(2,1)S(1)}, u32[]{:S(2)}, u32[]{:S(2)}) collective-permute-start(bf16[64,192]{1,0:T(8,128)(2,1)S(1)} %add_convert_fusion.6), channel_id=1, source_target_pairs={{0,4},{1,5},{2,6},{3,7},{4,0},{5,1},{6,2},{7,3},{8,12},{9,13},{10,... | collective-permute-start | bytes 73736 | tf_op jit(solution)/shard_map/ppermute | solution.py:493
  251.4 15.6 %all-to-all-start.7 = ((bf16[128,1,192]{2,1,0:T(2,128)(2,1)}), bf16[128,1,192]{2,1,0:T(2,128)(2,1)S(1)}, u32[]{:S(2)}, u32[]{:S(2)}) async-start(bf16[128,1,192]{2,1,0:T(2,128)(2,1)} %copy.122), calls=%async_computation.7 | async-start | bytes 262144 | tf_op jit(solution)/shard_map/all_to_all | solution.py:25
  257.1 10.7 %collective-permute-start.21 = (bf16[64,192]{1,0:T(8,128)(2,1)S(1)}, bf16[64,192]{1,0:T(8,128)(2,1)S(1)}, u32[]{:S(2)}, u32[]{:S(2)}) collective-permute-start(bf16[64,192]{1,0:T(8,128)(2,1)S(1)} %add_convert_fusion.5), channel_id=1, source_target_pairs={{0,1},{1,0},{2,3},{3,2},{4,5},{5,4},{6,7},{7,6},{8,9},{9,8},{10,11... | collective-permute-start | bytes 73736 | tf_op jit(solution)/shard_map/ppermute | solution.py:493
Sparse Core Ops, SparseCore 0:
  29.8 50.0 all-gather.4
  108.4 74.0 all-gather.6

commit v8 on v7

--- a/solution.py
+++ b/solution.py
@@ -363,27 +363,34 @@
     weights = gather_columns(weights, near_weights)
     depth = context_weight.shape[0]
     context_all = weights[:, :depth]
-    rows_y = jnp.stack(shifted + shifted[:-1])
-    rows_y = lax.dynamic_slice_in_dim(rows_y, n_y - 1 - seq_rank // 2, n_y, 0)
     column_sq = jnp.sum(jnp.square(jnp.stack(shifted).astype(F32)), (0, 2))
     column_other = lax.ppermute(column_sq, "seq", flip_z)
+    hidden, own_heads, first_heads, second_heads = lax.optimization_barrier(
+        (hidden, own_heads, first_heads, second_heads)
+    )
+    second_heads = lax.ppermute(second_heads, "seq", flip_z)
     ffn = t5_out(hidden, t5_out_weight, n_seq)
-    own_heads, ffn, first_heads, second_heads, column_other = lax.optimization_barrier(
-        (own_heads, ffn, first_heads, second_heads, column_other)
-    )
-    second_heads = lax.ppermute(second_heads, "seq", flip_z)
-
-    rows_f = rows_y.astype(F32)
+    ffn, column_other = lax.optimization_barrier((ffn, column_other))
+
     ratio = magnitude / jnp.sqrt(column_sq + column_other + EPSILON)
-    scaled_t = (rows_f * ratio[None, :, None]).astype(BF16)
-    scaled_t = scaled_t.transpose(1, 0, 2).reshape(own_cols, -1)
+    scaled_t = []
+    for row in range(n_y):
+        turned = [shifted[(row - at - 1) % n_y] for at in range(n_y)]
+        block = lax.select_n(seq_rank // 2, *turned)
+        scaled_t.append((block.astype(F32) * ratio[:, None]).astype(BF16))
+    scaled_t = jnp.concatenate(scaled_t, 1)
     reach = scaled_t.shape[1]
     up = jnp.pad((dora_b * ratio).astype(BF16).T, ((0, 0), (0, lanes - rank)))
     scaled_t = jnp.concatenate([scaled_t, up], 1)
     near_scaled = near_shard(scaled_t)
 
     ffn = swap(ffn, "seq")
-    ffn, second_heads = lax.optimization_barrier((ffn, second_heads))
+    ffn, second_heads, near_scaled, cotangent = lax.optimization_barrier(
+        (ffn, second_heads, near_scaled, cotangent)
+    )
+    cotangent_other = lax.ppermute(cotangent, "seq", flip_z)
+    scaled_all = gather_columns(scaled_t, near_scaled)
+    up_all = scaled_all[:, reach:]
     ffn_sum = jnp.sum(ffn.astype(F32), 0)
 
     other_heads = swap(jnp.concatenate([first_heads, second_heads], 1), "seq", Y_GROUPS)
@@ -392,11 +399,9 @@
     own_final = lax.dynamic_slice_in_dim(t5_final_gain, seq_rank * feat, feat, 0)
     encoded = ((own_tokens + ffn_sum) * own_final).astype(BF16)
     context = dot_t(encoded, context_all).astype(BF16).reshape(BLK, rows_of, lanes)
-    context, other_heads, near_scaled = lax.optimization_barrier(
-        (context, other_heads, near_scaled)
-    )
-    scaled_all = gather_columns(scaled_t, near_scaled)
-    up_all = scaled_all[:, reach:]
+    context, other_heads, cotangent_other = lax.optimization_barrier(
+        (context, other_heads, cotangent_other)
+    )
     arrived = swap(context, both)
     token_of = jnp.sum(arrived.reshape(n_dp, n_seq, rows_of, lanes).astype(F32), 1).astype(BF16)
     values = token_of.astype(F32)
@@ -431,9 +436,9 @@
     gathered = swap(attended, "seq", Y_GROUPS)
     down = jnp.dot(cotangent, up_all, preferred_element_type=F32).astype(BF16)
     down = jnp.concatenate([down, lax.ppermute(down, "seq", flip_z)], 0)
-    cotangent_other = lax.ppermute(cotangent, "seq", flip_z)
-    gathered, down, cotangent_other = lax.optimization_barrier((gathered, down, cotangent_other))
+    gathered, down = lax.optimization_barrier((gathered, down))
     lowered = jnp.sum(gathered[:, :, own_rows:].astype(F32), 0)
+    gathered, lowered = lax.optimization_barrier((gathered, lowered))
     lowered_other = lax.ppermute(lowered[BLK:].astype(BF16), "seq", flip_z)
     gathered = gathered[:, :, :own_rows].transpose(1, 0, 2).reshape(2 * BLK, -1)
     half = model // 2
@@ -457,7 +462,9 @@
     gathered, up_part = lax.optimization_barrier((gathered, up_part))
     up_part = swap(up_part, "dp")
     kept_second, sent, sum_second = project(gathered, half)
-    sent, landed_first = lax.optimization_barrier((sent, landed_first))
+    sent, sum_second, landed_first, up_part = lax.optimization_barrier(
+        (sent, sum_second, landed_first, up_part)
+    )
     landed_second = lax.ppermute(sent, "seq", flip_z)
 
     for bit in (2, 4):

time: 277 us -> 308 us (1.11)
  waiting for transfers between devices: 75.3 us -> 101 us
  other arithmetic: 21.3 us -> 28.4 us
  local copies, waits for them, and re-layouts: 22 us -> 17.1 us
    ppermute x1, waiting for transfers between devices: 19.3 us -> 34.2 us  [on_device(): second_heads = lax.ppermute(second_heads, 'seq', flip_z)]
    ppermute x1, waiting for transfers between devices: 0.01 us -> 11.4 us  [on_device(): first_heads = lax.ppermute(first_heads, 'seq', flip_z)]
    ppermute x1, waiting for transfers between devices: 0.01 us -> 9.7 us  [on_device(): cotangent_other = lax.ppermute(cotangent, 'seq', flip_z)]
    ppermute x2, waiting for transfers between devices: 7.59 us -> 0.01 us  [near_shard(): lax.ppermute(values, 'dp', [(i, (i + n_dp // 2) % n_dp) for i in range(n_...]
    all_to_all x8, waiting for transfers between devices: 42.5 us -> 36 us  [swap(): lax.all_to_all(values, axes, 0, 0, tiled=True, axis_index_groups=groups)]
    ppermute x3, waiting for transfers between devices: 0.01 us -> 4.45 us  [on_device(): moved = lax.ppermute(grad_a, 'dp', [(i, i ^ bit) for i in range(n_dp)])]
    unnamed x52 -> x43, local copies, waits for them, and re-layouts: 10.3 us -> 6.17 us
  transfers between devices with their start and end apart: 32 -> 32, of which waited for: 10 -> 11; matrix products, arithmetic and copies ran while one was open for 18% -> 18% of each run, Pallas kernels for 15% -> 14%
where the time goes in v8:
time: 308 us; the launch traced here: 305 us
  waiting for transfers between devices  101 us (33%)
  starting transfers between devices  86.5 us (28%)
  Pallas kernels  41.9 us (14%)
  other arithmetic  28.4 us (9%)
  local copies, waits for them, and re-layouts  17.1 us (6%)
  matrix products  16.2 us (5%)
  between operations  14.6 us (5%)
    all_to_all x8, starting transfers between devices, swap(): lax.all_to_all(values, axes, 0, 0, tiled=True, axis_index_groups=groups)  49.2 us
    all_to_all x8, waiting for transfers between devices, swap(): lax.all_to_all(values, axes, 0, 0, tiled=True, axis_index_groups=groups)  36 us
    ppermute x1, waiting for transfers between devices, on_device(): second_heads = lax.ppermute(second_heads, 'seq', flip_z)  34.2 us
    pallas_call x1, Pallas kernels, image_attention(): pl.pallas_call(image_kernel, grid=(heads, n_y), in_specs=[queries(), quer...  12.4 us
    ppermute x1, waiting for transfers between devices, on_device(): first_heads = lax.ppermute(first_heads, 'seq', flip_z)  11.4 us
    dot_general x3, matrix products, dot_t(): lax.dot_general(left, right, (((1,), (1,)), ((), ())), preferred_element_...  11.3 us
    ppermute x1, waiting for transfers between devices, on_device(): cotangent_other = lax.ppermute(cotangent, 'seq', flip_z)  9.7 us
    pallas_call x1, Pallas kernels, prompt_attention(): pl.pallas_call(prompt_kernel, grid=(heads + 1,), in_specs=[pl.BlockSpec(m...  9.47 us
  transfers between devices with their start and end apart: 32, of which 11 were waited for; matrix products, arithmetic and copies ran while one was open for 18% of the time, Pallas kernels for 14%

profile of v8, /device:TPU:1, one launch (start us, length us, event | category | flops | bytes accessed | tf_op | source)
XLA Modules:
  0.0 305.3 jit_solution(12513540002607284633)
XLA Ops:
  7.2 1.1 copy.129
  9.3 2.5 collective-permute-start
  12.3 2.8 collective-permute-start.1
  16.1 3.9 %shard_map.210 = (bf16[4,384,384]{2,1,0:T(8,128)(2,1)}, bf16[4,192,384]{2,1,0:T(8,128)(2,1)}, bf16[4,192,384]{2,1,0:T(8,128)(2,1)}) custom-call(s32[1]{0:T(128)} %bitcast.1._, bf16[3,128,3072]{2,1,0:T(8,128)(2,1)} %bitcast.89, bf16[3,128,3072]{2,1,0:T(8,128)(2,1)} %bitcast.90), custom_call_target="tpu_custom_call" | custom-call | bytes 4718592 | tf_op jit(solution)/shard_map/pallas_call | solution.py:80
  20.0 8.4 %shard_map.211.hidden_ref = bf16[128,640]{1,0:T(8,128)(2,1)} custom-call(bf16[1,256,4096]{2,1,0:T(8,128)(2,1)} %x_ref.1, f32[1,4096]{1,0:T(1,128)} %bitcast.116, bf16[2,4096,640]{2,1,0:T(8,128)(2,1)} %up_w.1, bf16[2,4096,640]{2,1,0:T(8,128)(2,1)} %up_w.1), custom_call_target="tpu_custom_call" | custom-call | flops 1342177280 | bytes 10485760 | tf_op jit(solution)/shard_map/pallas_call | solution.py:255
  28.6 1.0 pad_maximum_fusion.2
  29.7 3.7 %all-to-all-start = ((bf16[4,384,384]{2,1,0:T(8,128)(2,1)}), bf16[4,384,384]{2,1,0:T(8,128)(2,1)S(1)}, u32[]{:S(2)}, u32[]{:S(2)}) async-start(bf16[4,384,384]{2,1,0:T(8,128)(2,1)} %get-tuple-element.50), calls=%async_computation | async-start | bytes 2359296 | tf_op jit(solution)/shard_map/all_to_all | solution.py:25
  33.4 3.4 %collective-permute-start.4 = (bf16[4,192,384]{2,1,0:T(8,128)(2,1)S(1)}, bf16[4,192,384]{2,1,0:T(8,128)(2,1)S(1)}, u32[]{:S(2)}, u32[]{:S(2)}) collective-permute-start(bf16[4,192,384]{2,1,0:T(8,128)(2,1)S(1)} %copy-done.17), channel_id=1, source_target_pairs={{0,1},{1,0},{2,3},{3,2},{4,5},{5,4},{6,7},{7,6},{8,9},{9,8},{10,11... | collective-permute-start | bytes 1769480 | tf_op jit(solution)/shard_map/ppermute | solution.py:348
  37.2 11.4 %collective-permute-done.4 = bf16[4,192,384]{2,1,0:T(8,128)(2,1)S(1)} collective-permute-done((bf16[4,192,384]{2,1,0:T(8,128)(2,1)S(1)}, bf16[4,192,384]{2,1,0:T(8,128)(2,1)S(1)}, u32[]{:S(2)}, u32[]{:S(2)}) %collective-permute-start.4) | collective-permute-done | bytes 589856 | tf_op jit(solution)/shard_map/ppermute | solution.py:348
  48.6 7.7 %shard_map.212 = bf16[8,128,512]{2,1,0:T(8,128)(2,1)} custom-call(bf16[128,640]{1,0:T(8,128)(2,1)} %shard_map.211.hidden_ref, bf16[640,4096]{1,0:T(8,128)(2,1)} %out_w.1), custom_call_target="tpu_custom_call" | custom-call | flops 671088640 | bytes 5242880 | tf_op jit(solution)/shard_map/pallas_call | solution.py:284
  56.4 6.3 %all-to-all-start.1 = ((bf16[8,128,512]{2,1,0:T(8,128)(2,1)}), bf16[8,128,512]{2,1,0:T(8,128)(2,1)S(1)}, u32[]{:S(2)}, u32[]{:S(2)}) async-start(bf16[8,128,512]{2,1,0:T(8,128)(2,1)} %shard_map.212), calls=%async_computation.1 | async-start | bytes 2097152 | tf_op jit(solution)/shard_map/all_to_all | solution.py:25
  63.4 3.0 collective-permute-start.6
  66.4 1.5 copy.108
  68.0 34.2 %collective-permute-done.6 = bf16[4,192,384]{2,1,0:T(8,128)(2,1)} collective-permute-done((bf16[4,192,384]{2,1,0:T(8,128)(2,1)}, bf16[4,192,384]{2,1,0:T(8,128)(2,1)}, u32[]{:S(2)}, u32[]{:S(2)}) %collective-permute-start.6) | collective-permute-done | bytes 589856 | tf_op jit(solution)/shard_map/ppermute | solution.py:371
  102.2 1.6 select_bitcast_fusion.1
  103.8 1.2 pad_maximum_fusion
  105.0 2.2 pad_maximum_fusion.1
  107.2 5.0 %all-to-all-start.2 = ((bf16[4,384,384]{2,1,0:T(8,128)(2,1)}), bf16[4,384,384]{2,1,0:T(8,128)(2,1)S(1)}, u32[]{:S(2)}, u32[]{:S(2)}) async-start(bf16[4,384,384]{2,1,0:T(8,128)(2,1)} %pad_maximum_fusion.1), calls=%async_computation.2 | async-start | bytes 2359296 | tf_op jit(solution)/shard_map/all_to_all | solution.py:25
  112.2 1.2 copy.110
  113.4 1.8 collective-permute-start.8
  115.9 1.5 convert_reduce_fusion
  117.5 3.8 %fusion.7 = bf16[16,8,24,128]{3,1,2,0:T(8,128)(2,1)S(1)} fusion(bf16[3072,1280]{1,0:T(8,128)(2,1)} %bitcast.86, f32[128,512]{1,0:T(8,128)S(1)} %convert_reduce_fusion, f32[512]{0:T(512)S(1)} %dynamic_slice.7, bf16[1,128,4096]{2,1,0:T(8,128)(2,1)S(1)} %slice-done, s32[]{:T(128)S(6)} %select_n.153), kind=kOutput, calls=%fused_computation.12 | convolution fusion | flops 403308544 | bytes 4327428 | tf_op jit(solution)/shard_map/dot_general | solution.py:56
  121.3 1.0 copy.130
  122.3 9.7 %collective-permute-done.8 = bf16[128,3072]{1,0:T(8,128)(2,1)} collective-permute-done((bf16[128,3072]{1,0:T(8,128)(2,1)}, bf16[128,3072]{1,0:T(8,128)(2,1)}, u32[]{:S(2)}, u32[]{:S(2)}) %collective-permute-start.8) | collective-permute-done | bytes 786464 | tf_op jit(solution)/shard_map/ppermute | solution.py:391
  132.0 11.1 %all-to-all-start.3 = ((bf16[128,24,128]{2,1,0:T(8,128)(2,1)}), bf16[128,24,128]{2,1,0:T(8,128)(2,1)S(1)}, u32[]{:S(2)}, u32[]{:S(2)}) async-start(bf16[128,24,128]{2,1,0:T(8,128)(2,1)} %bitcast.47), calls=%async_computation.3 | async-start | bytes 1572864 | tf_op jit(solution)/shard_map/all_to_all | solution.py:25
  143.2 12.4 %shard_map.213 = (f32[1024,384]{1,0:T(8,128)}, f32[1024,384]{1,0:T(8,128)}) custom-call(bf16[4,384,384]{2,1,0:T(8,128)(2,1)} %copy-done, bf16[4,384,384]{2,1,0:T(8,128)(2,1)} %copy-done.1, bf16[4,384,384]{2,1,0:T(8,128)(2,1)} %copy-done, bf16[4,384,384]{2,1,0:T(8,128)(2,1)} %copy-done.1, bf16[4,384,384]{2,1,0:T(8,128)(2,1)} %copy-done, ...), custom_call_target="tpu_custom_call" | custom-call | flops 2415919104 | bytes 5505024 | tf_op jit(solution)/shard_map/pallas_call | solution.py:130
  155.5 11.2 %all-to-all-done.3 = bf16[128,24,128]{2,1,0:T(8,128)(2,1)S(1)} async-done(((bf16[128,24,128]{2,1,0:T(8,128)(2,1)}), bf16[128,24,128]{2,1,0:T(8,128)(2,1)S(1)}, u32[]{:S(2)}, u32[]{:S(2)}) %all-to-all-start.3) | async-done | bytes 786464 | tf_op jit(solution)/shard_map/all_to_all | solution.py:25
  168.0 1.4 copy.113
  169.4 5.5 %all-to-all-start.4 = ((bf16[128,24,128]{2,1,0:T(8,128)(2,1)}), bf16[128,24,128]{2,1,0:T(8,128)(2,1)S(1)}, u32[]{:S(2)}, u32[]{:S(2)}) async-start(bf16[128,24,128]{2,1,0:T(8,128)(2,1)} %copy.113), calls=%async_computation.4 | async-start | bytes 1572864 | tf_op jit(solution)/shard_map/all_to_all | solution.py:25
  178.0 12.1 %all-to-all-done.4 = bf16[128,24,128]{2,1,0:T(8,128)(2,1)S(1)} async-done(((bf16[128,24,128]{2,1,0:T(8,128)(2,1)}), bf16[128,24,128]{2,1,0:T(8,128)(2,1)S(1)}, u32[]{:S(2)}, u32[]{:S(2)}) %all-to-all-start.4) | async-done | bytes 786464 | tf_op jit(solution)/shard_map/all_to_all | solution.py:25
  190.3 1.1 fusion.6.text_ref
  191.4 9.5 %shard_map.214 = bf16[4,256,512]{2,1,0:T(8,128)(2,1)} custom-call(s32[1]{0:T(128)} %bitcast.length_ref, bf16[4,384,384]{2,1,0:T(8,128)(2,1)} %copy-done, bf16[4,384,384]{2,1,0:T(8,128)(2,1)} %copy-done.1, bf16[128,3072]{1,0:T(8,128)(2,1)} %fusion.6.text_ref, bf16[3072,1280]{1,0:T(8,128)(2,1)} %bitcast.87, bf16[3072,1280]{1,0:T(8,128)(2,1)} %bitcast.88, ...), custom_call_target="tpu_custom_call" | custom-call | flops 905969664 | bytes 9437184 | tf_op jit(solution)/shard_map/pallas_call | solution.py:214
  200.9 3.5 %all-to-all-start.5 = ((bf16[4,256,512]{2,1,0:T(8,128)(2,1)}), bf16[4,256,512]{2,1,0:T(8,128)(2,1)S(1)}, u32[]{:S(2)}, u32[]{:S(2)}) async-start(bf16[4,256,512]{2,1,0:T(8,128)(2,1)} %shard_map.214), calls=%async_computation.5 | async-start | bytes 2097152 | tf_op jit(solution)/shard_map/all_to_all | solution.py:25
  204.4 1.5 convolution_convert_fusion.4
  206.0 1.5 collective-permute-start.9
  207.5 2.9 collective-permute-done.9
  211.0 7.0 %all-to-all-done.5 = bf16[4,256,512]{2,1,0:T(8,128)(2,1)S(1)} async-done(((bf16[4,256,512]{2,1,0:T(8,128)(2,1)}), bf16[4,256,512]{2,1,0:T(8,128)(2,1)S(1)}, u32[]{:S(2)}, u32[]{:S(2)}) %all-to-all-start.5) | async-done | bytes 1048608 | tf_op jit(solution)/shard_map/all_to_all | solution.py:25
  218.8 3.8 %fusion.2 = f32[256,1536]{1,0:T(8,128)S(1)} fusion(bf16[256,1536]{0,1:T(8,128)(2,1)S(1)} %bitcast.107, bf16[3072,1664]{1,0:T(8,128)(2,1)} %bitcast.119), kind=kOutput, calls=%fused_computation.2 | convolution fusion | flops 1207959552 | bytes 7077888 | tf_op jit(solution)/shard_map/dot_general | solution.py:56
  222.7 1.4 collective-permute-start.10
  224.0 1.7 collective-permute-start.11
  226.6 1.9 collective-permute-start.14
  229.6 1.0 copy.117
  230.5 1.9 collective-permute-done.14
  232.4 2.0 convolution_convert_fusion.3
  234.5 4.0 %collective-permute-start.15 = (bf16[64,384]{1,0:T(8,128)(2,1)}, bf16[64,384]{1,0:T(8,128)(2,1)}, u32[]{:S(2)}, u32[]{:S(2)}) collective-permute-start(bf16[64,384]{1,0:T(8,128)(2,1)} %convolution_convert_fusion.3), channel_id=1, source_target_pairs={{0,8},{8,0},{16,24},{24,16},{32,40},{40,32},{48,56},{56,48},{64,72... | collective-permute-start | bytes 147464 | tf_op jit(solution)/shard_map/ppermute | solution.py:480
  238.5 3.8 %fusion = f32[256,1536]{1,0:T(8,128)S(1)} fusion(bf16[256,1536]{0,1:T(8,128)(2,1)S(1)} %bitcast.108, bf16[3072,1664]{1,0:T(8,128)(2,1)} %bitcast.120), kind=kOutput, calls=%fused_computation | convolution fusion | flops 1207959552 | bytes 7077888 | tf_op jit(solution)/shard_map/dot_general | solution.py:56
  242.3 4.1 %all-to-all-start.6 = ((bf16[16,64,192]{2,1,0:T(8,128)(2,1)}), bf16[16,64,192]{2,1,0:T(8,128)(2,1)}, u32[]{:S(2)}, u32[]{:S(2)}) async-start(bf16[16,64,192]{2,1,0:T(8,128)(2,1)} %bitcast.104), calls=%async_computation.6 | async-start | bytes 1048576 | tf_op jit(solution)/shard_map/all_to_all | solution.py:25
  247.3 1.3 collective-permute-start.16
  248.6 2.4 multiply_reduce_fusion.3
  251.0 4.3 %collective-permute-done.16 = bf16[64,384]{1,0:T(8,128)(2,1)S(1)} collective-permute-done((bf16[64,384]{1,0:T(8,128)(2,1)S(1)}, bf16[64,384]{1,0:T(8,128)(2,1)S(1)}, u32[]{:S(2)}, u32[]{:S(2)}) %collective-permute-start.16) | collective-permute-done | bytes 49184 | tf_op jit(solution)/shard_map/ppermute | solution.py:480
  255.9 2.4 collective-permute-start.17
  260.7 1.5 add_convert_fusion.4
  262.2 1.3 collective-permute-start.18
  265.0 1.1 reduce_sum.134
  266.2 1.3 collective-permute-start.19
  267.5 1.5 add_bitcast_fusion
  268.9 1.4 collective-permute-start.12
  271.7 1.1 add_convert_fusion.1
  273.0 1.6 copy.126
  274.5 9.9 %all-to-all-start.7 = ((bf16[128,1,192]{2,1,0:T(2,128)(2,1)}), bf16[128,1,192]{2,1,0:T(2,128)(2,1)S(1)}, u32[]{:S(2)}, u32[]{:S(2)}) async-start(bf16[128,1,192]{2,1,0:T(2,128)(2,1)} %copy.126), calls=%async_computation.7 | async-start | bytes 262144 | tf_op jit(solution)/shard_map/all_to_all | solution.py:25
  285.3 3.4 %collective-permute-start.21 = (bf16[64,192]{0,1:T(8,128)(2,1)S(1)}, bf16[64,192]{0,1:T(8,128)(2,1)S(1)}, u32[]{:S(2)}, u32[]{:S(2)}) collective-permute-start(bf16[64,192]{0,1:T(8,128)(2,1)S(1)} %add_convert_fusion.2), channel_id=1, source_target_pairs={{0,1},{1,0},{2,3},{3,2},{4,5},{5,4},{6,7},{7,6},{8,9},{9,8},{10,11... | collective-permute-start | bytes 73736 | tf_op jit(solution)/shard_map/ppermute | solution.py:500
  288.7 5.6 %all-to-all-done.7 = bf16[128,1,192]{2,1,0:T(2,128)(2,1)S(1)} async-done(((bf16[128,1,192]{2,1,0:T(2,128)(2,1)}), bf16[128,1,192]{2,1,0:T(2,128)(2,1)S(1)}, u32[]{:S(2)}, u32[]{:S(2)}) %all-to-all-start.7) | async-done | bytes 49184 | tf_op jit(solution)/shard_map/all_to_all | solution.py:25
  295.9 1.1 add_convert_fusion
  297.3 1.2 copy.127
  (139 shorter events, 22.2 us)
Async XLA Ops:
  7.2 4.7 %copy-start.9 = (f32[64,192]{1,0:T(8,128)S(1)}, f32[64,192]{1,0:T(8,128)}, u32[]{:S(2)}) copy-start(f32[64,192]{1,0:T(8,128)} %param.35) | copy-start | bytes 147460
  7.2 4.7 %copy-start.8 = (f32[384,64]{0,1:T(8,128)S(1)}, f32[384,64]{0,1:T(8,128)}, u32[]{:S(2)}) copy-start(f32[384,64]{0,1:T(8,128)} %param.34) | copy-start | bytes 294916
  7.2 4.6 %copy-start.10 = (bf16[384,192]{0,1:T(8,128)(2,1)S(1)}, bf16[384,192]{0,1:T(8,128)(2,1)}, u32[]{:S(2)}) copy-start(bf16[384,192]{0,1:T(8,128)(2,1)} %param.33) | copy-start | bytes 442372
  7.2 110.3 %all-gather.5.cloned.1.call-start = ((), (), s32[]{:S(2)}) async-start(), calls=%async_computation.8 | async-start | bytes 8847360 | tf_op jit(solution)/shard_map/all_gather | solution.py:39
  9.3 19.2 %collective-permute-start = (bf16[192,1280]{1,0:T(8,128)(2,1)S(1)}, bf16[192,1280]{1,0:T(8,128)(2,1)S(1)}, u32[]{:S(2)}, u32[]{:S(2)}) collective-permute-start(bf16[192,1280]{1,0:T(8,128)(2,1)S(1)} %pad_maximum_fusion.3), channel_id=1, source_target_pairs={{0,64},{8,72},{16,80},{24,88},{32,96},{40,104},{48,112},{56,120},{... | collective-permute-start | bytes 1474568 | tf_op jit(solution)/shard_map/ppermute | solution.py:30
  12.3 16.1 %collective-permute-start.1 = (bf16[192,384]{1,0:T(8,128)(2,1)S(1)}, bf16[192,384]{1,0:T(8,128)(2,1)S(1)}, u32[]{:S(2)}, u32[]{:S(2)}) collective-permute-start(bf16[192,384]{1,0:T(8,128)(2,1)S(1)} %fusion.10), channel_id=1, source_target_pairs={{0,6},{1,7},{2,0},{3,1},{4,2},{5,3},{6,4},{7,5},{8,14},{9,15},{10,... | collective-permute-start | bytes 442376 | tf_op jit(solution)/shard_map/ppermute | solution.py:356
  15.1 13.3 %collective-permute-start.2 = (bf16[192,384]{1,0:T(8,128)(2,1)S(1)}, bf16[192,384]{1,0:T(8,128)(2,1)S(1)}, u32[]{:S(2)}, u32[]{:S(2)}) collective-permute-start(bf16[192,384]{1,0:T(8,128)(2,1)S(1)} %fusion.10), channel_id=1, source_target_pairs={{0,4},{1,5},{2,6},{3,7},{4,0},{5,1},{6,2},{7,3},{8,12},{9,13},{10,... | collective-permute-start | bytes 442376 | tf_op jit(solution)/shard_map/ppermute | solution.py:356
  15.4 13.0 %collective-permute-start.3 = (bf16[192,384]{1,0:T(8,128)(2,1)S(1)}, bf16[192,384]{1,0:T(8,128)(2,1)S(1)}, u32[]{:S(2)}, u32[]{:S(2)}) collective-permute-start(bf16[192,384]{1,0:T(8,128)(2,1)S(1)} %fusion.10), channel_id=1, source_target_pairs={{0,2},{1,3},{2,4},{3,5},{4,6},{5,7},{6,0},{7,1},{8,10},{9,11},{10,... | collective-permute-start | bytes 442376 | tf_op jit(solution)/shard_map/ppermute | solution.py:356
  20.0 8.5 %copy-start.5 = (bf16[512,192]{0,1:T(8,128)(2,1)S(1)}, bf16[512,192]{0,1:T(8,128)(2,1)}, u32[]{:S(2)}) copy-start(bf16[512,192]{0,1:T(8,128)(2,1)} %param.26) | copy-start | bytes 589828
  29.7 3.7 %copy-start.17 = (bf16[4,192,384]{2,1,0:T(8,128)(2,1)S(1)}, bf16[4,192,384]{2,1,0:T(8,128)(2,1)}, u32[]{:S(2)}) copy-start(bf16[4,192,384]{2,1,0:T(8,128)(2,1)} %get-tuple-element.51) | copy-start | bytes 1769476
  29.7 18.9 %all-to-all-start = ((bf16[4,384,384]{2,1,0:T(8,128)(2,1)}), bf16[4,384,384]{2,1,0:T(8,128)(2,1)S(1)}, u32[]{:S(2)}, u32[]{:S(2)}) async-start(bf16[4,384,384]{2,1,0:T(8,128)(2,1)} %get-tuple-element.50), calls=%async_computation | async-start | bytes 2359296 | tf_op jit(solution)/shard_map/all_to_all | solution.py:25
  33.4 15.2 %collective-permute-start.4 = (bf16[4,192,384]{2,1,0:T(8,128)(2,1)S(1)}, bf16[4,192,384]{2,1,0:T(8,128)(2,1)S(1)}, u32[]{:S(2)}, u32[]{:S(2)}) collective-permute-start(bf16[4,192,384]{2,1,0:T(8,128)(2,1)S(1)} %copy-done.17), channel_id=1, source_target_pairs={{0,1},{1,0},{2,3},{3,2},{4,5},{5,4},{6,7},{7,6},{8,9},{9,8},{10,11... | collective-permute-start | bytes 1769480 | tf_op jit(solution)/shard_map/ppermute | solution.py:348
  37.1 19.3 %collective-permute-start.5 = (f32[192]{0:T(256)S(1)}, f32[192]{0:T(256)S(1)}, u32[]{:S(2)}, u32[]{:S(2)}) collective-permute-start(f32[192]{0:T(256)S(1)} %multiply_reduce_fusion), channel_id=1, source_target_pairs={{0,1},{1,0},{2,3},{3,2},{4,5},{5,4},{6,7},{7,6},{8,9},{9,8},{10,11... | collective-permute-start | bytes 2312 | tf_op jit(solution)/shard_map/ppermute | solution.py:367
  48.6 7.7 %copy-start.6 = (bf16[4,192,384]{2,1,0:T(8,128)(2,1)}, bf16[4,192,384]{2,1,0:T(8,128)(2,1)S(1)}, u32[]{:S(2)}) copy-start(bf16[4,192,384]{2,1,0:T(8,128)(2,1)S(1)} %collective-permute-done.4) | copy-start | bytes 1769476
  48.6 7.7 %copy-start = (bf16[4,384,384]{2,1,0:T(8,128)(2,1)}, bf16[4,384,384]{2,1,0:T(8,128)(2,1)S(1)}, u32[]{:S(2)}) copy-start(bf16[4,384,384]{2,1,0:T(8,128)(2,1)S(1)} %all-to-all-done.q_own.k_own.v_own) | copy-start | bytes 3538948
  56.3 6.4 %copy-start.13 = (f32[192]{0:T(256)S(1)}, f32[192]{0:T(256)}, u32[]{:S(2)}) copy-start(f32[192]{0:T(256)} %param.36) | copy-start | bytes 2308
  56.4 45.8 %all-to-all-start.1 = ((bf16[8,128,512]{2,1,0:T(8,128)(2,1)}), bf16[8,128,512]{2,1,0:T(8,128)(2,1)S(1)}, u32[]{:S(2)}, u32[]{:S(2)}) async-start(bf16[8,128,512]{2,1,0:T(8,128)(2,1)} %shard_map.212), calls=%async_computation.1 | async-start | bytes 2097152 | tf_op jit(solution)/shard_map/all_to_all | solution.py:25
  62.7 141.7 %all-gather.7.cloned.1.call-start = ((), (), s32[]{:S(2)}) async-start(), calls=%async_computation.9 | async-start | bytes 11501568 | tf_op jit(solution)/shard_map/all_gather | solution.py:39
  63.3 38.8 %collective-permute-start.7 = (bf16[192,1664]{1,0:T(8,128)(2,1)S(1)}, bf16[192,1664]{1,0:T(8,128)(2,1)}, u32[]{:S(2)}, u32[]{:S(2)}) collective-permute-start(bf16[192,1664]{1,0:T(8,128)(2,1)S(1)} %pad_dynamic-update-slice_fusion), channel_id=1, source_target_pairs={{0,64},{8,72},{16,80},{24,88},{32,96},{40,104},{48,112},{56,120},{... | collective-permute-start | bytes 1916936 | tf_op jit(solution)/shard_map/ppermute | solution.py:30
  63.4 38.7 %collective-permute-start.6 = (bf16[4,192,384]{2,1,0:T(8,128)(2,1)}, bf16[4,192,384]{2,1,0:T(8,128)(2,1)}, u32[]{:S(2)}, u32[]{:S(2)}) collective-permute-start(bf16[4,192,384]{2,1,0:T(8,128)(2,1)} %get-tuple-element.60), channel_id=1, source_target_pairs={{0,1},{1,0},{2,3},{3,2},{4,5},{5,4},{6,7},{7,6},{8,9},{9,8},{10,11... | collective-permute-start | bytes 1769480 | tf_op jit(solution)/shard_map/ppermute | solution.py:371
  102.1 2.8 copy-start.2
  103.7 1.3 copy-start.7
  107.2 24.8 %all-to-all-start.2 = ((bf16[4,384,384]{2,1,0:T(8,128)(2,1)}), bf16[4,384,384]{2,1,0:T(8,128)(2,1)S(1)}, u32[]{:S(2)}, u32[]{:S(2)}) async-start(bf16[4,384,384]{2,1,0:T(8,128)(2,1)} %pad_maximum_fusion.1), calls=%async_computation.2 | async-start | bytes 2359296 | tf_op jit(solution)/shard_map/all_to_all | solution.py:25
  113.4 4.1 %slice-start = ((bf16[1,256,4096]{2,1,0:T(8,128)(2,1)}), bf16[1,128,4096]{2,1,0:T(8,128)(2,1)S(1)}, s32[]{:S(2)}) async-start(bf16[1,256,4096]{2,1,0:T(8,128)(2,1)} %x_ref.1), calls=%async_computation.10 | async-start | bytes 2097152 | tf_op jit(solution)/shard_map/slice | solution.py:359
  113.4 18.6 %collective-permute-start.8 = (bf16[128,3072]{1,0:T(8,128)(2,1)}, bf16[128,3072]{1,0:T(8,128)(2,1)}, u32[]{:S(2)}, u32[]{:S(2)}) collective-permute-start(bf16[128,3072]{1,0:T(8,128)(2,1)} %copy.110), channel_id=1, source_target_pairs={{0,1},{1,0},{2,3},{3,2},{4,5},{5,4},{6,7},{7,6},{8,9},{9,8},{10,11... | collective-permute-start | bytes 2359304 | tf_op jit(solution)/shard_map/ppermute | solution.py:391
  132.0 11.1 %copy-start.1 = (bf16[4,384,384]{2,1,0:T(8,128)(2,1)}, bf16[4,384,384]{2,1,0:T(8,128)(2,1)S(1)}, u32[]{:S(2)}) copy-start(bf16[4,384,384]{2,1,0:T(8,128)(2,1)S(1)} %all-to-all-done.2.q_other.k_other.v_other) | copy-start | bytes 3538948
  132.0 34.7 %all-to-all-start.3 = ((bf16[128,24,128]{2,1,0:T(8,128)(2,1)}), bf16[128,24,128]{2,1,0:T(8,128)(2,1)S(1)}, u32[]{:S(2)}, u32[]{:S(2)}) async-start(bf16[128,24,128]{2,1,0:T(8,128)(2,1)} %bitcast.47), calls=%async_computation.3 | async-start | bytes 1572864 | tf_op jit(solution)/shard_map/all_to_all | solution.py:25
  143.2 24.3 %copy-start.15 = (s32[16]{0:T(128)S(1)}, s32[16]{0:T(128)}, u32[]{:S(2)}) copy-start(s32[16]{0:T(128)} %param.21) | copy-start | bytes 196
  168.0 7.5 %copy-start.11 = (f32[1,3072]{1,0:T(1,128)S(1)}, f32[1,3072]{1,0:T(1,128)}, u32[]{:S(2)}) copy-start(f32[1,3072]{1,0:T(1,128)} %param.27) | copy-start | bytes 36868
  168.0 8.3 %copy-start.12 = (f32[1,3072]{1,0:T(1,128)S(1)}, f32[1,3072]{1,0:T(1,128)}, u32[]{:S(2)}) copy-start(f32[1,3072]{1,0:T(1,128)} %param.28) | copy-start | bytes 36868
  168.0 9.3 %copy-start.16 = (s32[16]{0:T(128)S(1)}, s32[16]{0:T(128)}, u32[]{:S(2)}) copy-start(s32[16]{0:T(128)} %param.20) | copy-start | bytes 196
  169.4 20.7 %all-to-all-start.4 = ((bf16[128,24,128]{2,1,0:T(8,128)(2,1)}), bf16[128,24,128]{2,1,0:T(8,128)(2,1)S(1)}, u32[]{:S(2)}, u32[]{:S(2)}) async-start(bf16[128,24,128]{2,1,0:T(8,128)(2,1)} %copy.113), calls=%async_computation.4 | async-start | bytes 1572864 | tf_op jit(solution)/shard_map/all_to_all | solution.py:25
  200.9 17.1 %all-to-all-start.5 = ((bf16[4,256,512]{2,1,0:T(8,128)(2,1)}), bf16[4,256,512]{2,1,0:T(8,128)(2,1)S(1)}, u32[]{:S(2)}, u32[]{:S(2)}) async-start(bf16[4,256,512]{2,1,0:T(8,128)(2,1)} %shard_map.214), calls=%async_computation.5 | async-start | bytes 2097152 | tf_op jit(solution)/shard_map/all_to_all | solution.py:25
  206.0 4.3 %collective-permute-start.9 = (bf16[128,128]{1,0:T(8,128)(2,1)S(1)}, bf16[128,128]{1,0:T(8,128)(2,1)S(1)}, u32[]{:S(2)}, u32[]{:S(2)}) collective-permute-start(bf16[128,128]{1,0:T(8,128)(2,1)S(1)} %convolution_convert_fusion.4), channel_id=1, source_target_pairs={{0,1},{1,0},{2,3},{3,2},{4,5},{5,4},{6,7},{7,6},{8,9},{9,8},{10,11... | collective-permute-start | bytes 98312 | tf_op jit(solution)/shard_map/ppermute | solution.py:438
  218.4 4.2 %copy-start.3 = (bf16[256,4,384]{0,2,1:T(8,128)(2,1)}, bf16[256,4,384]{0,2,1:T(8,128)(2,1)S(1)}, u32[]{:S(2)}) copy-start(bf16[256,4,384]{0,2,1:T(8,128)(2,1)S(1)} %copy.116) | copy-start | bytes 2359300
  218.4 7.3 %collective-permute-start.13 = (bf16[256,128]{1,0:T(8,128)(2,1)}, bf16[256,128]{1,0:T(8,128)(2,1)S(1)}, u32[]{:S(2)}, u32[]{:S(2)}) collective-permute-start(bf16[256,128]{1,0:T(8,128)(2,1)} %pad_maximum_fusion.7), channel_id=1, source_target_pairs={{0,2},{1,3},{2,0},{3,1},{4,6},{5,7},{6,4},{7,5},{8,10},{9,11},{10,... | collective-permute-start | bytes 196616 | tf_op jit(solution)/shard_map/ppermute | solution.py:471
  222.7 5.8 %collective-permute-start.10 = (bf16[128,128]{1,0:T(8,128)(2,1)S(1)}, bf16[128,128]{1,0:T(8,128)(2,1)S(1)}, u32[]{:S(2)}, u32[]{:S(2)}) collective-permute-start(bf16[128,128]{1,0:T(8,128)(2,1)S(1)} %slice.136), channel_id=1, source_target_pairs={{0,1},{1,0},{2,3},{3,2},{4,5},{5,4},{6,7},{7,6},{8,9},{9,8},{10,11... | collective-permute-start | bytes 98312 | tf_op jit(solution)/shard_map/ppermute | solution.py:442
  224.0 39.5 %collective-permute-start.11 = (bf16[128,1536]{1,0:T(8,128)(2,1)S(1)}, bf16[128,1536]{1,0:T(8,128)(2,1)}, u32[]{:S(2)}, u32[]{:S(2)}) collective-permute-start(bf16[128,1536]{1,0:T(8,128)(2,1)S(1)} %slice.135), channel_id=1, source_target_pairs={{0,1},{1,0},{2,3},{3,2},{4,5},{5,4},{6,7},{7,6},{8,9},{9,8},{10,11... | collective-permute-start | bytes 1179656 | tf_op jit(solution)/shard_map/ppermute | solution.py:454
  226.6 5.8 %collective-permute-start.14 = (bf16[512,128]{1,0:T(8,128)(2,1)S(1)}, bf16[512,128]{1,0:T(8,128)(2,1)S(1)}, u32[]{:S(2)}, u32[]{:S(2)}) collective-permute-start(bf16[512,128]{1,0:T(8,128)(2,1)S(1)} %pad_maximum_fusion.6), channel_id=1, source_target_pairs={{0,4},{1,5},{2,6},{3,7},{4,0},{5,1},{6,2},{7,3},{8,12},{9,13},{10,... | collective-permute-start | bytes 393224 | tf_op jit(solution)/shard_map/ppermute | solution.py:471
  229.5 9.0 %copy-start.4 = (bf16[256,4,384]{0,2,1:T(8,128)(2,1)S(1)}, bf16[256,4,384]{0,2,1:T(8,128)(2,1)}, u32[]{:S(2)}) copy-start(bf16[256,4,384]{0,2,1:T(8,128)(2,1)} %copy-done.3) | copy-start | bytes 2359300
  234.5 12.0 %collective-permute-start.15 = (bf16[64,384]{1,0:T(8,128)(2,1)}, bf16[64,384]{1,0:T(8,128)(2,1)}, u32[]{:S(2)}, u32[]{:S(2)}) collective-permute-start(bf16[64,384]{1,0:T(8,128)(2,1)} %convolution_convert_fusion.3), channel_id=1, source_target_pairs={{0,8},{8,0},{16,24},{24,16},{32,40},{40,32},{48,56},{56,48},{64,72... | collective-permute-start | bytes 147464 | tf_op jit(solution)/shard_map/ppermute | solution.py:480
  242.3 21.2 %all-to-all-start.6 = ((bf16[16,64,192]{2,1,0:T(8,128)(2,1)}), bf16[16,64,192]{2,1,0:T(8,128)(2,1)}, u32[]{:S(2)}, u32[]{:S(2)}) async-start(bf16[16,64,192]{2,1,0:T(8,128)(2,1)} %bitcast.104), calls=%async_computation.6 | async-start | bytes 1048576 | tf_op jit(solution)/shard_map/all_to_all | solution.py:25
  247.3 8.0 %collective-permute-start.16 = (bf16[64,384]{1,0:T(8,128)(2,1)S(1)}, bf16[64,384]{1,0:T(8,128)(2,1)S(1)}, u32[]{:S(2)}, u32[]{:S(2)}) collective-permute-start(bf16[64,384]{1,0:T(8,128)(2,1)S(1)} %add_convert_fusion.6), channel_id=1, source_target_pairs={{0,16},{8,24},{16,0},{24,8},{32,48},{40,56},{48,32},{56,40},{64,80... | collective-permute-start | bytes 147464 | tf_op jit(solution)/shard_map/ppermute | solution.py:480
  255.9 4.8 %collective-permute-start.17 = (bf16[64,384]{1,0:T(8,128)(2,1)}, bf16[64,384]{1,0:T(8,128)(2,1)}, u32[]{:S(2)}, u32[]{:S(2)}) collective-permute-start(bf16[64,384]{1,0:T(8,128)(2,1)} %add_convert_fusion.5), channel_id=1, source_target_pairs={{0,32},{8,40},{16,48},{24,56},{32,0},{40,8},{48,16},{56,24},{64,96... | collective-permute-start | bytes 147464 | tf_op jit(solution)/shard_map/ppermute | solution.py:480
  262.2 5.3 %collective-permute-start.18 = (bf16[64,384]{1,0:T(8,128)(2,1)}, bf16[64,384]{1,0:T(8,128)(2,1)}, u32[]{:S(2)}, u32[]{:S(2)}) collective-permute-start(bf16[64,384]{1,0:T(8,128)(2,1)} %add_convert_fusion.4), channel_id=1, source_target_pairs={{0,64},{8,72},{16,80},{24,88},{32,96},{40,104},{48,112},{56,120},{... | collective-permute-start | bytes 147464 | tf_op jit(solution)/shard_map/ppermute | solution.py:495
  266.2 4.2 %collective-permute-start.19 = (bf16[64,192]{0,1:T(8,128)(2,1)S(1)}, bf16[64,192]{0,1:T(8,128)(2,1)S(1)}, u32[]{:S(2)}, u32[]{:S(2)}) collective-permute-start(bf16[64,192]{0,1:T(8,128)(2,1)S(1)} %copy.124), channel_id=1, source_target_pairs={{0,2},{1,3},{2,0},{3,1},{4,6},{5,7},{6,4},{7,5},{8,10},{9,11},{10,... | collective-permute-start | bytes 73736 | tf_op jit(solution)/shard_map/ppermute | solution.py:500
  268.9 26.9 %collective-permute-start.12 = (bf16[128,1536]{1,0:T(8,128)(2,1)}, bf16[128,1536]{1,0:T(8,128)(2,1)}, u32[]{:S(2)}, u32[]{:S(2)}) collective-permute-start(bf16[128,1536]{1,0:T(8,128)(2,1)} %slice.134), channel_id=1, source_target_pairs={{0,1},{1,0},{2,3},{3,2},{4,5},{5,4},{6,7},{7,6},{8,9},{9,8},{10,11... | collective-permute-start | bytes 1179656 | tf_op jit(solution)/shard_map/ppermute | solution.py:468
  271.0 23.5 %copy-start.14 = (f32[192]{0:T(256)S(1)}, f32[192]{0:T(256)}, u32[]{:S(2)}) copy-start(f32[192]{0:T(256)} %param.36) | copy-start | bytes 2308
  271.0 13.5 %collective-permute-start.20 = (bf16[64,192]{0,1:T(8,128)(2,1)}, bf16[64,192]{0,1:T(8,128)(2,1)}, u32[]{:S(2)}, u32[]{:S(2)}) collective-permute-start(bf16[64,192]{0,1:T(8,128)(2,1)} %add_convert_fusion.3), channel_id=1, source_target_pairs={{0,4},{1,5},{2,6},{3,7},{4,0},{5,1},{6,2},{7,3},{8,12},{9,13},{10,... | collective-permute-start | bytes 73736 | tf_op jit(solution)/shard_map/ppermute | solution.py:500
  274.5 19.7 %all-to-all-start.7 = ((bf16[128,1,192]{2,1,0:T(2,128)(2,1)}), bf16[128,1,192]{2,1,0:T(2,128)(2,1)S(1)}, u32[]{:S(2)}, u32[]{:S(2)}) async-start(bf16[128,1,192]{2,1,0:T(2,128)(2,1)} %copy.126), calls=%async_computation.7 | async-start | bytes 262144 | tf_op jit(solution)/shard_map/all_to_all | solution.py:25
  285.3 9.7 %collective-permute-start.21 = (bf16[64,192]{0,1:T(8,128)(2,1)S(1)}, bf16[64,192]{0,1:T(8,128)(2,1)S(1)}, u32[]{:S(2)}, u32[]{:S(2)}) collective-permute-start(bf16[64,192]{0,1:T(8,128)(2,1)S(1)} %add_convert_fusion.2), channel_id=1, source_target_pairs={{0,1},{1,0},{2,3},{3,2},{4,5},{5,4},{6,7},{7,6},{8,9},{9,8},{10,11... | collective-permute-start | bytes 73736 | tf_op jit(solution)/shard_map/ppermute | solution.py:500
Sparse Core Ops, SparseCore 0:
  29.8 50.0 all-gather.4
  105.1 67.1 all-gather.6

commit v9 on v7

--- a/solution.py
+++ b/solution.py
@@ -359,24 +359,27 @@
     tokens = enc_states[0, :BLK]
     feat = tokens.shape[1] // n_seq
     hidden = t5_in(enc_states, t5_gain, t5_in_weight)
-    hidden, near_weights, shifted = lax.optimization_barrier((hidden, near_weights, shifted))
+    hidden, near_weights, shifted, first_heads, second_heads = lax.optimization_barrier(
+        (hidden, near_weights, shifted, first_heads, second_heads)
+    )
+    second_heads = lax.ppermute(second_heads, "seq", flip_z)
     weights = gather_columns(weights, near_weights)
     depth = context_weight.shape[0]
     context_all = weights[:, :depth]
-    rows_y = jnp.stack(shifted + shifted[:-1])
-    rows_y = lax.dynamic_slice_in_dim(rows_y, n_y - 1 - seq_rank // 2, n_y, 0)
     column_sq = jnp.sum(jnp.square(jnp.stack(shifted).astype(F32)), (0, 2))
     column_other = lax.ppermute(column_sq, "seq", flip_z)
     ffn = t5_out(hidden, t5_out_weight, n_seq)
-    own_heads, ffn, first_heads, second_heads, column_other = lax.optimization_barrier(
-        (own_heads, ffn, first_heads, second_heads, column_other)
-    )
-    second_heads = lax.ppermute(second_heads, "seq", flip_z)
-
-    rows_f = rows_y.astype(F32)
+    own_heads, ffn, second_heads, column_other = lax.optimization_barrier(
+        (own_heads, ffn, second_heads, column_other)
+    )
+
     ratio = magnitude / jnp.sqrt(column_sq + column_other + EPSILON)
-    scaled_t = (rows_f * ratio[None, :, None]).astype(BF16)
-    scaled_t = scaled_t.transpose(1, 0, 2).reshape(own_cols, -1)
+    scaled_t = []
+    for row in range(n_y):
+        turned = [shifted[(row - at - 1) % n_y] for at in range(n_y)]
+        block = lax.select_n(seq_rank // 2, *turned)
+        scaled_t.append((block.astype(F32) * ratio[:, None]).astype(BF16))
+    scaled_t = jnp.concatenate(scaled_t, 1)
     reach = scaled_t.shape[1]
     up = jnp.pad((dora_b * ratio).astype(BF16).T, ((0, 0), (0, lanes - rank)))
     scaled_t = jnp.concatenate([scaled_t, up], 1)
@@ -431,9 +434,11 @@
     gathered = swap(attended, "seq", Y_GROUPS)
     down = jnp.dot(cotangent, up_all, preferred_element_type=F32).astype(BF16)
     down = jnp.concatenate([down, lax.ppermute(down, "seq", flip_z)], 0)
-    cotangent_other = lax.ppermute(cotangent, "seq", flip_z)
+    cotangent_other, _ = lax.optimization_barrier((cotangent, attended))
+    cotangent_other = lax.ppermute(cotangent_other, "seq", flip_z)
     gathered, down, cotangent_other = lax.optimization_barrier((gathered, down, cotangent_other))
     lowered = jnp.sum(gathered[:, :, own_rows:].astype(F32), 0)
+    gathered, lowered = lax.optimization_barrier((gathered, lowered))
     lowered_other = lax.ppermute(lowered[BLK:].astype(BF16), "seq", flip_z)
     gathered = gathered[:, :, :own_rows].transpose(1, 0, 2).reshape(2 * BLK, -1)
     half = model // 2

time: 277 us -> 286 us (1.032)
  waiting for transfers between devices: 75.3 us -> 87 us
  local copies, waits for them, and re-layouts: 22 us -> 16.3 us
    ppermute x1, waiting for transfers between devices: 19.3 us -> 0.01 us  [on_device(): second_heads = lax.ppermute(second_heads, 'seq', flip_z)]
    ppermute x1, waiting for transfers between devices: 3.11 us -> 15.1 us  [on_device(): down = jnp.concatenate([down, lax.ppermute(down, 'seq', flip_z)], 0)]
    ppermute x2, waiting for transfers between devices: 7.59 us -> 13.9 us  [near_shard(): lax.ppermute(values, 'dp', [(i, (i + n_dp // 2) % n_dp) for i in range(n_...]
    all_to_all x8, waiting for transfers between devices: 42.5 us -> 48.2 us  [swap(): lax.all_to_all(values, axes, 0, 0, tiled=True, axis_index_groups=groups)]
    unnamed x52 -> x51, local copies, waits for them, and re-layouts: 10.3 us -> 6.78 us
    ppermute x1, waiting for transfers between devices: 1.1 us -> 4.14 us  [on_device(): column_other = lax.ppermute(column_sq, 'seq', flip_z)]
  transfers between devices with their start and end apart: 32 -> 32, of which waited for: 10 -> 13; matrix products, arithmetic and copies ran while one was open for 18% -> 16% of each run, Pallas kernels for 15% -> 13%
where the time goes in v9:
time: 286 us; the launch traced here: 284 us
  starting transfers between devices  87.2 us (30%)
  waiting for transfers between devices  87 us (30%)
  Pallas kernels  41.8 us (15%)
  other arithmetic  22.6 us (8%)
  local copies, waits for them, and re-layouts  16.3 us (6%)
  between operations  14.6 us (5%)
  matrix products  14.1 us (5%)
    all_to_all x8, starting transfers between devices, swap(): lax.all_to_all(values, axes, 0, 0, tiled=True, axis_index_groups=groups)  49.5 us
    all_to_all x8, waiting for transfers between devices, swap(): lax.all_to_all(values, axes, 0, 0, tiled=True, axis_index_groups=groups)  48.2 us
    ppermute x1, waiting for transfers between devices, on_device(): down = jnp.concatenate([down, lax.ppermute(down, 'seq', flip_z)], 0)  15.1 us
    ppermute x2, waiting for transfers between devices, near_shard(): lax.ppermute(values, 'dp', [(i, (i + n_dp // 2) % n_dp) for i in range(n_...  13.9 us
    pallas_call x1, Pallas kernels, image_attention(): pl.pallas_call(image_kernel, grid=(heads, n_y), in_specs=[queries(), quer...  12.5 us
    dot_general x3, matrix products, dot_t(): lax.dot_general(left, right, (((1,), (1,)), ((), ())), preferred_element_...  10.9 us
    pallas_call x1, Pallas kernels, prompt_attention(): pl.pallas_call(prompt_kernel, grid=(heads + 1,), in_specs=[pl.BlockSpec(m...  9.61 us
    pallas_call x1, Pallas kernels, t5_in(): pl.pallas_call(t5_in_kernel, grid=(units // cut,), in_specs=[pl.BlockSpec...  8.39 us
  transfers between devices with their start and end apart: 32, of which 13 were waited for; matrix products, arithmetic and copies ran while one was open for 16% of the time, Pallas kernels for 13%

profile of v9, /device:TPU:1, one launch (start us, length us, event | category | flops | bytes accessed | tf_op | source)
XLA Modules:
  0.0 283.6 jit_solution(14701009745069485667)
XLA Ops:
  7.2 4.0 %shard_map.210 = (bf16[4,384,384]{2,1,0:T(8,128)(2,1)}, bf16[4,192,384]{2,1,0:T(8,128)(2,1)}, bf16[4,192,384]{2,1,0:T(8,128)(2,1)}) custom-call(s32[1]{0:T(128)} %bitcast.1._, bf16[3,128,3072]{2,1,0:T(8,128)(2,1)} %bitcast.95, bf16[3,128,3072]{2,1,0:T(8,128)(2,1)} %bitcast.96), custom_call_target="tpu_custom_call" | custom-call | bytes 4718592 | tf_op jit(solution)/shard_map/pallas_call | solution.py:80
  11.3 4.5 %collective-permute-start.4 = (bf16[4,192,384]{2,1,0:T(8,128)(2,1)}, bf16[4,192,384]{2,1,0:T(8,128)(2,1)S(1)}, u32[]{:S(2)}, u32[]{:S(2)}) collective-permute-start(bf16[4,192,384]{2,1,0:T(8,128)(2,1)} %get-tuple-element.48), channel_id=1, source_target_pairs={{0,1},{1,0},{2,3},{3,2},{4,5},{5,4},{6,7},{7,6},{8,9},{9,8},{10,11... | collective-permute-start | bytes 1769480 | tf_op jit(solution)/shard_map/ppermute | solution.py:348
  15.9 0.8 collective-permute-start
  17.2 2.8 collective-permute-start.1
  21.0 8.4 %shard_map.211.hidden_ref = bf16[128,640]{1,0:T(8,128)(2,1)} custom-call(bf16[1,256,4096]{2,1,0:T(8,128)(2,1)} %x_ref.1, f32[1,4096]{1,0:T(1,128)} %bitcast.118, bf16[2,4096,640]{2,1,0:T(8,128)(2,1)} %up_w.1, bf16[2,4096,640]{2,1,0:T(8,128)(2,1)} %up_w.1), custom_call_target="tpu_custom_call" | custom-call | flops 1342177280 | bytes 10485760 | tf_op jit(solution)/shard_map/pallas_call | solution.py:255
  29.8 10.2 %collective-permute-done = bf16[192,1280]{1,0:T(8,128)(2,1)S(1)} collective-permute-done((bf16[192,1280]{1,0:T(8,128)(2,1)S(1)}, bf16[192,1280]{1,0:T(8,128)(2,1)S(1)}, u32[]{:S(2)}, u32[]{:S(2)}) %collective-permute-start) | collective-permute-done | bytes 491552 | tf_op jit(solution)/shard_map/ppermute | solution.py:30
  40.2 1.0 pad_maximum_fusion.2
  41.2 4.2 %all-to-all-start = ((bf16[4,384,384]{2,1,0:T(8,128)(2,1)}), bf16[4,384,384]{2,1,0:T(8,128)(2,1)S(1)}, u32[]{:S(2)}, u32[]{:S(2)}) async-start(bf16[4,384,384]{2,1,0:T(8,128)(2,1)} %get-tuple-element.45), calls=%async_computation | async-start | bytes 2359296 | tf_op jit(solution)/shard_map/all_to_all | solution.py:25
  45.4 0.9 collective-permute-start.5
  46.6 2.2 collective-permute-start.6
  48.8 7.2 %shard_map.212 = bf16[8,128,512]{2,1,0:T(8,128)(2,1)} custom-call(bf16[128,640]{1,0:T(8,128)(2,1)} %shard_map.211.hidden_ref, bf16[640,4096]{1,0:T(8,128)(2,1)} %out_w.1), custom_call_target="tpu_custom_call" | custom-call | flops 671088640 | bytes 5242880 | tf_op jit(solution)/shard_map/pallas_call | solution.py:284
  56.0 4.1 %collective-permute-done.6 = f32[192]{0:T(256)S(1)} collective-permute-done((f32[192]{0:T(256)S(1)}, f32[192]{0:T(256)S(1)}, u32[]{:S(2)}, u32[]{:S(2)}) %collective-permute-start.6) | collective-permute-done | bytes 800 | tf_op jit(solution)/shard_map/ppermute | solution.py:370
  60.2 0.8 copy-done.10
  61.0 4.7 %all-to-all-start.1 = ((bf16[8,128,512]{2,1,0:T(8,128)(2,1)}), bf16[8,128,512]{2,1,0:T(8,128)(2,1)S(1)}, u32[]{:S(2)}, u32[]{:S(2)}) async-start(bf16[8,128,512]{2,1,0:T(8,128)(2,1)} %shard_map.212), calls=%async_computation.1 | async-start | bytes 2097152 | tf_op jit(solution)/shard_map/all_to_all | solution.py:25
  65.7 0.8 fusion.21
  68.8 9.7 %all-to-all-done.1 = bf16[8,128,512]{2,1,0:T(8,128)(2,1)S(1)} async-done(((bf16[8,128,512]{2,1,0:T(8,128)(2,1)}), bf16[8,128,512]{2,1,0:T(8,128)(2,1)S(1)}, u32[]{:S(2)}, u32[]{:S(2)}) %all-to-all-start.1) | async-done | bytes 1048608 | tf_op jit(solution)/shard_map/all_to_all | solution.py:25
  78.5 2.8 pad_maximum_fusion.1
  81.3 3.5 %all-to-all-start.2 = ((bf16[4,384,384]{2,1,0:T(8,128)(2,1)}), bf16[4,384,384]{2,1,0:T(8,128)(2,1)S(1)}, u32[]{:S(2)}, u32[]{:S(2)}) async-start(bf16[4,384,384]{2,1,0:T(8,128)(2,1)} %pad_maximum_fusion.1), calls=%async_computation.2 | async-start | bytes 2359296 | tf_op jit(solution)/shard_map/all_to_all | solution.py:25
  85.8 0.8 dynamic_slice.7
  86.6 1.4 convert_reduce_fusion
  88.0 1.6 all-gather.5.cloned.1.call-done
  89.7 3.0 %fusion.7 = bf16[16,8,24,128]{3,1,2,0:T(8,128)(2,1)S(1)} fusion(bf16[3072,1280]{1,0:T(8,128)(2,1)} %bitcast.88, f32[128,512]{1,0:T(8,128)S(1)} %convert_reduce_fusion, f32[512]{0:T(512)S(1)} %dynamic_slice.7, bf16[1,128,4096]{2,1,0:T(8,128)(2,1)S(1)} %slice-done, s32[]{:T(128)S(6)} %select_n.153), kind=kOutput, calls=%fused_computation.12 | convolution fusion | flops 403308544 | bytes 4327428 | tf_op jit(solution)/shard_map/dot_general | solution.py:56
  92.7 1.0 copy.132
  93.7 3.7 %collective-permute-done.7 = bf16[192,1664]{1,0:T(8,128)(2,1)} collective-permute-done((bf16[192,1664]{1,0:T(8,128)(2,1)}, bf16[192,1664]{1,0:T(8,128)(2,1)}, u32[]{:S(2)}, u32[]{:S(2)}) %collective-permute-start.7) | collective-permute-done | bytes 639008 | tf_op jit(solution)/shard_map/ppermute | solution.py:30
  97.5 1.8 select_bitcast_fusion.1
  99.3 1.2 pad_maximum_fusion
  100.5 14.9 %all-to-all-start.3 = ((bf16[128,24,128]{2,1,0:T(8,128)(2,1)}), bf16[128,24,128]{2,1,0:T(8,128)(2,1)S(1)}, u32[]{:S(2)}, u32[]{:S(2)}) async-start(bf16[128,24,128]{2,1,0:T(8,128)(2,1)} %bitcast.48), calls=%async_computation.3 | async-start | bytes 1572864 | tf_op jit(solution)/shard_map/all_to_all | solution.py:25
  115.4 12.5 %shard_map.213 = (f32[1024,384]{1,0:T(8,128)}, f32[1024,384]{1,0:T(8,128)}) custom-call(bf16[4,384,384]{2,1,0:T(8,128)(2,1)} %copy-done, bf16[4,384,384]{2,1,0:T(8,128)(2,1)} %copy-done.1, bf16[4,384,384]{2,1,0:T(8,128)(2,1)} %copy-done, bf16[4,384,384]{2,1,0:T(8,128)(2,1)} %copy-done.1, bf16[4,384,384]{2,1,0:T(8,128)(2,1)} %copy-done, ...), custom_call_target="tpu_custom_call" | custom-call | flops 2415919104 | bytes 5505024 | tf_op jit(solution)/shard_map/pallas_call | solution.py:130
  127.9 7.3 %all-to-all-done.3 = bf16[128,24,128]{2,1,0:T(8,128)(2,1)S(1)} async-done(((bf16[128,24,128]{2,1,0:T(8,128)(2,1)}), bf16[128,24,128]{2,1,0:T(8,128)(2,1)S(1)}, u32[]{:S(2)}, u32[]{:S(2)}) %all-to-all-start.3) | async-done | bytes 786464 | tf_op jit(solution)/shard_map/all_to_all | solution.py:25
  136.5 1.4 copy.110
  137.9 5.9 %all-to-all-start.4 = ((bf16[128,24,128]{2,1,0:T(8,128)(2,1)}), bf16[128,24,128]{2,1,0:T(8,128)(2,1)S(1)}, u32[]{:S(2)}, u32[]{:S(2)}) async-start(bf16[128,24,128]{2,1,0:T(8,128)(2,1)} %copy.110), calls=%async_computation.4 | async-start | bytes 1572864 | tf_op jit(solution)/shard_map/all_to_all | solution.py:25
  147.3 20.1 %all-to-all-done.4 = bf16[128,24,128]{2,1,0:T(8,128)(2,1)S(1)} async-done(((bf16[128,24,128]{2,1,0:T(8,128)(2,1)}), bf16[128,24,128]{2,1,0:T(8,128)(2,1)S(1)}, u32[]{:S(2)}, u32[]{:S(2)}) %all-to-all-start.4) | async-done | bytes 786464 | tf_op jit(solution)/shard_map/all_to_all | solution.py:25
  167.6 1.1 fusion.6.text_ref
  168.7 9.6 %shard_map.214 = bf16[4,256,512]{2,1,0:T(8,128)(2,1)} custom-call(s32[1]{0:T(128)} %bitcast.length_ref, bf16[4,384,384]{2,1,0:T(8,128)(2,1)} %copy-done, bf16[4,384,384]{2,1,0:T(8,128)(2,1)} %copy-done.1, bf16[128,3072]{1,0:T(8,128)(2,1)} %fusion.6.text_ref, bf16[3072,1280]{1,0:T(8,128)(2,1)} %bitcast.89, bf16[3072,1280]{1,0:T(8,128)(2,1)} %bitcast.90, ...), custom_call_target="tpu_custom_call" | custom-call | flops 905969664 | bytes 9437184 | tf_op jit(solution)/shard_map/pallas_call | solution.py:214
  178.4 3.5 %all-to-all-start.5 = ((bf16[4,256,512]{2,1,0:T(8,128)(2,1)}), bf16[4,256,512]{2,1,0:T(8,128)(2,1)S(1)}, u32[]{:S(2)}, u32[]{:S(2)}) async-start(bf16[4,256,512]{2,1,0:T(8,128)(2,1)} %shard_map.214), calls=%async_computation.5 | async-start | bytes 2097152 | tf_op jit(solution)/shard_map/all_to_all | solution.py:25
  182.2 1.3 collective-permute-start.9
  183.4 1.5 fusion.11
  185.0 1.9 collective-permute-start.8
  186.9 15.1 %collective-permute-done.8 = bf16[128,128]{1,0:T(8,128)(2,1)S(1)} collective-permute-done((bf16[128,128]{1,0:T(8,128)(2,1)S(1)}, bf16[128,128]{1,0:T(8,128)(2,1)S(1)}, u32[]{:S(2)}, u32[]{:S(2)}) %collective-permute-start.8) | collective-permute-done | bytes 32800 | tf_op jit(solution)/shard_map/ppermute | solution.py:436
  202.6 0.8 copy-done.5
  203.5 1.1 collective-permute-start.13
  204.9 2.0 collective-permute-done.13
  206.9 0.9 broadcast_select_fusion.3
  207.8 2.7 collective-permute-start.14
  210.5 3.9 %fusion.2 = f32[256,1536]{1,0:T(8,128)S(1)} fusion(bf16[256,1536]{0,1:T(8,128)(2,1)S(1)} %bitcast.109, bf16[3072,1664]{1,0:T(8,128)(2,1)} %bitcast.121), kind=kOutput, calls=%fused_computation.2 | convolution fusion | flops 1207959552 | bytes 7077888 | tf_op jit(solution)/shard_map/dot_general | solution.py:56
  215.2 1.7 collective-permute-start.10
  216.9 1.2 collective-permute-start.11
  218.5 4.9 %collective-permute-start.15 = (bf16[64,384]{1,0:T(8,128)(2,1)S(1)}, bf16[64,384]{1,0:T(8,128)(2,1)S(1)}, u32[]{:S(2)}, u32[]{:S(2)}) collective-permute-start(bf16[64,384]{1,0:T(8,128)(2,1)S(1)} %convolution_convert_fusion.3), channel_id=1, source_target_pairs={{0,8},{8,0},{16,24},{24,16},{32,40},{40,32},{48,56},{56,48},{64,72... | collective-permute-start | bytes 147464 | tf_op jit(solution)/shard_map/ppermute | solution.py:478
  224.5 0.9 copy.117
  225.8 4.0 %fusion = f32[256,1536]{1,0:T(8,128)S(1)} fusion(bf16[256,1536]{0,1:T(8,128)(2,1)} %bitcast.110, bf16[3072,1664]{1,0:T(8,128)(2,1)} %bitcast.122), kind=kOutput, calls=%fused_computation | convolution fusion | flops 1207959552 | bytes 7077888 | tf_op jit(solution)/shard_map/dot_general | solution.py:56
  229.9 0.9 slice.132
  231.4 1.8 collective-permute-start.17
  233.2 2.1 collective-permute-start.12
  235.6 0.9 copy.130
  236.5 6.1 %all-to-all-start.6 = ((bf16[16,64,192]{2,1,0:T(8,128)(2,1)}), bf16[16,64,192]{2,1,0:T(8,128)(2,1)S(1)}, u32[]{:S(2)}, u32[]{:S(2)}) async-start(bf16[16,64,192]{2,1,0:T(8,128)(2,1)} %bitcast.31), calls=%async_computation.6 | async-start | bytes 1048576 | tf_op jit(solution)/shard_map/all_to_all | solution.py:25
  242.6 0.8 add_convert_fusion.4
  243.4 1.7 collective-permute-start.18
  245.2 2.5 multiply_reduce_fusion.3
  247.9 4.6 %all-to-all-done.6 = bf16[16,64,192]{2,1,0:T(8,128)(2,1)S(1)} async-done(((bf16[16,64,192]{2,1,0:T(8,128)(2,1)}), bf16[16,64,192]{2,1,0:T(8,128)(2,1)S(1)}, u32[]{:S(2)}, u32[]{:S(2)}) %all-to-all-start.6) | async-done | bytes 393248 | tf_op jit(solution)/shard_map/all_to_all | solution.py:25
  254.3 1.6 collective-permute-done.19
  256.6 1.2 copy.127
  258.6 6.8 %all-to-all-start.7 = ((bf16[128,1,192]{2,1,0:T(2,128)(2,1)}), bf16[128,1,192]{2,1,0:T(2,128)(2,1)S(1)}, u32[]{:S(2)}, u32[]{:S(2)}) async-start(bf16[128,1,192]{2,1,0:T(2,128)(2,1)} %copy.126), calls=%async_computation.7 | async-start | bytes 262144 | tf_op jit(solution)/shard_map/all_to_all | solution.py:25
  265.4 3.4 %collective-permute-start.21 = (bf16[64,192]{0,1:T(8,128)(2,1)S(1)}, bf16[64,192]{0,1:T(8,128)(2,1)S(1)}, u32[]{:S(2)}, u32[]{:S(2)}) collective-permute-start(bf16[64,192]{0,1:T(8,128)(2,1)S(1)} %add_convert_fusion.2), channel_id=1, source_target_pairs={{0,1},{1,0},{2,3},{3,2},{4,5},{5,4},{6,7},{7,6},{8,9},{9,8},{10,11... | collective-permute-start | bytes 73736 | tf_op jit(solution)/shard_map/ppermute | solution.py:498
  268.8 6.4 %all-to-all-done.7 = bf16[128,1,192]{2,1,0:T(2,128)(2,1)S(1)} async-done(((bf16[128,1,192]{2,1,0:T(2,128)(2,1)}), bf16[128,1,192]{2,1,0:T(2,128)(2,1)S(1)}, u32[]{:S(2)}, u32[]{:S(2)}) %all-to-all-start.7) | async-done | bytes 49184 | tf_op jit(solution)/shard_map/all_to_all | solution.py:25
  (146 shorter events, 20.5 us)
Async XLA Ops:
  7.2 82.5 %all-gather.5.cloned.1.call-start = ((), (), s32[]{:S(2)}) async-start(), calls=%async_computation.8 | async-start | bytes 8847360 | tf_op jit(solution)/shard_map/all_gather | solution.py:39
  7.2 8.6 %copy-start.13 = (bf16[192,2,384]{2,1,0:T(2,128)(2,1)S(1)}, bf16[192,2,384]{2,1,0:T(2,128)(2,1)}, u32[]{:S(2)}) copy-start(bf16[192,2,384]{2,1,0:T(2,128)(2,1)} %param.29) | copy-start | bytes 884740
  7.2 8.6 %copy-start.8 = (bf16[512,192]{0,1:T(8,128)(2,1)S(1)}, bf16[512,192]{0,1:T(8,128)(2,1)}, u32[]{:S(2)}) copy-start(bf16[512,192]{0,1:T(8,128)(2,1)} %param.26) | copy-start | bytes 589828
  11.3 5.4 %copy-start.12 = (f32[384,64]{0,1:T(8,128)S(1)}, f32[384,64]{0,1:T(8,128)}, u32[]{:S(2)}) copy-start(f32[384,64]{0,1:T(8,128)} %param.34) | copy-start | bytes 294916
  11.3 5.4 %copy-start.14 = (f32[64,192]{1,0:T(8,128)S(1)}, f32[64,192]{1,0:T(8,128)}, u32[]{:S(2)}) copy-start(f32[64,192]{1,0:T(8,128)} %param.35) | copy-start | bytes 147460
  11.3 5.4 %copy-start.15 = (bf16[384,192]{0,1:T(8,128)(2,1)S(1)}, bf16[384,192]{0,1:T(8,128)(2,1)}, u32[]{:S(2)}) copy-start(bf16[384,192]{0,1:T(8,128)(2,1)} %param.33) | copy-start | bytes 442372
  11.3 28.7 %collective-permute-start.4 = (bf16[4,192,384]{2,1,0:T(8,128)(2,1)}, bf16[4,192,384]{2,1,0:T(8,128)(2,1)S(1)}, u32[]{:S(2)}, u32[]{:S(2)}) collective-permute-start(bf16[4,192,384]{2,1,0:T(8,128)(2,1)} %get-tuple-element.48), channel_id=1, source_target_pairs={{0,1},{1,0},{2,3},{3,2},{4,5},{5,4},{6,7},{7,6},{8,9},{9,8},{10,11... | collective-permute-start | bytes 1769480 | tf_op jit(solution)/shard_map/ppermute | solution.py:348
  15.9 24.1 %collective-permute-start = (bf16[192,1280]{1,0:T(8,128)(2,1)S(1)}, bf16[192,1280]{1,0:T(8,128)(2,1)S(1)}, u32[]{:S(2)}, u32[]{:S(2)}) collective-permute-start(bf16[192,1280]{1,0:T(8,128)(2,1)S(1)} %pad_maximum_fusion.3), channel_id=1, source_target_pairs={{0,64},{8,72},{16,80},{24,88},{32,96},{40,104},{48,112},{56,120},{... | collective-permute-start | bytes 1474568 | tf_op jit(solution)/shard_map/ppermute | solution.py:30
  17.2 12.2 %collective-permute-start.1 = (bf16[192,384]{1,0:T(8,128)(2,1)S(1)}, bf16[192,384]{1,0:T(8,128)(2,1)S(1)}, u32[]{:S(2)}, u32[]{:S(2)}) collective-permute-start(bf16[192,384]{1,0:T(8,128)(2,1)S(1)} %fusion.10), channel_id=1, source_target_pairs={{0,6},{1,7},{2,0},{3,1},{4,2},{5,3},{6,4},{7,5},{8,14},{9,15},{10,... | collective-permute-start | bytes 442376 | tf_op jit(solution)/shard_map/ppermute | solution.py:356
  20.0 9.4 %collective-permute-start.2 = (bf16[192,384]{1,0:T(8,128)(2,1)S(1)}, bf16[192,384]{1,0:T(8,128)(2,1)S(1)}, u32[]{:S(2)}, u32[]{:S(2)}) collective-permute-start(bf16[192,384]{1,0:T(8,128)(2,1)S(1)} %fusion.10), channel_id=1, source_target_pairs={{0,4},{1,5},{2,6},{3,7},{4,0},{5,1},{6,2},{7,3},{8,12},{9,13},{10,... | collective-permute-start | bytes 442376 | tf_op jit(solution)/shard_map/ppermute | solution.py:356
  20.3 9.5 %collective-permute-start.3 = (bf16[192,384]{1,0:T(8,128)(2,1)S(1)}, bf16[192,384]{1,0:T(8,128)(2,1)S(1)}, u32[]{:S(2)}, u32[]{:S(2)}) collective-permute-start(bf16[192,384]{1,0:T(8,128)(2,1)S(1)} %fusion.10), channel_id=1, source_target_pairs={{0,2},{1,3},{2,4},{3,5},{4,6},{5,7},{6,0},{7,1},{8,10},{9,11},{10,... | collective-permute-start | bytes 442376 | tf_op jit(solution)/shard_map/ppermute | solution.py:356
  40.0 1.2 copy-start.9
  41.2 18.9 %all-to-all-start = ((bf16[4,384,384]{2,1,0:T(8,128)(2,1)}), bf16[4,384,384]{2,1,0:T(8,128)(2,1)S(1)}, u32[]{:S(2)}, u32[]{:S(2)}) async-start(bf16[4,384,384]{2,1,0:T(8,128)(2,1)} %get-tuple-element.45), calls=%async_computation | async-start | bytes 2359296 | tf_op jit(solution)/shard_map/all_to_all | solution.py:25
  45.4 14.7 %collective-permute-start.5 = (bf16[4,192,384]{2,1,0:T(8,128)(2,1)}, bf16[4,192,384]{2,1,0:T(8,128)(2,1)S(1)}, u32[]{:S(2)}, u32[]{:S(2)}) collective-permute-start(bf16[4,192,384]{2,1,0:T(8,128)(2,1)} %get-tuple-element.51), channel_id=1, source_target_pairs={{0,1},{1,0},{2,3},{3,2},{4,5},{5,4},{6,7},{7,6},{8,9},{9,8},{10,11... | collective-permute-start | bytes 1769480 | tf_op jit(solution)/shard_map/ppermute | solution.py:365
  46.6 13.5 %collective-permute-start.6 = (f32[192]{0:T(256)S(1)}, f32[192]{0:T(256)S(1)}, u32[]{:S(2)}, u32[]{:S(2)}) collective-permute-start(f32[192]{0:T(256)S(1)} %multiply_reduce_fusion), channel_id=1, source_target_pairs={{0,1},{1,0},{2,3},{3,2},{4,5},{5,4},{6,7},{7,6},{8,9},{9,8},{10,11... | collective-permute-start | bytes 2312 | tf_op jit(solution)/shard_map/ppermute | solution.py:370
  56.0 9.7 %copy-start.18 = (f32[192]{0:T(256)S(1)}, f32[192]{0:T(256)}, u32[]{:S(2)}) copy-start(f32[192]{0:T(256)} %param.36) | copy-start | bytes 2308
  60.2 7.1 %copy-start = (bf16[4,384,384]{2,1,0:T(8,128)(2,1)}, bf16[4,384,384]{2,1,0:T(8,128)(2,1)S(1)}, u32[]{:S(2)}) copy-start(bf16[4,384,384]{2,1,0:T(8,128)(2,1)S(1)} %all-to-all-done.q_own.k_own.v_own) | copy-start | bytes 3538948
  60.2 0.8 copy-start.10
  61.0 17.5 %all-to-all-start.1 = ((bf16[8,128,512]{2,1,0:T(8,128)(2,1)}), bf16[8,128,512]{2,1,0:T(8,128)(2,1)S(1)}, u32[]{:S(2)}, u32[]{:S(2)}) async-start(bf16[8,128,512]{2,1,0:T(8,128)(2,1)} %shard_map.212), calls=%async_computation.1 | async-start | bytes 2097152 | tf_op jit(solution)/shard_map/all_to_all | solution.py:25
  78.5 2.8 copy-start.3
  81.3 16.2 %all-to-all-start.2 = ((bf16[4,384,384]{2,1,0:T(8,128)(2,1)}), bf16[4,384,384]{2,1,0:T(8,128)(2,1)S(1)}, u32[]{:S(2)}, u32[]{:S(2)}) async-start(bf16[4,384,384]{2,1,0:T(8,128)(2,1)} %pad_maximum_fusion.1), calls=%async_computation.2 | async-start | bytes 2359296 | tf_op jit(solution)/shard_map/all_to_all | solution.py:25
  84.8 98.6 %all-gather.7.cloned.1.call-start = ((), (), s32[]{:S(2)}) async-start(), calls=%async_computation.9 | async-start | bytes 11501568 | tf_op jit(solution)/shard_map/all_gather | solution.py:39
  85.6 4.0 %slice-start = ((bf16[1,256,4096]{2,1,0:T(8,128)(2,1)}), bf16[1,128,4096]{2,1,0:T(8,128)(2,1)S(1)}, s32[]{:S(2)}) async-start(bf16[1,256,4096]{2,1,0:T(8,128)(2,1)} %x_ref.1), calls=%async_computation.10 | async-start | bytes 2097152 | tf_op jit(solution)/shard_map/slice | solution.py:359
  85.6 11.8 %collective-permute-start.7 = (bf16[192,1664]{1,0:T(8,128)(2,1)}, bf16[192,1664]{1,0:T(8,128)(2,1)}, u32[]{:S(2)}, u32[]{:S(2)}) collective-permute-start(bf16[192,1664]{1,0:T(8,128)(2,1)} %pad_dynamic-update-slice_fusion), channel_id=1, source_target_pairs={{0,64},{8,72},{16,80},{24,88},{32,96},{40,104},{48,112},{56,120},{... | collective-permute-start | bytes 1916936 | tf_op jit(solution)/shard_map/ppermute | solution.py:30
  97.5 3.0 %copy-start.1 = (bf16[4,384,384]{2,1,0:T(8,128)(2,1)}, bf16[4,384,384]{2,1,0:T(8,128)(2,1)S(1)}, u32[]{:S(2)}) copy-start(bf16[4,384,384]{2,1,0:T(8,128)(2,1)S(1)} %all-to-all-done.2.q_other.k_other.v_other) | copy-start | bytes 3538948
  100.5 34.7 %all-to-all-start.3 = ((bf16[128,24,128]{2,1,0:T(8,128)(2,1)}), bf16[128,24,128]{2,1,0:T(8,128)(2,1)S(1)}, u32[]{:S(2)}, u32[]{:S(2)}) async-start(bf16[128,24,128]{2,1,0:T(8,128)(2,1)} %bitcast.48), calls=%async_computation.3 | async-start | bytes 1572864 | tf_op jit(solution)/shard_map/all_to_all | solution.py:25
  115.4 20.6 %copy-start.19 = (s32[16]{0:T(128)S(1)}, s32[16]{0:T(128)}, u32[]{:S(2)}) copy-start(s32[16]{0:T(128)} %param.21) | copy-start | bytes 196
  136.5 7.9 %copy-start.16 = (f32[1,3072]{1,0:T(1,128)S(1)}, f32[1,3072]{1,0:T(1,128)}, u32[]{:S(2)}) copy-start(f32[1,3072]{1,0:T(1,128)} %param.27) | copy-start | bytes 36868
  136.5 8.7 %copy-start.17 = (f32[1,3072]{1,0:T(1,128)S(1)}, f32[1,3072]{1,0:T(1,128)}, u32[]{:S(2)}) copy-start(f32[1,3072]{1,0:T(1,128)} %param.28) | copy-start | bytes 36868
  136.5 9.0 %copy-start.6 = (bf16[1,128,3072]{2,1,0:T(8,128)(2,1)S(1)}, bf16[1,128,3072]{2,1,0:T(8,128)(2,1)}, u32[]{:S(2)}) copy-start(bf16[1,128,3072]{2,1,0:T(8,128)(2,1)} %param.37) | copy-start | bytes 2359300
  137.9 29.5 %all-to-all-start.4 = ((bf16[128,24,128]{2,1,0:T(8,128)(2,1)}), bf16[128,24,128]{2,1,0:T(8,128)(2,1)S(1)}, u32[]{:S(2)}, u32[]{:S(2)}) async-start(bf16[128,24,128]{2,1,0:T(8,128)(2,1)} %copy.110), calls=%async_computation.4 | async-start | bytes 1572864 | tf_op jit(solution)/shard_map/all_to_all | solution.py:25
  145.6 1.1 copy-start.20
  178.4 24.2 %all-to-all-start.5 = ((bf16[4,256,512]{2,1,0:T(8,128)(2,1)}), bf16[4,256,512]{2,1,0:T(8,128)(2,1)S(1)}, u32[]{:S(2)}, u32[]{:S(2)}) async-start(bf16[4,256,512]{2,1,0:T(8,128)(2,1)} %shard_map.214), calls=%async_computation.5 | async-start | bytes 2097152 | tf_op jit(solution)/shard_map/all_to_all | solution.py:25
  182.2 20.4 %collective-permute-start.9 = (bf16[128,3072]{1,0:T(8,128)(2,1)S(1)}, bf16[128,3072]{1,0:T(8,128)(2,1)S(1)}, u32[]{:S(2)}, u32[]{:S(2)}) collective-permute-start(bf16[128,3072]{1,0:T(8,128)(2,1)S(1)} %copy.115), channel_id=1, source_target_pairs={{0,1},{1,0},{2,3},{3,2},{4,5},{5,4},{6,7},{7,6},{8,9},{9,8},{10,11... | collective-permute-start | bytes 2359304 | tf_op jit(solution)/shard_map/ppermute | solution.py:438
  185.0 17.0 %collective-permute-start.8 = (bf16[128,128]{1,0:T(8,128)(2,1)S(1)}, bf16[128,128]{1,0:T(8,128)(2,1)S(1)}, u32[]{:S(2)}, u32[]{:S(2)}) collective-permute-start(bf16[128,128]{1,0:T(8,128)(2,1)S(1)} %fusion.11), channel_id=1, source_target_pairs={{0,1},{1,0},{2,3},{3,2},{4,5},{5,4},{6,7},{7,6},{8,9},{9,8},{10,11... | collective-permute-start | bytes 98312 | tf_op jit(solution)/shard_map/ppermute | solution.py:436
  202.6 0.9 copy-start.5
  203.5 10.9 %copy-start.11 = (f32[256,128]{1,0:T(8,128)}, f32[256,128]{1,0:T(8,128)S(1)}, u32[]{:S(2)}) copy-start(f32[256,128]{1,0:T(8,128)S(1)} %convert_reduce_fusion.1) | copy-start | bytes 393220
  203.5 3.4 %collective-permute-start.13 = (bf16[256,128]{1,0:T(8,128)(2,1)}, bf16[256,128]{1,0:T(8,128)(2,1)}, u32[]{:S(2)}, u32[]{:S(2)}) collective-permute-start(bf16[256,128]{1,0:T(8,128)(2,1)} %pad_maximum_fusion.7), channel_id=1, source_target_pairs={{0,2},{1,3},{2,0},{3,1},{4,6},{5,7},{6,4},{7,5},{8,10},{9,11},{10,... | collective-permute-start | bytes 196616 | tf_op jit(solution)/shard_map/ppermute | solution.py:469
  204.9 9.4 %copy-start.7 = (bf16[256,4,384]{0,2,1:T(8,128)(2,1)}, bf16[256,4,384]{0,2,1:T(8,128)(2,1)S(1)}, u32[]{:S(2)}) copy-start(bf16[256,4,384]{0,2,1:T(8,128)(2,1)S(1)} %copy.116) | copy-start | bytes 2359300
  207.8 10.4 %collective-permute-start.14 = (bf16[512,128]{1,0:T(8,128)(2,1)S(1)}, bf16[512,128]{1,0:T(8,128)(2,1)S(1)}, u32[]{:S(2)}, u32[]{:S(2)}) collective-permute-start(bf16[512,128]{1,0:T(8,128)(2,1)S(1)} %pad_maximum_fusion.6), channel_id=1, source_target_pairs={{0,4},{1,5},{2,6},{3,7},{4,0},{5,1},{6,2},{7,3},{8,12},{9,13},{10,... | collective-permute-start | bytes 393224 | tf_op jit(solution)/shard_map/ppermute | solution.py:469
  210.5 7.7 %copy-start.2 = (bf16[4,256,512]{2,1,0:T(8,128)(2,1)S(1)}, bf16[4,256,512]{2,1,0:T(8,128)(2,1)}, u32[]{:S(2)}) copy-start(bf16[4,256,512]{2,1,0:T(8,128)(2,1)} %shard_map.214) | copy-start | bytes 3145732
  214.4 9.0 %slice-start.1 = ((f32[256,128]{1,0:T(8,128)}), f32[128,128]{1,0:T(8,128)S(1)}, s32[]{:S(2)}) async-start(f32[256,128]{1,0:T(8,128)} %copy-done.11), calls=%async_computation.11 | async-start | bytes 131072 | tf_op jit(solution)/shard_map/slice | solution.py:456
  215.2 8.2 %collective-permute-start.10 = (bf16[128,128]{1,0:T(8,128)(2,1)S(1)}, bf16[128,128]{1,0:T(8,128)(2,1)S(1)}, u32[]{:S(2)}, u32[]{:S(2)}) collective-permute-start(bf16[128,128]{1,0:T(8,128)(2,1)S(1)} %slice.134), channel_id=1, source_target_pairs={{0,1},{1,0},{2,3},{3,2},{4,5},{5,4},{6,7},{7,6},{8,9},{9,8},{10,11... | collective-permute-start | bytes 98312 | tf_op jit(solution)/shard_map/ppermute | solution.py:442
  216.9 16.3 %collective-permute-start.11 = (bf16[128,1536]{1,0:T(8,128)(2,1)}, bf16[128,1536]{1,0:T(8,128)(2,1)}, u32[]{:S(2)}, u32[]{:S(2)}) collective-permute-start(bf16[128,1536]{1,0:T(8,128)(2,1)} %slice.133), channel_id=1, source_target_pairs={{0,1},{1,0},{2,3},{3,2},{4,5},{5,4},{6,7},{7,6},{8,9},{9,8},{10,11... | collective-permute-start | bytes 1179656 | tf_op jit(solution)/shard_map/ppermute | solution.py:454
  218.5 6.9 %collective-permute-start.15 = (bf16[64,384]{1,0:T(8,128)(2,1)S(1)}, bf16[64,384]{1,0:T(8,128)(2,1)S(1)}, u32[]{:S(2)}, u32[]{:S(2)}) collective-permute-start(bf16[64,384]{1,0:T(8,128)(2,1)S(1)} %convolution_convert_fusion.3), channel_id=1, source_target_pairs={{0,8},{8,0},{16,24},{24,16},{32,40},{40,32},{48,56},{56,48},{64,72... | collective-permute-start | bytes 147464 | tf_op jit(solution)/shard_map/ppermute | solution.py:478
  225.5 5.3 %collective-permute-start.16 = (bf16[64,384]{1,0:T(8,128)(2,1)S(1)}, bf16[64,384]{1,0:T(8,128)(2,1)S(1)}, u32[]{:S(2)}, u32[]{:S(2)}) collective-permute-start(bf16[64,384]{1,0:T(8,128)(2,1)S(1)} %add_convert_fusion.6), channel_id=1, source_target_pairs={{0,16},{8,24},{16,0},{24,8},{32,48},{40,56},{48,32},{56,40},{64,80... | collective-permute-start | bytes 147464 | tf_op jit(solution)/shard_map/ppermute | solution.py:478
  229.9 5.5 %copy-start.4 = (f32[256,1536]{1,0:T(8,128)}, f32[256,1536]{1,0:T(8,128)S(1)}, u32[]{:S(2)}) copy-start(f32[256,1536]{1,0:T(8,128)S(1)} %fusion) | copy-start | bytes 4718596
  231.4 11.2 %collective-permute-start.17 = (bf16[64,384]{1,0:T(8,128)(2,1)}, bf16[64,384]{1,0:T(8,128)(2,1)}, u32[]{:S(2)}, u32[]{:S(2)}) collective-permute-start(bf16[64,384]{1,0:T(8,128)(2,1)} %add_convert_fusion.5), channel_id=1, source_target_pairs={{0,32},{8,40},{16,48},{24,56},{32,0},{40,8},{48,16},{56,24},{64,96... | collective-permute-start | bytes 147464 | tf_op jit(solution)/shard_map/ppermute | solution.py:478
  233.2 12.0 %collective-permute-start.12 = (bf16[128,1536]{1,0:T(8,128)(2,1)}, bf16[128,1536]{1,0:T(8,128)(2,1)}, u32[]{:S(2)}, u32[]{:S(2)}) collective-permute-start(bf16[128,1536]{1,0:T(8,128)(2,1)} %slice.132), channel_id=1, source_target_pairs={{0,1},{1,0},{2,3},{3,2},{4,5},{5,4},{6,7},{7,6},{8,9},{9,8},{10,11... | collective-permute-start | bytes 1179656 | tf_op jit(solution)/shard_map/ppermute | solution.py:466
  236.5 16.0 %all-to-all-start.6 = ((bf16[16,64,192]{2,1,0:T(8,128)(2,1)}), bf16[16,64,192]{2,1,0:T(8,128)(2,1)S(1)}, u32[]{:S(2)}, u32[]{:S(2)}) async-start(bf16[16,64,192]{2,1,0:T(8,128)(2,1)} %bitcast.31), calls=%async_computation.6 | async-start | bytes 1048576 | tf_op jit(solution)/shard_map/all_to_all | solution.py:25
  243.4 9.7 %collective-permute-start.18 = (bf16[64,384]{1,0:T(8,128)(2,1)S(1)}, bf16[64,384]{1,0:T(8,128)(2,1)S(1)}, u32[]{:S(2)}, u32[]{:S(2)}) collective-permute-start(bf16[64,384]{1,0:T(8,128)(2,1)S(1)} %add_convert_fusion.4), channel_id=1, source_target_pairs={{0,64},{8,72},{16,80},{24,88},{32,96},{40,104},{48,112},{56,120},{... | collective-permute-start | bytes 147464 | tf_op jit(solution)/shard_map/ppermute | solution.py:493
  252.8 3.0 %collective-permute-start.19 = (bf16[64,192]{0,1:T(8,128)(2,1)S(1)}, bf16[64,192]{0,1:T(8,128)(2,1)S(1)}, u32[]{:S(2)}, u32[]{:S(2)}) collective-permute-start(bf16[64,192]{0,1:T(8,128)(2,1)S(1)} %copy.124), channel_id=1, source_target_pairs={{0,2},{1,3},{2,0},{3,1},{4,6},{5,7},{6,4},{7,5},{8,10},{9,11},{10,... | collective-permute-start | bytes 73736 | tf_op jit(solution)/shard_map/ppermute | solution.py:498
  255.8 9.5 %collective-permute-start.20 = (bf16[64,192]{0,1:T(8,128)(2,1)S(1)}, bf16[64,192]{0,1:T(8,128)(2,1)S(1)}, u32[]{:S(2)}, u32[]{:S(2)}) collective-permute-start(bf16[64,192]{0,1:T(8,128)(2,1)S(1)} %add_convert_fusion.3), channel_id=1, source_target_pairs={{0,4},{1,5},{2,6},{3,7},{4,0},{5,1},{6,2},{7,3},{8,12},{9,13},{10,... | collective-permute-start | bytes 73736 | tf_op jit(solution)/shard_map/ppermute | solution.py:498
  258.6 16.6 %all-to-all-start.7 = ((bf16[128,1,192]{2,1,0:T(2,128)(2,1)}), bf16[128,1,192]{2,1,0:T(2,128)(2,1)S(1)}, u32[]{:S(2)}, u32[]{:S(2)}) async-start(bf16[128,1,192]{2,1,0:T(2,128)(2,1)} %copy.126), calls=%async_computation.7 | async-start | bytes 262144 | tf_op jit(solution)/shard_map/all_to_all | solution.py:25
  265.4 10.6 %collective-permute-start.21 = (bf16[64,192]{0,1:T(8,128)(2,1)S(1)}, bf16[64,192]{0,1:T(8,128)(2,1)S(1)}, u32[]{:S(2)}, u32[]{:S(2)}) collective-permute-start(bf16[64,192]{0,1:T(8,128)(2,1)S(1)} %add_convert_fusion.2), channel_id=1, source_target_pairs={{0,1},{1,0},{2,3},{3,2},{4,5},{5,4},{6,7},{7,6},{8,9},{9,8},{10,11... | collective-permute-start | bytes 73736 | tf_op jit(solution)/shard_map/ppermute | solution.py:498
Sparse Core Ops, SparseCore 0:
  41.4 48.2 all-gather.4
  100.7 77.8 all-gather.6

commit v10 on v9

--- a/solution.py
+++ b/solution.py
@@ -434,11 +434,9 @@
     gathered = swap(attended, "seq", Y_GROUPS)
     down = jnp.dot(cotangent, up_all, preferred_element_type=F32).astype(BF16)
     down = jnp.concatenate([down, lax.ppermute(down, "seq", flip_z)], 0)
-    cotangent_other, _ = lax.optimization_barrier((cotangent, attended))
-    cotangent_other = lax.ppermute(cotangent_other, "seq", flip_z)
+    cotangent_other = lax.ppermute(cotangent, "seq", flip_z)
     gathered, down, cotangent_other = lax.optimization_barrier((gathered, down, cotangent_other))
     lowered = jnp.sum(gathered[:, :, own_rows:].astype(F32), 0)
-    gathered, lowered = lax.optimization_barrier((gathered, lowered))
     lowered_other = lax.ppermute(lowered[BLK:].astype(BF16), "seq", flip_z)
     gathered = gathered[:, :, :own_rows].transpose(1, 0, 2).reshape(2 * BLK, -1)
     half = model // 2
@@ -450,7 +448,7 @@
         return product[:BLK], product[BLK:].astype(BF16), sums
 
     kept_first, sent, sum_first = project(gathered, 0)
-    gathered, sent = lax.optimization_barrier((gathered, sent))
+    gathered, sent, down = lax.optimization_barrier((gathered, sent, down))
     landed_first = lax.ppermute(sent, "seq", flip_z)
 
     lowered = (lowered[:BLK] + lowered_other.astype(F32)).astype(BF16)[:, :rank]

time: 286 us -> 282 us (0.986)
  waiting for transfers between devices: 87 us -> 79.6 us
    ppermute x1, waiting for transfers between devices: 15.1 us -> 3.11 us  [on_device(): down = jnp.concatenate([down, lax.ppermute(down, 'seq', flip_z)], 0)]
    ppermute x2, starting transfers between devices: 3.79 us -> 0.9 us  [on_device(): moved = lax.ppermute(down, 'seq', [(i, i ^ bit) for i in range(n_seq)])]
    unnamed x51 -> x55, local copies, waits for them, and re-layouts: 6.78 us -> 7.16 us
  transfers between devices with their start and end apart: 32 -> 32, of which waited for: 13 -> 15; matrix products, arithmetic and copies ran while one was open for 16% -> 14% of each run, Pallas kernels for 13% -> 13%
where the time goes in v10:
time: 282 us; the launch traced here: 280 us
  starting transfers between devices  88.9 us (32%)
  waiting for transfers between devices  79.6 us (28%)
  Pallas kernels  41.8 us (15%)
  other arithmetic  22.3 us (8%)
  local copies, waits for them, and re-layouts  18.5 us (7%)
  between operations  14.6 us (5%)
  matrix products  14.1 us (5%)
    all_to_all x8, starting transfers between devices, swap(): lax.all_to_all(values, axes, 0, 0, tiled=True, axis_index_groups=groups)  50.4 us
    all_to_all x8, waiting for transfers between devices, swap(): lax.all_to_all(values, axes, 0, 0, tiled=True, axis_index_groups=groups)  49.8 us
    ppermute x2, waiting for transfers between devices, near_shard(): lax.ppermute(values, 'dp', [(i, (i + n_dp // 2) % n_dp) for i in range(n_...  13.9 us
    pallas_call x1, Pallas kernels, image_attention(): pl.pallas_call(image_kernel, grid=(heads, n_y), in_specs=[queries(), quer...  12.5 us
    dot_general x3, matrix products, dot_t(): lax.dot_general(left, right, (((1,), (1,)), ((), ())), preferred_element_...  10.9 us
    pallas_call x1, Pallas kernels, prompt_attention(): pl.pallas_call(prompt_kernel, grid=(heads + 1,), in_specs=[pl.BlockSpec(m...  9.61 us
    pallas_call x1, Pallas kernels, t5_in(): pl.pallas_call(t5_in_kernel, grid=(units // cut,), in_specs=[pl.BlockSpec...  8.39 us
    ppermute x3, starting transfers between devices, on_device(): moved = lax.ppermute(grad_a, 'dp', [(i, i ^ bit) for i in range(n_dp)])  7.93 us
  transfers between devices with their start and end apart: 32, of which 15 were waited for; matrix products, arithmetic and copies ran while one was open for 14% of the time, Pallas kernels for 13%

profile of v10, /device:TPU:1, one launch (start us, length us, event | category | flops | bytes accessed | tf_op | source)
XLA Modules:
  0.0 280.0 jit_solution(1924789356954491184)
XLA Ops:
  7.2 4.0 %shard_map.210 = (bf16[4,384,384]{2,1,0:T(8,128)(2,1)}, bf16[4,192,384]{2,1,0:T(8,128)(2,1)}, bf16[4,192,384]{2,1,0:T(8,128)(2,1)}) custom-call(s32[1]{0:T(128)} %bitcast.1._, bf16[3,128,3072]{2,1,0:T(8,128)(2,1)} %bitcast.91, bf16[3,128,3072]{2,1,0:T(8,128)(2,1)} %bitcast.92), custom_call_target="tpu_custom_call" | custom-call | bytes 4718592 | tf_op jit(solution)/shard_map/pallas_call | solution.py:80
  11.3 4.5 %collective-permute-start.4 = (bf16[4,192,384]{2,1,0:T(8,128)(2,1)}, bf16[4,192,384]{2,1,0:T(8,128)(2,1)S(1)}, u32[]{:S(2)}, u32[]{:S(2)}) collective-permute-start(bf16[4,192,384]{2,1,0:T(8,128)(2,1)} %get-tuple-element.46), channel_id=1, source_target_pairs={{0,1},{1,0},{2,3},{3,2},{4,5},{5,4},{6,7},{7,6},{8,9},{9,8},{10,11... | collective-permute-start | bytes 1769480 | tf_op jit(solution)/shard_map/ppermute | solution.py:348
  15.9 0.8 collective-permute-start
  17.2 2.8 %collective-permute-start.1 = (bf16[192,384]{1,0:T(8,128)(2,1)S(1)}, bf16[192,384]{1,0:T(8,128)(2,1)S(1)}, u32[]{:S(2)}, u32[]{:S(2)}) collective-permute-start(bf16[192,384]{1,0:T(8,128)(2,1)S(1)} %fusion.10), channel_id=1, source_target_pairs={{0,6},{1,7},{2,0},{3,1},{4,2},{5,3},{6,4},{7,5},{8,14},{9,15},{10,... | collective-permute-start | bytes 442376 | tf_op jit(solution)/shard_map/ppermute | solution.py:356
  21.0 8.4 %shard_map.211.hidden_ref = bf16[128,640]{1,0:T(8,128)(2,1)} custom-call(bf16[1,256,4096]{2,1,0:T(8,128)(2,1)} %x_ref.1, f32[1,4096]{1,0:T(1,128)} %bitcast.117, bf16[2,4096,640]{2,1,0:T(8,128)(2,1)} %up_w.1, bf16[2,4096,640]{2,1,0:T(8,128)(2,1)} %up_w.1), custom_call_target="tpu_custom_call" | custom-call | flops 1342177280 | bytes 10485760 | tf_op jit(solution)/shard_map/pallas_call | solution.py:255
  29.8 10.2 %collective-permute-done = bf16[192,1280]{1,0:T(8,128)(2,1)S(1)} collective-permute-done((bf16[192,1280]{1,0:T(8,128)(2,1)S(1)}, bf16[192,1280]{1,0:T(8,128)(2,1)S(1)}, u32[]{:S(2)}, u32[]{:S(2)}) %collective-permute-start) | collective-permute-done | bytes 491552 | tf_op jit(solution)/shard_map/ppermute | solution.py:30
  40.2 1.0 pad_maximum_fusion.2
  41.2 4.2 %all-to-all-start = ((bf16[4,384,384]{2,1,0:T(8,128)(2,1)}), bf16[4,384,384]{2,1,0:T(8,128)(2,1)S(1)}, u32[]{:S(2)}, u32[]{:S(2)}) async-start(bf16[4,384,384]{2,1,0:T(8,128)(2,1)} %get-tuple-element.43), calls=%async_computation | async-start | bytes 2359296 | tf_op jit(solution)/shard_map/all_to_all | solution.py:25
  45.4 0.9 collective-permute-start.5
  46.6 2.2 collective-permute-start.6
  48.8 7.2 %shard_map.212 = bf16[8,128,512]{2,1,0:T(8,128)(2,1)} custom-call(bf16[128,640]{1,0:T(8,128)(2,1)} %shard_map.211.hidden_ref, bf16[640,4096]{1,0:T(8,128)(2,1)} %out_w.1), custom_call_target="tpu_custom_call" | custom-call | flops 671088640 | bytes 5242880 | tf_op jit(solution)/shard_map/pallas_call | solution.py:284
  56.0 4.1 %collective-permute-done.6 = f32[192]{0:T(256)S(1)} collective-permute-done((f32[192]{0:T(256)S(1)}, f32[192]{0:T(256)S(1)}, u32[]{:S(2)}, u32[]{:S(2)}) %collective-permute-start.6) | collective-permute-done | bytes 800 | tf_op jit(solution)/shard_map/ppermute | solution.py:370
  60.2 0.8 copy-done.13
  61.0 4.7 %all-to-all-start.1 = ((bf16[8,128,512]{2,1,0:T(8,128)(2,1)}), bf16[8,128,512]{2,1,0:T(8,128)(2,1)S(1)}, u32[]{:S(2)}, u32[]{:S(2)}) async-start(bf16[8,128,512]{2,1,0:T(8,128)(2,1)} %shard_map.212), calls=%async_computation.1 | async-start | bytes 2097152 | tf_op jit(solution)/shard_map/all_to_all | solution.py:25
  68.8 9.7 %all-to-all-done.1 = bf16[8,128,512]{2,1,0:T(8,128)(2,1)S(1)} async-done(((bf16[8,128,512]{2,1,0:T(8,128)(2,1)}), bf16[8,128,512]{2,1,0:T(8,128)(2,1)S(1)}, u32[]{:S(2)}, u32[]{:S(2)}) %all-to-all-start.1) | async-done | bytes 1048608 | tf_op jit(solution)/shard_map/all_to_all | solution.py:25
  78.5 2.8 pad_maximum_fusion.1
  81.3 3.5 %all-to-all-start.2 = ((bf16[4,384,384]{2,1,0:T(8,128)(2,1)}), bf16[4,384,384]{2,1,0:T(8,128)(2,1)S(1)}, u32[]{:S(2)}, u32[]{:S(2)}) async-start(bf16[4,384,384]{2,1,0:T(8,128)(2,1)} %pad_maximum_fusion.1), calls=%async_computation.2 | async-start | bytes 2359296 | tf_op jit(solution)/shard_map/all_to_all | solution.py:25
  85.8 0.8 dynamic_slice.7
  86.6 1.4 convert_reduce_fusion
  88.0 1.6 all-gather.5.cloned.1.call-done
  89.7 3.0 %fusion.7 = bf16[16,8,24,128]{3,1,2,0:T(8,128)(2,1)S(1)} fusion(bf16[3072,1280]{1,0:T(8,128)(2,1)} %bitcast.88, f32[128,512]{1,0:T(8,128)S(1)} %convert_reduce_fusion, f32[512]{0:T(512)S(1)} %dynamic_slice.7, bf16[1,128,4096]{2,1,0:T(8,128)(2,1)S(1)} %slice-done, s32[]{:T(128)S(6)} %select_n.153), kind=kOutput, calls=%fused_computation.12 | convolution fusion | flops 403308544 | bytes 4327428 | tf_op jit(solution)/shard_map/dot_general | solution.py:56
  92.7 1.0 copy.130
  93.7 3.7 %collective-permute-done.7 = bf16[192,1664]{1,0:T(8,128)(2,1)} collective-permute-done((bf16[192,1664]{1,0:T(8,128)(2,1)}, bf16[192,1664]{1,0:T(8,128)(2,1)}, u32[]{:S(2)}, u32[]{:S(2)}) %collective-permute-start.7) | collective-permute-done | bytes 639008 | tf_op jit(solution)/shard_map/ppermute | solution.py:30
  97.5 1.8 select_bitcast_fusion.1
  99.3 1.2 pad_maximum_fusion
  100.5 14.9 %all-to-all-start.3 = ((bf16[128,24,128]{2,1,0:T(8,128)(2,1)}), bf16[128,24,128]{2,1,0:T(8,128)(2,1)S(1)}, u32[]{:S(2)}, u32[]{:S(2)}) async-start(bf16[128,24,128]{2,1,0:T(8,128)(2,1)} %bitcast.48), calls=%async_computation.3 | async-start | bytes 1572864 | tf_op jit(solution)/shard_map/all_to_all | solution.py:25
  115.4 12.5 %shard_map.213 = (f32[1024,384]{1,0:T(8,128)}, f32[1024,384]{1,0:T(8,128)}) custom-call(bf16[4,384,384]{2,1,0:T(8,128)(2,1)} %copy-done, bf16[4,384,384]{2,1,0:T(8,128)(2,1)} %copy-done.1, bf16[4,384,384]{2,1,0:T(8,128)(2,1)} %copy-done, bf16[4,384,384]{2,1,0:T(8,128)(2,1)} %copy-done.1, bf16[4,384,384]{2,1,0:T(8,128)(2,1)} %copy-done, ...), custom_call_target="tpu_custom_call" | custom-call | flops 2415919104 | bytes 5505024 | tf_op jit(solution)/shard_map/pallas_call | solution.py:130
  127.9 7.3 %all-to-all-done.3 = bf16[128,24,128]{2,1,0:T(8,128)(2,1)S(1)} async-done(((bf16[128,24,128]{2,1,0:T(8,128)(2,1)}), bf16[128,24,128]{2,1,0:T(8,128)(2,1)S(1)}, u32[]{:S(2)}, u32[]{:S(2)}) %all-to-all-start.3) | async-done | bytes 786464 | tf_op jit(solution)/shard_map/all_to_all | solution.py:25
  136.5 1.4 copy.110
  137.9 5.9 %all-to-all-start.4 = ((bf16[128,24,128]{2,1,0:T(8,128)(2,1)}), bf16[128,24,128]{2,1,0:T(8,128)(2,1)S(1)}, u32[]{:S(2)}, u32[]{:S(2)}) async-start(bf16[128,24,128]{2,1,0:T(8,128)(2,1)} %copy.110), calls=%async_computation.4 | async-start | bytes 1572864 | tf_op jit(solution)/shard_map/all_to_all | solution.py:25
  144.6 3.5 %collective-permute-start.9 = (bf16[128,3072]{1,0:T(8,128)(2,1)S(1)}, bf16[128,3072]{1,0:T(8,128)(2,1)}, u32[]{:S(2)}, u32[]{:S(2)}) collective-permute-start(bf16[128,3072]{1,0:T(8,128)(2,1)S(1)} %copy.115), channel_id=1, source_target_pairs={{0,1},{1,0},{2,3},{3,2},{4,5},{5,4},{6,7},{7,6},{8,9},{9,8},{10,11... | collective-permute-start | bytes 2359304 | tf_op jit(solution)/shard_map/ppermute | solution.py:437
  151.2 16.3 %all-to-all-done.4 = bf16[128,24,128]{2,1,0:T(8,128)(2,1)S(1)} async-done(((bf16[128,24,128]{2,1,0:T(8,128)(2,1)}), bf16[128,24,128]{2,1,0:T(8,128)(2,1)S(1)}, u32[]{:S(2)}, u32[]{:S(2)}) %all-to-all-start.4) | async-done | bytes 786464 | tf_op jit(solution)/shard_map/all_to_all | solution.py:25
  167.6 1.1 fusion.6.text_ref
  168.7 9.6 %shard_map.214 = bf16[4,256,512]{2,1,0:T(8,128)(2,1)} custom-call(s32[1]{0:T(128)} %bitcast.length_ref, bf16[4,384,384]{2,1,0:T(8,128)(2,1)} %copy-done, bf16[4,384,384]{2,1,0:T(8,128)(2,1)} %copy-done.1, bf16[128,3072]{1,0:T(8,128)(2,1)} %fusion.6.text_ref, bf16[3072,1280]{1,0:T(8,128)(2,1)} %bitcast.89, bf16[3072,1280]{1,0:T(8,128)(2,1)} %bitcast.90, ...), custom_call_target="tpu_custom_call" | custom-call | flops 905969664 | bytes 9437184 | tf_op jit(solution)/shard_map/pallas_call | solution.py:214
  178.3 3.5 %all-to-all-start.5 = ((bf16[4,256,512]{2,1,0:T(8,128)(2,1)}), bf16[4,256,512]{2,1,0:T(8,128)(2,1)S(1)}, u32[]{:S(2)}, u32[]{:S(2)}) async-start(bf16[4,256,512]{2,1,0:T(8,128)(2,1)} %shard_map.214), calls=%async_computation.5 | async-start | bytes 2097152 | tf_op jit(solution)/shard_map/all_to_all | solution.py:25
  181.9 1.5 fusion.11
  183.4 1.2 collective-permute-start.8
  184.7 3.1 %collective-permute-done.8 = bf16[128,128]{1,0:T(8,128)(2,1)S(1)} collective-permute-done((bf16[128,128]{1,0:T(8,128)(2,1)S(1)}, bf16[128,128]{1,0:T(8,128)(2,1)S(1)}, u32[]{:S(2)}, u32[]{:S(2)}) %collective-permute-start.8) | collective-permute-done | bytes 32800 | tf_op jit(solution)/shard_map/ppermute | solution.py:436
  187.8 7.4 %all-to-all-done.5 = bf16[4,256,512]{2,1,0:T(8,128)(2,1)S(1)} async-done(((bf16[4,256,512]{2,1,0:T(8,128)(2,1)}), bf16[4,256,512]{2,1,0:T(8,128)(2,1)S(1)}, u32[]{:S(2)}, u32[]{:S(2)}) %all-to-all-start.5) | async-done | bytes 1048608 | tf_op jit(solution)/shard_map/all_to_all | solution.py:25
  195.3 1.2 copy.116
  196.5 4.0 %fusion.2 = f32[256,1536]{1,0:T(8,128)S(1)} fusion(bf16[256,1536]{0,1:T(8,128)(2,1)} %bitcast.108, bf16[3072,1664]{1,0:T(8,128)(2,1)} %bitcast.120), kind=kOutput, calls=%fused_computation.2 | convolution fusion | flops 1207959552 | bytes 7077888 | tf_op jit(solution)/shard_map/dot_general | solution.py:56
  200.5 1.1 copy-done.6
  202.8 2.8 %collective-permute-done.13 = bf16[256,128]{1,0:T(8,128)(2,1)S(1)} collective-permute-done((bf16[256,128]{1,0:T(8,128)(2,1)S(1)}, bf16[256,128]{1,0:T(8,128)(2,1)S(1)}, u32[]{:S(2)}, u32[]{:S(2)}) %collective-permute-start.13) | collective-permute-done | bytes 65568 | tf_op jit(solution)/shard_map/ppermute | solution.py:467
  206.9 1.8 collective-permute-start.10
  208.7 1.2 collective-permute-start.11
  210.0 1.8 collective-permute-done.14
  212.2 5.0 %collective-permute-start.15 = (bf16[64,384]{1,0:T(8,128)(2,1)S(1)}, bf16[64,384]{1,0:T(8,128)(2,1)S(1)}, u32[]{:S(2)}, u32[]{:S(2)}) collective-permute-start(bf16[64,384]{1,0:T(8,128)(2,1)S(1)} %convolution_convert_fusion.3), channel_id=1, source_target_pairs={{0,8},{8,0},{16,24},{24,16},{32,40},{40,32},{48,56},{56,48},{64,72... | collective-permute-start | bytes 147464 | tf_op jit(solution)/shard_map/ppermute | solution.py:476
  218.3 1.0 copy.117
  219.7 3.9 %fusion = f32[256,1536]{1,0:T(8,128)S(1)} fusion(bf16[256,1536]{0,1:T(8,128)(2,1)S(1)} %bitcast.109, bf16[3072,1664]{1,0:T(8,128)(2,1)} %bitcast.121), kind=kOutput, calls=%fused_computation | convolution fusion | flops 1207959552 | bytes 7077888 | tf_op jit(solution)/shard_map/dot_general | solution.py:56
  223.6 1.2 copy-done.8
  225.6 1.5 collective-permute-start.12
  227.1 2.5 collective-permute-start.17
  229.6 4.2 %all-to-all-start.6 = ((bf16[16,64,192]{2,1,0:T(8,128)(2,1)}), bf16[16,64,192]{2,1,0:T(8,128)(2,1)S(1)}, u32[]{:S(2)}, u32[]{:S(2)}) async-start(bf16[16,64,192]{2,1,0:T(8,128)(2,1)} %bitcast.31), calls=%async_computation.6 | async-start | bytes 1048576 | tf_op jit(solution)/shard_map/all_to_all | solution.py:25
  234.4 1.4 collective-permute-start.18
  235.9 1.9 collective-permute-done.12
  237.8 3.1 %multiply_reduce_fusion.1 = (f32[1536]{0:T(1024)S(1)}, f32[1536]{0:T(1024)S(1)}, f32[1536]{0:T(1024)S(1)}, f32[1536]{0:T(1024)S(1)}, bf16[128,1536]{1,0:T(8,128)(2,1)S(1)}, /*index=5*/bf16[128,1536]{1,0:T(8,128)(2,1)}) fusion(f32[256,1536]{1,0:T(8,128)} %copy-done.8, bf16[128,3072]{1,0:T(8,128)(2,1)} %collective-permute-done.9, ...), kind=kLoop, calls=%fused_computation.26 | loop fusion | flops 3532800 | bytes 6316032 | tf_op jit(solution)/shard_map/reduce_sum | solution.py:447
  241.1 2.6 all-to-all-done.6
  244.7 1.5 add_bitcast_fusion
  246.1 1.2 copy.119
  247.6 2.5 collective-permute-start.20
  250.2 1.2 copy.127
  252.1 9.6 %all-to-all-start.7 = ((bf16[128,1,192]{2,1,0:T(2,128)(2,1)}), bf16[128,1,192]{2,1,0:T(2,128)(2,1)S(1)}, u32[]{:S(2)}, u32[]{:S(2)}) async-start(bf16[128,1,192]{2,1,0:T(2,128)(2,1)} %copy.126), calls=%async_computation.7 | async-start | bytes 262144 | tf_op jit(solution)/shard_map/all_to_all | solution.py:25
  261.7 3.4 %collective-permute-start.21 = (bf16[64,192]{0,1:T(8,128)(2,1)S(1)}, bf16[64,192]{0,1:T(8,128)(2,1)S(1)}, u32[]{:S(2)}, u32[]{:S(2)}) collective-permute-start(bf16[64,192]{0,1:T(8,128)(2,1)S(1)} %add_convert_fusion.2), channel_id=1, source_target_pairs={{0,1},{1,0},{2,3},{3,2},{4,5},{5,4},{6,7},{7,6},{8,9},{9,8},{10,11... | collective-permute-start | bytes 73736 | tf_op jit(solution)/shard_map/ppermute | solution.py:496
  265.1 6.4 %all-to-all-done.7 = bf16[128,1,192]{2,1,0:T(2,128)(2,1)S(1)} async-done(((bf16[128,1,192]{2,1,0:T(2,128)(2,1)}), bf16[128,1,192]{2,1,0:T(2,128)(2,1)S(1)}, u32[]{:S(2)}, u32[]{:S(2)}) %all-to-all-start.7) | async-done | bytes 49184 | tf_op jit(solution)/shard_map/all_to_all | solution.py:25
  (148 shorter events, 21.4 us)
Async XLA Ops:
  7.2 82.5 %all-gather.5.cloned.1.call-start = ((), (), s32[]{:S(2)}) async-start(), calls=%async_computation.8 | async-start | bytes 8847360 | tf_op jit(solution)/shard_map/all_gather | solution.py:39
  7.2 8.6 %copy-start.16 = (bf16[192,2,384]{2,1,0:T(2,128)(2,1)S(1)}, bf16[192,2,384]{2,1,0:T(2,128)(2,1)}, u32[]{:S(2)}) copy-start(bf16[192,2,384]{2,1,0:T(2,128)(2,1)} %param.29) | copy-start | bytes 884740
  7.2 8.6 %copy-start.11 = (bf16[512,192]{0,1:T(8,128)(2,1)S(1)}, bf16[512,192]{0,1:T(8,128)(2,1)}, u32[]{:S(2)}) copy-start(bf16[512,192]{0,1:T(8,128)(2,1)} %param.26) | copy-start | bytes 589828
  11.3 5.4 %copy-start.15 = (f32[384,64]{0,1:T(8,128)S(1)}, f32[384,64]{0,1:T(8,128)}, u32[]{:S(2)}) copy-start(f32[384,64]{0,1:T(8,128)} %param.34) | copy-start | bytes 294916
  11.3 5.4 %copy-start.17 = (f32[64,192]{1,0:T(8,128)S(1)}, f32[64,192]{1,0:T(8,128)}, u32[]{:S(2)}) copy-start(f32[64,192]{1,0:T(8,128)} %param.35) | copy-start | bytes 147460
  11.3 5.4 %copy-start.18 = (bf16[384,192]{0,1:T(8,128)(2,1)S(1)}, bf16[384,192]{0,1:T(8,128)(2,1)}, u32[]{:S(2)}) copy-start(bf16[384,192]{0,1:T(8,128)(2,1)} %param.33) | copy-start | bytes 442372
  11.3 28.7 %collective-permute-start.4 = (bf16[4,192,384]{2,1,0:T(8,128)(2,1)}, bf16[4,192,384]{2,1,0:T(8,128)(2,1)S(1)}, u32[]{:S(2)}, u32[]{:S(2)}) collective-permute-start(bf16[4,192,384]{2,1,0:T(8,128)(2,1)} %get-tuple-element.46), channel_id=1, source_target_pairs={{0,1},{1,0},{2,3},{3,2},{4,5},{5,4},{6,7},{7,6},{8,9},{9,8},{10,11... | collective-permute-start | bytes 1769480 | tf_op jit(solution)/shard_map/ppermute | solution.py:348
  15.9 24.1 %collective-permute-start = (bf16[192,1280]{1,0:T(8,128)(2,1)S(1)}, bf16[192,1280]{1,0:T(8,128)(2,1)S(1)}, u32[]{:S(2)}, u32[]{:S(2)}) collective-permute-start(bf16[192,1280]{1,0:T(8,128)(2,1)S(1)} %pad_maximum_fusion.3), channel_id=1, source_target_pairs={{0,64},{8,72},{16,80},{24,88},{32,96},{40,104},{48,112},{56,120},{... | collective-permute-start | bytes 1474568 | tf_op jit(solution)/shard_map/ppermute | solution.py:30
  17.2 12.2 %collective-permute-start.1 = (bf16[192,384]{1,0:T(8,128)(2,1)S(1)}, bf16[192,384]{1,0:T(8,128)(2,1)S(1)}, u32[]{:S(2)}, u32[]{:S(2)}) collective-permute-start(bf16[192,384]{1,0:T(8,128)(2,1)S(1)} %fusion.10), channel_id=1, source_target_pairs={{0,6},{1,7},{2,0},{3,1},{4,2},{5,3},{6,4},{7,5},{8,14},{9,15},{10,... | collective-permute-start | bytes 442376 | tf_op jit(solution)/shard_map/ppermute | solution.py:356
  20.0 9.4 %collective-permute-start.2 = (bf16[192,384]{1,0:T(8,128)(2,1)S(1)}, bf16[192,384]{1,0:T(8,128)(2,1)S(1)}, u32[]{:S(2)}, u32[]{:S(2)}) collective-permute-start(bf16[192,384]{1,0:T(8,128)(2,1)S(1)} %fusion.10), channel_id=1, source_target_pairs={{0,4},{1,5},{2,6},{3,7},{4,0},{5,1},{6,2},{7,3},{8,12},{9,13},{10,... | collective-permute-start | bytes 442376 | tf_op jit(solution)/shard_map/ppermute | solution.py:356
  20.3 9.5 %collective-permute-start.3 = (bf16[192,384]{1,0:T(8,128)(2,1)S(1)}, bf16[192,384]{1,0:T(8,128)(2,1)S(1)}, u32[]{:S(2)}, u32[]{:S(2)}) collective-permute-start(bf16[192,384]{1,0:T(8,128)(2,1)S(1)} %fusion.10), channel_id=1, source_target_pairs={{0,2},{1,3},{2,4},{3,5},{4,6},{5,7},{6,0},{7,1},{8,10},{9,11},{10,... | collective-permute-start | bytes 442376 | tf_op jit(solution)/shard_map/ppermute | solution.py:356
  40.0 1.2 copy-start.12
  41.2 18.9 %all-to-all-start = ((bf16[4,384,384]{2,1,0:T(8,128)(2,1)}), bf16[4,384,384]{2,1,0:T(8,128)(2,1)S(1)}, u32[]{:S(2)}, u32[]{:S(2)}) async-start(bf16[4,384,384]{2,1,0:T(8,128)(2,1)} %get-tuple-element.43), calls=%async_computation | async-start | bytes 2359296 | tf_op jit(solution)/shard_map/all_to_all | solution.py:25
  45.4 14.7 %collective-permute-start.5 = (bf16[4,192,384]{2,1,0:T(8,128)(2,1)}, bf16[4,192,384]{2,1,0:T(8,128)(2,1)S(1)}, u32[]{:S(2)}, u32[]{:S(2)}) collective-permute-start(bf16[4,192,384]{2,1,0:T(8,128)(2,1)} %get-tuple-element.49), channel_id=1, source_target_pairs={{0,1},{1,0},{2,3},{3,2},{4,5},{5,4},{6,7},{7,6},{8,9},{9,8},{10,11... | collective-permute-start | bytes 1769480 | tf_op jit(solution)/shard_map/ppermute | solution.py:365
  46.6 13.5 %collective-permute-start.6 = (f32[192]{0:T(256)S(1)}, f32[192]{0:T(256)S(1)}, u32[]{:S(2)}, u32[]{:S(2)}) collective-permute-start(f32[192]{0:T(256)S(1)} %multiply_reduce_fusion), channel_id=1, source_target_pairs={{0,1},{1,0},{2,3},{3,2},{4,5},{5,4},{6,7},{7,6},{8,9},{9,8},{10,11... | collective-permute-start | bytes 2312 | tf_op jit(solution)/shard_map/ppermute | solution.py:370
  56.0 9.7 %copy-start.21 = (f32[192]{0:T(256)S(1)}, f32[192]{0:T(256)}, u32[]{:S(2)}) copy-start(f32[192]{0:T(256)} %param.36) | copy-start | bytes 2308
  60.2 7.1 %copy-start = (bf16[4,384,384]{2,1,0:T(8,128)(2,1)}, bf16[4,384,384]{2,1,0:T(8,128)(2,1)S(1)}, u32[]{:S(2)}) copy-start(bf16[4,384,384]{2,1,0:T(8,128)(2,1)S(1)} %all-to-all-done.q_own.k_own.v_own) | copy-start | bytes 3538948
  60.2 0.8 copy-start.13
  61.0 17.5 %all-to-all-start.1 = ((bf16[8,128,512]{2,1,0:T(8,128)(2,1)}), bf16[8,128,512]{2,1,0:T(8,128)(2,1)S(1)}, u32[]{:S(2)}, u32[]{:S(2)}) async-start(bf16[8,128,512]{2,1,0:T(8,128)(2,1)} %shard_map.212), calls=%async_computation.1 | async-start | bytes 2097152 | tf_op jit(solution)/shard_map/all_to_all | solution.py:25
  78.5 2.8 copy-start.3
  81.3 16.2 %all-to-all-start.2 = ((bf16[4,384,384]{2,1,0:T(8,128)(2,1)}), bf16[4,384,384]{2,1,0:T(8,128)(2,1)S(1)}, u32[]{:S(2)}, u32[]{:S(2)}) async-start(bf16[4,384,384]{2,1,0:T(8,128)(2,1)} %pad_maximum_fusion.1), calls=%async_computation.2 | async-start | bytes 2359296 | tf_op jit(solution)/shard_map/all_to_all | solution.py:25
  84.8 97.0 %all-gather.7.cloned.1.call-start = ((), (), s32[]{:S(2)}) async-start(), calls=%async_computation.9 | async-start | bytes 11501568 | tf_op jit(solution)/shard_map/all_gather | solution.py:39
  85.6 4.0 %slice-start = ((bf16[1,256,4096]{2,1,0:T(8,128)(2,1)}), bf16[1,128,4096]{2,1,0:T(8,128)(2,1)S(1)}, s32[]{:S(2)}) async-start(bf16[1,256,4096]{2,1,0:T(8,128)(2,1)} %x_ref.1), calls=%async_computation.10 | async-start | bytes 2097152 | tf_op jit(solution)/shard_map/slice | solution.py:359
  85.6 11.8 %collective-permute-start.7 = (bf16[192,1664]{1,0:T(8,128)(2,1)}, bf16[192,1664]{1,0:T(8,128)(2,1)}, u32[]{:S(2)}, u32[]{:S(2)}) collective-permute-start(bf16[192,1664]{1,0:T(8,128)(2,1)} %pad_dynamic-update-slice_fusion), channel_id=1, source_target_pairs={{0,64},{8,72},{16,80},{24,88},{32,96},{40,104},{48,112},{56,120},{... | collective-permute-start | bytes 1916936 | tf_op jit(solution)/shard_map/ppermute | solution.py:30
  97.5 3.0 %copy-start.1 = (bf16[4,384,384]{2,1,0:T(8,128)(2,1)}, bf16[4,384,384]{2,1,0:T(8,128)(2,1)S(1)}, u32[]{:S(2)}) copy-start(bf16[4,384,384]{2,1,0:T(8,128)(2,1)S(1)} %all-to-all-done.2.q_other.k_other.v_other) | copy-start | bytes 3538948
  100.5 34.7 %all-to-all-start.3 = ((bf16[128,24,128]{2,1,0:T(8,128)(2,1)}), bf16[128,24,128]{2,1,0:T(8,128)(2,1)S(1)}, u32[]{:S(2)}, u32[]{:S(2)}) async-start(bf16[128,24,128]{2,1,0:T(8,128)(2,1)} %bitcast.48), calls=%async_computation.3 | async-start | bytes 1572864 | tf_op jit(solution)/shard_map/all_to_all | solution.py:25
  115.4 20.6 %copy-start.22 = (s32[16]{0:T(128)S(1)}, s32[16]{0:T(128)}, u32[]{:S(2)}) copy-start(s32[16]{0:T(128)} %param.21) | copy-start | bytes 196
  136.5 7.3 %copy-start.9 = (bf16[1,128,3072]{2,1,0:T(8,128)(2,1)S(1)}, bf16[1,128,3072]{2,1,0:T(8,128)(2,1)}, u32[]{:S(2)}) copy-start(bf16[1,128,3072]{2,1,0:T(8,128)(2,1)} %param.37) | copy-start | bytes 2359300
  137.9 29.5 %all-to-all-start.4 = ((bf16[128,24,128]{2,1,0:T(8,128)(2,1)}), bf16[128,24,128]{2,1,0:T(8,128)(2,1)S(1)}, u32[]{:S(2)}, u32[]{:S(2)}) async-start(bf16[128,24,128]{2,1,0:T(8,128)(2,1)} %copy.110), calls=%async_computation.4 | async-start | bytes 1572864 | tf_op jit(solution)/shard_map/all_to_all | solution.py:25
  144.2 4.5 %copy-start.19 = (f32[1,3072]{1,0:T(1,128)S(1)}, f32[1,3072]{1,0:T(1,128)}, u32[]{:S(2)}) copy-start(f32[1,3072]{1,0:T(1,128)} %param.27) | copy-start | bytes 36868
  144.2 5.3 %copy-start.20 = (f32[1,3072]{1,0:T(1,128)S(1)}, f32[1,3072]{1,0:T(1,128)}, u32[]{:S(2)}) copy-start(f32[1,3072]{1,0:T(1,128)} %param.28) | copy-start | bytes 36868
  144.2 6.3 %copy-start.23 = (s32[16]{0:T(128)S(1)}, s32[16]{0:T(128)}, u32[]{:S(2)}) copy-start(s32[16]{0:T(128)} %param.20) | copy-start | bytes 196
  144.6 24.2 %copy-start.4 = (bf16[128,3072]{1,0:T(8,128)(2,1)}, bf16[128,3072]{1,0:T(8,128)(2,1)S(1)}, u32[]{:S(2)}) copy-start(bf16[128,3072]{1,0:T(8,128)(2,1)S(1)} %copy.115) | copy-start | bytes 2359300
  144.6 43.2 %collective-permute-start.9 = (bf16[128,3072]{1,0:T(8,128)(2,1)S(1)}, bf16[128,3072]{1,0:T(8,128)(2,1)}, u32[]{:S(2)}, u32[]{:S(2)}) collective-permute-start(bf16[128,3072]{1,0:T(8,128)(2,1)S(1)} %copy.115), channel_id=1, source_target_pairs={{0,1},{1,0},{2,3},{3,2},{4,5},{5,4},{6,7},{7,6},{8,9},{9,8},{10,11... | collective-permute-start | bytes 2359304 | tf_op jit(solution)/shard_map/ppermute | solution.py:437
  178.3 16.9 %all-to-all-start.5 = ((bf16[4,256,512]{2,1,0:T(8,128)(2,1)}), bf16[4,256,512]{2,1,0:T(8,128)(2,1)S(1)}, u32[]{:S(2)}, u32[]{:S(2)}) async-start(bf16[4,256,512]{2,1,0:T(8,128)(2,1)} %shard_map.214), calls=%async_computation.5 | async-start | bytes 2097152 | tf_op jit(solution)/shard_map/all_to_all | solution.py:25
  183.4 4.3 %collective-permute-start.8 = (bf16[128,128]{1,0:T(8,128)(2,1)S(1)}, bf16[128,128]{1,0:T(8,128)(2,1)S(1)}, u32[]{:S(2)}, u32[]{:S(2)}) collective-permute-start(bf16[128,128]{1,0:T(8,128)(2,1)S(1)} %fusion.11), channel_id=1, source_target_pairs={{0,1},{1,0},{2,3},{3,2},{4,5},{5,4},{6,7},{7,6},{8,9},{9,8},{10,11... | collective-permute-start | bytes 98312 | tf_op jit(solution)/shard_map/ppermute | solution.py:436
  200.5 1.1 copy-start.6
  201.7 10.2 %copy-start.2 = (bf16[4,256,512]{2,1,0:T(8,128)(2,1)S(1)}, bf16[4,256,512]{2,1,0:T(8,128)(2,1)}, u32[]{:S(2)}) copy-start(bf16[4,256,512]{2,1,0:T(8,128)(2,1)} %shard_map.214) | copy-start | bytes 3145732
  202.5 3.1 %collective-permute-start.13 = (bf16[256,128]{1,0:T(8,128)(2,1)S(1)}, bf16[256,128]{1,0:T(8,128)(2,1)S(1)}, u32[]{:S(2)}, u32[]{:S(2)}) collective-permute-start(bf16[256,128]{1,0:T(8,128)(2,1)S(1)} %pad_maximum_fusion.7), channel_id=1, source_target_pairs={{0,2},{1,3},{2,0},{3,1},{4,6},{5,7},{6,4},{7,5},{8,10},{9,11},{10,... | collective-permute-start | bytes 196616 | tf_op jit(solution)/shard_map/ppermute | solution.py:467
  206.3 5.5 %collective-permute-start.14 = (bf16[512,128]{1,0:T(8,128)(2,1)}, bf16[512,128]{1,0:T(8,128)(2,1)S(1)}, u32[]{:S(2)}, u32[]{:S(2)}) collective-permute-start(bf16[512,128]{1,0:T(8,128)(2,1)} %pad_maximum_fusion.6), channel_id=1, source_target_pairs={{0,4},{1,5},{2,6},{3,7},{4,0},{5,1},{6,2},{7,3},{8,12},{9,13},{10,... | collective-permute-start | bytes 393224 | tf_op jit(solution)/shard_map/ppermute | solution.py:467
  206.9 10.2 %collective-permute-start.10 = (bf16[128,128]{1,0:T(8,128)(2,1)S(1)}, bf16[128,128]{1,0:T(8,128)(2,1)S(1)}, u32[]{:S(2)}, u32[]{:S(2)}) collective-permute-start(bf16[128,128]{1,0:T(8,128)(2,1)S(1)} %slice.137), channel_id=1, source_target_pairs={{0,1},{1,0},{2,3},{3,2},{4,5},{5,4},{6,7},{7,6},{8,9},{9,8},{10,11... | collective-permute-start | bytes 98312 | tf_op jit(solution)/shard_map/ppermute | solution.py:440
  208.7 16.8 %collective-permute-start.11 = (bf16[128,1536]{1,0:T(8,128)(2,1)}, bf16[128,1536]{1,0:T(8,128)(2,1)S(1)}, u32[]{:S(2)}, u32[]{:S(2)}) collective-permute-start(bf16[128,1536]{1,0:T(8,128)(2,1)} %slice.136), channel_id=1, source_target_pairs={{0,1},{1,0},{2,3},{3,2},{4,5},{5,4},{6,7},{7,6},{8,9},{9,8},{10,11... | collective-permute-start | bytes 1179656 | tf_op jit(solution)/shard_map/ppermute | solution.py:452
  212.2 7.5 %copy-start.10 = (bf16[256,4,384]{0,2,1:T(8,128)(2,1)S(1)}, bf16[256,4,384]{0,2,1:T(8,128)(2,1)}, u32[]{:S(2)}) copy-start(bf16[256,4,384]{0,2,1:T(8,128)(2,1)} %copy.116) | copy-start | bytes 2359300
  212.2 7.1 %collective-permute-start.15 = (bf16[64,384]{1,0:T(8,128)(2,1)S(1)}, bf16[64,384]{1,0:T(8,128)(2,1)S(1)}, u32[]{:S(2)}, u32[]{:S(2)}) collective-permute-start(bf16[64,384]{1,0:T(8,128)(2,1)S(1)} %convolution_convert_fusion.3), channel_id=1, source_target_pairs={{0,8},{8,0},{16,24},{24,16},{32,40},{40,32},{48,56},{56,48},{64,72... | collective-permute-start | bytes 147464 | tf_op jit(solution)/shard_map/ppermute | solution.py:476
  219.2 7.8 %collective-permute-start.16 = (bf16[64,384]{1,0:T(8,128)(2,1)S(1)}, bf16[64,384]{1,0:T(8,128)(2,1)S(1)}, u32[]{:S(2)}, u32[]{:S(2)}) collective-permute-start(bf16[64,384]{1,0:T(8,128)(2,1)S(1)} %add_convert_fusion.6), channel_id=1, source_target_pairs={{0,16},{8,24},{16,0},{24,8},{32,48},{40,56},{48,32},{56,40},{64,80... | collective-permute-start | bytes 147464 | tf_op jit(solution)/shard_map/ppermute | solution.py:476
  219.7 18.1 %copy-start.7 = (f32[256,1536]{1,0:T(8,128)S(1)}, f32[256,1536]{1,0:T(8,128)}, u32[]{:S(2)}) copy-start(f32[256,1536]{1,0:T(8,128)} %copy-done.6) | copy-start | bytes 4718596
  223.6 1.2 copy-start.8
  224.8 13.0 %copy-start.5 = (bf16[128,3072]{1,0:T(8,128)(2,1)S(1)}, bf16[128,3072]{1,0:T(8,128)(2,1)}, u32[]{:S(2)}) copy-start(bf16[128,3072]{1,0:T(8,128)(2,1)} %copy-done.4) | copy-start | bytes 2359300
  225.6 10.3 %copy-start.14 = (bf16[128,1536]{1,0:T(8,128)(2,1)}, bf16[128,1536]{1,0:T(8,128)(2,1)S(1)}, u32[]{:S(2)}) copy-start(bf16[128,1536]{1,0:T(8,128)(2,1)S(1)} %collective-permute-done.11) | copy-start | bytes 1179652
  225.6 12.2 %collective-permute-start.12 = (bf16[128,1536]{1,0:T(8,128)(2,1)}, bf16[128,1536]{1,0:T(8,128)(2,1)}, u32[]{:S(2)}, u32[]{:S(2)}) collective-permute-start(bf16[128,1536]{1,0:T(8,128)(2,1)} %slice.135), channel_id=1, source_target_pairs={{0,1},{1,0},{2,3},{3,2},{4,5},{5,4},{6,7},{7,6},{8,9},{9,8},{10,11... | collective-permute-start | bytes 1179656 | tf_op jit(solution)/shard_map/ppermute | solution.py:464
  227.1 6.7 %collective-permute-start.17 = (bf16[64,384]{1,0:T(8,128)(2,1)S(1)}, bf16[64,384]{1,0:T(8,128)(2,1)S(1)}, u32[]{:S(2)}, u32[]{:S(2)}) collective-permute-start(bf16[64,384]{1,0:T(8,128)(2,1)S(1)} %add_convert_fusion.5), channel_id=1, source_target_pairs={{0,32},{8,40},{16,48},{24,56},{32,0},{40,8},{48,16},{56,24},{64,96... | collective-permute-start | bytes 147464 | tf_op jit(solution)/shard_map/ppermute | solution.py:476
  229.6 14.2 %all-to-all-start.6 = ((bf16[16,64,192]{2,1,0:T(8,128)(2,1)}), bf16[16,64,192]{2,1,0:T(8,128)(2,1)S(1)}, u32[]{:S(2)}, u32[]{:S(2)}) async-start(bf16[16,64,192]{2,1,0:T(8,128)(2,1)} %bitcast.31), calls=%async_computation.6 | async-start | bytes 1048576 | tf_op jit(solution)/shard_map/all_to_all | solution.py:25
  234.4 10.2 %collective-permute-start.18 = (bf16[64,384]{1,0:T(8,128)(2,1)}, bf16[64,384]{1,0:T(8,128)(2,1)}, u32[]{:S(2)}, u32[]{:S(2)}) collective-permute-start(bf16[64,384]{1,0:T(8,128)(2,1)} %add_convert_fusion.4), channel_id=1, source_target_pairs={{0,64},{8,72},{16,80},{24,88},{32,96},{40,104},{48,112},{56,120},{... | collective-permute-start | bytes 147464 | tf_op jit(solution)/shard_map/ppermute | solution.py:491
  244.0 3.6 %collective-permute-start.19 = (bf16[64,192]{0,1:T(8,128)(2,1)S(1)}, bf16[64,192]{0,1:T(8,128)(2,1)S(1)}, u32[]{:S(2)}, u32[]{:S(2)}) collective-permute-start(bf16[64,192]{0,1:T(8,128)(2,1)S(1)} %copy.124), channel_id=1, source_target_pairs={{0,2},{1,3},{2,0},{3,1},{4,6},{5,7},{6,4},{7,5},{8,10},{9,11},{10,... | collective-permute-start | bytes 73736 | tf_op jit(solution)/shard_map/ppermute | solution.py:496
  247.6 14.1 %collective-permute-start.20 = (bf16[64,192]{0,1:T(8,128)(2,1)S(1)}, bf16[64,192]{0,1:T(8,128)(2,1)S(1)}, u32[]{:S(2)}, u32[]{:S(2)}) collective-permute-start(bf16[64,192]{0,1:T(8,128)(2,1)S(1)} %add_convert_fusion.3), channel_id=1, source_target_pairs={{0,4},{1,5},{2,6},{3,7},{4,0},{5,1},{6,2},{7,3},{8,12},{9,13},{10,... | collective-permute-start | bytes 73736 | tf_op jit(solution)/shard_map/ppermute | solution.py:496
  252.1 19.4 %all-to-all-start.7 = ((bf16[128,1,192]{2,1,0:T(2,128)(2,1)}), bf16[128,1,192]{2,1,0:T(2,128)(2,1)S(1)}, u32[]{:S(2)}, u32[]{:S(2)}) async-start(bf16[128,1,192]{2,1,0:T(2,128)(2,1)} %copy.126), calls=%async_computation.7 | async-start | bytes 262144 | tf_op jit(solution)/shard_map/all_to_all | solution.py:25
  261.7 10.6 %collective-permute-start.21 = (bf16[64,192]{0,1:T(8,128)(2,1)S(1)}, bf16[64,192]{0,1:T(8,128)(2,1)S(1)}, u32[]{:S(2)}, u32[]{:S(2)}) collective-permute-start(bf16[64,192]{0,1:T(8,128)(2,1)S(1)} %add_convert_fusion.2), channel_id=1, source_target_pairs={{0,1},{1,0},{2,3},{3,2},{4,5},{5,4},{6,7},{7,6},{8,9},{9,8},{10,11... | collective-permute-start | bytes 73736 | tf_op jit(solution)/shard_map/ppermute | solution.py:496
Sparse Core Ops, SparseCore 0:
  41.4 48.2 all-gather.4
  100.7 77.8 all-gather.6

commit v11 on v10

--- a/solution.py
+++ b/solution.py
@@ -448,7 +448,7 @@
         return product[:BLK], product[BLK:].astype(BF16), sums
 
     kept_first, sent, sum_first = project(gathered, 0)
-    gathered, sent, down = lax.optimization_barrier((gathered, sent, down))
+    gathered, sent = lax.optimization_barrier((gathered, sent))
     landed_first = lax.ppermute(sent, "seq", flip_z)
 
     lowered = (lowered[:BLK] + lowered_other.astype(F32)).astype(BF16)[:, :rank]

time: 282 us -> 274 us (0.972)
    ppermute x2, waiting for transfers between devices: 4.63 us -> 1.58 us  [on_device(): moved = lax.ppermute(down, 'seq', [(i, i ^ bit) for i in range(n_seq)])]
    unnamed x55 -> x51, local copies, waits for them, and re-layouts: 7.16 us -> 6.04 us
  transfers between devices with their start and end apart: 32 -> 32, of which waited for: 15 -> 14; matrix products, arithmetic and copies ran while one was open for 14% -> 16% of each run, Pallas kernels for 13% -> 14%
where the time goes in v11:
time: 274 us; the launch traced here: 272 us
  starting transfers between devices  87.2 us (32%)
  waiting for transfers between devices  77.2 us (28%)
  Pallas kernels  41.7 us (15%)
  other arithmetic  20.3 us (7%)
  local copies, waits for them, and re-layouts  16.6 us (6%)
  between operations  14.6 us (5%)
  matrix products  14 us (5%)
    all_to_all x8, waiting for transfers between devices, swap(): lax.all_to_all(values, axes, 0, 0, tiled=True, axis_index_groups=groups)  52.4 us
    all_to_all x8, starting transfers between devices, swap(): lax.all_to_all(values, axes, 0, 0, tiled=True, axis_index_groups=groups)  48.4 us
    ppermute x2, waiting for transfers between devices, near_shard(): lax.ppermute(values, 'dp', [(i, (i + n_dp // 2) % n_dp) for i in range(n_...  13.9 us
    pallas_call x1, Pallas kernels, image_attention(): pl.pallas_call(image_kernel, grid=(heads, n_y), in_specs=[queries(), quer...  12.6 us
    dot_general x3, matrix products, dot_t(): lax.dot_general(left, right, (((1,), (1,)), ((), ())), preferred_element_...  10.8 us
    pallas_call x1, Pallas kernels, prompt_attention(): pl.pallas_call(prompt_kernel, grid=(heads + 1,), in_specs=[pl.BlockSpec(m...  9.59 us
    pallas_call x1, Pallas kernels, t5_in(): pl.pallas_call(t5_in_kernel, grid=(units // cut,), in_specs=[pl.BlockSpec...  8.38 us
    ppermute x3, starting transfers between devices, on_device(): moved = lax.ppermute(grad_a, 'dp', [(i, i ^ bit) for i in range(n_dp)])  7.35 us
  transfers between devices with their start and end apart: 32, of which 14 were waited for; matrix products, arithmetic and copies ran while one was open for 16% of the time, Pallas kernels for 14%

profile of v11, /device:TPU:1, one launch (start us, length us, event | category | flops | bytes accessed | tf_op | source)
XLA Modules:
  0.0 271.7 jit_solution(5244794740653323828)
XLA Ops:
  7.2 4.0 %shard_map.210 = (bf16[4,384,384]{2,1,0:T(8,128)(2,1)}, bf16[4,192,384]{2,1,0:T(8,128)(2,1)}, bf16[4,192,384]{2,1,0:T(8,128)(2,1)}) custom-call(s32[1]{0:T(128)} %bitcast.1._, bf16[3,128,3072]{2,1,0:T(8,128)(2,1)} %bitcast.91, bf16[3,128,3072]{2,1,0:T(8,128)(2,1)} %bitcast.92), custom_call_target="tpu_custom_call" | custom-call | bytes 4718592 | tf_op jit(solution)/shard_map/pallas_call | solution.py:80
  11.3 4.5 %collective-permute-start.4 = (bf16[4,192,384]{2,1,0:T(8,128)(2,1)}, bf16[4,192,384]{2,1,0:T(8,128)(2,1)S(1)}, u32[]{:S(2)}, u32[]{:S(2)}) collective-permute-start(bf16[4,192,384]{2,1,0:T(8,128)(2,1)} %get-tuple-element.45), channel_id=1, source_target_pairs={{0,1},{1,0},{2,3},{3,2},{4,5},{5,4},{6,7},{7,6},{8,9},{9,8},{10,11... | collective-permute-start | bytes 1769480 | tf_op jit(solution)/shard_map/ppermute | solution.py:348
  15.9 0.8 collective-permute-start
  17.1 2.8 %collective-permute-start.1 = (bf16[192,384]{1,0:T(8,128)(2,1)S(1)}, bf16[192,384]{1,0:T(8,128)(2,1)S(1)}, u32[]{:S(2)}, u32[]{:S(2)}) collective-permute-start(bf16[192,384]{1,0:T(8,128)(2,1)S(1)} %fusion.10), channel_id=1, source_target_pairs={{0,6},{1,7},{2,0},{3,1},{4,2},{5,3},{6,4},{7,5},{8,14},{9,15},{10,... | collective-permute-start | bytes 442376 | tf_op jit(solution)/shard_map/ppermute | solution.py:356
  21.0 8.4 %shard_map.211.hidden_ref = bf16[128,640]{1,0:T(8,128)(2,1)} custom-call(bf16[1,256,4096]{2,1,0:T(8,128)(2,1)} %x_ref.1, f32[1,4096]{1,0:T(1,128)} %bitcast.118, bf16[2,4096,640]{2,1,0:T(8,128)(2,1)} %up_w.1, bf16[2,4096,640]{2,1,0:T(8,128)(2,1)} %up_w.1), custom_call_target="tpu_custom_call" | custom-call | flops 1342177280 | bytes 10485760 | tf_op jit(solution)/shard_map/pallas_call | solution.py:255
  29.8 10.2 %collective-permute-done = bf16[192,1280]{1,0:T(8,128)(2,1)S(1)} collective-permute-done((bf16[192,1280]{1,0:T(8,128)(2,1)S(1)}, bf16[192,1280]{1,0:T(8,128)(2,1)S(1)}, u32[]{:S(2)}, u32[]{:S(2)}) %collective-permute-start) | collective-permute-done | bytes 491552 | tf_op jit(solution)/shard_map/ppermute | solution.py:30
  40.1 1.0 pad_maximum_fusion.2
  41.2 4.3 %all-to-all-start = ((bf16[4,384,384]{2,1,0:T(8,128)(2,1)}), bf16[4,384,384]{2,1,0:T(8,128)(2,1)S(1)}, u32[]{:S(2)}, u32[]{:S(2)}) async-start(bf16[4,384,384]{2,1,0:T(8,128)(2,1)} %get-tuple-element.42), calls=%async_computation | async-start | bytes 2359296 | tf_op jit(solution)/shard_map/all_to_all | solution.py:25
  45.5 0.9 collective-permute-start.5
  46.7 2.2 collective-permute-start.6
  48.9 7.2 %shard_map.212 = bf16[8,128,512]{2,1,0:T(8,128)(2,1)} custom-call(bf16[128,640]{1,0:T(8,128)(2,1)} %shard_map.211.hidden_ref, bf16[640,4096]{1,0:T(8,128)(2,1)} %out_w.1), custom_call_target="tpu_custom_call" | custom-call | flops 671088640 | bytes 5242880 | tf_op jit(solution)/shard_map/pallas_call | solution.py:284
  56.1 4.0 %collective-permute-done.6 = f32[192]{0:T(256)S(1)} collective-permute-done((f32[192]{0:T(256)S(1)}, f32[192]{0:T(256)S(1)}, u32[]{:S(2)}, u32[]{:S(2)}) %collective-permute-start.6) | collective-permute-done | bytes 800 | tf_op jit(solution)/shard_map/ppermute | solution.py:370
  60.2 0.8 copy-done.11
  61.1 4.5 %all-to-all-start.1 = ((bf16[8,128,512]{2,1,0:T(8,128)(2,1)}), bf16[8,128,512]{2,1,0:T(8,128)(2,1)S(1)}, u32[]{:S(2)}, u32[]{:S(2)}) async-start(bf16[8,128,512]{2,1,0:T(8,128)(2,1)} %shard_map.212), calls=%async_computation.1 | async-start | bytes 2097152 | tf_op jit(solution)/shard_map/all_to_all | solution.py:25
  66.4 0.8 fusion.22
  67.2 0.8 fusion.23
  68.7 9.7 %all-to-all-done.1 = bf16[8,128,512]{2,1,0:T(8,128)(2,1)S(1)} async-done(((bf16[8,128,512]{2,1,0:T(8,128)(2,1)}), bf16[8,128,512]{2,1,0:T(8,128)(2,1)S(1)}, u32[]{:S(2)}, u32[]{:S(2)}) %all-to-all-start.1) | async-done | bytes 1048608 | tf_op jit(solution)/shard_map/all_to_all | solution.py:25
  78.4 2.8 %pad_maximum_fusion.1 = bf16[4,384,384]{2,1,0:T(8,128)(2,1)} fusion(bf16[4,192,384]{2,1,0:T(8,128)(2,1)} %copy-done.11, bf16[4,192,384]{2,1,0:T(8,128)(2,1)} %copy-done.10), kind=kLoop, calls=%fused_computation.14 | loop fusion | flops 2359296 | bytes 2359296 | tf_op jit(solution)/shard_map/concatenate | solution.py:392
  81.2 3.5 %all-to-all-start.2 = ((bf16[4,384,384]{2,1,0:T(8,128)(2,1)}), bf16[4,384,384]{2,1,0:T(8,128)(2,1)S(1)}, u32[]{:S(2)}, u32[]{:S(2)}) async-start(bf16[4,384,384]{2,1,0:T(8,128)(2,1)} %pad_maximum_fusion.1), calls=%async_computation.2 | async-start | bytes 2359296 | tf_op jit(solution)/shard_map/all_to_all | solution.py:25
  85.7 0.8 dynamic_slice.7
  86.5 1.4 convert_reduce_fusion
  87.9 1.7 all-gather.5.cloned.1.call-done
  89.6 3.0 %fusion.7 = bf16[16,8,24,128]{3,1,2,0:T(8,128)(2,1)S(1)} fusion(bf16[3072,1280]{1,0:T(8,128)(2,1)} %bitcast.88, f32[128,512]{1,0:T(8,128)S(1)} %convert_reduce_fusion, f32[512]{0:T(512)S(1)} %dynamic_slice.7, bf16[1,128,4096]{2,1,0:T(8,128)(2,1)S(1)} %slice-done, s32[]{:T(128)S(6)} %select_n.153), kind=kOutput, calls=%fused_computation.12 | convolution fusion | flops 403308544 | bytes 4327428 | tf_op jit(solution)/shard_map/dot_general | solution.py:56
  92.7 1.0 copy.130
  93.7 3.7 %collective-permute-done.7 = bf16[192,1664]{1,0:T(8,128)(2,1)} collective-permute-done((bf16[192,1664]{1,0:T(8,128)(2,1)}, bf16[192,1664]{1,0:T(8,128)(2,1)}, u32[]{:S(2)}, u32[]{:S(2)}) %collective-permute-start.7) | collective-permute-done | bytes 639008 | tf_op jit(solution)/shard_map/ppermute | solution.py:30
  97.4 1.8 select_bitcast_fusion.1
  99.2 1.2 pad_maximum_fusion
  100.5 14.8 %all-to-all-start.3 = ((bf16[128,24,128]{2,1,0:T(8,128)(2,1)}), bf16[128,24,128]{2,1,0:T(8,128)(2,1)S(1)}, u32[]{:S(2)}, u32[]{:S(2)}) async-start(bf16[128,24,128]{2,1,0:T(8,128)(2,1)} %bitcast.48), calls=%async_computation.3 | async-start | bytes 1572864 | tf_op jit(solution)/shard_map/all_to_all | solution.py:25
  115.3 12.6 %shard_map.213 = (f32[1024,384]{1,0:T(8,128)}, f32[1024,384]{1,0:T(8,128)}) custom-call(bf16[4,384,384]{2,1,0:T(8,128)(2,1)} %copy-done, bf16[4,384,384]{2,1,0:T(8,128)(2,1)} %copy-done.1, bf16[4,384,384]{2,1,0:T(8,128)(2,1)} %copy-done, bf16[4,384,384]{2,1,0:T(8,128)(2,1)} %copy-done.1, bf16[4,384,384]{2,1,0:T(8,128)(2,1)} %copy-done, ...), custom_call_target="tpu_custom_call" | custom-call | flops 2415919104 | bytes 5505024 | tf_op jit(solution)/shard_map/pallas_call | solution.py:130
  127.9 7.3 %all-to-all-done.3 = bf16[128,24,128]{2,1,0:T(8,128)(2,1)S(1)} async-done(((bf16[128,24,128]{2,1,0:T(8,128)(2,1)}), bf16[128,24,128]{2,1,0:T(8,128)(2,1)S(1)}, u32[]{:S(2)}, u32[]{:S(2)}) %all-to-all-start.3) | async-done | bytes 786464 | tf_op jit(solution)/shard_map/all_to_all | solution.py:25
  136.4 1.4 copy.110
  137.8 5.9 %all-to-all-start.4 = ((bf16[128,24,128]{2,1,0:T(8,128)(2,1)}), bf16[128,24,128]{2,1,0:T(8,128)(2,1)S(1)}, u32[]{:S(2)}, u32[]{:S(2)}) async-start(bf16[128,24,128]{2,1,0:T(8,128)(2,1)} %copy.110), calls=%async_computation.4 | async-start | bytes 1572864 | tf_op jit(solution)/shard_map/all_to_all | solution.py:25
  144.4 3.5 %collective-permute-start.9 = (bf16[128,3072]{1,0:T(8,128)(2,1)S(1)}, bf16[128,3072]{1,0:T(8,128)(2,1)}, u32[]{:S(2)}, u32[]{:S(2)}) collective-permute-start(bf16[128,3072]{1,0:T(8,128)(2,1)S(1)} %copy.115), channel_id=1, source_target_pairs={{0,1},{1,0},{2,3},{3,2},{4,5},{5,4},{6,7},{7,6},{8,9},{9,8},{10,11... | collective-permute-start | bytes 2359304 | tf_op jit(solution)/shard_map/ppermute | solution.py:437
  151.0 16.3 %all-to-all-done.4 = bf16[128,24,128]{2,1,0:T(8,128)(2,1)S(1)} async-done(((bf16[128,24,128]{2,1,0:T(8,128)(2,1)}), bf16[128,24,128]{2,1,0:T(8,128)(2,1)S(1)}, u32[]{:S(2)}, u32[]{:S(2)}) %all-to-all-start.4) | async-done | bytes 786464 | tf_op jit(solution)/shard_map/all_to_all | solution.py:25
  167.5 1.1 fusion.6.text_ref
  168.6 9.6 %shard_map.214 = bf16[4,256,512]{2,1,0:T(8,128)(2,1)} custom-call(s32[1]{0:T(128)} %bitcast.length_ref, bf16[4,384,384]{2,1,0:T(8,128)(2,1)} %copy-done, bf16[4,384,384]{2,1,0:T(8,128)(2,1)} %copy-done.1, bf16[128,3072]{1,0:T(8,128)(2,1)} %fusion.6.text_ref, bf16[3072,1280]{1,0:T(8,128)(2,1)} %bitcast.89, bf16[3072,1280]{1,0:T(8,128)(2,1)} %bitcast.90, ...), custom_call_target="tpu_custom_call" | custom-call | flops 905969664 | bytes 9437184 | tf_op jit(solution)/shard_map/pallas_call | solution.py:214
  178.2 3.5 %all-to-all-start.5 = ((bf16[4,256,512]{2,1,0:T(8,128)(2,1)}), bf16[4,256,512]{2,1,0:T(8,128)(2,1)S(1)}, u32[]{:S(2)}, u32[]{:S(2)}) async-start(bf16[4,256,512]{2,1,0:T(8,128)(2,1)} %shard_map.214), calls=%async_computation.5 | async-start | bytes 2097152 | tf_op jit(solution)/shard_map/all_to_all | solution.py:25
  181.8 1.5 fusion.11
  183.3 1.2 collective-permute-start.8
  184.5 3.1 %collective-permute-done.8 = bf16[128,128]{1,0:T(8,128)(2,1)S(1)} collective-permute-done((bf16[128,128]{1,0:T(8,128)(2,1)S(1)}, bf16[128,128]{1,0:T(8,128)(2,1)S(1)}, u32[]{:S(2)}, u32[]{:S(2)}) %collective-permute-start.8) | collective-permute-done | bytes 32800 | tf_op jit(solution)/shard_map/ppermute | solution.py:436
  187.7 7.4 %all-to-all-done.5 = bf16[4,256,512]{2,1,0:T(8,128)(2,1)S(1)} async-done(((bf16[4,256,512]{2,1,0:T(8,128)(2,1)}), bf16[4,256,512]{2,1,0:T(8,128)(2,1)S(1)}, u32[]{:S(2)}, u32[]{:S(2)}) %all-to-all-start.5) | async-done | bytes 1048608 | tf_op jit(solution)/shard_map/all_to_all | solution.py:25
  195.5 1.2 copy.116
  196.6 1.6 collective-permute-done.13
  198.9 4.0 %fusion.2 = f32[256,1536]{1,0:T(8,128)S(1)} fusion(bf16[256,1536]{0,1:T(8,128)(2,1)} %bitcast.109, bf16[3072,1664]{1,0:T(8,128)(2,1)} %bitcast.121), kind=kOutput, calls=%fused_computation.2 | convolution fusion | flops 1207959552 | bytes 7077888 | tf_op jit(solution)/shard_map/dot_general | solution.py:56
  203.1 0.8 slice.136
  203.9 1.7 collective-permute-start.10
  205.6 1.2 collective-permute-start.11
  207.3 4.4 %collective-permute-start.15 = (bf16[64,384]{1,0:T(8,128)(2,1)S(1)}, bf16[64,384]{1,0:T(8,128)(2,1)S(1)}, u32[]{:S(2)}, u32[]{:S(2)}) collective-permute-start(bf16[64,384]{1,0:T(8,128)(2,1)S(1)} %convolution_convert_fusion.3), channel_id=1, source_target_pairs={{0,8},{8,0},{16,24},{24,16},{32,40},{40,32},{48,56},{56,48},{64,72... | collective-permute-start | bytes 147464 | tf_op jit(solution)/shard_map/ppermute | solution.py:476
  212.8 1.0 copy.117
  214.2 3.8 %fusion = f32[256,1536]{1,0:T(8,128)S(1)} fusion(bf16[256,1536]{0,1:T(8,128)(2,1)S(1)} %bitcast.110, bf16[3072,1664]{1,0:T(8,128)(2,1)} %bitcast.122), kind=kOutput, calls=%fused_computation | convolution fusion | flops 1207959552 | bytes 7077888 | tf_op jit(solution)/shard_map/dot_general | solution.py:56
  218.0 1.2 copy-done.6
  219.2 1.6 collective-permute-start.12
  220.8 2.5 collective-permute-start.17
  223.3 6.0 %all-to-all-start.6 = ((bf16[16,64,192]{2,1,0:T(8,128)(2,1)}), bf16[16,64,192]{2,1,0:T(8,128)(2,1)S(1)}, u32[]{:S(2)}, u32[]{:S(2)}) async-start(bf16[16,64,192]{2,1,0:T(8,128)(2,1)} %bitcast.106), calls=%async_computation.6 | async-start | bytes 1048576 | tf_op jit(solution)/shard_map/all_to_all | solution.py:25
  229.4 1.5 collective-permute-start.18
  230.9 3.1 %multiply_reduce_fusion.1 = (f32[1536]{0:T(1024)S(1)}, f32[1536]{0:T(1024)S(1)}, f32[1536]{0:T(1024)S(1)}, f32[1536]{0:T(1024)S(1)}, bf16[128,1536]{1,0:T(8,128)(2,1)S(1)}, /*index=5*/bf16[128,1536]{1,0:T(8,128)(2,1)}) fusion(f32[256,1536]{1,0:T(8,128)} %copy-done.6, bf16[128,3072]{1,0:T(8,128)(2,1)} %collective-permute-done.9, ...), kind=kLoop, calls=%fused_computation.26 | loop fusion | flops 3532800 | bytes 6316032 | tf_op jit(solution)/shard_map/reduce_sum | solution.py:447
  234.2 5.1 %all-to-all-done.6 = bf16[16,64,192]{2,1,0:T(8,128)(2,1)S(1)} async-done(((bf16[16,64,192]{2,1,0:T(8,128)(2,1)}), bf16[16,64,192]{2,1,0:T(8,128)(2,1)S(1)}, u32[]{:S(2)}, u32[]{:S(2)}) %all-to-all-start.6) | async-done | bytes 393248 | tf_op jit(solution)/shard_map/all_to_all | solution.py:25
  239.5 1.2 collective-permute-start.19
  241.4 1.2 copy.119
  242.9 2.5 collective-permute-start.20
  245.5 1.2 copy.127
  247.4 5.8 %all-to-all-start.7 = ((bf16[128,1,192]{2,1,0:T(2,128)(2,1)}), bf16[128,1,192]{2,1,0:T(2,128)(2,1)S(1)}, u32[]{:S(2)}, u32[]{:S(2)}) async-start(bf16[128,1,192]{2,1,0:T(2,128)(2,1)} %copy.126), calls=%async_computation.7 | async-start | bytes 262144 | tf_op jit(solution)/shard_map/all_to_all | solution.py:25
  253.3 3.5 %collective-permute-start.21 = (bf16[64,192]{0,1:T(8,128)(2,1)S(1)}, bf16[64,192]{0,1:T(8,128)(2,1)S(1)}, u32[]{:S(2)}, u32[]{:S(2)}) collective-permute-start(bf16[64,192]{0,1:T(8,128)(2,1)S(1)} %add_convert_fusion.2), channel_id=1, source_target_pairs={{0,1},{1,0},{2,3},{3,2},{4,5},{5,4},{6,7},{7,6},{8,9},{9,8},{10,11... | collective-permute-start | bytes 73736 | tf_op jit(solution)/shard_map/ppermute | solution.py:496
  256.8 6.4 %all-to-all-done.7 = bf16[128,1,192]{2,1,0:T(2,128)(2,1)S(1)} async-done(((bf16[128,1,192]{2,1,0:T(2,128)(2,1)}), bf16[128,1,192]{2,1,0:T(2,128)(2,1)S(1)}, u32[]{:S(2)}, u32[]{:S(2)}) %all-to-all-start.7) | async-done | bytes 49184 | tf_op jit(solution)/shard_map/all_to_all | solution.py:25
  (144 shorter events, 17.3 us)
Async XLA Ops:
  7.2 82.5 %all-gather.5.cloned.1.call-start = ((), (), s32[]{:S(2)}) async-start(), calls=%async_computation.8 | async-start | bytes 8847360 | tf_op jit(solution)/shard_map/all_gather | solution.py:39
  7.2 8.5 %copy-start.13 = (bf16[192,2,384]{2,1,0:T(2,128)(2,1)S(1)}, bf16[192,2,384]{2,1,0:T(2,128)(2,1)}, u32[]{:S(2)}) copy-start(bf16[192,2,384]{2,1,0:T(2,128)(2,1)} %param.29) | copy-start | bytes 884740
  7.2 8.6 %copy-start.9 = (bf16[512,192]{0,1:T(8,128)(2,1)S(1)}, bf16[512,192]{0,1:T(8,128)(2,1)}, u32[]{:S(2)}) copy-start(bf16[512,192]{0,1:T(8,128)(2,1)} %param.26) | copy-start | bytes 589828
  11.2 5.4 %copy-start.12 = (f32[384,64]{0,1:T(8,128)S(1)}, f32[384,64]{0,1:T(8,128)}, u32[]{:S(2)}) copy-start(f32[384,64]{0,1:T(8,128)} %param.34) | copy-start | bytes 294916
  11.2 5.4 %copy-start.14 = (f32[64,192]{1,0:T(8,128)S(1)}, f32[64,192]{1,0:T(8,128)}, u32[]{:S(2)}) copy-start(f32[64,192]{1,0:T(8,128)} %param.35) | copy-start | bytes 147460
  11.2 5.4 %copy-start.15 = (bf16[384,192]{0,1:T(8,128)(2,1)S(1)}, bf16[384,192]{0,1:T(8,128)(2,1)}, u32[]{:S(2)}) copy-start(bf16[384,192]{0,1:T(8,128)(2,1)} %param.33) | copy-start | bytes 442372
  11.3 28.7 %collective-permute-start.4 = (bf16[4,192,384]{2,1,0:T(8,128)(2,1)}, bf16[4,192,384]{2,1,0:T(8,128)(2,1)S(1)}, u32[]{:S(2)}, u32[]{:S(2)}) collective-permute-start(bf16[4,192,384]{2,1,0:T(8,128)(2,1)} %get-tuple-element.45), channel_id=1, source_target_pairs={{0,1},{1,0},{2,3},{3,2},{4,5},{5,4},{6,7},{7,6},{8,9},{9,8},{10,11... | collective-permute-start | bytes 1769480 | tf_op jit(solution)/shard_map/ppermute | solution.py:348
  15.9 24.1 %collective-permute-start = (bf16[192,1280]{1,0:T(8,128)(2,1)S(1)}, bf16[192,1280]{1,0:T(8,128)(2,1)S(1)}, u32[]{:S(2)}, u32[]{:S(2)}) collective-permute-start(bf16[192,1280]{1,0:T(8,128)(2,1)S(1)} %pad_maximum_fusion.3), channel_id=1, source_target_pairs={{0,64},{8,72},{16,80},{24,88},{32,96},{40,104},{48,112},{56,120},{... | collective-permute-start | bytes 1474568 | tf_op jit(solution)/shard_map/ppermute | solution.py:30
  17.1 12.2 %collective-permute-start.1 = (bf16[192,384]{1,0:T(8,128)(2,1)S(1)}, bf16[192,384]{1,0:T(8,128)(2,1)S(1)}, u32[]{:S(2)}, u32[]{:S(2)}) collective-permute-start(bf16[192,384]{1,0:T(8,128)(2,1)S(1)} %fusion.10), channel_id=1, source_target_pairs={{0,6},{1,7},{2,0},{3,1},{4,2},{5,3},{6,4},{7,5},{8,14},{9,15},{10,... | collective-permute-start | bytes 442376 | tf_op jit(solution)/shard_map/ppermute | solution.py:356
  19.9 9.4 %collective-permute-start.2 = (bf16[192,384]{1,0:T(8,128)(2,1)S(1)}, bf16[192,384]{1,0:T(8,128)(2,1)S(1)}, u32[]{:S(2)}, u32[]{:S(2)}) collective-permute-start(bf16[192,384]{1,0:T(8,128)(2,1)S(1)} %fusion.10), channel_id=1, source_target_pairs={{0,4},{1,5},{2,6},{3,7},{4,0},{5,1},{6,2},{7,3},{8,12},{9,13},{10,... | collective-permute-start | bytes 442376 | tf_op jit(solution)/shard_map/ppermute | solution.py:356
  20.3 9.5 %collective-permute-start.3 = (bf16[192,384]{1,0:T(8,128)(2,1)S(1)}, bf16[192,384]{1,0:T(8,128)(2,1)S(1)}, u32[]{:S(2)}, u32[]{:S(2)}) collective-permute-start(bf16[192,384]{1,0:T(8,128)(2,1)S(1)} %fusion.10), channel_id=1, source_target_pairs={{0,2},{1,3},{2,4},{3,5},{4,6},{5,7},{6,0},{7,1},{8,10},{9,11},{10,... | collective-permute-start | bytes 442376 | tf_op jit(solution)/shard_map/ppermute | solution.py:356
  40.0 1.2 copy-start.10
  41.2 4.4 %copy-start.21 = (bf16[4,192,384]{2,1,0:T(8,128)(2,1)S(1)}, bf16[4,192,384]{2,1,0:T(8,128)(2,1)}, u32[]{:S(2)}) copy-start(bf16[4,192,384]{2,1,0:T(8,128)(2,1)} %get-tuple-element.48) | copy-start | bytes 1769476
  41.2 19.0 %all-to-all-start = ((bf16[4,384,384]{2,1,0:T(8,128)(2,1)}), bf16[4,384,384]{2,1,0:T(8,128)(2,1)S(1)}, u32[]{:S(2)}, u32[]{:S(2)}) async-start(bf16[4,384,384]{2,1,0:T(8,128)(2,1)} %get-tuple-element.42), calls=%async_computation | async-start | bytes 2359296 | tf_op jit(solution)/shard_map/all_to_all | solution.py:25
  45.5 14.7 %collective-permute-start.5 = (bf16[4,192,384]{2,1,0:T(8,128)(2,1)S(1)}, bf16[4,192,384]{2,1,0:T(8,128)(2,1)S(1)}, u32[]{:S(2)}, u32[]{:S(2)}) collective-permute-start(bf16[4,192,384]{2,1,0:T(8,128)(2,1)S(1)} %copy-done.21), channel_id=1, source_target_pairs={{0,1},{1,0},{2,3},{3,2},{4,5},{5,4},{6,7},{7,6},{8,9},{9,8},{10,11... | collective-permute-start | bytes 1769480 | tf_op jit(solution)/shard_map/ppermute | solution.py:365
  46.7 13.3 %collective-permute-start.6 = (f32[192]{0:T(256)S(1)}, f32[192]{0:T(256)S(1)}, u32[]{:S(2)}, u32[]{:S(2)}) collective-permute-start(f32[192]{0:T(256)S(1)} %multiply_reduce_fusion), channel_id=1, source_target_pairs={{0,1},{1,0},{2,3},{3,2},{4,5},{5,4},{6,7},{7,6},{8,9},{9,8},{10,11... | collective-permute-start | bytes 2312 | tf_op jit(solution)/shard_map/ppermute | solution.py:370
  56.1 9.5 %copy-start.18 = (f32[192]{0:T(256)S(1)}, f32[192]{0:T(256)}, u32[]{:S(2)}) copy-start(f32[192]{0:T(256)} %param.36) | copy-start | bytes 2308
  60.2 7.0 %copy-start = (bf16[4,384,384]{2,1,0:T(8,128)(2,1)}, bf16[4,384,384]{2,1,0:T(8,128)(2,1)S(1)}, u32[]{:S(2)}) copy-start(bf16[4,384,384]{2,1,0:T(8,128)(2,1)S(1)} %all-to-all-done.q_own.k_own.v_own) | copy-start | bytes 3538948
  60.2 0.8 copy-start.11
  61.1 17.3 %all-to-all-start.1 = ((bf16[8,128,512]{2,1,0:T(8,128)(2,1)}), bf16[8,128,512]{2,1,0:T(8,128)(2,1)S(1)}, u32[]{:S(2)}, u32[]{:S(2)}) async-start(bf16[8,128,512]{2,1,0:T(8,128)(2,1)} %shard_map.212), calls=%async_computation.1 | async-start | bytes 2097152 | tf_op jit(solution)/shard_map/all_to_all | solution.py:25
  78.4 2.8 %copy-start.3 = (bf16[8,128,512]{2,1,0:T(8,128)(2,1)}, bf16[8,128,512]{2,1,0:T(8,128)(2,1)S(1)}, u32[]{:S(2)}) copy-start(bf16[8,128,512]{2,1,0:T(8,128)(2,1)S(1)} %all-to-all-done.1) | copy-start | bytes 3145732
  81.2 16.2 %all-to-all-start.2 = ((bf16[4,384,384]{2,1,0:T(8,128)(2,1)}), bf16[4,384,384]{2,1,0:T(8,128)(2,1)S(1)}, u32[]{:S(2)}, u32[]{:S(2)}) async-start(bf16[4,384,384]{2,1,0:T(8,128)(2,1)} %pad_maximum_fusion.1), calls=%async_computation.2 | async-start | bytes 2359296 | tf_op jit(solution)/shard_map/all_to_all | solution.py:25
  84.7 97.0 %all-gather.7.cloned.1.call-start = ((), (), s32[]{:S(2)}) async-start(), calls=%async_computation.9 | async-start | bytes 11501568 | tf_op jit(solution)/shard_map/all_gather | solution.py:39
  85.5 4.1 %slice-start = ((bf16[1,256,4096]{2,1,0:T(8,128)(2,1)}), bf16[1,128,4096]{2,1,0:T(8,128)(2,1)S(1)}, s32[]{:S(2)}) async-start(bf16[1,256,4096]{2,1,0:T(8,128)(2,1)} %x_ref.1), calls=%async_computation.10 | async-start | bytes 2097152 | tf_op jit(solution)/shard_map/slice | solution.py:359
  85.5 11.9 %collective-permute-start.7 = (bf16[192,1664]{1,0:T(8,128)(2,1)}, bf16[192,1664]{1,0:T(8,128)(2,1)}, u32[]{:S(2)}, u32[]{:S(2)}) collective-permute-start(bf16[192,1664]{1,0:T(8,128)(2,1)} %pad_dynamic-update-slice_fusion), channel_id=1, source_target_pairs={{0,64},{8,72},{16,80},{24,88},{32,96},{40,104},{48,112},{56,120},{... | collective-permute-start | bytes 1916936 | tf_op jit(solution)/shard_map/ppermute | solution.py:30
  97.4 3.0 %copy-start.1 = (bf16[4,384,384]{2,1,0:T(8,128)(2,1)}, bf16[4,384,384]{2,1,0:T(8,128)(2,1)S(1)}, u32[]{:S(2)}) copy-start(bf16[4,384,384]{2,1,0:T(8,128)(2,1)S(1)} %all-to-all-done.2.q_other.k_other.v_other) | copy-start | bytes 3538948
  100.5 34.7 %all-to-all-start.3 = ((bf16[128,24,128]{2,1,0:T(8,128)(2,1)}), bf16[128,24,128]{2,1,0:T(8,128)(2,1)S(1)}, u32[]{:S(2)}, u32[]{:S(2)}) async-start(bf16[128,24,128]{2,1,0:T(8,128)(2,1)} %bitcast.48), calls=%async_computation.3 | async-start | bytes 1572864 | tf_op jit(solution)/shard_map/all_to_all | solution.py:25
  115.3 20.6 %copy-start.19 = (s32[16]{0:T(128)S(1)}, s32[16]{0:T(128)}, u32[]{:S(2)}) copy-start(s32[16]{0:T(128)} %param.21) | copy-start | bytes 196
  136.4 7.3 %copy-start.7 = (bf16[1,128,3072]{2,1,0:T(8,128)(2,1)S(1)}, bf16[1,128,3072]{2,1,0:T(8,128)(2,1)}, u32[]{:S(2)}) copy-start(bf16[1,128,3072]{2,1,0:T(8,128)(2,1)} %param.37) | copy-start | bytes 2359300
  137.8 29.5 %all-to-all-start.4 = ((bf16[128,24,128]{2,1,0:T(8,128)(2,1)}), bf16[128,24,128]{2,1,0:T(8,128)(2,1)S(1)}, u32[]{:S(2)}, u32[]{:S(2)}) async-start(bf16[128,24,128]{2,1,0:T(8,128)(2,1)} %copy.110), calls=%async_computation.4 | async-start | bytes 1572864 | tf_op jit(solution)/shard_map/all_to_all | solution.py:25
  144.1 4.5 %copy-start.16 = (f32[1,3072]{1,0:T(1,128)S(1)}, f32[1,3072]{1,0:T(1,128)}, u32[]{:S(2)}) copy-start(f32[1,3072]{1,0:T(1,128)} %param.27) | copy-start | bytes 36868
  144.1 5.3 %copy-start.17 = (f32[1,3072]{1,0:T(1,128)S(1)}, f32[1,3072]{1,0:T(1,128)}, u32[]{:S(2)}) copy-start(f32[1,3072]{1,0:T(1,128)} %param.28) | copy-start | bytes 36868
  144.1 6.3 %copy-start.20 = (s32[16]{0:T(128)S(1)}, s32[16]{0:T(128)}, u32[]{:S(2)}) copy-start(s32[16]{0:T(128)} %param.20) | copy-start | bytes 196
  144.4 43.2 %collective-permute-start.9 = (bf16[128,3072]{1,0:T(8,128)(2,1)S(1)}, bf16[128,3072]{1,0:T(8,128)(2,1)}, u32[]{:S(2)}, u32[]{:S(2)}) collective-permute-start(bf16[128,3072]{1,0:T(8,128)(2,1)S(1)} %copy.115), channel_id=1, source_target_pairs={{0,1},{1,0},{2,3},{3,2},{4,5},{5,4},{6,7},{7,6},{8,9},{9,8},{10,11... | collective-permute-start | bytes 2359304 | tf_op jit(solution)/shard_map/ppermute | solution.py:437
  178.2 16.9 %all-to-all-start.5 = ((bf16[4,256,512]{2,1,0:T(8,128)(2,1)}), bf16[4,256,512]{2,1,0:T(8,128)(2,1)S(1)}, u32[]{:S(2)}, u32[]{:S(2)}) async-start(bf16[4,256,512]{2,1,0:T(8,128)(2,1)} %shard_map.214), calls=%async_computation.5 | async-start | bytes 2097152 | tf_op jit(solution)/shard_map/all_to_all | solution.py:25
  183.3 4.3 %collective-permute-start.8 = (bf16[128,128]{1,0:T(8,128)(2,1)S(1)}, bf16[128,128]{1,0:T(8,128)(2,1)S(1)}, u32[]{:S(2)}, u32[]{:S(2)}) collective-permute-start(bf16[128,128]{1,0:T(8,128)(2,1)S(1)} %fusion.11), channel_id=1, source_target_pairs={{0,1},{1,0},{2,3},{3,2},{4,5},{5,4},{6,7},{7,6},{8,9},{9,8},{10,11... | collective-permute-start | bytes 98312 | tf_op jit(solution)/shard_map/ppermute | solution.py:436
  195.1 3.1 %collective-permute-start.13 = (bf16[256,128]{1,0:T(8,128)(2,1)S(1)}, bf16[256,128]{1,0:T(8,128)(2,1)S(1)}, u32[]{:S(2)}, u32[]{:S(2)}) collective-permute-start(bf16[256,128]{1,0:T(8,128)(2,1)S(1)} %pad_maximum_fusion.7), channel_id=1, source_target_pairs={{0,2},{1,3},{2,0},{3,1},{4,6},{5,7},{6,4},{7,5},{8,10},{9,11},{10,... | collective-permute-start | bytes 196616 | tf_op jit(solution)/shard_map/ppermute | solution.py:467
  198.3 8.6 %collective-permute-start.14 = (bf16[512,128]{1,0:T(8,128)(2,1)S(1)}, bf16[512,128]{1,0:T(8,128)(2,1)S(1)}, u32[]{:S(2)}, u32[]{:S(2)}) collective-permute-start(bf16[512,128]{1,0:T(8,128)(2,1)S(1)} %pad_maximum_fusion.6), channel_id=1, source_target_pairs={{0,4},{1,5},{2,6},{3,7},{4,0},{5,1},{6,2},{7,3},{8,12},{9,13},{10,... | collective-permute-start | bytes 393224 | tf_op jit(solution)/shard_map/ppermute | solution.py:467
  203.0 4.3 %copy-start.4 = (f32[256,1536]{1,0:T(8,128)}, f32[256,1536]{1,0:T(8,128)S(1)}, u32[]{:S(2)}) copy-start(f32[256,1536]{1,0:T(8,128)S(1)} %fusion.2) | copy-start | bytes 4718596
  203.0 3.9 %copy-start.2 = (bf16[4,256,512]{2,1,0:T(8,128)(2,1)S(1)}, bf16[4,256,512]{2,1,0:T(8,128)(2,1)}, u32[]{:S(2)}) copy-start(bf16[4,256,512]{2,1,0:T(8,128)(2,1)} %shard_map.214) | copy-start | bytes 3145732
  203.9 7.8 %collective-permute-start.10 = (bf16[128,128]{1,0:T(8,128)(2,1)S(1)}, bf16[128,128]{1,0:T(8,128)(2,1)S(1)}, u32[]{:S(2)}, u32[]{:S(2)}) collective-permute-start(bf16[128,128]{1,0:T(8,128)(2,1)S(1)} %slice.137), channel_id=1, source_target_pairs={{0,1},{1,0},{2,3},{3,2},{4,5},{5,4},{6,7},{7,6},{8,9},{9,8},{10,11... | collective-permute-start | bytes 98312 | tf_op jit(solution)/shard_map/ppermute | solution.py:440
  205.6 13.6 %collective-permute-start.11 = (bf16[128,1536]{1,0:T(8,128)(2,1)}, bf16[128,1536]{1,0:T(8,128)(2,1)}, u32[]{:S(2)}, u32[]{:S(2)}) collective-permute-start(bf16[128,1536]{1,0:T(8,128)(2,1)} %slice.136), channel_id=1, source_target_pairs={{0,1},{1,0},{2,3},{3,2},{4,5},{5,4},{6,7},{7,6},{8,9},{9,8},{10,11... | collective-permute-start | bytes 1179656 | tf_op jit(solution)/shard_map/ppermute | solution.py:452
  207.2 6.9 %copy-start.8 = (bf16[256,4,384]{0,2,1:T(8,128)(2,1)S(1)}, bf16[256,4,384]{0,2,1:T(8,128)(2,1)}, u32[]{:S(2)}) copy-start(bf16[256,4,384]{0,2,1:T(8,128)(2,1)} %copy.116) | copy-start | bytes 2359300
  207.3 6.5 %collective-permute-start.15 = (bf16[64,384]{1,0:T(8,128)(2,1)S(1)}, bf16[64,384]{1,0:T(8,128)(2,1)S(1)}, u32[]{:S(2)}, u32[]{:S(2)}) collective-permute-start(bf16[64,384]{1,0:T(8,128)(2,1)S(1)} %convolution_convert_fusion.3), channel_id=1, source_target_pairs={{0,8},{8,0},{16,24},{24,16},{32,40},{40,32},{48,56},{56,48},{64,72... | collective-permute-start | bytes 147464 | tf_op jit(solution)/shard_map/ppermute | solution.py:476
  213.7 7.1 %collective-permute-start.16 = (bf16[64,384]{1,0:T(8,128)(2,1)S(1)}, bf16[64,384]{1,0:T(8,128)(2,1)S(1)}, u32[]{:S(2)}, u32[]{:S(2)}) collective-permute-start(bf16[64,384]{1,0:T(8,128)(2,1)S(1)} %add_convert_fusion.6), channel_id=1, source_target_pairs={{0,16},{8,24},{16,0},{24,8},{32,48},{40,56},{48,32},{56,40},{64,80... | collective-permute-start | bytes 147464 | tf_op jit(solution)/shard_map/ppermute | solution.py:476
  218.0 1.2 copy-start.6
  219.2 11.7 %copy-start.5 = (f32[256,1536]{1,0:T(8,128)S(1)}, f32[256,1536]{1,0:T(8,128)}, u32[]{:S(2)}) copy-start(f32[256,1536]{1,0:T(8,128)} %copy-done.4) | copy-start | bytes 4718596
  219.2 11.7 %collective-permute-start.12 = (bf16[128,1536]{1,0:T(8,128)(2,1)S(1)}, bf16[128,1536]{1,0:T(8,128)(2,1)}, u32[]{:S(2)}, u32[]{:S(2)}) collective-permute-start(bf16[128,1536]{1,0:T(8,128)(2,1)S(1)} %slice.135), channel_id=1, source_target_pairs={{0,1},{1,0},{2,3},{3,2},{4,5},{5,4},{6,7},{7,6},{8,9},{9,8},{10,11... | collective-permute-start | bytes 1179656 | tf_op jit(solution)/shard_map/ppermute | solution.py:464
  220.8 8.5 %collective-permute-start.17 = (bf16[64,384]{1,0:T(8,128)(2,1)S(1)}, bf16[64,384]{1,0:T(8,128)(2,1)S(1)}, u32[]{:S(2)}, u32[]{:S(2)}) collective-permute-start(bf16[64,384]{1,0:T(8,128)(2,1)S(1)} %add_convert_fusion.5), channel_id=1, source_target_pairs={{0,32},{8,40},{16,48},{24,56},{32,0},{40,8},{48,16},{56,24},{64,96... | collective-permute-start | bytes 147464 | tf_op jit(solution)/shard_map/ppermute | solution.py:476
  223.3 16.0 %all-to-all-start.6 = ((bf16[16,64,192]{2,1,0:T(8,128)(2,1)}), bf16[16,64,192]{2,1,0:T(8,128)(2,1)S(1)}, u32[]{:S(2)}, u32[]{:S(2)}) async-start(bf16[16,64,192]{2,1,0:T(8,128)(2,1)} %bitcast.106), calls=%async_computation.6 | async-start | bytes 1048576 | tf_op jit(solution)/shard_map/all_to_all | solution.py:25
  229.4 11.4 %collective-permute-start.18 = (bf16[64,384]{1,0:T(8,128)(2,1)S(1)}, bf16[64,384]{1,0:T(8,128)(2,1)S(1)}, u32[]{:S(2)}, u32[]{:S(2)}) collective-permute-start(bf16[64,384]{1,0:T(8,128)(2,1)S(1)} %add_convert_fusion.4), channel_id=1, source_target_pairs={{0,64},{8,72},{16,80},{24,88},{32,96},{40,104},{48,112},{56,120},{... | collective-permute-start | bytes 147464 | tf_op jit(solution)/shard_map/ppermute | solution.py:491
  239.5 3.3 %collective-permute-start.19 = (bf16[64,192]{0,1:T(8,128)(2,1)S(1)}, bf16[64,192]{0,1:T(8,128)(2,1)S(1)}, u32[]{:S(2)}, u32[]{:S(2)}) collective-permute-start(bf16[64,192]{0,1:T(8,128)(2,1)S(1)} %copy.124), channel_id=1, source_target_pairs={{0,2},{1,3},{2,0},{3,1},{4,6},{5,7},{6,4},{7,5},{8,10},{9,11},{10,... | collective-permute-start | bytes 73736 | tf_op jit(solution)/shard_map/ppermute | solution.py:496
  242.9 10.4 %collective-permute-start.20 = (bf16[64,192]{0,1:T(8,128)(2,1)S(1)}, bf16[64,192]{0,1:T(8,128)(2,1)S(1)}, u32[]{:S(2)}, u32[]{:S(2)}) collective-permute-start(bf16[64,192]{0,1:T(8,128)(2,1)S(1)} %add_convert_fusion.3), channel_id=1, source_target_pairs={{0,4},{1,5},{2,6},{3,7},{4,0},{5,1},{6,2},{7,3},{8,12},{9,13},{10,... | collective-permute-start | bytes 73736 | tf_op jit(solution)/shard_map/ppermute | solution.py:496
  247.4 15.8 %all-to-all-start.7 = ((bf16[128,1,192]{2,1,0:T(2,128)(2,1)}), bf16[128,1,192]{2,1,0:T(2,128)(2,1)S(1)}, u32[]{:S(2)}, u32[]{:S(2)}) async-start(bf16[128,1,192]{2,1,0:T(2,128)(2,1)} %copy.126), calls=%async_computation.7 | async-start | bytes 262144 | tf_op jit(solution)/shard_map/all_to_all | solution.py:25
  253.3 10.7 %collective-permute-start.21 = (bf16[64,192]{0,1:T(8,128)(2,1)S(1)}, bf16[64,192]{0,1:T(8,128)(2,1)S(1)}, u32[]{:S(2)}, u32[]{:S(2)}) collective-permute-start(bf16[64,192]{0,1:T(8,128)(2,1)S(1)} %add_convert_fusion.2), channel_id=1, source_target_pairs={{0,1},{1,0},{2,3},{3,2},{4,5},{5,4},{6,7},{7,6},{8,9},{9,8},{10,11... | collective-permute-start | bytes 73736 | tf_op jit(solution)/shard_map/ppermute | solution.py:496
Sparse Core Ops, SparseCore 0:
  41.3 48.2 all-gather.4
  100.6 77.7 all-gather.6
